TPU v7x, 128 devices: a whole 4x4x4 slice. The times are simulated.
128 devices in a mesh: pipe: 8 (over x, y_hi), dp: 16 (over z, y_lo, core).
Axes of the slice: x: 4, y: 4 (y_hi: 2, y_lo: 2; y = y_hi * 2 + y_lo), z: 4, core: 2. Of those that a mesh axis runs over, the one named last changes fastest.
Arguments:
- hidden_in: bfloat16 [8, 8192, 7168], P('pipe', 'dp'), may hold values from -6 to 6
- weight: bfloat16 [8, 7168, 576], P('pipe'), may hold values from -0.0625 to 0.0625
- gain: float32 [8, 512], P('pipe'), may hold values from 0.25 to 1.75
- latent_cot: bfloat16 [8, 8192, 512], P('pipe', 'dp'), may hold values from -0.06591797 to 0.06591797
- rope_cot: bfloat16 [8, 8192, 64], P('pipe', 'dp'), may hold values from -0.06591797 to 0.06591797
- master_weight: float32 [8, 7168, 576], P('pipe', 'dp'), may hold values from -0.0625 to 0.0625
- first_moment: float32 [8, 7168, 576], P('pipe', 'dp'), may hold values from -2 to 2
- second_moment: float32 [8, 7168, 576], P('pipe', 'dp'), may hold values from 0.01 to 1
- gain_master: float32 [8, 512], P('pipe', 'dp'), may hold values from 0.25 to 1.75
- gain_first: float32 [8, 512], P('pipe', 'dp'), may hold values from -2 to 2
- gain_second: float32 [8, 512], P('pipe', 'dp'), may hold values from 0.01 to 1
Outputs:
- received_grad: bfloat16 [8, 8192, 7168], P('pipe', 'dp')
- next_master: float32 [8, 7168, 576], P('pipe', 'dp')
- next_first: float32 [8, 7168, 576], P('pipe', 'dp')
- next_second: float32 [8, 7168, 576], P('pipe', 'dp')
- next_gain_master: float32 [8, 512], P('pipe', 'dp')
- next_gain_first: float32 [8, 512], P('pipe', 'dp')
- next_gain_second: float32 [8, 512], P('pipe', 'dp')
All inputs are finite; a program needn't handle non-finite values.
Results may differ from a plain program's by a relative error of at most 0.0049.
Values may be sent and summed in bfloat16 or wider, within the bound.
No kernel may reach another device: no remote copies, remote signals or barrier semaphores. Data moves between devices by JAX's collectives and lax.ppermute only.
A program may use at most 192 MiB of HBM per device.

v0:
```python
import jax
import jax.numpy as jnp
from jax import lax
from jax.sharding import PartitionSpec as P

beta_one = 0.9
beta_two = 0.95
adam_count = 10
learn_rate = 0.00022
adam_eps = 1e-08
decay_rate = 0.1


def from_behind(value, axis, steps):
    count = lax.axis_size(axis)
    first, last = (max(0, -steps), min(count, count - steps))
    return lax.ppermute(value, axis, [(source, source + steps) for source in range(first, last)])


def swapped(shard, axis, bit):
    return lax.ppermute(shard, axis, [(i, i ^ 1 << bit) for i in range(lax.axis_size(axis))])


def adamw(master, first, second, grad):
    new_first = beta_one * first + (1.0 - beta_one) * grad
    new_second = beta_two * second + (1.0 - beta_two) * grad * grad
    first_hat = new_first / (1.0 - beta_one**adam_count)
    second_hat = new_second / (1.0 - beta_two**adam_count)
    new_master = master - learn_rate * (
        first_hat / (jnp.sqrt(second_hat) + adam_eps) + decay_rate * master
    )
    return (new_master, new_first, new_second)


def on_device(
    hidden_in,
    weight,
    gain,
    latent_cot,
    rope_cot,
    master_weight,
    first_moment,
    second_moment,
    gain_master,
    gain_first,
    gain_second,
):
    tokens = hidden_in[0]
    matrix = weight[0]
    rows = tokens.shape[0]
    lat_width = latent_cot.shape[2]
    rope_width = rope_cot.shape[2]
    latent = jnp.dot(tokens, matrix[:, :lat_width], preferred_element_type=jnp.float32)
    inv = lax.rsqrt(jnp.mean(latent * latent, axis=-1, keepdims=True) + 1e-06)
    normed = latent * inv
    cot = latent_cot[0].astype(jnp.float32)
    scaled = cot * gain[0][None, :]
    latent_grad = inv * (scaled - normed * jnp.mean(scaled * normed, axis=-1, keepdims=True))
    gain_local = jnp.sum(cot * normed, axis=0)
    half = rope_width // 2
    position = jnp.arange(rows).astype(jnp.float32)
    freqs = 10000.0 ** (-2.0 * jnp.arange(half).astype(jnp.float32) / rope_width)
    angle = position[:, None] * freqs[None, :]
    cosine = jnp.cos(angle)
    sine = jnp.sin(angle)
    rope = rope_cot[0].astype(jnp.float32)
    first = rope[:, :half]
    second = rope[:, half:]
    out_grad = jnp.concatenate(
        [latent_grad, first * cosine + second * sine, second * cosine - first * sine], axis=-1
    ).astype(jnp.bfloat16)
    input_grad = lax.dot_general(
        out_grad, matrix, (((1,), (1,)), ((), ())), preferred_element_type=jnp.float32
    ).astype(jnp.bfloat16)
    received_grad = from_behind(input_grad[None], "pipe", -1)
    weight_local = lax.dot_general(
        tokens, out_grad, (((0,), (0,)), ((), ())), preferred_element_type=jnp.float32
    )
    weight_shard, gain_shard = (
        lax.psum_scatter(weight_local, "dp", scatter_dimension=0, tiled=True),
        lax.psum_scatter(gain_local, "dp", scatter_dimension=0, tiled=True),
    )
    pipe_count = lax.axis_size("pipe")
    moved_weight, moved_gain = (weight_shard, gain_shard)
    for level in range(pipe_count.bit_length() - 1):
        moved_weight, moved_gain = swapped((moved_weight, moved_gain), "pipe", level)
    weight_total = weight_shard + moved_weight
    gain_total = gain_shard + moved_gain
    next_master, next_first, next_second = adamw(
        master_weight[0], first_moment[0], second_moment[0], weight_total
    )
    next_gain_master, next_gain_first, next_gain_second = adamw(
        gain_master[0], gain_first[0], gain_second[0], gain_total
    )
    return (
        received_grad,
        next_master[None],
        next_first[None],
        next_second[None],
        next_gain_master[None],
        next_gain_first[None],
        next_gain_second[None],
    )


def solution(mesh):
    placed = (
        P("pipe", "dp", None),
        P("pipe", None, None),
        P("pipe", None),
        P("pipe", "dp", None),
        P("pipe", "dp", None),
        P("pipe", "dp", None),
        P("pipe", "dp", None),
        P("pipe", "dp", None),
        P("pipe", "dp"),
        P("pipe", "dp"),
        P("pipe", "dp"),
    )
    return jax.shard_map(
        on_device,
        mesh=mesh,
        in_specs=placed,
        out_specs=(
            P("pipe", "dp", None),
            P("pipe", "dp", None),
            P("pipe", "dp", None),
            P("pipe", "dp", None),
            P("pipe", "dp"),
            P("pipe", "dp"),
            P("pipe", "dp"),
        ),
        check_vma=False,
    )
```

profile of v0, /device:TPU:1, one launch (start us, length us, event | category | flops | bytes accessed | tf_op | source)
XLA Modules:
  0.0 531.0 jit_solution(9279861901098801266)
XLA Ops:
  7.2 0.0 reduce-scatter.4.cloned.1.call-start
  7.2 0.0 copy-start.4
  7.2 0.0 copy-start.6
  7.3 8.5 %multiply_reduce_fusion = (f32[512]{0:T(512)S(1)}, f32[512,512]{0,1:T(8,128)S(1)}) fusion(bf16[7168,576]{0,1:T(8,128)(2,1)} %bitcast.79, bf16[1,512,7168]{2,1,0:T(8,128)(2,1)} %param.11), kind=kOutput, calls=%fused_computation.23 | convolution fusion | flops 3758620160 | bytes 15730688 | tf_op jit(solution)/shard_map/dot_general | solution.py:53
  15.8 0.0 copy-done.4
  15.8 0.2 copy.25
  16.0 0.4 fusion.14
  16.5 0.3 fusion.13
  16.7 0.6 copy-done.5
  17.3 0.3 fusion.20
  17.6 11.5 %convolution_bitcast_fusion = f32[7168,576]{0,1:T(8,128)} fusion(bf16[1,512,7168]{2,1,0:T(8,128)(2,1)} %param.11, bf16[512,32]{0,1:T(8,128)(2,1)S(1)} %get-tuple-element.30, bf16[512,32]{0,1:T(8,128)(2,1)S(1)} %get-tuple-element.29, bf16[512,512]{0,1:T(8,128)(2,1)S(1)} %fusion.13), kind=kOutput, calls=%fused_computation | convolution fusion | flops 4229627904 | bytes 24444928 | tf_op jit(solution)/shard_map/dot_general | solution.py:76
  29.1 18.1 %copy.34 = f32[7168,576]{1,0:T(8,128)} copy(f32[7168,576]{0,1:T(8,128)} %convolution_bitcast_fusion) | data formatting | bytes 33030144
  47.2 0.0 reduce-scatter.4.cloned.1.call-update
  47.2 0.0 copy-start.10
  47.2 0.0 copy-start.2
  47.3 11.4 %fusion = bf16[1,512,7168]{2,1,0:T(8,128)(2,1)} fusion(bf16[512,32]{0,1:T(8,128)(2,1)S(1)} %get-tuple-element.30, bf16[512,32]{0,1:T(8,128)(2,1)S(1)} %get-tuple-element.29, bf16[512,512]{0,1:T(8,128)(2,1)S(1)} %fusion.13, bf16[1,7168,576]{1,2,0:T(8,128)(2,1)} %param.12), kind=kOutput, calls=%fused_computation.2 | convolution fusion | flops 4233297920 | bytes 16187392 | tf_op jit(solution)/shard_map/dot_general | solution.py:72
  58.7 1.3 collective-permute-start
  60.0 344.4 %reduce-scatter.4.cloned.1.call-done = f32[448,576]{1,0:T(8,128)} async-done(((f32[7168,576]{1,0:T(8,128)}), f32[448,576]{1,0:T(8,128)}) %reduce-scatter.4.cloned.1.call-update) | async-done | bytes 1032208 | tf_op jit(solution)/shard_map/reduce_scatter | solution.py:80
  404.4 2.4 collective-permute-start.1
  406.9 23.5 %collective-permute-done.1 = f32[448,576]{1,0:T(8,128)S(1)} collective-permute-done((f32[448,576]{1,0:T(8,128)}, f32[448,576]{1,0:T(8,128)S(1)}, u32[]{:S(2)}, u32[]{:S(2)}) %collective-permute-start.1) | collective-permute-done | bytes 1032224 | tf_op jit(solution)/shard_map/ppermute | solution.py:21
  430.3 1.2 collective-permute-start.2
  431.5 22.2 %collective-permute-done.2 = f32[448,576]{1,0:T(8,128)} collective-permute-done((f32[448,576]{1,0:T(8,128)S(1)}, f32[448,576]{1,0:T(8,128)}, u32[]{:S(2)}, u32[]{:S(2)}) %collective-permute-start.2) | collective-permute-done | bytes 1032224 | tf_op jit(solution)/shard_map/ppermute | solution.py:21
  453.7 2.7 collective-permute-start.3
  456.4 0.6 dynamic-slice
  457.7 32.9 %all-reduce = f32[512]{0:T(512)S(1)} all-reduce(f32[512]{0:T(512)S(1)} %get-tuple-element.21), channel_id=3, replica_groups=mesh['pipe'=8,'dp'=16] {'dp'}, use_global_device_ids=true, to_apply=%region_4.0.clone | all-reduce | flops 512 | bytes 4096
  490.6 0.1 dynamic-slice.1
  490.6 2.7 collective-permute-start.4
  493.3 0.4 copy.26
  493.7 0.8 collective-permute-done.4
  494.5 0.0 collective-permute-start.5
  494.5 0.4 copy.27
  494.9 0.0 copy-start.7
  494.9 0.0 copy-start.8
  494.9 0.0 copy-start.9
  495.0 2.1 collective-permute-done.5
  497.0 0.6 collective-permute-start.6
  497.6 1.6 copy.30
  499.2 1.9 collective-permute-done.6
  501.1 1.2 fusion.26
  502.3 0.0 collective-permute-done
  502.3 2.7 copy.35
  505.0 0.0 collective-permute-done.3
  505.0 2.7 copy.29
  507.7 4.3 fusion.31
  512.0 2.8 copy.31
  514.7 1.4 copy.32
  516.1 1.4 copy.33
  517.5 6.6 %copy.37 = bf16[1,512,7168]{2,1,0:T(8,128)(2,1)} copy(bf16[1,512,7168]{2,1,0:T(8,128)(2,1)} %collective-permute-done) | data formatting | bytes 14680064
  (18 shorter events, 0.1 us)
Async XLA Ops:
  7.2 397.3 %reduce-scatter.4.cloned.1.call-start = ((), (), s32[]{:S(2)}) async-start(), calls=%async_computation.1 | async-start | bytes 19496960 | tf_op jit(solution)/shard_map/reduce_scatter | solution.py:80
  7.2 8.6 %copy-start.4 = (bf16[1,512,512]{2,1,0:T(8,128)(2,1)S(1)}, bf16[1,512,512]{2,1,0:T(8,128)(2,1)}, u32[]{:S(2)}) copy-start(bf16[1,512,512]{2,1,0:T(8,128)(2,1)} %param.14) | copy-start | bytes 1572868
  7.2 8.8 %copy-start.6 = (f32[1,512]{1,0:T(1,128)S(1)}, f32[1,512]{1,0:T(1,128)}, u32[]{:S(2)}) copy-start(f32[1,512]{1,0:T(1,128)} %param.13) | copy-start | bytes 6148
  16.5 0.8 copy-start.5
  47.2 409.2 %copy-start.10 = (u32[128]{0:T(128)S(1)}, u32[128]{0:T(128)}, u32[]{:S(2)}) copy-start(u32[128]{0:T(128)} %constant.56) | copy-start | bytes 1540
  47.2 446.1 %copy-start.2 = (f32[1,448,576]{2,1,0:T(8,128)S(1)}, f32[1,448,576]{2,1,0:T(8,128)}, u32[]{:S(2)}) copy-start(f32[1,448,576]{2,1,0:T(8,128)} %param.16) | copy-start | bytes 3096580
  58.7 443.6 %collective-permute-start = (bf16[1,512,7168]{2,1,0:T(8,128)(2,1)}, bf16[1,512,7168]{2,1,0:T(8,128)(2,1)}, u32[]{:S(2)}, u32[]{:S(2)}) collective-permute-start(bf16[1,512,7168]{2,1,0:T(8,128)(2,1)} %fusion), channel_id=1, source_target_pairs={{16,0},{32,16},{48,32},{64,48},{80,64},{96,80},{112,96},{17,1},{33... | collective-permute-start | bytes 22020104 | tf_op jit(solution)/shard_map/ppermute | solution.py:17
  404.4 25.9 %collective-permute-start.1 = (f32[448,576]{1,0:T(8,128)}, f32[448,576]{1,0:T(8,128)S(1)}, u32[]{:S(2)}, u32[]{:S(2)}) collective-permute-start(f32[448,576]{1,0:T(8,128)} %reduce-scatter.4.cloned.1.call-done), channel_id=1, source_target_pairs={{0,16},{16,0},{32,48},{48,32},{64,80},{80,64},{96,112},{112,96},{1... | collective-permute-start | bytes 3096584 | tf_op jit(solution)/shard_map/ppermute | solution.py:21
  430.3 23.4 %collective-permute-start.2 = (f32[448,576]{1,0:T(8,128)S(1)}, f32[448,576]{1,0:T(8,128)}, u32[]{:S(2)}, u32[]{:S(2)}) collective-permute-start(f32[448,576]{1,0:T(8,128)S(1)} %collective-permute-done.1), channel_id=1, source_target_pairs={{0,32},{16,48},{32,0},{48,16},{64,96},{80,112},{96,64},{112,80},{1... | collective-permute-start | bytes 3096584 | tf_op jit(solution)/shard_map/ppermute | solution.py:21
  453.7 51.3 %collective-permute-start.3 = (f32[448,576]{1,0:T(8,128)}, f32[448,576]{1,0:T(8,128)}, u32[]{:S(2)}, u32[]{:S(2)}) collective-permute-start(f32[448,576]{1,0:T(8,128)} %collective-permute-done.2), channel_id=1, source_target_pairs={{0,64},{16,80},{32,96},{48,112},{64,0},{80,16},{96,32},{112,48},{1... | collective-permute-start | bytes 3096584 | tf_op jit(solution)/shard_map/ppermute | solution.py:21
  456.4 38.1 %copy-start.3 = (f32[1,448,576]{2,1,0:T(8,128)S(1)}, f32[1,448,576]{2,1,0:T(8,128)}, u32[]{:S(2)}) copy-start(f32[1,448,576]{2,1,0:T(8,128)} %param.17) | copy-start | bytes 3096580
  490.6 3.9 collective-permute-start.4
  494.5 2.5 collective-permute-start.5
  494.9 6.2 %copy-start.7 = (f32[1,32]{1,0:T(1,128)S(1)}, f32[1,32]{1,0:T(1,128)}, u32[]{:S(2)}) copy-start(f32[1,32]{1,0:T(1,128)} %param.19) | copy-start | bytes 388
  494.9 6.2 %copy-start.8 = (f32[1,32]{1,0:T(1,128)S(1)}, f32[1,32]{1,0:T(1,128)}, u32[]{:S(2)}) copy-start(f32[1,32]{1,0:T(1,128)} %param.20) | copy-start | bytes 388
  494.9 6.1 %copy-start.9 = (f32[1,32]{1,0:T(1,128)S(1)}, f32[1,32]{1,0:T(1,128)}, u32[]{:S(2)}) copy-start(f32[1,32]{1,0:T(1,128)} %param.21) | copy-start | bytes 388
  497.0 4.1 collective-permute-start.6
  512.0 2.8 copy-start.1
  514.7 1.4 copy-start
Sparse Core Ops, SparseCore 0:
  47.4 357.0 reduce-scatter.3
where the time goes:
time: 535 us; the launch traced here: 531 us
  waiting for transfers between devices  395 us (74%)
  local copies, waits for them, and re-layouts  39.4 us (7%)
  blocking collectives  32.9 us (6%)
  matrix products  31.5 us (6%)
  between operations  14.9 us (3%)
  starting transfers between devices  11 us (2%)
  other arithmetic  6.59 us (1%)
    reduce_scatter x1, waiting for transfers between devices, on_device(): lax.psum_scatter(weight_local, 'dp', scatter_dimension=0, tiled=True)  344 us
    ppermute x6, waiting for transfers between devices, swapped(): lax.ppermute(shard, axis, [(i, i ^ 1 << bit) for i in range(lax.axis_size...  50.3 us
    unnamed x34, local copies, waits for them, and re-layouts  36.7 us
    unnamed x1, blocking collectives  32.9 us
    dot_general x1, matrix products, on_device(): lax.dot_general(tokens, out_grad, (((0,), (0,)), ((), ())), preferred_ele...  11.5 us
    dot_general x1, matrix products, on_device(): lax.dot_general(out_grad, matrix, (((1,), (1,)), ((), ())), preferred_ele...  11.4 us
  transfers between devices with their start and end apart: 8, of which 6 were waited for; matrix products, arithmetic and copies ran while one was open for 3% of the time, Pallas kernels for 0%

commit v1 on v0

v1 whole, which is shorter than its diff:
```python
import jax
import jax.numpy as jnp
from jax import lax
from jax.experimental import pallas as pl
from jax.experimental.pallas import tpu as pltpu
from jax.sharding import PartitionSpec as P

beta_one = 0.9
beta_two = 0.95
adam_count = 10
learn_rate = 0.00022
adam_eps = 1e-08
decay_rate = 0.1

RANKS, SHARDS = 8, 16
TOK, WIDTH, LAT, ROPE = 512, 7168, 512, 64
COLS = LAT + ROPE
BLOCK = WIDTH // 8
TILE = 512
HALF = COLS // 2
ROWS_A = 3 * HALF + HALF // 2
ROWS_B = ROWS_A + 16
EXT = COLS + 16
BF, F32 = jnp.bfloat16, jnp.float32
MIB = 1 << 20


def params(mib):
    return pltpu.CompilerParams(vmem_limit_bytes=mib * MIB)


def cost(flops, moved):
    return pl.CostEstimate(flops=flops, bytes_accessed=moved, transcendentals=0)


def moved(value, target):
    pairs = []
    for r in range(RANKS):
        for d in range(SHARDS):
            to = target(r, d)
            if 0 <= to[0] < RANKS:
                pairs.append((r * SHARDS + d, to[0] * SHARDS + to[1]))
    return lax.ppermute(value, ("pipe", "dp"), pairs)


def to_core(r, d):
    return r, d ^ 1


def to_ylo(r, d):
    return r, d ^ 2


def to_z(steps):
    return lambda r, d: (r, (d + 4 * steps) % SHARDS)


def to_mirror(r, d):
    return RANKS - 1 - r, d


def to_before(r, d):
    return r - 1, d


def to_before_near(r, d):
    return r - 1, d ^ 2


def cut_kernel(s, hidden, weight, part, piece):
    part[...] = hidden[:, pl.ds(pl.multiple_of(384 * (1 - s[2]), 128), TILE)]

    @pl.when(pl.program_id(0) == 0)
    def _():
        piece[...] = weight[...]


def cut(s, hidden, weight):
    return pl.pallas_call(
        cut_kernel,
        grid_spec=pltpu.PrefetchScalarGridSpec(
            num_scalar_prefetch=1,
            grid=(8,),
            in_specs=[
                pl.BlockSpec((TOK, BLOCK), lambda b, s: (0, b)),
                pl.BlockSpec((HALF, BLOCK), lambda b, s: (s[2], 2 * s[0] + 1 - s[1])),
            ],
            out_specs=[
                pl.BlockSpec((TOK, TILE), lambda b, s: (0, b)),
                pl.BlockSpec((HALF, BLOCK), lambda b, s: (0, 0)),
            ],
        ),
        out_shape=[
            jax.ShapeDtypeStruct((TOK, 8 * TILE), BF),
            jax.ShapeDtypeStruct((HALF, BLOCK), BF),
        ],
        compiler_params=params(24),
        cost_estimate=cost(0, 12_500_000),
        name="cut",
    )(s, hidden, weight)


def latent_kernel(hidden, weight, cot, gain, rope, out, total):
    k = pl.program_id(0)
    part = lax.dot_general(
        hidden[...], weight[...], (((1,), (1,)), ((), ())), preferred_element_type=F32
    )

    @pl.when(k == 0)
    def _():
        total[...] = part

    @pl.when(k > 0)
    def _():
        total[...] += part

    @pl.when(k == pl.num_programs(0) - 1)
    def _():
        latent = total[...]
        inv = lax.rsqrt(jnp.mean(latent * latent, axis=-1, keepdims=True) + 1e-06)
        normed = latent * inv
        c = cot[...].astype(F32)
        scaled = c * gain[...]
        grad = inv * (scaled - normed * jnp.mean(scaled * normed, axis=-1, keepdims=True))
        gain_part = jnp.sum(c * normed, axis=0, keepdims=True)
        out[0:LAT, :] = grad.T.astype(BF)
        out[LAT:COLS, :] = rope[...]
        high = gain_part.astype(BF)
        low = (gain_part - high.astype(F32)).astype(BF)
        row = lax.broadcasted_iota(jnp.int32, (16, LAT), 0)
        high = jnp.broadcast_to(high.astype(F32), (16, LAT))
        low = jnp.broadcast_to(low.astype(F32), (16, LAT))
        both = jnp.where(row == 0, high, jnp.where(row == 1, low, 0.0))
        out[COLS:EXT, :] = both.astype(BF)


def latent_step(hidden, weight, cot, gain, rope):
    width = 1024
    return pl.pallas_call(
        latent_kernel,
        grid=(WIDTH // width,),
        in_specs=[
            pl.BlockSpec((TOK, width), lambda k: (0, k)),
            pl.BlockSpec((LAT, width), lambda k: (0, k)),
            pl.BlockSpec((TOK, LAT), lambda k: (0, 0)),
            pl.BlockSpec((1, LAT), lambda k: (0, 0)),
            pl.BlockSpec((ROPE, TOK), lambda k: (0, 0)),
        ],
        out_specs=pl.BlockSpec((EXT, TOK), lambda k: (0, 0)),
        out_shape=jax.ShapeDtypeStruct((EXT, TOK), BF),
        scratch_shapes=[pltpu.VMEM((TOK, LAT), F32)],
        compiler_params=params(32),
        cost_estimate=cost(2 * TOK * WIDTH * LAT, 16_000_000),
        name="latent_grad",
    )(hidden, weight, cot, gain, rope)


def weight_kernel(
    s, hidden, other, grad, grad_other, own_a, z1, z2, z3, own_b, send_b, gain
):
    g = pl.program_id(0)
    k, e = g // 2, g % 2
    core = s[2]

    @pl.when(g == 0)
    def _():
        sums = jnp.zeros((1, LAT), F32)
        for ref in (grad, grad_other):
            pair = ref[COLS:EXT, :].astype(F32)
            sums = sums + pair[0:1] + pair[1:2]
        gain[...] = jnp.zeros_like(gain)
        for i in range(4):
            gain[i : i + 1, :] = sums[:, 128 * i : 128 * i + 128]

    own = hidden[:, pl.ds(pl.multiple_of(384 * core, 128), TILE)]
    lane = lax.broadcasted_iota(jnp.int32, (HALF // 2, 128), 1)
    first = core == 0

    def packed(h):
        rows = slice(h * HALF, h * HALF + HALF)
        full = jnp.dot(grad[rows, :], own, preferred_element_type=F32)
        full += jnp.dot(grad_other[rows, :], other[...], preferred_element_type=F32)
        col = [full[:, 128 * j : 128 * j + 128] for j in range(4)]
        edge = jnp.where(first, col[3], col[0])
        top, low = edge[: HALF // 2], edge[HALF // 2 :]
        left = jnp.where(first, top, pltpu.roll(top, 64, 1))
        right = jnp.where(first, pltpu.roll(low, 64, 1), low)
        return [jnp.where(first, col[i], col[i + 1]) for i in range(3)] + [
            jnp.where(lane < 64, left, right)
        ]

    a, b = packed(0), packed(1)

    def put(ref, parts, with_gain):
        at = 0
        for part in parts:
            n = part.shape[0]
            ref[0, at : at + n, :] = part.astype(ref.dtype)
            at += n
        if with_gain:
            ref[0, at : at + 16, :] = gain[...].astype(ref.dtype)

    for number, ref in enumerate((own_a, z1, z2, z3)):
        pl.when(k == number)(lambda ref=ref: put(ref, a, False))
    pl.when(e == 0)(lambda: put(own_b, b, True))
    pl.when(e == 1)(lambda: put(send_b, b, True))


def weight_step(s, hidden, other, grad, grad_other):
    def at(k):
        return lambda g, s: (jnp.clip(g - 2 * k, 0, 1), 0, 0)

    def block(g, s):
        z = lax.rem(s[0] + g // 2, 4)
        return 2 * z + lax.rem(s[1] + g % 2, 2)

    return pl.pallas_call(
        weight_kernel,
        grid_spec=pltpu.PrefetchScalarGridSpec(
            num_scalar_prefetch=1,
            grid=(8,),
            in_specs=[
                pl.BlockSpec((TOK, BLOCK), lambda g, s: (0, block(g, s))),
                pl.BlockSpec((TOK, TILE), lambda g, s: (0, block(g, s))),
                pl.BlockSpec((EXT, TOK), lambda g, s: (0, 0)),
                pl.BlockSpec((EXT, TOK), lambda g, s: (0, 0)),
            ],
            out_specs=[pl.BlockSpec((1, ROWS_A, 128), at(k)) for k in range(4)]
            + [pl.BlockSpec((1, ROWS_B, 128), lambda g, s: (g // 2, 0, 0))] * 2,
            scratch_shapes=[pltpu.VMEM((16, 128), F32)],
        ),
        out_shape=[jax.ShapeDtypeStruct((2, ROWS_A, 128), F32)]
        + [jax.ShapeDtypeStruct((2, ROWS_A, 128), BF)] * 3
        + [
            jax.ShapeDtypeStruct((4, ROWS_B, 128), F32),
            jax.ShapeDtypeStruct((4, ROWS_B, 128), BF),
        ],
        compiler_params=params(40),
        cost_estimate=cost(2 * 2 * TOK * 8 * TILE * COLS, 20_000_000),
        name="weight_grad",
    )(s, hidden, other, grad, grad_other)


def sum_a_kernel(own, r1, r2, r3, keep, send):
    total = own[0] + r1[0].astype(F32) + r2[0].astype(F32) + r3[0].astype(F32)

    @pl.when(pl.program_id(0) == 0)
    def _():
        keep[...] = total

    @pl.when(pl.program_id(0) == 1)
    def _():
        send[...] = total.astype(BF)


def sum_a(own, r1, r2, r3):
    return pl.pallas_call(
        sum_a_kernel,
        grid=(2,),
        in_specs=[pl.BlockSpec((1, ROWS_A, 128), lambda e: (e, 0, 0))] * 4,
        out_specs=[pl.BlockSpec((ROWS_A, 128), lambda e: (0, 0))] * 2,
        out_shape=[
            jax.ShapeDtypeStruct((ROWS_A, 128), F32),
            jax.ShapeDtypeStruct((ROWS_A, 128), BF),
        ],
        compiler_params=params(16),
        cost_estimate=cost(0, 3_500_000),
        name="sum_z",
    )(own, r1, r2, r3)


def sum_b_kernel(own, r, keep, s1, s2, s3):
    total = own[0] + r[0].astype(F32)
    k = pl.program_id(0)
    for number, ref in enumerate((keep, s1, s2, s3)):

        def put(ref=ref):
            ref[...] = total.astype(ref.dtype)

        pl.when(k == number)(put)


def sum_b(own, r):
    return pl.pallas_call(
        sum_b_kernel,
        grid=(4,),
        in_specs=[pl.BlockSpec((1, ROWS_B, 128), lambda k: (k, 0, 0))] * 2,
        out_specs=[pl.BlockSpec((ROWS_B, 128), lambda k: (0, 0))] * 4,
        out_shape=[jax.ShapeDtypeStruct((ROWS_B, 128), F32)]
        + [jax.ShapeDtypeStruct((ROWS_B, 128), BF)] * 3,
        compiler_params=params(16),
        cost_estimate=cost(0, 4_500_000),
        name="sum_y",
    )(own, r)


def sum_all_kernel(keep_a, ra, keep_b, r1, r2, r3, total, send):
    a = keep_a[...] + ra[...].astype(F32)
    b = keep_b[...] + r1[...].astype(F32) + r2[...].astype(F32) + r3[...].astype(F32)
    total[:ROWS_A, :] = a
    total[ROWS_A:, :] = b
    send[:ROWS_A, :] = a.astype(BF)
    send[ROWS_A:, :] = b.astype(BF)


def sum_all(*parts):
    return pl.pallas_call(
        sum_all_kernel,
        out_shape=[
            jax.ShapeDtypeStruct((ROWS_A + ROWS_B, 128), F32),
            jax.ShapeDtypeStruct((ROWS_A + ROWS_B, 128), BF),
        ],
        compiler_params=params(16),
        cost_estimate=cost(0, 4_000_000),
        name="sum_shard",
    )(*parts)


def adamw(master, first, second, grad):
    new_first = beta_one * first + (1.0 - beta_one) * grad
    new_second = beta_two * second + (1.0 - beta_two) * grad * grad
    first_hat = new_first / (1.0 - beta_one**adam_count)
    second_hat = new_second / (1.0 - beta_two**adam_count)
    new_master = master - learn_rate * (
        first_hat / (jnp.sqrt(second_hat) + adam_eps) + decay_rate * master
    )
    return (new_master, new_first, new_second)


def adam_kernel(s, own, far, master, first, second, n_master, n_first, n_second, gain, grad):
    total = own[...] + far[...].astype(F32)
    core = s[2]
    gain[...] = total[2 * ROWS_A : 2 * ROWS_A + 8]

    def both(lo, n):
        return [total[h * ROWS_A + lo : h * ROWS_A + lo + n] for h in range(2)]

    for i in range(3):
        block = jnp.concatenate(both(i * HALF, HALF), axis=0)
        grad[pl.ds(pl.multiple_of(64 * core + 128 * i, 64), 128), :] = block.T
    edge = []
    for part in both(3 * HALF, HALF // 2):
        edge += [part, pltpu.roll(part, 64, 1)]
    block = jnp.concatenate(edge, axis=0)
    grad[pl.ds(pl.multiple_of(384 * (1 - core), 64), 64), :] = block.T[:64]
    n_master[...], n_first[...], n_second[...] = adamw(
        master[...], first[...], second[...], grad[...]
    )


def adam_step(s, own, far, master, first, second):
    shape = jax.ShapeDtypeStruct(master.shape, F32)
    spec = pl.BlockSpec(memory_space=pltpu.VMEM)
    return pl.pallas_call(
        adam_kernel,
        in_specs=[pl.BlockSpec(memory_space=pltpu.SMEM)] + [spec] * 5,
        out_specs=[spec] * 4,
        out_shape=[shape] * 3 + [jax.ShapeDtypeStruct((8, 128), F32)],
        scratch_shapes=[pltpu.VMEM(master.shape, F32)],
        compiler_params=params(32),
        cost_estimate=cost(0, 9_000_000),
        name="adamw",
    )(s, own, far, master, first, second)


def input_kernel(grad, weight, out, turned):
    @pl.when(pl.program_id(0) == 0)
    def _():
        turned[...] = grad[:COLS, :].astype(F32).T.astype(BF)

    block = weight[...].reshape(COLS, BLOCK)
    out[...] = jnp.dot(turned[...], block, preferred_element_type=F32).astype(BF)


def input_step(grad, weight):
    return pl.pallas_call(
        input_kernel,
        grid=(8,),
        in_specs=[
            pl.BlockSpec((EXT, TOK), lambda b: (0, 0)),
            pl.BlockSpec((2, HALF, BLOCK), lambda b: (b, 0, 0)),
        ],
        out_specs=pl.BlockSpec((TOK, BLOCK), lambda b: (0, b)),
        out_shape=jax.ShapeDtypeStruct((TOK, WIDTH), BF),
        scratch_shapes=[pltpu.VMEM((TOK, COLS), BF)],
        compiler_params=params(32),
        cost_estimate=cost(2 * TOK * WIDTH * COLS, 16_000_000),
        name="input_grad",
    )(grad, weight)


def rope_step(rope_cot):
    half = ROPE // 2
    position = jnp.arange(TOK).astype(F32)
    freqs = 10000.0 ** (-2.0 * jnp.arange(half).astype(F32) / ROPE)
    angle = freqs[:, None] * position[None, :]
    cosine = jnp.cos(angle)
    sine = jnp.sin(angle)
    rope = rope_cot.T.astype(F32)
    first, second = rope[:half], rope[half:]
    return jnp.concatenate(
        [first * cosine + second * sine, second * cosine - first * sine], axis=0
    ).astype(BF)


def on_device(
    hidden_in,
    weight,
    gain,
    latent_cot,
    rope_cot,
    master_weight,
    first_moment,
    second_moment,
    gain_master,
    gain_first,
    gain_second,
):
    shard = lax.axis_index("dp")
    s = jnp.stack([shard // 4, (shard // 2) % 2, shard % 2]).astype(jnp.int32)
    hidden = hidden_in[0]
    turned = weight[0].T
    part, piece = cut(s, hidden, turned)
    piece_next = moved(piece, to_before_near)
    other = moved(part, to_core)
    weight_next = lax.all_gather(piece_next, "dp")
    grad = latent_step(hidden, turned, latent_cot[0], gain, rope_step(rope_cot[0]))
    grad_other = moved(grad, to_core)
    grad_next = moved(grad, to_before)
    own_a, z1, z2, z3, own_b, send_b = weight_step(s, hidden, other, grad, grad_other)
    r1, r2, r3 = moved(z1, to_z(1)), moved(z2, to_z(2)), moved(z3, to_z(3))
    rb = moved(send_b, to_ylo)
    keep_a, send_a = sum_a(own_a, r1, r2, r3)
    keep_b, s1, s2, s3 = sum_b(own_b, rb)
    ra = moved(send_a, to_ylo)
    r1, r2, r3 = moved(s1, to_z(1)), moved(s2, to_z(2)), moved(s3, to_z(3))
    total, send = sum_all(keep_a, ra, keep_b, r1, r2, r3)
    far = moved(send, to_mirror)
    received = input_step(grad_next, weight_next)
    next_master, next_first, next_second, gain_rows = adam_step(
        s, total, far, master_weight[0], first_moment[0], second_moment[0]
    )
    gain_total = lax.dynamic_slice(gain_rows[:4].reshape(LAT), (shard * 32,), (32,))
    next_gain = adamw(gain_master[0], gain_first[0], gain_second[0], gain_total)
    return (
        received[None],
        next_master[None],
        next_first[None],
        next_second[None],
        *(value[None] for value in next_gain),
    )


def solution(mesh):
    tokens, shared = P("pipe", "dp", None), P("pipe", None)
    split = P("pipe", "dp")
    return jax.shard_map(
        on_device,
        mesh=mesh,
        in_specs=(tokens, P("pipe", None, None), shared) + (tokens,) * 5 + (split,) * 3,
        out_specs=(tokens,) * 4 + (split,) * 3,
        check_vma=False,
    )
```

time: 535 us -> 181 us (0.34)
  waiting for transfers between devices: 395 us -> 90.4 us
  Pallas kernels: 0 us -> 37.2 us
  blocking collectives: 32.9 us -> 0 us
  matrix products: 31.5 us -> 0 us
  local copies, waits for them, and re-layouts: 39.4 us -> 21.2 us
  other arithmetic: 6.59 us -> 1.04 us
    reduce_scatter x1 -> x0, waiting for transfers between devices: 344 us -> none  [on_device(): lax.psum_scatter(weight_local, 'dp', scatter_dimension=0, tiled=True)]
    ppermute x7 -> x13, waiting for transfers between devices: 50.3 us -> 90.4 us  [moved(): return lax.ppermute(value, ('pipe', 'dp'), pairs)]
    pallas_call x0 -> x8, Pallas kernels: none -> 37.2 us  [the longest x1 10.6 us: weight_step(): pl.pallas_call(weight_kernel, grid_spec=pltpu.PrefetchScalarGridSpec(num_...]
    unnamed x1 -> x0, blocking collectives: 32.9 us -> none
    dot_general x3 -> x0, matrix products: 31.5 us -> none  [the longest x1 11.5 us: on_device(): lax.dot_general(tokens, out_grad, (((0,), (0,)), ((), ())), preferred_ele...]
    unnamed x34 -> x36, local copies, waits for them, and re-layouts: 36.7 us -> 21.2 us
    ppermute x7 -> x13, starting transfers between devices: 10.9 us -> 16.2 us  [moved(): return lax.ppermute(value, ('pipe', 'dp'), pairs)]
  transfers between devices with their start and end apart: 8 -> 14, of which waited for: 6 -> 8; matrix products, arithmetic and copies ran while one was open for 3% -> 1% of each run, Pallas kernels for 0% -> 14%
where the time goes in v1:
time: 181 us; the launch traced here: 180 us
  waiting for transfers between devices  90.4 us (50%)
  Pallas kernels  37.2 us (21%)
  local copies, waits for them, and re-layouts  21.2 us (12%)
  starting transfers between devices  16.3 us (9%)
  between operations  14.2 us (8%)
    ppermute x13, waiting for transfers between devices, moved(): return lax.ppermute(value, ('pipe', 'dp'), pairs)  90.4 us
    unnamed x36, local copies, waits for them, and re-layouts  21.2 us
    ppermute x13, starting transfers between devices, moved(): return lax.ppermute(value, ('pipe', 'dp'), pairs)  16.2 us
    pallas_call x1, Pallas kernels, weight_step(): pl.pallas_call(weight_kernel, grid_spec=pltpu.PrefetchScalarGridSpec(num_...  10.6 us
    pallas_call x1, Pallas kernels, input_step(): pl.pallas_call(input_kernel, grid=(8,), in_specs=[pl.BlockSpec((EXT, TOK)...  9.86 us
    pallas_call x1, Pallas kernels, latent_step(): pl.pallas_call(latent_kernel, grid=(WIDTH // width,), in_specs=[pl.BlockS...  8.34 us
    pallas_call x1, Pallas kernels, adam_step(): pl.pallas_call(adam_kernel, in_specs=[pl.BlockSpec(memory_space=pltpu.SME...  4.46 us
  transfers between devices with their start and end apart: 14, of which 8 were waited for; matrix products, arithmetic and copies ran while one was open for 1% of the time, Pallas kernels for 14%

profile of v1, /device:TPU:1, one launch (start us, length us, event | category | flops | bytes accessed | tf_op | source)
XLA Modules:
  0.0 180.3 jit_solution(1266092090047348333)
XLA Ops:
  7.2 0.0 all-gather.3.cloned.1.call-start
  7.3 0.1 pad_add_fusion.s
  7.3 3.3 %copy-done = bf16[1,7168,576]{1,2,0:T(8,128)(2,1)S(1)} copy-done((bf16[1,7168,576]{1,2,0:T(8,128)(2,1)S(1)}, bf16[1,7168,576]{1,2,0:T(8,128)(2,1)}, u32[]{:S(2)}) %copy-start) | copy-done | bytes 8257560
  10.7 3.1 %copy-done.2 = bf16[1,512,7168]{2,1,0:T(8,128)(2,1)S(1)} copy-done((bf16[1,512,7168]{2,1,0:T(8,128)(2,1)S(1)}, bf16[1,512,7168]{2,1,0:T(8,128)(2,1)}, u32[]{:S(2)}) %copy-start.2) | copy-done | bytes 7340056
  13.8 2.1 %cut.1 = (bf16[512,4096]{1,0:T(8,128)(2,1)S(1)}, bf16[288,896]{1,0:T(8,128)(2,1)S(1)}) custom-call(s32[3]{0:T(128)S(1)} %pad_add_fusion.s, bf16[512,7168]{1,0:T(8,128)(2,1)S(1)} %bitcast.47, bf16[576,7168]{1,0:T(8,128)(2,1)S(1)} %bitcast.44), custom_call_target="tpu_custom_call" | custom-call | bytes 12500000 | tf_op jit(solution)/shard_map/cut/pallas_call | solution.py:79
  15.9 0.0 copy-start.12
  15.9 2.0 %copy-done.12 = bf16[512,4096]{1,0:T(8,128)(2,1)} copy-done((bf16[512,4096]{1,0:T(8,128)(2,1)}, bf16[512,4096]{1,0:T(8,128)(2,1)S(1)}, u32[]{:S(2)}) %copy-start.12) | copy-done | bytes 4194328
  17.9 1.3 collective-permute-start.1
  19.2 15.5 %collective-permute-done.1 = bf16[288,896]{1,0:T(8,128)(2,1)S(1)} collective-permute-done((bf16[288,896]{1,0:T(8,128)(2,1)S(1)}, bf16[288,896]{1,0:T(8,128)(2,1)S(1)}, u32[]{:S(2)}, u32[]{:S(2)}) %collective-permute-start.1) | collective-permute-done | bytes 516128 | tf_op jit(solution)/shard_map/ppermute | solution.py:43
  34.7 0.8 copy-done.13
  35.5 0.0 all-gather.3.cloned.1.call-update
  35.5 1.5 collective-permute-start.2
  37.0 0.3 fusion.5
  37.4 0.0 copy-start.1
  37.4 3.3 %copy-done.1 = bf16[1,7168,576]{1,2,0:T(8,128)(2,1)S(1)} copy-done((bf16[1,7168,576]{1,2,0:T(8,128)(2,1)S(1)}, bf16[1,7168,576]{1,2,0:T(8,128)(2,1)}, u32[]{:S(2)}) %copy-start.1) | copy-done | bytes 8257560
  40.7 3.1 %copy-done.3 = bf16[1,512,7168]{2,1,0:T(8,128)(2,1)S(1)} copy-done((bf16[1,512,7168]{2,1,0:T(8,128)(2,1)S(1)}, bf16[1,512,7168]{2,1,0:T(8,128)(2,1)}, u32[]{:S(2)}) %copy-start.3) | copy-done | bytes 7340056
  43.8 8.3 %latent_grad.1.grad = bf16[592,512]{1,0:T(8,128)(2,1)} custom-call(bf16[512,7168]{1,0:T(8,128)(2,1)S(1)} %bitcast.48, bf16[576,7168]{1,0:T(8,128)(2,1)S(1)} %bitcast.45, bf16[512,512]{1,0:T(8,128)(2,1)S(1)} %bitcast.53, f32[1,512]{1,0:T(1,128)S(1)} %copy-done.11, bf16[64,512]{1,0:T(8,128)(2,1)S(1)} %pad_maximum_fusion.rope), custom_call_target="tpu_custom_call" | custom-call | flops 3758096384 | bytes 16000000 | tf_op jit(solution)/shard_map/latent_grad/pallas_call | solution.py:139
  52.1 0.0 collective-permute-start.3
  52.2 2.2 %collective-permute-done.3.grad_other = bf16[592,512]{1,0:T(8,128)(2,1)S(1)} collective-permute-done((bf16[592,512]{1,0:T(8,128)(2,1)}, bf16[592,512]{1,0:T(8,128)(2,1)S(1)}, u32[]{:S(2)}, u32[]{:S(2)}) %collective-permute-start.3) | collective-permute-done | bytes 606240 | tf_op jit(solution)/shard_map/ppermute | solution.py:43
  54.4 10.6 %weight_grad.1 = (f32[2,1008,128]{2,1,0:T(8,128)S(1)}, bf16[2,1008,128]{2,1,0:T(8,128)(2,1)S(1)}, bf16[2,1008,128]{2,1,0:T(8,128)(2,1)S(1)}, bf16[2,1008,128]{2,...) custom-call(s32[3]{0:T(128)S(1)} %pad_add_fusion.s, bf16[512,7168]{1,0:T(8,128)(2,1)} %bitcast.46, ...), custom_call_target="tpu_custom_call" | custom-call | flops 4831838208 | bytes 20000000 | tf_op jit(solution)/shard_map/weight_grad/pallas_call | solution.py:217
  64.9 0.1 collective-permute-start.8
  65.0 1.7 collective-permute-start.4
  66.7 3.3 %collective-permute-start.5 = (bf16[2,1008,128]{2,1,0:T(8,128)(2,1)S(1)}, bf16[2,1008,128]{2,1,0:T(8,128)(2,1)S(1)}, u32[]{:S(2)}, u32[]{:S(2)}) collective-permute-start(bf16[2,1008,128]{2,1,0:T(8,128)(2,1)S(1)} %get-tuple-element.31), channel_id=1, source_target_pairs={{0,8},{1,9},{2,10},{3,11},{4,12},{5,13},{6,14},{7,15},{8,0},{9,1},... | collective-permute-start | bytes 1548296 | tf_op jit(solution)/shard_map/ppermute | solution.py:43
  70.0 0.7 collective-permute-start.6
  70.7 41.1 %collective-permute-done.8.r = bf16[4,1024,128]{2,1,0:T(8,128)(2,1)S(1)} collective-permute-done((bf16[4,1024,128]{2,1,0:T(8,128)(2,1)S(1)}, bf16[4,1024,128]{2,1,0:T(8,128)(2,1)S(1)}, u32[]{:S(2)}, u32[]{:S(2)}) %collective-permute-start.8) | collective-permute-done | bytes 1048608 | tf_op jit(solution)/shard_map/ppermute | solution.py:43
  111.8 0.4 sum_y.1
  112.2 0.1 collective-permute-start.10
  112.3 2.6 %collective-permute-start.11 = (bf16[1024,128]{1,0:T(8,128)(2,1)S(1)}, bf16[1024,128]{1,0:T(8,128)(2,1)S(1)}, u32[]{:S(2)}, u32[]{:S(2)}) collective-permute-start(bf16[1024,128]{1,0:T(8,128)(2,1)S(1)} %get-tuple-element.40), channel_id=1, source_target_pairs={{0,12},{1,13},{2,14},{3,15},{4,0},{5,1},{6,2},{7,3},{8,4},{9,5},{1... | collective-permute-start | bytes 786440 | tf_op jit(solution)/shard_map/ppermute | solution.py:43
  115.0 0.5 collective-permute-start.9
  115.5 0.0 copy-start.6
  115.5 0.0 copy-start.7
  115.5 0.4 sum_z.1
  115.9 0.3 collective-permute-start.7
  116.3 6.3 %collective-permute-done.7.ra = bf16[1008,128]{1,0:T(8,128)(2,1)S(1)} collective-permute-done((bf16[1008,128]{1,0:T(8,128)(2,1)S(1)}, bf16[1008,128]{1,0:T(8,128)(2,1)S(1)}, u32[]{:S(2)}, u32[]{:S(2)}) %collective-permute-start.7) | collective-permute-done | bytes 258080 | tf_op jit(solution)/shard_map/ppermute | solution.py:43
  122.6 4.4 %collective-permute-done.11.r3 = bf16[1024,128]{1,0:T(8,128)(2,1)S(1)} collective-permute-done((bf16[1024,128]{1,0:T(8,128)(2,1)S(1)}, bf16[1024,128]{1,0:T(8,128)(2,1)S(1)}, u32[]{:S(2)}, u32[]{:S(2)}) %collective-permute-start.11) | collective-permute-done | bytes 262176 | tf_op jit(solution)/shard_map/ppermute | solution.py:43
  126.9 0.7 collective-permute-done.9.r1
  127.7 1.0 sum_shard.1
  128.7 1.0 copy-done.8
  129.6 2.8 %collective-permute-start.12 = (bf16[2032,128]{1,0:T(8,128)(2,1)}, bf16[2032,128]{1,0:T(8,128)(2,1)}, u32[]{:S(2)}, u32[]{:S(2)}) collective-permute-start(bf16[2032,128]{1,0:T(8,128)(2,1)} %get-tuple-element.42), channel_id=1, source_target_pairs={{0,112},{1,113},{2,114},{3,115},{4,116},{5,117},{6,118},{7,119},{8... | collective-permute-start | bytes 1560584 | tf_op jit(solution)/shard_map/ppermute | solution.py:43
  132.4 1.3 collective-permute-start
  133.7 12.5 %collective-permute-done.12.far = bf16[2032,128]{1,0:T(8,128)(2,1)} collective-permute-done((bf16[2032,128]{1,0:T(8,128)(2,1)}, bf16[2032,128]{1,0:T(8,128)(2,1)}, u32[]{:S(2)}, u32[]{:S(2)}) %collective-permute-start.12) | collective-permute-done | bytes 520224 | tf_op jit(solution)/shard_map/ppermute | solution.py:43
  146.3 0.0 copy-start.9
  146.3 1.2 copy-done.9
  147.5 4.5 %adamw.1 = (f32[448,576]{1,0:T(8,128)}, f32[448,576]{1,0:T(8,128)}, f32[448,576]{1,0:T(8,128)}, f32[8,128]{1,0:T(8,128)S(1)}) custom-call(s32[3]{0:T(128)S(1)} %pad_add_fusion.s, f32[2032,128]{1,0:T(8,128)S(1)} %copy-done.9, bf16[2032,128]{1,0:T(8,128)(2,1)} %collective-permute-done.12.far, f32[448,576]{1,0:T(8,128)S(1)} %bitcast.50, ...), custom_call_target="tpu_custom_call" | custom-call | bytes 9000000 | tf_op jit(solution)/shard_map/adamw/pallas_call | solution.py:354
  152.0 0.6 fusion.11
  152.6 7.7 %collective-permute-done.grad = bf16[592,512]{1,0:T(8,128)(2,1)} collective-permute-done((bf16[592,512]{1,0:T(8,128)(2,1)}, bf16[592,512]{1,0:T(8,128)(2,1)}, u32[]{:S(2)}, u32[]{:S(2)}) %collective-permute-start) | collective-permute-done | bytes 606240 | tf_op jit(solution)/shard_map/ppermute | solution.py:43
  160.3 3.3 %copy-done.4 = bf16[4608,896]{1,0:T(8,128)(2,1)S(1)} copy-done((bf16[4608,896]{1,0:T(8,128)(2,1)S(1)}, bf16[4608,896]{1,0:T(8,128)(2,1)}, u32[]{:S(2)}) %copy-start.4) | copy-done | bytes 8257560
  163.6 9.9 %input_grad.1 = bf16[512,7168]{1,0:T(8,128)(2,1)} custom-call(bf16[592,512]{1,0:T(8,128)(2,1)} %collective-permute-done.grad, bf16[16,288,896]{2,1,0:T(8,128)(2,1)S(1)} %bitcast.49), custom_call_target="tpu_custom_call" | custom-call | flops 4227858432 | bytes 16000000 | tf_op jit(solution)/shard_map/input_grad/pallas_call | solution.py:376
  (33 shorter events, 0.1 us)
Async XLA Ops:
  7.2 153.1 %all-gather.3.cloned.1.call-start = ((), (), s32[]{:S(2)}) async-start(), calls=%async_computation | async-start | bytes 8773632 | tf_op jit(solution)/shard_map/all_gather | solution.py:426
  7.3 3.3 %copy-start = (bf16[1,7168,576]{1,2,0:T(8,128)(2,1)S(1)}, bf16[1,7168,576]{1,2,0:T(8,128)(2,1)}, u32[]{:S(2)}) copy-start(bf16[1,7168,576]{1,2,0:T(8,128)(2,1)} %param.12) | copy-start | bytes 24772612
  10.7 3.1 %copy-start.2 = (bf16[1,512,7168]{2,1,0:T(8,128)(2,1)S(1)}, bf16[1,512,7168]{2,1,0:T(8,128)(2,1)}, u32[]{:S(2)}) copy-start(bf16[1,512,7168]{2,1,0:T(8,128)(2,1)} %param.11) | copy-start | bytes 22020100
  13.8 23.2 %copy-start.14 = (bf16[1,512,64]{1,2,0:T(8,128)(2,1)S(1)}, bf16[1,512,64]{1,2,0:T(8,128)(2,1)}, u32[]{:S(2)}) copy-start(bf16[1,512,64]{1,2,0:T(8,128)(2,1)} %param.15) | copy-start | bytes 196612
  13.8 23.6 %copy-start.10 = (bf16[1,512,512]{2,1,0:T(8,128)(2,1)S(1)}, bf16[1,512,512]{2,1,0:T(8,128)(2,1)}, u32[]{:S(2)}) copy-start(bf16[1,512,512]{2,1,0:T(8,128)(2,1)} %param.14) | copy-start | bytes 1572868
  13.8 23.6 %copy-start.11 = (f32[1,512]{1,0:T(1,128)S(1)}, f32[1,512]{1,0:T(1,128)}, u32[]{:S(2)}) copy-start(f32[1,512]{1,0:T(1,128)} %gain.1) | copy-start | bytes 6148
  15.9 2.0 %copy-start.12 = (bf16[512,4096]{1,0:T(8,128)(2,1)}, bf16[512,4096]{1,0:T(8,128)(2,1)S(1)}, u32[]{:S(2)}) copy-start(bf16[512,4096]{1,0:T(8,128)(2,1)S(1)} %get-tuple-element.28) | copy-start | bytes 12582916
  17.9 16.8 %collective-permute-start.1 = (bf16[288,896]{1,0:T(8,128)(2,1)S(1)}, bf16[288,896]{1,0:T(8,128)(2,1)S(1)}, u32[]{:S(2)}, u32[]{:S(2)}) collective-permute-start(bf16[288,896]{1,0:T(8,128)(2,1)S(1)} %get-tuple-element.27), channel_id=1, source_target_pairs={{16,2},{17,3},{18,0},{19,1},{20,6},{21,7},{22,4},{23,5},{24,10},{2... | collective-permute-start | bytes 1548296 | tf_op jit(solution)/shard_map/ppermute | solution.py:43
  34.7 0.8 copy-start.13
  35.5 18.9 %collective-permute-start.2 = (bf16[512,4096]{1,0:T(8,128)(2,1)}, bf16[512,4096]{1,0:T(8,128)(2,1)S(1)}, u32[]{:S(2)}, u32[]{:S(2)}) collective-permute-start(bf16[512,4096]{1,0:T(8,128)(2,1)} %copy-done.12), channel_id=1, source_target_pairs={{0,1},{1,0},{2,3},{3,2},{4,5},{5,4},{6,7},{7,6},{8,9},{9,8},{10,11... | collective-permute-start | bytes 12582920 | tf_op jit(solution)/shard_map/ppermute | solution.py:43
  37.4 3.3 %copy-start.1 = (bf16[1,7168,576]{1,2,0:T(8,128)(2,1)S(1)}, bf16[1,7168,576]{1,2,0:T(8,128)(2,1)}, u32[]{:S(2)}) copy-start(bf16[1,7168,576]{1,2,0:T(8,128)(2,1)} %param.12) | copy-start | bytes 24772612
  40.7 3.1 %copy-start.3 = (bf16[1,512,7168]{2,1,0:T(8,128)(2,1)S(1)}, bf16[1,512,7168]{2,1,0:T(8,128)(2,1)}, u32[]{:S(2)}) copy-start(bf16[1,512,7168]{2,1,0:T(8,128)(2,1)} %param.11) | copy-start | bytes 22020100
  52.1 2.2 %collective-permute-start.3 = (bf16[592,512]{1,0:T(8,128)(2,1)}, bf16[592,512]{1,0:T(8,128)(2,1)S(1)}, u32[]{:S(2)}, u32[]{:S(2)}) collective-permute-start(bf16[592,512]{1,0:T(8,128)(2,1)} %latent_grad.1.grad), channel_id=1, source_target_pairs={{0,1},{1,0},{2,3},{3,2},{4,5},{5,4},{6,7},{7,6},{8,9},{9,8},{10,11... | collective-permute-start | bytes 1818632 | tf_op jit(solution)/shard_map/ppermute | solution.py:43
  64.9 46.9 %collective-permute-start.8 = (bf16[4,1024,128]{2,1,0:T(8,128)(2,1)S(1)}, bf16[4,1024,128]{2,1,0:T(8,128)(2,1)S(1)}, u32[]{:S(2)}, u32[]{:S(2)}) collective-permute-start(bf16[4,1024,128]{2,1,0:T(8,128)(2,1)S(1)} %get-tuple-element.36), channel_id=1, source_target_pairs={{0,2},{1,3},{2,0},{3,1},{4,6},{5,7},{6,4},{7,5},{8,10},{9,11},{10,... | collective-permute-start | bytes 3145736 | tf_op jit(solution)/shard_map/ppermute | solution.py:43
  65.0 49.9 %collective-permute-start.4 = (bf16[2,1008,128]{2,1,0:T(8,128)(2,1)S(1)}, bf16[2,1008,128]{2,1,0:T(8,128)(2,1)S(1)}, u32[]{:S(2)}, u32[]{:S(2)}) collective-permute-start(bf16[2,1008,128]{2,1,0:T(8,128)(2,1)S(1)} %get-tuple-element.30), channel_id=1, source_target_pairs={{0,4},{1,5},{2,6},{3,7},{4,8},{5,9},{6,10},{7,11},{8,12},{9,13},{1... | collective-permute-start | bytes 1548296 | tf_op jit(solution)/shard_map/ppermute | solution.py:43
  66.7 48.7 %collective-permute-start.5 = (bf16[2,1008,128]{2,1,0:T(8,128)(2,1)S(1)}, bf16[2,1008,128]{2,1,0:T(8,128)(2,1)S(1)}, u32[]{:S(2)}, u32[]{:S(2)}) collective-permute-start(bf16[2,1008,128]{2,1,0:T(8,128)(2,1)S(1)} %get-tuple-element.31), channel_id=1, source_target_pairs={{0,8},{1,9},{2,10},{3,11},{4,12},{5,13},{6,14},{7,15},{8,0},{9,1},... | collective-permute-start | bytes 1548296 | tf_op jit(solution)/shard_map/ppermute | solution.py:43
  70.0 45.4 %collective-permute-start.6 = (bf16[2,1008,128]{2,1,0:T(8,128)(2,1)S(1)}, bf16[2,1008,128]{2,1,0:T(8,128)(2,1)S(1)}, u32[]{:S(2)}, u32[]{:S(2)}) collective-permute-start(bf16[2,1008,128]{2,1,0:T(8,128)(2,1)S(1)} %get-tuple-element.32), channel_id=1, source_target_pairs={{0,12},{1,13},{2,14},{3,15},{4,0},{5,1},{6,2},{7,3},{8,4},{9,5},{1... | collective-permute-start | bytes 1548296 | tf_op jit(solution)/shard_map/ppermute | solution.py:43
  112.2 10.3 %collective-permute-start.10 = (bf16[1024,128]{1,0:T(8,128)(2,1)S(1)}, bf16[1024,128]{1,0:T(8,128)(2,1)S(1)}, u32[]{:S(2)}, u32[]{:S(2)}) collective-permute-start(bf16[1024,128]{1,0:T(8,128)(2,1)S(1)} %get-tuple-element.39), channel_id=1, source_target_pairs={{0,8},{1,9},{2,10},{3,11},{4,12},{5,13},{6,14},{7,15},{8,0},{9,1},... | collective-permute-start | bytes 786440 | tf_op jit(solution)/shard_map/ppermute | solution.py:43
  112.3 14.6 %collective-permute-start.11 = (bf16[1024,128]{1,0:T(8,128)(2,1)S(1)}, bf16[1024,128]{1,0:T(8,128)(2,1)S(1)}, u32[]{:S(2)}, u32[]{:S(2)}) collective-permute-start(bf16[1024,128]{1,0:T(8,128)(2,1)S(1)} %get-tuple-element.40), channel_id=1, source_target_pairs={{0,12},{1,13},{2,14},{3,15},{4,0},{5,1},{6,2},{7,3},{8,4},{9,5},{1... | collective-permute-start | bytes 786440 | tf_op jit(solution)/shard_map/ppermute | solution.py:43
  115.0 12.7 %collective-permute-start.9 = (bf16[1024,128]{1,0:T(8,128)(2,1)S(1)}, bf16[1024,128]{1,0:T(8,128)(2,1)S(1)}, u32[]{:S(2)}, u32[]{:S(2)}) collective-permute-start(bf16[1024,128]{1,0:T(8,128)(2,1)S(1)} %get-tuple-element.38), channel_id=1, source_target_pairs={{0,4},{1,5},{2,6},{3,7},{4,8},{5,9},{6,10},{7,11},{8,12},{9,13},{1... | collective-permute-start | bytes 786440 | tf_op jit(solution)/shard_map/ppermute | solution.py:43
  115.5 30.8 %copy-start.5 = (f32[1,448,576]{2,1,0:T(8,128)S(1)}, f32[1,448,576]{2,1,0:T(8,128)}, u32[]{:S(2)}) copy-start(f32[1,448,576]{2,1,0:T(8,128)} %param.16) | copy-start | bytes 3096580
  115.5 30.8 %copy-start.6 = (f32[1,448,576]{2,1,0:T(8,128)S(1)}, f32[1,448,576]{2,1,0:T(8,128)}, u32[]{:S(2)}) copy-start(f32[1,448,576]{2,1,0:T(8,128)} %param.17) | copy-start | bytes 3096580
  115.5 30.8 %copy-start.7 = (f32[1,448,576]{2,1,0:T(8,128)S(1)}, f32[1,448,576]{2,1,0:T(8,128)}, u32[]{:S(2)}) copy-start(f32[1,448,576]{2,1,0:T(8,128)} %param.18) | copy-start | bytes 3096580
  115.9 6.6 %collective-permute-start.7 = (bf16[1008,128]{1,0:T(8,128)(2,1)S(1)}, bf16[1008,128]{1,0:T(8,128)(2,1)S(1)}, u32[]{:S(2)}, u32[]{:S(2)}) collective-permute-start(bf16[1008,128]{1,0:T(8,128)(2,1)S(1)} %get-tuple-element.34), channel_id=1, source_target_pairs={{0,2},{1,3},{2,0},{3,1},{4,6},{5,7},{6,4},{7,5},{8,10},{9,11},{10,... | collective-permute-start | bytes 774152 | tf_op jit(solution)/shard_map/ppermute | solution.py:43
  128.6 1.0 copy-start.8
  129.6 16.6 %collective-permute-start.12 = (bf16[2032,128]{1,0:T(8,128)(2,1)}, bf16[2032,128]{1,0:T(8,128)(2,1)}, u32[]{:S(2)}, u32[]{:S(2)}) collective-permute-start(bf16[2032,128]{1,0:T(8,128)(2,1)} %get-tuple-element.42), channel_id=1, source_target_pairs={{0,112},{1,113},{2,114},{3,115},{4,116},{5,117},{6,118},{7,119},{8... | collective-permute-start | bytes 1560584 | tf_op jit(solution)/shard_map/ppermute | solution.py:43
  132.4 27.9 %collective-permute-start = (bf16[592,512]{1,0:T(8,128)(2,1)}, bf16[592,512]{1,0:T(8,128)(2,1)}, u32[]{:S(2)}, u32[]{:S(2)}) collective-permute-start(bf16[592,512]{1,0:T(8,128)(2,1)} %latent_grad.1.grad), channel_id=1, source_target_pairs={{16,0},{17,1},{18,2},{19,3},{20,4},{21,5},{22,6},{23,7},{24,8},{25... | collective-permute-start | bytes 1818632 | tf_op jit(solution)/shard_map/ppermute | solution.py:43
  146.3 1.2 copy-start.9
  147.5 4.5 %copy-start.15 = (f32[1,32]{1,0:T(1,128)S(1)}, f32[1,32]{1,0:T(1,128)}, u32[]{:S(2)}) copy-start(f32[1,32]{1,0:T(1,128)} %param.19) | copy-start | bytes 388
  147.5 4.5 %copy-start.16 = (f32[1,32]{1,0:T(1,128)S(1)}, f32[1,32]{1,0:T(1,128)}, u32[]{:S(2)}) copy-start(f32[1,32]{1,0:T(1,128)} %param.20) | copy-start | bytes 388
  147.5 4.5 %copy-start.17 = (f32[1,32]{1,0:T(1,128)S(1)}, f32[1,32]{1,0:T(1,128)}, u32[]{:S(2)}) copy-start(f32[1,32]{1,0:T(1,128)} %param.21) | copy-start | bytes 388
  160.3 3.3 %copy-start.4 = (bf16[4608,896]{1,0:T(8,128)(2,1)S(1)}, bf16[4608,896]{1,0:T(8,128)(2,1)}, u32[]{:S(2)}) copy-start(bf16[4608,896]{1,0:T(8,128)(2,1)} %all-gather.3.cloned.1.call-done) | copy-start | bytes 24772612
Sparse Core Ops, SparseCore 0:
  35.6 77.8 all-gather.2

commit v2 on v1

--- a/solution.py
+++ b/solution.py
@@ -67,15 +67,52 @@
     return r - 1, d ^ 2
 
 
-def cut_kernel(s, hidden, weight, part, piece):
+FLAG = jax.ShapeDtypeStruct((8, 128), F32)
+ANYWHERE = pl.BlockSpec(memory_space=pl.ANY)
+
+
+def after_kernel(value, *rest):
+    pass
+
+
+def after(value, *earlier):
+    return pl.pallas_call(
+        after_kernel,
+        in_specs=[ANYWHERE] * (1 + len(earlier)),
+        out_specs=ANYWHERE,
+        out_shape=jax.ShapeDtypeStruct(value.shape, value.dtype),
+        input_output_aliases={0: 0},
+        cost_estimate=cost(0, 0),
+        name="after",
+    )(value, *earlier)
+
+
+def copy_kernel(s, value, out):
+    out[...] = value[...]
+
+
+def cut_weight(s, weight):
+    return pl.pallas_call(
+        copy_kernel,
+        grid_spec=pltpu.PrefetchScalarGridSpec(
+            num_scalar_prefetch=1,
+            grid=(1,),
+            in_specs=[pl.BlockSpec((HALF, BLOCK), lambda b, s: (s[2], 2 * s[0] + 1 - s[1]))],
+            out_specs=pl.BlockSpec((HALF, BLOCK), lambda b, s: (0, 0)),
+        ),
+        out_shape=jax.ShapeDtypeStruct((HALF, BLOCK), BF),
+        compiler_params=params(60),
+        cost_estimate=cost(0, 1_000_000),
+        name="cut_weight",
+    )(s, weight)
+
+
+def cut_kernel(s, hidden, earlier, part, flag):
     part[...] = hidden[:, pl.ds(pl.multiple_of(384 * (1 - s[2]), 128), TILE)]
-
-    @pl.when(pl.program_id(0) == 0)
-    def _():
-        piece[...] = weight[...]
-
-
-def cut(s, hidden, weight):
+    flag[...] = jnp.zeros_like(flag)
+
+
+def cut(s, hidden, earlier):
     return pl.pallas_call(
         cut_kernel,
         grid_spec=pltpu.PrefetchScalarGridSpec(
@@ -83,24 +120,21 @@
             grid=(8,),
             in_specs=[
                 pl.BlockSpec((TOK, BLOCK), lambda b, s: (0, b)),
-                pl.BlockSpec((HALF, BLOCK), lambda b, s: (s[2], 2 * s[0] + 1 - s[1])),
+                ANYWHERE,
             ],
             out_specs=[
                 pl.BlockSpec((TOK, TILE), lambda b, s: (0, b)),
-                pl.BlockSpec((HALF, BLOCK), lambda b, s: (0, 0)),
+                pl.BlockSpec((8, 128), lambda b, s: (0, 0)),
             ],
         ),
-        out_shape=[
-            jax.ShapeDtypeStruct((TOK, 8 * TILE), BF),
-            jax.ShapeDtypeStruct((HALF, BLOCK), BF),
-        ],
-        compiler_params=params(24),
+        out_shape=[jax.ShapeDtypeStruct((TOK, 8 * TILE), BF), FLAG],
+        compiler_params=params(60),
         cost_estimate=cost(0, 12_500_000),
-        name="cut",
-    )(s, hidden, weight)
-
-
-def latent_kernel(hidden, weight, cot, gain, rope, out, total):
+        name="cut_hidden",
+    )(s, hidden, earlier)
+
+
+def latent_kernel(hidden, weight, cot, gain, rope, earlier, out, total):
     k = pl.program_id(0)
     part = lax.dot_general(
         hidden[...], weight[...], (((1,), (1,)), ((), ())), preferred_element_type=F32
@@ -134,7 +168,7 @@
         out[COLS:EXT, :] = both.astype(BF)
 
 
-def latent_step(hidden, weight, cot, gain, rope):
+def latent_step(hidden, weight, cot, gain, rope, earlier):
     width = 1024
     return pl.pallas_call(
         latent_kernel,
@@ -145,14 +179,15 @@
             pl.BlockSpec((TOK, LAT), lambda k: (0, 0)),
             pl.BlockSpec((1, LAT), lambda k: (0, 0)),
             pl.BlockSpec((ROPE, TOK), lambda k: (0, 0)),
+            ANYWHERE,
         ],
         out_specs=pl.BlockSpec((EXT, TOK), lambda k: (0, 0)),
         out_shape=jax.ShapeDtypeStruct((EXT, TOK), BF),
         scratch_shapes=[pltpu.VMEM((TOK, LAT), F32)],
-        compiler_params=params(32),
+        compiler_params=params(60),
         cost_estimate=cost(2 * TOK * WIDTH * LAT, 16_000_000),
         name="latent_grad",
-    )(hidden, weight, cot, gain, rope)
+    )(hidden, weight, cot, gain, rope, earlier)
 
 
 def weight_kernel(
@@ -176,10 +211,11 @@
     lane = lax.broadcasted_iota(jnp.int32, (HALF // 2, 128), 1)
     first = core == 0
 
+    whole = jnp.dot(grad[:COLS, :], own, preferred_element_type=F32)
+    whole += jnp.dot(grad_other[:COLS, :], other[...], preferred_element_type=F32)
+
     def packed(h):
-        rows = slice(h * HALF, h * HALF + HALF)
-        full = jnp.dot(grad[rows, :], own, preferred_element_type=F32)
-        full += jnp.dot(grad_other[rows, :], other[...], preferred_element_type=F32)
+        full = whole[h * HALF : h * HALF + HALF]
         col = [full[:, 128 * j : 128 * j + 128] for j in range(4)]
         edge = jnp.where(first, col[3], col[0])
         top, low = edge[: HALF // 2], edge[HALF // 2 :]
@@ -235,7 +271,7 @@
             jax.ShapeDtypeStruct((4, ROWS_B, 128), F32),
             jax.ShapeDtypeStruct((4, ROWS_B, 128), BF),
         ],
-        compiler_params=params(40),
+        compiler_params=params(60),
         cost_estimate=cost(2 * 2 * TOK * 8 * TILE * COLS, 20_000_000),
         name="weight_grad",
     )(s, hidden, other, grad, grad_other)
@@ -294,13 +330,14 @@
     )(own, r)
 
 
-def sum_all_kernel(keep_a, ra, keep_b, r1, r2, r3, total, send):
+def sum_all_kernel(keep_a, ra, keep_b, r1, r2, r3, total, send, flag):
     a = keep_a[...] + ra[...].astype(F32)
     b = keep_b[...] + r1[...].astype(F32) + r2[...].astype(F32) + r3[...].astype(F32)
     total[:ROWS_A, :] = a
     total[ROWS_A:, :] = b
     send[:ROWS_A, :] = a.astype(BF)
     send[ROWS_A:, :] = b.astype(BF)
+    flag[...] = jnp.zeros_like(flag)
 
 
 def sum_all(*parts):
@@ -309,6 +346,7 @@
         out_shape=[
             jax.ShapeDtypeStruct((ROWS_A + ROWS_B, 128), F32),
             jax.ShapeDtypeStruct((ROWS_A + ROWS_B, 128), BF),
+            FLAG,
         ],
         compiler_params=params(16),
         cost_estimate=cost(0, 4_000_000),
@@ -327,7 +365,7 @@
     return (new_master, new_first, new_second)
 
 
-def adam_kernel(s, own, far, master, first, second, n_master, n_first, n_second, gain, grad):
+def adam_kernel(s, own, far, master, first, second, earlier, n_master, n_first, n_second, gain, grad):
     total = own[...] + far[...].astype(F32)
     core = s[2]
     gain[...] = total[2 * ROWS_A : 2 * ROWS_A + 8]
@@ -348,45 +386,52 @@
     )
 
 
-def adam_step(s, own, far, master, first, second):
+def adam_step(s, own, far, master, first, second, earlier):
     shape = jax.ShapeDtypeStruct(master.shape, F32)
     spec = pl.BlockSpec(memory_space=pltpu.VMEM)
     return pl.pallas_call(
         adam_kernel,
-        in_specs=[pl.BlockSpec(memory_space=pltpu.SMEM)] + [spec] * 5,
+        in_specs=[pl.BlockSpec(memory_space=pltpu.SMEM)]
+        + [spec] * 5
+        + [ANYWHERE],
         out_specs=[spec] * 4,
         out_shape=[shape] * 3 + [jax.ShapeDtypeStruct((8, 128), F32)],
         scratch_shapes=[pltpu.VMEM(master.shape, F32)],
         compiler_params=params(32),
         cost_estimate=cost(0, 9_000_000),
         name="adamw",
-    )(s, own, far, master, first, second)
-
-
-def input_kernel(grad, weight, out, turned):
+    )(s, own, far, master, first, second, earlier)
+
+
+def input_kernel(grad, weight, earlier, out, flag, turned):
     @pl.when(pl.program_id(0) == 0)
     def _():
         turned[...] = grad[:COLS, :].astype(F32).T.astype(BF)
+        flag[...] = jnp.zeros_like(flag)
 
     block = weight[...].reshape(COLS, BLOCK)
     out[...] = jnp.dot(turned[...], block, preferred_element_type=F32).astype(BF)
 
 
-def input_step(grad, weight):
+def input_step(grad, weight, earlier):
     return pl.pallas_call(
         input_kernel,
         grid=(8,),
         in_specs=[
             pl.BlockSpec((EXT, TOK), lambda b: (0, 0)),
             pl.BlockSpec((2, HALF, BLOCK), lambda b: (b, 0, 0)),
+            ANYWHERE,
         ],
-        out_specs=pl.BlockSpec((TOK, BLOCK), lambda b: (0, b)),
-        out_shape=jax.ShapeDtypeStruct((TOK, WIDTH), BF),
+        out_specs=[
+            pl.BlockSpec((TOK, BLOCK), lambda b: (0, b)),
+            pl.BlockSpec((8, 128), lambda b: (0, 0)),
+        ],
+        out_shape=[jax.ShapeDtypeStruct((TOK, WIDTH), BF), FLAG],
         scratch_shapes=[pltpu.VMEM((TOK, COLS), BF)],
-        compiler_params=params(32),
+        compiler_params=params(60),
         cost_estimate=cost(2 * TOK * WIDTH * COLS, 16_000_000),
         name="input_grad",
-    )(grad, weight)
+    )(grad, weight, earlier)
 
 
 def rope_step(rope_cot):
@@ -417,16 +462,18 @@
     gain_second,
 ):
     shard = lax.axis_index("dp")
-    s = jnp.stack([shard // 4, (shard // 2) % 2, shard % 2]).astype(jnp.int32)
+    s = jnp.stack([shard >> 2, (shard >> 1) & 1, shard & 1]).astype(jnp.int32)
     hidden = hidden_in[0]
     turned = weight[0].T
-    part, piece = cut(s, hidden, turned)
+    piece = cut_weight(s, turned)
     piece_next = moved(piece, to_before_near)
+    part, is_cut = cut(s, hidden, piece)
+    rope = rope_step(rope_cot[0])
     other = moved(part, to_core)
-    weight_next = lax.all_gather(piece_next, "dp")
-    grad = latent_step(hidden, turned, latent_cot[0], gain, rope_step(rope_cot[0]))
+    grad = latent_step(hidden, turned, latent_cot[0], gain, rope, is_cut)
     grad_other = moved(grad, to_core)
     grad_next = moved(grad, to_before)
+    weight_next = lax.all_gather(after(piece_next, grad, other), "dp")
     own_a, z1, z2, z3, own_b, send_b = weight_step(s, hidden, other, grad, grad_other)
     r1, r2, r3 = moved(z1, to_z(1)), moved(z2, to_z(2)), moved(z3, to_z(3))
     rb = moved(send_b, to_ylo)
@@ -434,11 +481,11 @@
     keep_b, s1, s2, s3 = sum_b(own_b, rb)
     ra = moved(send_a, to_ylo)
     r1, r2, r3 = moved(s1, to_z(1)), moved(s2, to_z(2)), moved(s3, to_z(3))
-    total, send = sum_all(keep_a, ra, keep_b, r1, r2, r3)
+    total, send, is_summed = sum_all(keep_a, ra, keep_b, r1, r2, r3)
     far = moved(send, to_mirror)
-    received = input_step(grad_next, weight_next)
+    received, is_received = input_step(grad_next, weight_next, is_summed)
     next_master, next_first, next_second, gain_rows = adam_step(
-        s, total, far, master_weight[0], first_moment[0], second_moment[0]
+        s, total, far, master_weight[0], first_moment[0], second_moment[0], is_received
     )
     gain_total = lax.dynamic_slice(gain_rows[:4].reshape(LAT), (shard * 32,), (32,))
     next_gain = adamw(gain_master[0], gain_first[0], gain_second[0], gain_total)

time: 181 us -> 168 us (0.928)
  waiting for transfers between devices: 90.4 us -> 70.6 us
  Pallas kernels: 37.2 us -> 53.4 us
  local copies, waits for them, and re-layouts: 21.2 us -> 7.59 us
    ppermute x13, waiting for transfers between devices: 90.4 us -> 70.6 us  [moved(): return lax.ppermute(value, ('pipe', 'dp'), pairs)]
    unnamed x36 -> x40, local copies, waits for them, and re-layouts: 21.2 us -> 7.59 us
    pallas_call x1, Pallas kernels: 2.11 us -> 8.17 us  [cut(): pl.pallas_call(cut_kernel, grid_spec=pltpu.PrefetchScalarGridSpec(num_sca...]
    pallas_call x1, Pallas kernels: 10.6 us -> 13.5 us  [weight_step(): pl.pallas_call(weight_kernel, grid_spec=pltpu.PrefetchScalarGridSpec(num_...]
    pallas_call x1, Pallas kernels: 8.34 us -> 11.2 us  [latent_step(): pl.pallas_call(latent_kernel, grid=(WIDTH // width,), in_specs=[pl.BlockS...]
    pallas_call x0 -> x2, Pallas kernels: none -> 2.53 us  [the longest x1 2.53 us: cut_weight(): pl.pallas_call(copy_kernel, grid_spec=pltpu.PrefetchScalarGridSpec(num_sc...]
    pallas_call x1, Pallas kernels: 9.86 us -> 12.3 us  [input_step(): pl.pallas_call(input_kernel, grid=(8,), in_specs=[pl.BlockSpec((EXT, TOK)...]
  transfers between devices with their start and end apart: 14 -> 14, of which waited for: 8 -> 7; matrix products, arithmetic and copies ran while one was open for 1% -> 1% of each run, Pallas kernels for 14% -> 23%
where the time goes in v2:
time: 168 us; the launch traced here: 166 us
  waiting for transfers between devices  70.6 us (42%)
  Pallas kernels  53.4 us (32%)
  starting transfers between devices  17.7 us (11%)
  between operations  14.2 us (8%)
  local copies, waits for them, and re-layouts  7.59 us (5%)
  other arithmetic  2.21 us (1%)
    ppermute x13, waiting for transfers between devices, moved(): return lax.ppermute(value, ('pipe', 'dp'), pairs)  70.6 us
    ppermute x13, starting transfers between devices, moved(): return lax.ppermute(value, ('pipe', 'dp'), pairs)  17.7 us
    pallas_call x1, Pallas kernels, weight_step(): pl.pallas_call(weight_kernel, grid_spec=pltpu.PrefetchScalarGridSpec(num_...  13.5 us
    pallas_call x1, Pallas kernels, input_step(): pl.pallas_call(input_kernel, grid=(8,), in_specs=[pl.BlockSpec((EXT, TOK)...  12.3 us
    pallas_call x1, Pallas kernels, latent_step(): pl.pallas_call(latent_kernel, grid=(WIDTH // width,), in_specs=[pl.BlockS...  11.2 us
    pallas_call x1, Pallas kernels, cut(): pl.pallas_call(cut_kernel, grid_spec=pltpu.PrefetchScalarGridSpec(num_sca...  8.17 us
    unnamed x40, local copies, waits for them, and re-layouts  7.59 us
    pallas_call x1, Pallas kernels, adam_step(): pl.pallas_call(adam_kernel, in_specs=[pl.BlockSpec(memory_space=pltpu.SME...  3.85 us
  transfers between devices with their start and end apart: 14, of which 7 were waited for; matrix products, arithmetic and copies ran while one was open for 1% of the time, Pallas kernels for 23%

profile of v2, /device:TPU:1, one launch (start us, length us, event | category | flops | bytes accessed | tf_op | source)
XLA Modules:
  0.0 165.7 jit_solution(14370697473753596777)
XLA Ops:
  7.2 0.0 all-gather.3.cloned.1.call-start
  7.2 0.6 pad_add_fusion.s
  7.8 2.5 %cut_weight.1.earlier = bf16[288,896]{1,0:T(8,128)(2,1)} custom-call(s32[3]{0:T(128)} %pad_add_fusion.s, bf16[576,7168]{1,0:T(8,128)(2,1)} %bitcast.47), custom_call_target="tpu_custom_call" | custom-call | bytes 1000000 | tf_op jit(solution)/shard_map/cut_weight/pallas_call | solution.py:95
  10.4 8.2 %cut_hidden.1 = (bf16[512,4096]{1,0:T(8,128)(2,1)}, f32[8,128]{1,0:T(8,128)}) custom-call(s32[3]{0:T(128)} %pad_add_fusion.s, bf16[512,7168]{1,0:T(8,128)(2,1)} %bitcast.49, bf16[288,896]{1,0:T(8,128)(2,1)} %cut_weight.1.earlier), custom_call_target="tpu_custom_call" | custom-call | bytes 12500000 | tf_op jit(solution)/shard_map/cut_hidden/pallas_call | solution.py:116
  18.5 1.4 collective-permute-start.2
  20.0 1.3 collective-permute-start.1
  21.3 0.3 fusion.5
  21.6 0.6 pad_maximum_fusion.rope
  22.3 11.2 %latent_grad.1.rest_0_.grad = bf16[592,512]{1,0:T(8,128)(2,1)} custom-call(bf16[512,7168]{1,0:T(8,128)(2,1)} %bitcast.50, bf16[576,7168]{1,0:T(8,128)(2,1)} %bitcast.48, bf16[512,512]{1,0:T(8,128)(2,1)} %bitcast.52, f32[1,512]{1,0:T(1,128)} %gain.1, bf16[64,512]{1,0:T(8,128)(2,1)} %pad_maximum_fusion.rope, f32[8,128]{1,0:T(8,128)} %get-tuple-element.30.earlier), custom_call_target="tpu_custom_call" | custom-call | flops 3758096384 | bytes 16000000 | tf_op jit(solution)/shard_map/latent_grad/pallas_call | solution.py:173
  33.5 3.1 %collective-permute-done.1.value = bf16[288,896]{1,0:T(8,128)(2,1)S(1)} collective-permute-done((bf16[288,896]{1,0:T(8,128)(2,1)S(1)}, bf16[288,896]{1,0:T(8,128)(2,1)S(1)}, u32[]{:S(2)}, u32[]{:S(2)}) %collective-permute-start.1) | collective-permute-done | bytes 516128 | tf_op jit(solution)/shard_map/ppermute | solution.py:43
  36.7 0.0 collective-permute-done.2.rest_1_.other
  36.7 0.8 copy-done.13
  37.5 0.0 all-gather.3.cloned.1.call-update
  37.5 0.0 copy-start.11
  37.5 0.8 collective-permute-start.3
  38.3 1.7 collective-permute-done.3.grad_other
  39.9 0.9 copy-done.19
  40.8 13.5 %weight_grad.1 = (f32[2,1008,128]{2,1,0:T(8,128)}, bf16[2,1008,128]{2,1,0:T(8,128)(2,1)}, bf16[2,1008,128]{2,1,0:T(8,128)(2,1)}, bf16[2,1008,128]{2,1,0:T(8,128)...) custom-call(s32[3]{0:T(128)} %pad_add_fusion.s, bf16[512,7168]{1,0:T(8,128)(2,1)} %bitcast.51, ...), custom_call_target="tpu_custom_call" | custom-call | flops 4831838208 | bytes 20000000 | tf_op jit(solution)/shard_map/weight_grad/pallas_call | solution.py:253
  54.3 0.3 collective-permute-start.8
  54.7 1.5 collective-permute-start.4
  56.1 3.3 %collective-permute-start.5 = (bf16[2,1008,128]{2,1,0:T(8,128)(2,1)}, bf16[2,1008,128]{2,1,0:T(8,128)(2,1)S(1)}, u32[]{:S(2)}, u32[]{:S(2)}) collective-permute-start(bf16[2,1008,128]{2,1,0:T(8,128)(2,1)} %get-tuple-element.34), channel_id=1, source_target_pairs={{0,8},{1,9},{2,10},{3,11},{4,12},{5,13},{6,14},{7,15},{8,0},{9,1},... | collective-permute-start | bytes 1548296 | tf_op jit(solution)/shard_map/ppermute | solution.py:43
  59.5 0.6 collective-permute-start.6
  60.1 1.3 collective-permute-start
  61.4 53.6 %collective-permute-done.8.r = bf16[4,1024,128]{2,1,0:T(8,128)(2,1)S(1)} collective-permute-done((bf16[4,1024,128]{2,1,0:T(8,128)(2,1)}, bf16[4,1024,128]{2,1,0:T(8,128)(2,1)S(1)}, u32[]{:S(2)}, u32[]{:S(2)}) %collective-permute-start.8) | collective-permute-done | bytes 1048608 | tf_op jit(solution)/shard_map/ppermute | solution.py:43
  115.0 1.6 copy-done
  116.6 0.4 sum_y.1
  117.0 0.1 collective-permute-start.10
  117.1 0.0 collective-permute-done.4.r1
  117.2 3.9 %collective-permute-start.11 = (bf16[1024,128]{1,0:T(8,128)(2,1)S(1)}, bf16[1024,128]{1,0:T(8,128)(2,1)S(1)}, u32[]{:S(2)}, u32[]{:S(2)}) collective-permute-start(bf16[1024,128]{1,0:T(8,128)(2,1)S(1)} %get-tuple-element.43), channel_id=1, source_target_pairs={{0,12},{1,13},{2,14},{3,15},{4,0},{5,1},{6,2},{7,3},{8,4},{9,5},{1... | collective-permute-start | bytes 786440 | tf_op jit(solution)/shard_map/ppermute | solution.py:43
  121.1 0.0 collective-permute-done.5.r2
  121.1 0.6 collective-permute-start.9
  121.7 0.4 sum_z.1
  122.1 0.1 collective-permute-start.7
  122.2 8.7 %collective-permute-done.7.ra = bf16[1008,128]{1,0:T(8,128)(2,1)S(1)} collective-permute-done((bf16[1008,128]{1,0:T(8,128)(2,1)S(1)}, bf16[1008,128]{1,0:T(8,128)(2,1)S(1)}, u32[]{:S(2)}, u32[]{:S(2)}) %collective-permute-start.7) | collective-permute-done | bytes 258080 | tf_op jit(solution)/shard_map/ppermute | solution.py:43
  130.8 1.7 %collective-permute-done.11.r3 = bf16[1024,128]{1,0:T(8,128)(2,1)S(1)} collective-permute-done((bf16[1024,128]{1,0:T(8,128)(2,1)S(1)}, bf16[1024,128]{1,0:T(8,128)(2,1)S(1)}, u32[]{:S(2)}, u32[]{:S(2)}) %collective-permute-start.11) | collective-permute-done | bytes 262176 | tf_op jit(solution)/shard_map/ppermute | solution.py:43
  132.5 1.1 collective-permute-done.9.r1
  133.6 1.0 sum_shard.1
  134.6 1.0 copy-done.4
  135.6 0.6 copy-done.9
  136.2 2.5 %collective-permute-start.12 = (bf16[2032,128]{1,0:T(8,128)(2,1)}, bf16[2032,128]{1,0:T(8,128)(2,1)S(1)}, u32[]{:S(2)}, u32[]{:S(2)}) collective-permute-start(bf16[2032,128]{1,0:T(8,128)(2,1)} %get-tuple-element.47), channel_id=1, source_target_pairs={{0,112},{1,113},{2,114},{3,115},{4,116},{5,117},{6,118},{7,119},{8... | collective-permute-start | bytes 1560584 | tf_op jit(solution)/shard_map/ppermute | solution.py:43
  138.6 0.8 copy-done.18
  139.4 12.3 %input_grad.1 = (bf16[512,7168]{1,0:T(8,128)(2,1)}, f32[8,128]{1,0:T(8,128)}) custom-call(bf16[592,512]{1,0:T(8,128)(2,1)} %copy-done.18, bf16[16,288,896]{2,1,0:T(8,128)(2,1)} %bitcast.55, f32[8,128]{1,0:T(8,128)} %copy-done.9), custom_call_target="tpu_custom_call" | custom-call | flops 4227858432 | bytes 16000000 | tf_op jit(solution)/shard_map/input_grad/pallas_call | solution.py:417
  151.8 0.7 collective-permute-done.12.far
  152.5 0.0 copy-start.5
  152.5 1.2 copy-done.5
  153.7 0.7 copy-done.8
  154.4 3.8 %adamw.1 = (f32[448,576]{1,0:T(8,128)}, f32[448,576]{1,0:T(8,128)}, f32[448,576]{1,0:T(8,128)}, f32[8,128]{1,0:T(8,128)S(1)}) custom-call(s32[3]{0:T(128)S(1)} %copy-done.7, f32[2032,128]{1,0:T(8,128)S(1)} %copy-done.5, bf16[2032,128]{1,0:T(8,128)(2,1)S(1)} %collective-permute-done.12.far, f32[448,576]{1,0:T(8,128)S(1)} %bitcast.44, ...), custom_call_target="tpu_custom_call" | custom-call | bytes 9000000 | tf_op jit(solution)/shard_map/adamw/pallas_call | solution.py:392
  158.3 0.6 fusion.11
  (39 shorter events, 0.1 us)
Async XLA Ops:
  7.2 131.4 %all-gather.3.cloned.1.call-start = ((), (), s32[]{:S(2)}) async-start(), calls=%async_computation | async-start | bytes 8773632 | tf_op jit(solution)/shard_map/all_gather | solution.py:476
  10.4 9.6 %copy-start.12 = (bf16[288,896]{1,0:T(8,128)(2,1)S(1)}, bf16[288,896]{1,0:T(8,128)(2,1)}, u32[]{:S(2)}) copy-start(bf16[288,896]{1,0:T(8,128)(2,1)} %cut_weight.1.earlier) | copy-start | bytes 1548292
  10.4 10.9 %copy-start.14 = (bf16[1,512,64]{1,2,0:T(8,128)(2,1)S(1)}, bf16[1,512,64]{1,2,0:T(8,128)(2,1)}, u32[]{:S(2)}) copy-start(bf16[1,512,64]{1,2,0:T(8,128)(2,1)} %param.15) | copy-start | bytes 196612
  18.5 18.1 %collective-permute-start.2 = (bf16[512,4096]{1,0:T(8,128)(2,1)}, bf16[512,4096]{1,0:T(8,128)(2,1)}, u32[]{:S(2)}, u32[]{:S(2)}) collective-permute-start(bf16[512,4096]{1,0:T(8,128)(2,1)} %get-tuple-element.31), channel_id=1, source_target_pairs={{0,1},{1,0},{2,3},{3,2},{4,5},{5,4},{6,7},{7,6},{8,9},{9,8},{10,11... | collective-permute-start | bytes 12582920 | tf_op jit(solution)/shard_map/ppermute | solution.py:43
  20.0 16.7 %collective-permute-start.1 = (bf16[288,896]{1,0:T(8,128)(2,1)S(1)}, bf16[288,896]{1,0:T(8,128)(2,1)S(1)}, u32[]{:S(2)}, u32[]{:S(2)}) collective-permute-start(bf16[288,896]{1,0:T(8,128)(2,1)S(1)} %copy-done.12), channel_id=1, source_target_pairs={{16,2},{17,3},{18,0},{19,1},{20,6},{21,7},{22,4},{23,5},{24,10},{2... | collective-permute-start | bytes 1548296 | tf_op jit(solution)/shard_map/ppermute | solution.py:43
  33.5 4.0 %copy-start.10 = (bf16[592,512]{1,0:T(8,128)(2,1)S(1)}, bf16[592,512]{1,0:T(8,128)(2,1)}, u32[]{:S(2)}) copy-start(bf16[592,512]{1,0:T(8,128)(2,1)} %latent_grad.1.rest_0_.grad) | copy-start | bytes 1818628
  36.7 0.8 copy-start.13
  37.5 22.6 %copy-start.11 = (bf16[592,512]{1,0:T(8,128)(2,1)S(1)}, bf16[592,512]{1,0:T(8,128)(2,1)}, u32[]{:S(2)}) copy-start(bf16[592,512]{1,0:T(8,128)(2,1)} %latent_grad.1.rest_0_.grad) | copy-start | bytes 1818628
  37.5 2.4 %collective-permute-start.3 = (bf16[592,512]{1,0:T(8,128)(2,1)S(1)}, bf16[592,512]{1,0:T(8,128)(2,1)S(1)}, u32[]{:S(2)}, u32[]{:S(2)}) collective-permute-start(bf16[592,512]{1,0:T(8,128)(2,1)S(1)} %copy-done.10), channel_id=1, source_target_pairs={{0,1},{1,0},{2,3},{3,2},{4,5},{5,4},{6,7},{7,6},{8,9},{9,8},{10,11... | collective-permute-start | bytes 1818632 | tf_op jit(solution)/shard_map/ppermute | solution.py:43
  39.9 0.9 copy-start.19
  54.3 60.7 %collective-permute-start.8 = (bf16[4,1024,128]{2,1,0:T(8,128)(2,1)}, bf16[4,1024,128]{2,1,0:T(8,128)(2,1)S(1)}, u32[]{:S(2)}, u32[]{:S(2)}) collective-permute-start(bf16[4,1024,128]{2,1,0:T(8,128)(2,1)} %get-tuple-element.39), channel_id=1, source_target_pairs={{0,2},{1,3},{2,0},{3,1},{4,6},{5,7},{6,4},{7,5},{8,10},{9,11},{10,... | collective-permute-start | bytes 3145736 | tf_op jit(solution)/shard_map/ppermute | solution.py:43
  54.7 62.5 %collective-permute-start.4 = (bf16[2,1008,128]{2,1,0:T(8,128)(2,1)}, bf16[2,1008,128]{2,1,0:T(8,128)(2,1)S(1)}, u32[]{:S(2)}, u32[]{:S(2)}) collective-permute-start(bf16[2,1008,128]{2,1,0:T(8,128)(2,1)} %get-tuple-element.33), channel_id=1, source_target_pairs={{0,4},{1,5},{2,6},{3,7},{4,8},{5,9},{6,10},{7,11},{8,12},{9,13},{1... | collective-permute-start | bytes 1548296 | tf_op jit(solution)/shard_map/ppermute | solution.py:43
  56.1 65.0 %collective-permute-start.5 = (bf16[2,1008,128]{2,1,0:T(8,128)(2,1)}, bf16[2,1008,128]{2,1,0:T(8,128)(2,1)S(1)}, u32[]{:S(2)}, u32[]{:S(2)}) collective-permute-start(bf16[2,1008,128]{2,1,0:T(8,128)(2,1)} %get-tuple-element.34), channel_id=1, source_target_pairs={{0,8},{1,9},{2,10},{3,11},{4,12},{5,13},{6,14},{7,15},{8,0},{9,1},... | collective-permute-start | bytes 1548296 | tf_op jit(solution)/shard_map/ppermute | solution.py:43
  59.5 62.2 %collective-permute-start.6 = (bf16[2,1008,128]{2,1,0:T(8,128)(2,1)}, bf16[2,1008,128]{2,1,0:T(8,128)(2,1)S(1)}, u32[]{:S(2)}, u32[]{:S(2)}) collective-permute-start(bf16[2,1008,128]{2,1,0:T(8,128)(2,1)} %get-tuple-element.35), channel_id=1, source_target_pairs={{0,12},{1,13},{2,14},{3,15},{4,0},{5,1},{6,2},{7,3},{8,4},{9,5},{1... | collective-permute-start | bytes 1548296 | tf_op jit(solution)/shard_map/ppermute | solution.py:43
  60.1 78.5 %collective-permute-start = (bf16[592,512]{1,0:T(8,128)(2,1)S(1)}, bf16[592,512]{1,0:T(8,128)(2,1)S(1)}, u32[]{:S(2)}, u32[]{:S(2)}) collective-permute-start(bf16[592,512]{1,0:T(8,128)(2,1)S(1)} %copy-done.11), channel_id=1, source_target_pairs={{16,0},{17,1},{18,2},{19,3},{20,4},{21,5},{22,6},{23,7},{24,8},{25... | collective-permute-start | bytes 1818632 | tf_op jit(solution)/shard_map/ppermute | solution.py:43
  115.0 1.6 copy-start
  116.6 5.0 %copy-start.6 = (f32[2,1008,128]{2,1,0:T(8,128)S(1)}, f32[2,1008,128]{2,1,0:T(8,128)}, u32[]{:S(2)}) copy-start(f32[2,1008,128]{2,1,0:T(8,128)} %get-tuple-element.32.own) | copy-start | bytes 3096580
  117.0 13.8 %collective-permute-start.10 = (bf16[1024,128]{1,0:T(8,128)(2,1)S(1)}, bf16[1024,128]{1,0:T(8,128)(2,1)S(1)}, u32[]{:S(2)}, u32[]{:S(2)}) collective-permute-start(bf16[1024,128]{1,0:T(8,128)(2,1)S(1)} %get-tuple-element.42), channel_id=1, source_target_pairs={{0,8},{1,9},{2,10},{3,11},{4,12},{5,13},{6,14},{7,15},{8,0},{9,1},... | collective-permute-start | bytes 786440 | tf_op jit(solution)/shard_map/ppermute | solution.py:43
  117.2 15.4 %collective-permute-start.11 = (bf16[1024,128]{1,0:T(8,128)(2,1)S(1)}, bf16[1024,128]{1,0:T(8,128)(2,1)S(1)}, u32[]{:S(2)}, u32[]{:S(2)}) collective-permute-start(bf16[1024,128]{1,0:T(8,128)(2,1)S(1)} %get-tuple-element.43), channel_id=1, source_target_pairs={{0,12},{1,13},{2,14},{3,15},{4,0},{5,1},{6,2},{7,3},{8,4},{9,5},{1... | collective-permute-start | bytes 786440 | tf_op jit(solution)/shard_map/ppermute | solution.py:43
  121.1 12.5 %collective-permute-start.9 = (bf16[1024,128]{1,0:T(8,128)(2,1)S(1)}, bf16[1024,128]{1,0:T(8,128)(2,1)S(1)}, u32[]{:S(2)}, u32[]{:S(2)}) collective-permute-start(bf16[1024,128]{1,0:T(8,128)(2,1)S(1)} %get-tuple-element.41), channel_id=1, source_target_pairs={{0,4},{1,5},{2,6},{3,7},{4,8},{5,9},{6,10},{7,11},{8,12},{9,13},{1... | collective-permute-start | bytes 786440 | tf_op jit(solution)/shard_map/ppermute | solution.py:43
  122.1 8.8 %collective-permute-start.7 = (bf16[1008,128]{1,0:T(8,128)(2,1)S(1)}, bf16[1008,128]{1,0:T(8,128)(2,1)S(1)}, u32[]{:S(2)}, u32[]{:S(2)}) collective-permute-start(bf16[1008,128]{1,0:T(8,128)(2,1)S(1)} %get-tuple-element.37), channel_id=1, source_target_pairs={{0,2},{1,3},{2,0},{3,1},{4,6},{5,7},{6,4},{7,5},{8,10},{9,11},{10,... | collective-permute-start | bytes 774152 | tf_op jit(solution)/shard_map/ppermute | solution.py:43
  134.6 1.0 copy-start.4
  135.6 0.6 copy-start.9
  136.2 16.3 %collective-permute-start.12 = (bf16[2032,128]{1,0:T(8,128)(2,1)}, bf16[2032,128]{1,0:T(8,128)(2,1)S(1)}, u32[]{:S(2)}, u32[]{:S(2)}) collective-permute-start(bf16[2032,128]{1,0:T(8,128)(2,1)} %get-tuple-element.47), channel_id=1, source_target_pairs={{0,112},{1,113},{2,114},{3,115},{4,116},{5,117},{6,118},{7,119},{8... | collective-permute-start | bytes 1560584 | tf_op jit(solution)/shard_map/ppermute | solution.py:43
  138.6 0.8 copy-start.18
  139.4 13.0 %copy-start.1 = (f32[1,448,576]{2,1,0:T(8,128)S(1)}, f32[1,448,576]{2,1,0:T(8,128)}, u32[]{:S(2)}) copy-start(f32[1,448,576]{2,1,0:T(8,128)} %param.16) | copy-start | bytes 3096580
  139.4 13.0 %copy-start.2 = (f32[1,448,576]{2,1,0:T(8,128)S(1)}, f32[1,448,576]{2,1,0:T(8,128)}, u32[]{:S(2)}) copy-start(f32[1,448,576]{2,1,0:T(8,128)} %param.17) | copy-start | bytes 3096580
  139.4 13.0 %copy-start.3 = (f32[1,448,576]{2,1,0:T(8,128)S(1)}, f32[1,448,576]{2,1,0:T(8,128)}, u32[]{:S(2)}) copy-start(f32[1,448,576]{2,1,0:T(8,128)} %param.18) | copy-start | bytes 3096580
  139.4 13.0 %copy-start.7 = (s32[3]{0:T(128)S(1)}, s32[3]{0:T(128)}, u32[]{:S(2)}) copy-start(s32[3]{0:T(128)} %pad_add_fusion.s) | copy-start | bytes 40
  152.5 1.2 copy-start.5
  153.7 0.7 copy-start.8
  154.4 3.9 %copy-start.15 = (f32[1,32]{1,0:T(1,128)S(1)}, f32[1,32]{1,0:T(1,128)}, u32[]{:S(2)}) copy-start(f32[1,32]{1,0:T(1,128)} %param.19) | copy-start | bytes 388
  154.4 3.9 %copy-start.16 = (f32[1,32]{1,0:T(1,128)S(1)}, f32[1,32]{1,0:T(1,128)}, u32[]{:S(2)}) copy-start(f32[1,32]{1,0:T(1,128)} %param.20) | copy-start | bytes 388
  154.4 3.9 %copy-start.17 = (f32[1,32]{1,0:T(1,128)S(1)}, f32[1,32]{1,0:T(1,128)}, u32[]{:S(2)}) copy-start(f32[1,32]{1,0:T(1,128)} %param.21) | copy-start | bytes 388
Sparse Core Ops, SparseCore 0:
  37.6 91.1 all-gather.2

commit v3 on v2

v3 whole, which is shorter than its diff:
```python
import jax
import jax.numpy as jnp
from jax import lax
from jax.experimental import pallas as pl
from jax.experimental.pallas import tpu as pltpu
from jax.sharding import PartitionSpec as P

beta_one = 0.9
beta_two = 0.95
adam_count = 10
learn_rate = 0.00022
adam_eps = 1e-08
decay_rate = 0.1

RANKS, SHARDS = 8, 16
TOK, WIDTH, LAT, ROPE = 512, 7168, 512, 64
COLS = LAT + ROPE
BLOCK = WIDTH // 8
TILE = 512
HALF = COLS // 2
ROWS_A = 3 * HALF + HALF // 2
ROWS_B = ROWS_A + 16
EXT = COLS + 16
BF, F32 = jnp.bfloat16, jnp.float32
MIB = 1 << 20


def params(mib):
    return pltpu.CompilerParams(vmem_limit_bytes=mib * MIB)


def cost(flops, moved):
    return pl.CostEstimate(flops=flops, bytes_accessed=moved, transcendentals=0)


def moved(value, target):
    pairs = []
    for r in range(RANKS):
        for d in range(SHARDS):
            to = target(r, d)
            if 0 <= to[0] < RANKS:
                pairs.append((r * SHARDS + d, to[0] * SHARDS + to[1]))
    return lax.ppermute(value, ("pipe", "dp"), pairs)


def to_core(r, d):
    return r, d ^ 1


def to_ylo(r, d):
    return r, d ^ 2


def to_z(steps):
    return lambda r, d: (r, (d + 4 * steps) % SHARDS)


def to_mirror(r, d):
    return RANKS - 1 - r, d


def to_before(r, d):
    return r - 1, d


def to_before_near(r, d):
    return r - 1, d ^ 2


FLAG = jax.ShapeDtypeStruct((8, 128), F32)
ANYWHERE = pl.BlockSpec(memory_space=pltpu.HBM)
LATER = pl.BlockSpec(memory_space=pl.ANY)


def place():
    shard = lax.axis_index("dp")
    return shard >> 2, (shard >> 1) & 1, shard & 1


def columns(block, core):
    return pl.ds(pl.multiple_of(block * BLOCK + 384 * core, 128), TILE)


def start_all(copies):
    for copy in copies:
        copy.start()


def wait_all(copies):
    for copy in copies:
        copy.wait()


def after(value, *earlier):
    def kernel(*refs):
        pass

    return pl.pallas_call(
        kernel,
        in_specs=[ANYWHERE] + [LATER] * len(earlier),
        out_specs=ANYWHERE,
        out_shape=jax.ShapeDtypeStruct(value.shape, value.dtype),
        input_output_aliases={0: 0},
        cost_estimate=cost(0, 0),
        name="after",
    )(value, *earlier)


def cut_weight(weight, blocks, *earlier):
    def kernel(weight, *rest):
        out, sems = rest[-2:]
        z, y, core = place()
        rows = pl.ds(pl.multiple_of(core * HALF, HALF), HALF)
        copies = []
        for i, (dz, e) in enumerate(blocks):
            block = 2 * ((z + dz) & 3) + ((1 - y) ^ e)
            cols = pl.ds(pl.multiple_of(block * BLOCK, BLOCK), BLOCK)
            copies.append(pltpu.make_async_copy(weight.at[rows, cols], out.at[i], sems.at[i]))
        start_all(copies)
        wait_all(copies)

    count = len(blocks)
    return pl.pallas_call(
        kernel,
        in_specs=[ANYWHERE] + [LATER] * len(earlier),
        out_shape=jax.ShapeDtypeStruct((count, HALF, BLOCK), BF),
        scratch_shapes=[pltpu.SemaphoreType.DMA((count,))],
        compiler_params=params(60),
        cost_estimate=cost(0, 1_000),
        name="cut_weight",
    )(weight, *earlier)


PARTS = 7
PART = WIDTH // PARTS


def latent_kernel(hidden, weight, cot, gain, rope, earlier, out, tokens, matrix, sems):
    copies = []
    for i in range(PARTS):
        cols = pl.ds(i * PART, PART)
        copies.append(
            (
                pltpu.make_async_copy(hidden.at[:, cols], tokens.at[:, cols], sems.at[0, i]),
                pltpu.make_async_copy(
                    weight.at[pl.ds(0, LAT), cols], matrix.at[:, cols], sems.at[1, i]
                ),
            )
        )
    for pair in copies:
        start_all(pair)
    latent = jnp.zeros((TOK, LAT), F32)
    for i in range(PARTS):
        wait_all(copies[i])
        cols = slice(i * PART, i * PART + PART)
        latent += lax.dot_general(
            tokens[:, cols],
            matrix[:, cols],
            (((1,), (1,)), ((), ())),
            preferred_element_type=F32,
        )
    inv = lax.rsqrt(jnp.mean(latent * latent, axis=-1, keepdims=True) + 1e-06)
    normed = latent * inv
    c = cot[...].astype(F32)
    scaled = c * gain[...]
    grad = inv * (scaled - normed * jnp.mean(scaled * normed, axis=-1, keepdims=True))
    gain_part = jnp.sum(c * normed, axis=0, keepdims=True)
    out[0:LAT, :] = grad.T.astype(BF)
    out[LAT:COLS, :] = rope[...]
    high = gain_part.astype(BF)
    low = (gain_part - high.astype(F32)).astype(BF)
    row = lax.broadcasted_iota(jnp.int32, (16, LAT), 0)
    high = jnp.broadcast_to(high.astype(F32), (16, LAT))
    low = jnp.broadcast_to(low.astype(F32), (16, LAT))
    both = jnp.where(row == 0, high, jnp.where(row == 1, low, 0.0))
    out[COLS:EXT, :] = both.astype(BF)


def latent_step(hidden, weight, cot, gain, rope, earlier):
    inside = pl.BlockSpec(memory_space=pltpu.VMEM)
    return pl.pallas_call(
        latent_kernel,
        in_specs=[ANYWHERE, ANYWHERE, inside, inside, inside, LATER],
        out_shape=jax.ShapeDtypeStruct((EXT, TOK), BF),
        scratch_shapes=[
            pltpu.VMEM((TOK, WIDTH), BF),
            pltpu.VMEM((LAT, WIDTH), BF),
            pltpu.SemaphoreType.DMA((2, PARTS)),
        ],
        compiler_params=params(60),
        cost_estimate=cost(0, 1_000),
        name="latent_grad",
    )(hidden, weight, cot, gain, rope, earlier)


def weight_kernel(
    hidden,
    other,
    grad,
    grad_other,
    earlier,
    own_a,
    send_a,
    own_b,
    send_b,
    tiles,
    tiles_other,
    turned,
    turned_other,
    first_a,
    rest_a,
    keep_b,
    give_b,
    gain,
    in_sems,
    out_sems,
    grad_sems,
):
    z, y, core = place()
    steps = [(k, e) for k in (1, 2, 3, 0) for e in (1, 0)]
    incoming = []
    for i, (k, e) in enumerate(steps):
        cols = columns(2 * ((z + k) & 3) + (y ^ e), core)
        incoming.append(
            (
                pltpu.make_async_copy(hidden.at[:, cols], tiles.at[i], in_sems.at[0, i]),
                pltpu.make_async_copy(other.at[:, cols], tiles_other.at[i], in_sems.at[1, i]),
            )
        )
    grads = [
        pltpu.make_async_copy(grad, turned, grad_sems.at[0]),
        pltpu.make_async_copy(grad_other, turned_other, grad_sems.at[1]),
    ]
    start_all(grads)
    for pair in incoming:
        start_all(pair)
    wait_all(grads)

    sums = jnp.zeros((1, LAT), F32)
    for ref in (turned, turned_other):
        pair = ref[COLS:EXT, :].astype(F32)
        sums = sums + pair[0:1] + pair[1:2]
    gain[...] = jnp.zeros_like(gain)
    for i in range(4):
        gain[i : i + 1, :] = sums[:, 128 * i : 128 * i + 128]

    lane = lax.broadcasted_iota(jnp.int32, (HALF // 2, 128), 1)
    first = core == 0

    def packed(full):
        col = [full[:, 128 * j : 128 * j + 128] for j in range(4)]
        edge = jnp.where(first, col[3], col[0])
        top, low = edge[: HALF // 2], edge[HALF // 2 :]
        left = jnp.where(first, top, pltpu.roll(top, 64, 1))
        right = jnp.where(first, pltpu.roll(low, 64, 1), low)
        return [jnp.where(first, col[i], col[i + 1]) for i in range(3)] + [
            jnp.where(lane < 64, left, right)
        ]

    def put(ref, parts):
        at = 0
        for part in parts:
            n = part.shape[0]
            ref[at : at + n, :] = part.astype(ref.dtype)
            at += n

    outgoing = []
    for i, (k, e) in enumerate(steps):
        wait_all(incoming[i])
        whole = jnp.dot(turned[:COLS, :], tiles[i], preferred_element_type=F32)
        whole += jnp.dot(turned_other[:COLS, :], tiles_other[i], preferred_element_type=F32)
        buffer_a = first_a.at[e] if k == 0 else rest_a.at[2 * (k - 1) + e]
        buffer_b = keep_b.at[k] if e == 0 else give_b.at[k]
        put(buffer_a, packed(whole[:HALF]))
        put(buffer_b, packed(whole[HALF:]) + [gain[...]])
        to_a = own_a.at[e] if k == 0 else send_a.at[(z + k) & 3, e]
        to_b = (own_b, send_b)[e].at[k]
        outgoing.append(pltpu.make_async_copy(buffer_a, to_a, out_sems.at[0, i]))
        outgoing.append(pltpu.make_async_copy(buffer_b, to_b, out_sems.at[1, i]))
        start_all(outgoing[-2:])
    wait_all(outgoing)


def weight_step(hidden, other, grad, grad_other, earlier):
    return pl.pallas_call(
        weight_kernel,
        in_specs=[ANYWHERE] * 4 + [LATER],
        out_specs=[ANYWHERE] * 4,
        out_shape=[
            jax.ShapeDtypeStruct((2, ROWS_A, 128), F32),
            jax.ShapeDtypeStruct((4, 2, ROWS_A, 128), BF),
            jax.ShapeDtypeStruct((4, ROWS_B, 128), F32),
            jax.ShapeDtypeStruct((4, ROWS_B, 128), BF),
        ],
        scratch_shapes=[
            pltpu.VMEM((8, TOK, TILE), BF),
            pltpu.VMEM((8, TOK, TILE), BF),
            pltpu.VMEM((EXT, TOK), BF),
            pltpu.VMEM((EXT, TOK), BF),
            pltpu.VMEM((2, ROWS_A, 128), F32),
            pltpu.VMEM((6, ROWS_A, 128), BF),
            pltpu.VMEM((4, ROWS_B, 128), F32),
            pltpu.VMEM((4, ROWS_B, 128), BF),
            pltpu.VMEM((16, 128), F32),
            pltpu.SemaphoreType.DMA((2, 8)),
            pltpu.SemaphoreType.DMA((2, 8)),
            pltpu.SemaphoreType.DMA((2,)),
        ],
        compiler_params=params(60),
        cost_estimate=cost(0, 1_000),
        name="weight_grad",
    )(hidden, other, grad, grad_other, earlier)


def received_sum(ref, own, z):
    for other in range(4):
        own = own + jnp.where(z == other, 0.0, ref[other].astype(F32))
    return own


def whole(shape):
    return pl.BlockSpec(shape, lambda k: (0,) * len(shape))


FLAGGED = whole((8, 128))


def sum_a_kernel(own, r, *rest):
    keep, send, flag = rest[-3:]
    z, _, _ = place()
    total = received_sum(r.at[:, 0], own[0], z)

    @pl.when(pl.program_id(0) == 0)
    def _():
        keep[...] = total
        flag[...] = jnp.zeros_like(flag)

    @pl.when(pl.program_id(0) == 1)
    def _():
        send[...] = total.astype(BF)


def sum_a(own, r, *earlier):
    return pl.pallas_call(
        sum_a_kernel,
        grid=(2,),
        in_specs=[
            pl.BlockSpec((1, ROWS_A, 128), lambda e: (e, 0, 0)),
            pl.BlockSpec((4, 1, ROWS_A, 128), lambda e: (0, e, 0, 0)),
        ]
        + [LATER] * len(earlier),
        out_specs=[whole((ROWS_A, 128))] * 2 + [FLAGGED],
        out_shape=[
            jax.ShapeDtypeStruct((ROWS_A, 128), F32),
            jax.ShapeDtypeStruct((ROWS_A, 128), BF),
            FLAG,
        ],
        compiler_params=params(16),
        cost_estimate=cost(0, 3_500_000),
        name="sum_z",
    )(own, r, *earlier)


def sum_b_kernel(own, r, keep, send, flag):
    z, _, _ = place()
    k = pl.program_id(0)
    total = own[0] + r[0].astype(F32)
    send[(z + k) & 3] = total.astype(BF)

    @pl.when(k == 0)
    def _():
        keep[...] = total
        flag[...] = jnp.zeros_like(flag)


def sum_b(own, r):
    return pl.pallas_call(
        sum_b_kernel,
        grid=(4,),
        in_specs=[pl.BlockSpec((1, ROWS_B, 128), lambda k: (k, 0, 0))] * 2,
        out_specs=[whole((ROWS_B, 128)), whole((4, ROWS_B, 128)), FLAGGED],
        out_shape=[
            jax.ShapeDtypeStruct((ROWS_B, 128), F32),
            jax.ShapeDtypeStruct((4, ROWS_B, 128), BF),
            FLAG,
        ],
        compiler_params=params(16),
        cost_estimate=cost(0, 4_500_000),
        name="sum_y",
    )(own, r)


def sum_all_kernel(keep_a, ra, keep_b, rb, earlier, total, send, flag):
    z, _, _ = place()
    a = keep_a[...] + ra[...].astype(F32)
    b = received_sum(rb, keep_b[...], z)
    total[:ROWS_A, :] = a
    total[ROWS_A:, :] = b
    send[:ROWS_A, :] = a.astype(BF)
    send[ROWS_A:, :] = b.astype(BF)
    flag[...] = jnp.zeros_like(flag)


def sum_all(*parts):
    rows = ROWS_A + ROWS_B
    return pl.pallas_call(
        sum_all_kernel,
        grid=(1,),
        in_specs=[whole(part.shape) for part in parts[:-1]] + [LATER],
        out_specs=[whole((rows, 128)), whole((rows, 128)), FLAGGED],
        out_shape=[
            jax.ShapeDtypeStruct((rows, 128), F32),
            jax.ShapeDtypeStruct((rows, 128), BF),
            FLAG,
        ],
        compiler_params=params(16),
        cost_estimate=cost(0, 4_000_000),
        name="sum_shard",
    )(*parts)


def adamw(master, first, second, grad):
    new_first = beta_one * first + (1.0 - beta_one) * grad
    new_second = beta_two * second + (1.0 - beta_two) * grad * grad
    first_hat = new_first / (1.0 - beta_one**adam_count)
    second_hat = new_second / (1.0 - beta_two**adam_count)
    new_master = master - learn_rate * (
        first_hat / (jnp.sqrt(second_hat) + adam_eps) + decay_rate * master
    )
    return (new_master, new_first, new_second)


def adam_kernel(s, own, far, master, first, second, earlier, n_master, n_first, n_second, gain, grad):
    total = own[...] + far[...].astype(F32)
    core = s[0]
    gain[...] = total[2 * ROWS_A : 2 * ROWS_A + 8]

    def both(lo, n):
        return [total[h * ROWS_A + lo : h * ROWS_A + lo + n] for h in range(2)]

    for i in range(3):
        block = jnp.concatenate(both(i * HALF, HALF), axis=0)
        grad[pl.ds(pl.multiple_of(64 * core + 128 * i, 64), 128), :] = block.T
    edge = []
    for part in both(3 * HALF, HALF // 2):
        edge += [part, pltpu.roll(part, 64, 1)]
    block = jnp.concatenate(edge, axis=0)
    grad[pl.ds(pl.multiple_of(384 * (1 - core), 64), 64), :] = block.T[:64]
    n_master[...], n_first[...], n_second[...] = adamw(
        master[...], first[...], second[...], grad[...]
    )


def adam_step(s, own, far, master, first, second, earlier):
    shape = jax.ShapeDtypeStruct(master.shape, F32)
    spec = pl.BlockSpec(memory_space=pltpu.VMEM)
    return pl.pallas_call(
        adam_kernel,
        in_specs=[pl.BlockSpec(memory_space=pltpu.SMEM)]
        + [spec] * 5
        + [LATER],
        out_specs=[spec] * 4,
        out_shape=[shape] * 3 + [jax.ShapeDtypeStruct((8, 128), F32)],
        scratch_shapes=[pltpu.VMEM(master.shape, F32)],
        compiler_params=params(32),
        cost_estimate=cost(0, 9_000_000),
        name="adamw",
    )(s, own, far, master, first, second, earlier)


def input_step(grad, pieces, earlier, begun=None):
    places = [(n, i, dz, e) for n, piece in enumerate(pieces) for i, (dz, e) in enumerate(piece[2])]
    count, arrays = len(places), len(pieces)

    def kernel(grad, *rest):
        halves = rest[: 2 * arrays]
        out, flag, held, blocks, in_sems, out_sems = rest[-6:]
        z, y, core = place()
        incoming = []
        for at, (n, i, _, _) in enumerate(places):
            for half in range(2):
                slot = core ^ half
                rows = pl.ds(pl.multiple_of(slot * HALF, HALF), HALF)
                incoming.append(
                    pltpu.make_async_copy(
                        halves[2 * n + half].at[i], held.at[at, rows], in_sems.at[at, half]
                    )
                )
        start_all(incoming)
        flag[...] = jnp.zeros_like(flag)
        turned = grad[:COLS, :].astype(F32).T.astype(BF)
        outgoing = []
        for at, (_, _, dz, e) in enumerate(places):
            wait_all(incoming[2 * at : 2 * at + 2])
            blocks[at] = jnp.dot(turned, held[at], preferred_element_type=F32).astype(BF)
            block = 2 * ((z + dz) & 3) + (y ^ e)
            cols = pl.ds(pl.multiple_of(block * BLOCK, BLOCK), BLOCK)
            outgoing.append(
                pltpu.make_async_copy(blocks.at[at], out.at[:, cols], out_sems.at[at])
            )
            outgoing[-1].start()
        wait_all(outgoing)

    inside = pl.BlockSpec(memory_space=pltpu.VMEM)
    operands = [grad]
    for own, far, _ in pieces:
        operands += [own, far]
    halves = len(operands) - 1
    operands += earlier + ([] if begun is None else [begun])
    return pl.pallas_call(
        kernel,
        in_specs=[inside]
        + [ANYWHERE] * halves
        + [LATER] * len(earlier)
        + ([] if begun is None else [ANYWHERE]),
        out_specs=[ANYWHERE, inside],
        out_shape=[jax.ShapeDtypeStruct((TOK, WIDTH), BF), FLAG],
        scratch_shapes=[
            pltpu.VMEM((count, COLS, BLOCK), BF),
            pltpu.VMEM((count, TOK, BLOCK), BF),
            pltpu.SemaphoreType.DMA((count, 2)),
            pltpu.SemaphoreType.DMA((count,)),
        ],
        input_output_aliases={} if begun is None else {len(operands) - 1: 0},
        compiler_params=params(36),
        cost_estimate=cost(TOK * WIDTH * COLS, 8_000_000),
        name="input_grad",
    )(*operands)


def rope_step(rope_cot):
    half = ROPE // 2
    position = jnp.arange(TOK).astype(F32)
    freqs = 10000.0 ** (-2.0 * jnp.arange(half).astype(F32) / ROPE)
    angle = freqs[:, None] * position[None, :]
    cosine = jnp.cos(angle)
    sine = jnp.sin(angle)
    rope = rope_cot.T.astype(F32)
    first, second = rope[:half], rope[half:]
    return jnp.concatenate(
        [first * cosine + second * sine, second * cosine - first * sine], axis=0
    ).astype(BF)


def on_device(
    hidden_in,
    weight,
    gain,
    latent_cot,
    rope_cot,
    master_weight,
    first_moment,
    second_moment,
    gain_master,
    gain_first,
    gain_second,
):
    shard = lax.axis_index("dp")
    s = (shard & 1).astype(jnp.int32)[None]
    hidden = hidden_in[0]
    turned = weight[0].T
    other = moved(hidden, to_core)
    cuts = [cut_weight(turned, [(0, 0)])]
    cuts.append(cut_weight(turned, [(0, 1)], cuts[0]))
    cuts.append(cut_weight(turned, [(2, 0), (2, 1)], cuts[1]))
    here, beside, across = (moved(value, to_before_near) for value in cuts)
    rope = rope_step(rope_cot[0])
    grad = latent_step(hidden, turned, latent_cot[0], gain, rope, cuts[2])
    grad_other = moved(grad, to_core)
    grad_next = moved(grad, to_before)
    above, below = moved(here, to_z(-1)), moved(here, to_z(1))
    def both(value, *blocks):
        return value, moved(value, to_core), blocks

    pieces = (
        both(here, (0, 0)),
        both(across, (2, 0), (2, 1)),
        both(above, (1, 0)),
        both(below, (3, 0)),
        both(beside, (0, 1)),
    )
    own_a, send_a, own_b, send_b = weight_step(hidden, other, grad, grad_other, pieces[0][1])
    along_z = [[4 * z + k for z in range(4)] for k in range(4)]

    def exchanged(value):
        return lax.all_to_all(value, "dp", 0, 0, axis_index_groups=along_z, tiled=True)

    rb = moved(send_b, to_ylo)
    keep_a, send_a, is_a = sum_a(own_a, exchanged(send_a), *(piece[1] for piece in pieces))
    ra = moved(send_a, to_ylo)
    keep_b, send_b, is_b = sum_b(own_b, rb)
    received, is_begun = input_step(grad_next, pieces, [is_a, is_b])
    total, send, is_summed = sum_all(keep_a, ra, keep_b, exchanged(send_b), is_begun)
    far = moved(send, to_mirror)
    beside = after(beside, is_begun)
    above_2, below_2 = moved(beside, to_z(-1)), moved(beside, to_z(1))
    pieces = both(above_2, (1, 1)), both(below_2, (3, 1))
    received, is_received = input_step(grad_next, pieces, [is_summed], received)
    next_master, next_first, next_second, gain_rows = adam_step(
        s, total, far, master_weight[0], first_moment[0], second_moment[0], is_received
    )
    gain_total = lax.dynamic_slice(gain_rows[:4].reshape(LAT), (shard * 32,), (32,))
    next_gain = adamw(gain_master[0], gain_first[0], gain_second[0], gain_total)
    return (
        received[None],
        next_master[None],
        next_first[None],
        next_second[None],
        *(value[None] for value in next_gain),
    )


def solution(mesh):
    tokens, shared = P("pipe", "dp", None), P("pipe", None)
    split = P("pipe", "dp")
    return jax.shard_map(
        on_device,
        mesh=mesh,
        in_specs=(tokens, P("pipe", None, None), shared) + (tokens,) * 5 + (split,) * 3,
        out_specs=(tokens,) * 4 + (split,) * 3,
        check_vma=False,
    )
```

time: 168 us -> 148 us (0.88)
  waiting for transfers between devices: 70.6 us -> 48.7 us
  starting transfers between devices: 17.7 us -> 39.3 us
  between operations: 14.2 us -> 0.98 us
  Pallas kernels: 53.4 us -> 46.7 us
  local copies, waits for them, and re-layouts: 7.59 us -> 9.58 us
    ppermute x13 -> x20, waiting for transfers between devices: 70.6 us -> 48.7 us  [moved(): return lax.ppermute(value, ('pipe', 'dp'), pairs)]
    ppermute x13 -> x20, starting transfers between devices: 17.7 us -> 30.6 us  [moved(): return lax.ppermute(value, ('pipe', 'dp'), pairs)]
    all_to_all x0 -> x2, starting transfers between devices: none -> 8.73 us  [exchanged(): lax.all_to_all(value, 'dp', 0, 0, axis_index_groups=along_z, tiled=True)]
    pallas_call x7 -> x9, Pallas kernels: 48.8 us -> 42.2 us  [the longest x2 14.4 us: input_step(): pl.pallas_call(kernel, in_specs=[inside] + [ANYWHERE] * halves + [LATER]...]
    unnamed x40 -> x44, local copies, waits for them, and re-layouts: 7.59 us -> 9.58 us
  transfers between devices with their start and end apart: 14 -> 22, of which waited for: 7 -> 8; matrix products, arithmetic and copies ran while one was open for 1% -> 1% of each run, Pallas kernels for 23% -> 30%
where the time goes in v3:
time: 148 us; the launch traced here: 147 us
  waiting for transfers between devices  48.7 us (33%)
  Pallas kernels  46.7 us (32%)
  starting transfers between devices  39.3 us (27%)
  local copies, waits for them, and re-layouts  9.58 us (6%)
  other arithmetic  1.59 us (1%)
    ppermute x20, waiting for transfers between devices, moved(): return lax.ppermute(value, ('pipe', 'dp'), pairs)  48.7 us
    ppermute x20, starting transfers between devices, moved(): return lax.ppermute(value, ('pipe', 'dp'), pairs)  30.6 us
    pallas_call x2, Pallas kernels, input_step(): pl.pallas_call(kernel, in_specs=[inside] + [ANYWHERE] * halves + [LATER]...  14.4 us
    pallas_call x1, Pallas kernels, weight_step(): pl.pallas_call(weight_kernel, in_specs=[ANYWHERE] * 4 + [LATER], out_spec...  11.6 us
    unnamed x44, local copies, waits for them, and re-layouts  9.58 us
    pallas_call x1, Pallas kernels, latent_step(): pl.pallas_call(latent_kernel, in_specs=[ANYWHERE, ANYWHERE, inside, insid...  9.18 us
    all_to_all x2, starting transfers between devices, exchanged(): lax.all_to_all(value, 'dp', 0, 0, axis_index_groups=along_z, tiled=True)  8.73 us
    pallas_call x3, Pallas kernels, cut_weight(): pl.pallas_call(kernel, in_specs=[ANYWHERE] + [LATER] * len(earlier), out_...  5.9 us
  transfers between devices with their start and end apart: 22, of which 8 were waited for; matrix products, arithmetic and copies ran while one was open for 1% of the time, Pallas kernels for 30%

profile of v3, /device:TPU:1, one launch (start us, length us, event | category | flops | bytes accessed | tf_op | source)
XLA Modules:
  0.0 146.8 jit_solution(16031632440748106587)
XLA Ops:
  0.6 1.5 %collective-permute-start.11 = (bf16[512,7168]{1,0:T(8,128)(2,1)}, bf16[512,7168]{1,0:T(8,128)(2,1)}, u32[]{:S(2)}, u32[]{:S(2)}) collective-permute-start(bf16[512,7168]{1,0:T(8,128)(2,1)} %bitcast.48), channel_id=1, source_target_pairs={{0,1},{1,0},{2,3},{3,2},{4,5},{5,4},{6,7},{7,6},{8,9},{9,8},{10,11... | collective-permute-start | bytes 22020104 | tf_op jit(solution)/shard_map/ppermute | solution.py:43
  2.1 1.8 %cut_weight.3.rest_0_ = bf16[1,288,896]{2,1,0:T(8,128)(2,1)} custom-call(bf16[576,7168]{1,0:T(8,128)(2,1)} %bitcast.44), custom_call_target="tpu_custom_call" | custom-call | bytes 1000 | tf_op jit(solution)/shard_map/cut_weight/pallas_call | solution.py:123
  4.0 1.3 collective-permute-start.2
  5.3 1.9 %cut_weight.4.rest_0_ = bf16[1,288,896]{2,1,0:T(8,128)(2,1)} custom-call(bf16[576,7168]{1,0:T(8,128)(2,1)} %bitcast.45, bf16[1,288,896]{2,1,0:T(8,128)(2,1)} %cut_weight.3.rest_0_), custom_call_target="tpu_custom_call" | custom-call | bytes 1000 | tf_op jit(solution)/shard_map/cut_weight/pallas_call | solution.py:123
  7.1 2.2 %cut_weight.5.earlier = bf16[2,288,896]{2,1,0:T(8,128)(2,1)} custom-call(bf16[576,7168]{1,0:T(8,128)(2,1)} %bitcast.46, bf16[1,288,896]{2,1,0:T(8,128)(2,1)} %cut_weight.4.rest_0_), custom_call_target="tpu_custom_call" | custom-call | bytes 1000 | tf_op jit(solution)/shard_map/cut_weight/pallas_call | solution.py:123
  9.4 0.3 fusion.5
  9.7 0.6 pad_maximum_fusion.rope
  10.4 9.2 %latent_grad.1.grad = bf16[592,512]{1,0:T(8,128)(2,1)} custom-call(bf16[512,7168]{1,0:T(8,128)(2,1)} %bitcast.49, bf16[576,7168]{1,0:T(8,128)(2,1)} %bitcast.47, bf16[512,512]{1,0:T(8,128)(2,1)} %bitcast.52, f32[1,512]{1,0:T(1,128)} %gain.1, bf16[64,512]{1,0:T(8,128)(2,1)} %pad_maximum_fusion.rope, bf16[2,288,896]{2,1,0:T(8,128)(2,1)} %cut_weight.5.earlier), custom_call_target="tpu_custom_call" | custom-call | bytes 1000 | tf_op jit(solution)/shard_map/latent_grad/pallas_call | solution.py:181
  19.7 1.2 collective-permute-done.2.rest_0_
  20.9 0.7 collective-permute-start.3
  21.6 1.3 collective-permute-start.4
  23.1 0.6 copy-done.17
  24.0 11.6 %weight_grad.1 = (f32[2,1008,128]{2,1,0:T(8,128)}, bf16[4,2,1008,128]{3,2,1,0:T(8,128)(2,1)}, f32[4,1024,128]{2,1,0:T(8,128)}, bf16[4,1024,128]{2,1,0:T(8,128)(2,1)}) custom-call(bf16[512,7168]{1,0:T(8,128)(2,1)} %bitcast.50, bf16[512,7168]{1,0:T(8,128)(2,1)} %collective-permute-done.11.other, bf16[592,512]{1,0:T(8,128)(2,1)} %latent_grad.1.grad, ...), custom_call_target="tpu_custom_call" | custom-call | bytes 1000 | tf_op jit(solution)/shard_map/weight_grad/pallas_call | solution.py:285
  35.6 0.7 collective-permute-start.13
  36.4 5.0 %all-to-all-start = ((bf16[4,2,1008,128]{3,2,1,0:T(8,128)(2,1)}), bf16[4,2,1008,128]{3,2,1,0:T(8,128)(2,1)S(1)}, u32[]{:S(2)}, u32[]{:S(2)}) async-start(bf16[4,2,1008,128]{3,2,1,0:T(8,128)(2,1)} %get-tuple-element.29), calls=%async_computation | async-start | bytes 4128768 | tf_op jit(solution)/shard_map/all_to_all | solution.py:586
  41.4 1.3 collective-permute-start.1
  42.7 2.7 %collective-permute-start.6 = (bf16[1,288,896]{2,1,0:T(8,128)(2,1)}, bf16[1,288,896]{2,1,0:T(8,128)(2,1)}, u32[]{:S(2)}, u32[]{:S(2)}) collective-permute-start(bf16[1,288,896]{2,1,0:T(8,128)(2,1)} %copy-done.15), channel_id=1, source_target_pairs={{0,12},{1,13},{2,14},{3,15},{4,0},{5,1},{6,2},{7,3},{8,4},{9,5},{1... | collective-permute-start | bytes 1548296 | tf_op jit(solution)/shard_map/ppermute | solution.py:43
  45.4 5.1 %collective-permute-done.4.rest_2_ = bf16[2,288,896]{2,1,0:T(8,128)(2,1)} collective-permute-done((bf16[2,288,896]{2,1,0:T(8,128)(2,1)}, bf16[2,288,896]{2,1,0:T(8,128)(2,1)}, u32[]{:S(2)}, u32[]{:S(2)}) %collective-permute-start.4) | collective-permute-done | bytes 1032224 | tf_op jit(solution)/shard_map/ppermute | solution.py:43
  50.6 0.8 collective-permute-start.5
  51.3 10.3 %collective-permute-done.1.rest_8_.refs_0_ = bf16[1,288,896]{2,1,0:T(8,128)(2,1)} collective-permute-done((bf16[1,288,896]{2,1,0:T(8,128)(2,1)}, bf16[1,288,896]{2,1,0:T(8,128)(2,1)}, u32[]{:S(2)}, u32[]{:S(2)}) %collective-permute-start.1) | collective-permute-done | bytes 516128 | tf_op jit(solution)/shard_map/ppermute | solution.py:43
  61.6 1.3 collective-permute-start
  62.9 13.5 %collective-permute-done.6.rest_4_ = bf16[1,288,896]{2,1,0:T(8,128)(2,1)} collective-permute-done((bf16[1,288,896]{2,1,0:T(8,128)(2,1)}, bf16[1,288,896]{2,1,0:T(8,128)(2,1)}, u32[]{:S(2)}, u32[]{:S(2)}) %collective-permute-start.6) | collective-permute-done | bytes 516128 | tf_op jit(solution)/shard_map/ppermute | solution.py:43
  76.4 1.6 %collective-permute-start.10 = (bf16[1,288,896]{2,1,0:T(8,128)(2,1)}, bf16[1,288,896]{2,1,0:T(8,128)(2,1)}, u32[]{:S(2)}, u32[]{:S(2)}) collective-permute-start(bf16[1,288,896]{2,1,0:T(8,128)(2,1)} %collective-permute-done.1.rest_8_.refs_0_), channel_id=1, source_target_pairs={{0,1},{1,0},{2,3},{3,2},{4,5},{5,4},{6,7},{7,6},{8,9},{9,8},{10,11... | collective-permute-start | bytes 1548296 | tf_op jit(solution)/shard_map/ppermute | solution.py:43
  78.0 1.2 collective-permute-start.7
  79.2 1.6 %copy-done = f32[4,1024,128]{2,1,0:T(8,128)S(1)} copy-done((f32[4,1024,128]{2,1,0:T(8,128)S(1)}, f32[4,1024,128]{2,1,0:T(8,128)}, u32[]{:S(2)}) %copy-start) | copy-done | bytes 2097176
  81.1 1.0 copy-done.7
  82.0 0.8 copy-done.9
  82.8 3.7 %all-to-all-start.1 = ((bf16[4,1024,128]{2,1,0:T(8,128)(2,1)}), bf16[4,1024,128]{2,1,0:T(8,128)(2,1)S(1)}, u32[]{:S(2)}, u32[]{:S(2)}) async-start(bf16[4,1024,128]{2,1,0:T(8,128)(2,1)} %copy-done.7), calls=%async_computation.1 | async-start | bytes 2097152 | tf_op jit(solution)/shard_map/all_to_all | solution.py:586
  86.6 1.0 copy-done.2
  87.6 1.2 copy-done.8
  88.9 0.9 sum_z.1
  89.8 0.8 copy-done.11
  90.6 9.1 %input_grad.2 = (bf16[512,7168]{1,0:T(8,128)(2,1)}, f32[8,128]{1,0:T(8,128)S(1)}) custom-call(bf16[592,512]{1,0:T(8,128)(2,1)} %collective-permute-done.grad, bf16[1,288,896]{2,1,0:T(8,128)(2,1)S(1)} %copy-done.16, bf16[1,288,896]{2,1,0:T(8,128)(2,1)S(1)} %copy-done.3, bf16[2,288,896]{2,1,0:T(8,128)(2,1)} %collective-permute-done.4.rest_2_, ...), custom_call_target="tpu_custom_call" | custom-call | flops 2113929216 | bytes 8000000 | tf_op jit(solution)/shard_map/input_grad/pallas_call | solution.py:510
  99.7 0.6 copy-done.13
  100.3 2.4 %collective-permute-start.14 = (bf16[1,288,896]{2,1,0:T(8,128)(2,1)}, bf16[1,288,896]{2,1,0:T(8,128)(2,1)}, u32[]{:S(2)}, u32[]{:S(2)}) collective-permute-start(bf16[1,288,896]{2,1,0:T(8,128)(2,1)} %after.1), channel_id=1, source_target_pairs={{0,12},{1,13},{2,14},{3,15},{4,0},{5,1},{6,2},{7,3},{8,4},{9,5},{1... | collective-permute-start | bytes 1548296 | tf_op jit(solution)/shard_map/ppermute | solution.py:43
  102.7 0.8 collective-permute-start.18
  103.5 9.9 %collective-permute-done.14.rest_0_ = bf16[1,288,896]{2,1,0:T(8,128)(2,1)} collective-permute-done((bf16[1,288,896]{2,1,0:T(8,128)(2,1)}, bf16[1,288,896]{2,1,0:T(8,128)(2,1)}, u32[]{:S(2)}, u32[]{:S(2)}) %collective-permute-start.14) | collective-permute-done | bytes 516128 | tf_op jit(solution)/shard_map/ppermute | solution.py:43
  113.4 1.6 %collective-permute-start.15 = (bf16[1,288,896]{2,1,0:T(8,128)(2,1)}, bf16[1,288,896]{2,1,0:T(8,128)(2,1)}, u32[]{:S(2)}, u32[]{:S(2)}) collective-permute-start(bf16[1,288,896]{2,1,0:T(8,128)(2,1)} %collective-permute-done.14.rest_0_), channel_id=1, source_target_pairs={{0,1},{1,0},{2,3},{3,2},{4,5},{5,4},{6,7},{7,6},{8,9},{9,8},{10,11... | collective-permute-start | bytes 1548296 | tf_op jit(solution)/shard_map/ppermute | solution.py:43
  115.0 1.4 collective-permute-done.16.rest_2_
  116.4 2.0 %collective-permute-start.17 = (bf16[1,288,896]{2,1,0:T(8,128)(2,1)}, bf16[1,288,896]{2,1,0:T(8,128)(2,1)}, u32[]{:S(2)}, u32[]{:S(2)}) collective-permute-start(bf16[1,288,896]{2,1,0:T(8,128)(2,1)} %collective-permute-done.16.rest_2_), channel_id=1, source_target_pairs={{0,1},{1,0},{2,3},{3,2},{4,5},{5,4},{6,7},{7,6},{8,9},{9,8},{10,11... | collective-permute-start | bytes 1548296 | tf_op jit(solution)/shard_map/ppermute | solution.py:43
  118.4 1.0 copy-done.12
  119.5 0.7 copy-done.14
  120.1 1.1 sum_shard.1
  121.2 9.2 %collective-permute-start.19 = (bf16[2032,128]{1,0:T(8,128)(2,1)}, bf16[2032,128]{1,0:T(8,128)(2,1)S(1)}, u32[]{:S(2)}, u32[]{:S(2)}) collective-permute-start(bf16[2032,128]{1,0:T(8,128)(2,1)} %get-tuple-element.43), channel_id=1, source_target_pairs={{0,112},{1,113},{2,114},{3,115},{4,116},{5,117},{6,118},{7,119},{8... | collective-permute-start | bytes 1560584 | tf_op jit(solution)/shard_map/ppermute | solution.py:43
  130.5 5.4 %input_grad.3 = (bf16[512,7168]{1,0:T(8,128)(2,1)}, f32[8,128]{1,0:T(8,128)S(1)}) custom-call(bf16[592,512]{1,0:T(8,128)(2,1)} %collective-permute-done.grad, bf16[1,288,896]{2,1,0:T(8,128)(2,1)} %collective-permute-done.14.rest_0_, bf16[1,288,896]{2,1,0:T(8,128)(2,1)} %collective-permute-done.15.rest_1_, ...), custom_call_target="tpu_custom_call", output_to_operand_aliasing={{0}: (6, {})} | custom-call | flops 2113929216 | bytes 8000000 | tf_op jit(solution)/shard_map/input_grad/pallas_call | solution.py:510
  135.8 7.0 %collective-permute-done.19.far = bf16[2032,128]{1,0:T(8,128)(2,1)S(1)} collective-permute-done((bf16[2032,128]{1,0:T(8,128)(2,1)}, bf16[2032,128]{1,0:T(8,128)(2,1)S(1)}, u32[]{:S(2)}, u32[]{:S(2)}) %collective-permute-start.19) | collective-permute-done | bytes 520224 | tf_op jit(solution)/shard_map/ppermute | solution.py:43
  142.9 3.3 %adamw.1 = (f32[448,576]{1,0:T(8,128)}, f32[448,576]{1,0:T(8,128)}, f32[448,576]{1,0:T(8,128)}, f32[8,128]{1,0:T(8,128)S(1)}) custom-call(s32[1]{0:T(128)} %bitcast.9.s, f32[2032,128]{1,0:T(8,128)S(1)} %get-tuple-element.42.own, bf16[2032,128]{1,0:T(8,128)(2,1)S(1)} %collective-permute-done.19.far, f32[448,576]{1,0:T(8,128)S(1)} %bitcast.41, ...), custom_call_target="tpu_custom_call" | custom-call | bytes 9000000 | tf_op jit(solution)/shard_map/adamw/pallas_call | solution.py:457
  146.2 0.6 fusion.11
  (59 shorter events, 1.0 us)
Async XLA Ops:
  0.6 22.5 %collective-permute-start.11 = (bf16[512,7168]{1,0:T(8,128)(2,1)}, bf16[512,7168]{1,0:T(8,128)(2,1)}, u32[]{:S(2)}, u32[]{:S(2)}) collective-permute-start(bf16[512,7168]{1,0:T(8,128)(2,1)} %bitcast.48), channel_id=1, source_target_pairs={{0,1},{1,0},{2,3},{3,2},{4,5},{5,4},{6,7},{7,6},{8,9},{9,8},{10,11... | collective-permute-start | bytes 22020104 | tf_op jit(solution)/shard_map/ppermute | solution.py:43
  4.0 16.9 %collective-permute-start.2 = (bf16[1,288,896]{2,1,0:T(8,128)(2,1)}, bf16[1,288,896]{2,1,0:T(8,128)(2,1)S(1)}, u32[]{:S(2)}, u32[]{:S(2)}) collective-permute-start(bf16[1,288,896]{2,1,0:T(8,128)(2,1)} %cut_weight.3.rest_0_), channel_id=1, source_target_pairs={{16,2},{17,3},{18,0},{19,1},{20,6},{21,7},{22,4},{23,5},{24,10},{2... | collective-permute-start | bytes 1548296 | tf_op jit(solution)/shard_map/ppermute | solution.py:43
  7.1 2.2 %copy-start.18 = (bf16[1,512,64]{1,2,0:T(8,128)(2,1)S(1)}, bf16[1,512,64]{1,2,0:T(8,128)(2,1)}, u32[]{:S(2)}) copy-start(bf16[1,512,64]{1,2,0:T(8,128)(2,1)} %param.15) | copy-start | bytes 196612
  19.6 3.3 %collective-permute-start.12 = (bf16[592,512]{1,0:T(8,128)(2,1)}, bf16[592,512]{1,0:T(8,128)(2,1)S(1)}, u32[]{:S(2)}, u32[]{:S(2)}) collective-permute-start(bf16[592,512]{1,0:T(8,128)(2,1)} %latent_grad.1.grad), channel_id=1, source_target_pairs={{0,1},{1,0},{2,3},{3,2},{4,5},{5,4},{6,7},{7,6},{8,9},{9,8},{10,11... | collective-permute-start | bytes 1818632 | tf_op jit(solution)/shard_map/ppermute | solution.py:43
  20.9 14.7 %copy-start.15 = (bf16[1,288,896]{2,1,0:T(8,128)(2,1)}, bf16[1,288,896]{2,1,0:T(8,128)(2,1)S(1)}, u32[]{:S(2)}) copy-start(bf16[1,288,896]{2,1,0:T(8,128)(2,1)S(1)} %collective-permute-done.2.rest_0_) | copy-start | bytes 1548292
  20.9 2.3 %collective-permute-start.3 = (bf16[1,288,896]{2,1,0:T(8,128)(2,1)S(1)}, bf16[1,288,896]{2,1,0:T(8,128)(2,1)S(1)}, u32[]{:S(2)}, u32[]{:S(2)}) collective-permute-start(bf16[1,288,896]{2,1,0:T(8,128)(2,1)S(1)} %collective-permute-done.2.rest_0_), channel_id=1, source_target_pairs={{0,1},{1,0},{2,3},{3,2},{4,5},{5,4},{6,7},{7,6},{8,9},{9,8},{10,11... | collective-permute-start | bytes 1548296 | tf_op jit(solution)/shard_map/ppermute | solution.py:43
  21.6 28.9 %collective-permute-start.4 = (bf16[2,288,896]{2,1,0:T(8,128)(2,1)}, bf16[2,288,896]{2,1,0:T(8,128)(2,1)}, u32[]{:S(2)}, u32[]{:S(2)}) collective-permute-start(bf16[2,288,896]{2,1,0:T(8,128)(2,1)} %cut_weight.5.earlier), channel_id=1, source_target_pairs={{16,2},{17,3},{18,0},{19,1},{20,6},{21,7},{22,4},{23,5},{24,10},{2... | collective-permute-start | bytes 3096584 | tf_op jit(solution)/shard_map/ppermute | solution.py:43
  22.9 0.8 copy-start.17
  23.1 0.9 copy-start.1
  35.6 43.6 %collective-permute-start.13 = (bf16[4,1024,128]{2,1,0:T(8,128)(2,1)}, bf16[4,1024,128]{2,1,0:T(8,128)(2,1)S(1)}, u32[]{:S(2)}, u32[]{:S(2)}) collective-permute-start(bf16[4,1024,128]{2,1,0:T(8,128)(2,1)} %get-tuple-element.32), channel_id=1, source_target_pairs={{0,2},{1,3},{2,0},{3,1},{4,6},{5,7},{6,4},{7,5},{8,10},{9,11},{10,... | collective-permute-start | bytes 3145736 | tf_op jit(solution)/shard_map/ppermute | solution.py:43
  36.4 46.5 %all-to-all-start = ((bf16[4,2,1008,128]{3,2,1,0:T(8,128)(2,1)}), bf16[4,2,1008,128]{3,2,1,0:T(8,128)(2,1)S(1)}, u32[]{:S(2)}, u32[]{:S(2)}) async-start(bf16[4,2,1008,128]{3,2,1,0:T(8,128)(2,1)} %get-tuple-element.29), calls=%async_computation | async-start | bytes 4128768 | tf_op jit(solution)/shard_map/all_to_all | solution.py:586
  41.4 20.2 %collective-permute-start.1 = (bf16[1,288,896]{2,1,0:T(8,128)(2,1)}, bf16[1,288,896]{2,1,0:T(8,128)(2,1)}, u32[]{:S(2)}, u32[]{:S(2)}) collective-permute-start(bf16[1,288,896]{2,1,0:T(8,128)(2,1)} %cut_weight.4.rest_0_), channel_id=1, source_target_pairs={{16,2},{17,3},{18,0},{19,1},{20,6},{21,7},{22,4},{23,5},{24,10},{2... | collective-permute-start | bytes 1548296 | tf_op jit(solution)/shard_map/ppermute | solution.py:43
  42.7 33.8 %collective-permute-start.6 = (bf16[1,288,896]{2,1,0:T(8,128)(2,1)}, bf16[1,288,896]{2,1,0:T(8,128)(2,1)}, u32[]{:S(2)}, u32[]{:S(2)}) collective-permute-start(bf16[1,288,896]{2,1,0:T(8,128)(2,1)} %copy-done.15), channel_id=1, source_target_pairs={{0,12},{1,13},{2,14},{3,15},{4,0},{5,1},{6,2},{7,3},{8,4},{9,5},{1... | collective-permute-start | bytes 1548296 | tf_op jit(solution)/shard_map/ppermute | solution.py:43
  45.4 32.6 %collective-permute-start.8 = (bf16[1,288,896]{2,1,0:T(8,128)(2,1)}, bf16[1,288,896]{2,1,0:T(8,128)(2,1)}, u32[]{:S(2)}, u32[]{:S(2)}) collective-permute-start(bf16[1,288,896]{2,1,0:T(8,128)(2,1)} %copy-done.15), channel_id=1, source_target_pairs={{0,4},{1,5},{2,6},{3,7},{4,8},{5,9},{6,10},{7,11},{8,12},{9,13},{1... | collective-permute-start | bytes 1548296 | tf_op jit(solution)/shard_map/ppermute | solution.py:43
  50.6 36.0 %collective-permute-start.5 = (bf16[2,288,896]{2,1,0:T(8,128)(2,1)}, bf16[2,288,896]{2,1,0:T(8,128)(2,1)}, u32[]{:S(2)}, u32[]{:S(2)}) collective-permute-start(bf16[2,288,896]{2,1,0:T(8,128)(2,1)} %collective-permute-done.4.rest_2_), channel_id=1, source_target_pairs={{0,1},{1,0},{2,3},{3,2},{4,5},{5,4},{6,7},{7,6},{8,9},{9,8},{10,11... | collective-permute-start | bytes 3096584 | tf_op jit(solution)/shard_map/ppermute | solution.py:43
  61.6 29.0 %collective-permute-start = (bf16[592,512]{1,0:T(8,128)(2,1)}, bf16[592,512]{1,0:T(8,128)(2,1)}, u32[]{:S(2)}, u32[]{:S(2)}) collective-permute-start(bf16[592,512]{1,0:T(8,128)(2,1)} %latent_grad.1.grad), channel_id=1, source_target_pairs={{16,0},{17,1},{18,2},{19,3},{20,4},{21,5},{22,6},{23,7},{24,8},{25... | collective-permute-start | bytes 1818632 | tf_op jit(solution)/shard_map/ppermute | solution.py:43
  76.4 10.1 %collective-permute-start.10 = (bf16[1,288,896]{2,1,0:T(8,128)(2,1)}, bf16[1,288,896]{2,1,0:T(8,128)(2,1)}, u32[]{:S(2)}, u32[]{:S(2)}) collective-permute-start(bf16[1,288,896]{2,1,0:T(8,128)(2,1)} %collective-permute-done.1.rest_8_.refs_0_), channel_id=1, source_target_pairs={{0,1},{1,0},{2,3},{3,2},{4,5},{5,4},{6,7},{7,6},{8,9},{9,8},{10,11... | collective-permute-start | bytes 1548296 | tf_op jit(solution)/shard_map/ppermute | solution.py:43
  78.0 8.5 %collective-permute-start.7 = (bf16[1,288,896]{2,1,0:T(8,128)(2,1)}, bf16[1,288,896]{2,1,0:T(8,128)(2,1)}, u32[]{:S(2)}, u32[]{:S(2)}) collective-permute-start(bf16[1,288,896]{2,1,0:T(8,128)(2,1)} %collective-permute-done.6.rest_4_), channel_id=1, source_target_pairs={{0,1},{1,0},{2,3},{3,2},{4,5},{5,4},{6,7},{7,6},{8,9},{9,8},{10,11... | collective-permute-start | bytes 1548296 | tf_op jit(solution)/shard_map/ppermute | solution.py:43
  79.2 7.4 %collective-permute-start.9 = (bf16[1,288,896]{2,1,0:T(8,128)(2,1)}, bf16[1,288,896]{2,1,0:T(8,128)(2,1)}, u32[]{:S(2)}, u32[]{:S(2)}) collective-permute-start(bf16[1,288,896]{2,1,0:T(8,128)(2,1)} %collective-permute-done.8.rest_6_), channel_id=1, source_target_pairs={{0,1},{1,0},{2,3},{3,2},{4,5},{5,4},{6,7},{7,6},{8,9},{9,8},{10,11... | collective-permute-start | bytes 1548296 | tf_op jit(solution)/shard_map/ppermute | solution.py:43
  79.2 1.6 %copy-start = (f32[4,1024,128]{2,1,0:T(8,128)S(1)}, f32[4,1024,128]{2,1,0:T(8,128)}, u32[]{:S(2)}) copy-start(f32[4,1024,128]{2,1,0:T(8,128)} %get-tuple-element.31.own) | copy-start | bytes 6291460
  81.1 1.0 copy-start.7
  82.0 0.8 copy-start.9
  82.8 35.6 %all-to-all-start.1 = ((bf16[4,1024,128]{2,1,0:T(8,128)(2,1)}), bf16[4,1024,128]{2,1,0:T(8,128)(2,1)S(1)}, u32[]{:S(2)}, u32[]{:S(2)}) async-start(bf16[4,1024,128]{2,1,0:T(8,128)(2,1)} %copy-done.7), calls=%async_computation.1 | async-start | bytes 2097152 | tf_op jit(solution)/shard_map/all_to_all | solution.py:586
  86.6 1.0 copy-start.2
  87.6 1.2 copy-start.8
  88.8 1.7 %copy-start.3 = (bf16[1,288,896]{2,1,0:T(8,128)(2,1)S(1)}, bf16[1,288,896]{2,1,0:T(8,128)(2,1)}, u32[]{:S(2)}) copy-start(bf16[1,288,896]{2,1,0:T(8,128)(2,1)} %copy-done.1) | copy-start | bytes 1548292
  88.9 1.7 %copy-start.16 = (bf16[1,288,896]{2,1,0:T(8,128)(2,1)S(1)}, bf16[1,288,896]{2,1,0:T(8,128)(2,1)}, u32[]{:S(2)}) copy-start(bf16[1,288,896]{2,1,0:T(8,128)(2,1)} %copy-done.15) | copy-start | bytes 1548292
  89.8 0.8 copy-start.11
  90.6 27.8 %copy-start.10 = (f32[1024,128]{1,0:T(8,128)S(1)}, f32[1024,128]{1,0:T(8,128)}, u32[]{:S(2)}) copy-start(f32[1024,128]{1,0:T(8,128)} %copy-done.9) | copy-start | bytes 1572868
  99.7 0.6 copy-start.13
  100.3 13.1 %collective-permute-start.14 = (bf16[1,288,896]{2,1,0:T(8,128)(2,1)}, bf16[1,288,896]{2,1,0:T(8,128)(2,1)}, u32[]{:S(2)}, u32[]{:S(2)}) collective-permute-start(bf16[1,288,896]{2,1,0:T(8,128)(2,1)} %after.1), channel_id=1, source_target_pairs={{0,12},{1,13},{2,14},{3,15},{4,0},{5,1},{6,2},{7,3},{8,4},{9,5},{1... | collective-permute-start | bytes 1548296 | tf_op jit(solution)/shard_map/ppermute | solution.py:43
  102.7 13.7 %collective-permute-start.16 = (bf16[1,288,896]{2,1,0:T(8,128)(2,1)}, bf16[1,288,896]{2,1,0:T(8,128)(2,1)}, u32[]{:S(2)}, u32[]{:S(2)}) collective-permute-start(bf16[1,288,896]{2,1,0:T(8,128)(2,1)} %after.1), channel_id=1, source_target_pairs={{0,4},{1,5},{2,6},{3,7},{4,8},{5,9},{6,10},{7,11},{8,12},{9,13},{1... | collective-permute-start | bytes 1548296 | tf_op jit(solution)/shard_map/ppermute | solution.py:43
  102.7 15.7 %collective-permute-start.18 = (bf16[1008,128]{1,0:T(8,128)(2,1)S(1)}, bf16[1008,128]{1,0:T(8,128)(2,1)S(1)}, u32[]{:S(2)}, u32[]{:S(2)}) collective-permute-start(bf16[1008,128]{1,0:T(8,128)(2,1)S(1)} %get-tuple-element.36), channel_id=1, source_target_pairs={{0,2},{1,3},{2,0},{3,1},{4,6},{5,7},{6,4},{7,5},{8,10},{9,11},{10,... | collective-permute-start | bytes 774152 | tf_op jit(solution)/shard_map/ppermute | solution.py:43
  113.4 17.0 %collective-permute-start.15 = (bf16[1,288,896]{2,1,0:T(8,128)(2,1)}, bf16[1,288,896]{2,1,0:T(8,128)(2,1)}, u32[]{:S(2)}, u32[]{:S(2)}) collective-permute-start(bf16[1,288,896]{2,1,0:T(8,128)(2,1)} %collective-permute-done.14.rest_0_), channel_id=1, source_target_pairs={{0,1},{1,0},{2,3},{3,2},{4,5},{5,4},{6,7},{7,6},{8,9},{9,8},{10,11... | collective-permute-start | bytes 1548296 | tf_op jit(solution)/shard_map/ppermute | solution.py:43
  116.4 14.0 %collective-permute-start.17 = (bf16[1,288,896]{2,1,0:T(8,128)(2,1)}, bf16[1,288,896]{2,1,0:T(8,128)(2,1)}, u32[]{:S(2)}, u32[]{:S(2)}) collective-permute-start(bf16[1,288,896]{2,1,0:T(8,128)(2,1)} %collective-permute-done.16.rest_2_), channel_id=1, source_target_pairs={{0,1},{1,0},{2,3},{3,2},{4,5},{5,4},{6,7},{7,6},{8,9},{9,8},{10,11... | collective-permute-start | bytes 1548296 | tf_op jit(solution)/shard_map/ppermute | solution.py:43
  118.4 1.0 copy-start.12
  119.5 0.7 copy-start.14
  121.2 21.6 %collective-permute-start.19 = (bf16[2032,128]{1,0:T(8,128)(2,1)}, bf16[2032,128]{1,0:T(8,128)(2,1)S(1)}, u32[]{:S(2)}, u32[]{:S(2)}) collective-permute-start(bf16[2032,128]{1,0:T(8,128)(2,1)} %get-tuple-element.43), channel_id=1, source_target_pairs={{0,112},{1,113},{2,114},{3,115},{4,116},{5,117},{6,118},{7,119},{8... | collective-permute-start | bytes 1560584 | tf_op jit(solution)/shard_map/ppermute | solution.py:43
  130.4 12.4 %copy-start.4 = (f32[1,448,576]{2,1,0:T(8,128)S(1)}, f32[1,448,576]{2,1,0:T(8,128)}, u32[]{:S(2)}) copy-start(f32[1,448,576]{2,1,0:T(8,128)} %param.16) | copy-start | bytes 3096580
  130.4 12.4 %copy-start.5 = (f32[1,448,576]{2,1,0:T(8,128)S(1)}, f32[1,448,576]{2,1,0:T(8,128)}, u32[]{:S(2)}) copy-start(f32[1,448,576]{2,1,0:T(8,128)} %param.17) | copy-start | bytes 3096580
  130.4 12.4 %copy-start.6 = (f32[1,448,576]{2,1,0:T(8,128)S(1)}, f32[1,448,576]{2,1,0:T(8,128)}, u32[]{:S(2)}) copy-start(f32[1,448,576]{2,1,0:T(8,128)} %param.18) | copy-start | bytes 3096580
  142.8 3.4 %copy-start.19 = (f32[1,32]{1,0:T(1,128)S(1)}, f32[1,32]{1,0:T(1,128)}, u32[]{:S(2)}) copy-start(f32[1,32]{1,0:T(1,128)} %param.19) | copy-start | bytes 388
  142.9 3.3 %copy-start.20 = (f32[1,32]{1,0:T(1,128)S(1)}, f32[1,32]{1,0:T(1,128)}, u32[]{:S(2)}) copy-start(f32[1,32]{1,0:T(1,128)} %param.20) | copy-start | bytes 388
  142.9 3.3 %copy-start.21 = (f32[1,32]{1,0:T(1,128)S(1)}, f32[1,32]{1,0:T(1,128)}, u32[]{:S(2)}) copy-start(f32[1,32]{1,0:T(1,128)} %param.21) | copy-start | bytes 388

commit v4 on v3

--- a/solution.py
+++ b/solution.py
@@ -101,6 +101,7 @@
         out_specs=ANYWHERE,
         out_shape=jax.ShapeDtypeStruct(value.shape, value.dtype),
         input_output_aliases={0: 0},
+        compiler_params=params(1),
         cost_estimate=cost(0, 0),
         name="after",
     )(value, *earlier)
@@ -204,9 +205,7 @@
     own_b,
     send_b,
     tiles,
-    tiles_other,
     turned,
-    turned_other,
     first_a,
     rest_a,
     keep_b,
@@ -223,13 +222,17 @@
         cols = columns(2 * ((z + k) & 3) + (y ^ e), core)
         incoming.append(
             (
-                pltpu.make_async_copy(hidden.at[:, cols], tiles.at[i], in_sems.at[0, i]),
-                pltpu.make_async_copy(other.at[:, cols], tiles_other.at[i], in_sems.at[1, i]),
+                pltpu.make_async_copy(
+                    hidden.at[:, cols], tiles.at[i, pl.ds(0, TOK)], in_sems.at[0, i]
+                ),
+                pltpu.make_async_copy(
+                    other.at[:, cols], tiles.at[i, pl.ds(TOK, TOK)], in_sems.at[1, i]
+                ),
             )
         )
     grads = [
-        pltpu.make_async_copy(grad, turned, grad_sems.at[0]),
-        pltpu.make_async_copy(grad_other, turned_other, grad_sems.at[1]),
+        pltpu.make_async_copy(grad, turned.at[:, pl.ds(0, TOK)], grad_sems.at[0]),
+        pltpu.make_async_copy(grad_other, turned.at[:, pl.ds(TOK, TOK)], grad_sems.at[1]),
     ]
     start_all(grads)
     for pair in incoming:
@@ -237,8 +240,8 @@
     wait_all(grads)
 
     sums = jnp.zeros((1, LAT), F32)
-    for ref in (turned, turned_other):
-        pair = ref[COLS:EXT, :].astype(F32)
+    for at in (0, TOK):
+        pair = turned[COLS:EXT, at : at + TOK].astype(F32)
         sums = sums + pair[0:1] + pair[1:2]
     gain[...] = jnp.zeros_like(gain)
     for i in range(4):
@@ -268,13 +271,12 @@
     for i, (k, e) in enumerate(steps):
         wait_all(incoming[i])
         whole = jnp.dot(turned[:COLS, :], tiles[i], preferred_element_type=F32)
-        whole += jnp.dot(turned_other[:COLS, :], tiles_other[i], preferred_element_type=F32)
         buffer_a = first_a.at[e] if k == 0 else rest_a.at[2 * (k - 1) + e]
         buffer_b = keep_b.at[k] if e == 0 else give_b.at[k]
         put(buffer_a, packed(whole[:HALF]))
         put(buffer_b, packed(whole[HALF:]) + [gain[...]])
         to_a = own_a.at[e] if k == 0 else send_a.at[(z + k) & 3, e]
-        to_b = (own_b, send_b)[e].at[k]
+        to_b = (own_b, send_b)[e].at[(z + k) & 3]
         outgoing.append(pltpu.make_async_copy(buffer_a, to_a, out_sems.at[0, i]))
         outgoing.append(pltpu.make_async_copy(buffer_b, to_b, out_sems.at[1, i]))
         start_all(outgoing[-2:])
@@ -293,10 +295,8 @@
             jax.ShapeDtypeStruct((4, ROWS_B, 128), BF),
         ],
         scratch_shapes=[
-            pltpu.VMEM((8, TOK, TILE), BF),
-            pltpu.VMEM((8, TOK, TILE), BF),
-            pltpu.VMEM((EXT, TOK), BF),
-            pltpu.VMEM((EXT, TOK), BF),
+            pltpu.VMEM((8, 2 * TOK, TILE), BF),
+            pltpu.VMEM((EXT, 2 * TOK), BF),
             pltpu.VMEM((2, ROWS_A, 128), F32),
             pltpu.VMEM((6, ROWS_A, 128), BF),
             pltpu.VMEM((4, ROWS_B, 128), F32),
@@ -312,111 +312,10 @@
     )(hidden, other, grad, grad_other, earlier)
 
 
-def received_sum(ref, own, z):
+def received_sum(own, parts, z):
     for other in range(4):
-        own = own + jnp.where(z == other, 0.0, ref[other].astype(F32))
+        own = own + jnp.where(z == other, 0.0, parts[other].astype(F32))
     return own
-
-
-def whole(shape):
-    return pl.BlockSpec(shape, lambda k: (0,) * len(shape))
-
-
-FLAGGED = whole((8, 128))
-
-
-def sum_a_kernel(own, r, *rest):
-    keep, send, flag = rest[-3:]
-    z, _, _ = place()
-    total = received_sum(r.at[:, 0], own[0], z)
-
-    @pl.when(pl.program_id(0) == 0)
-    def _():
-        keep[...] = total
-        flag[...] = jnp.zeros_like(flag)
-
-    @pl.when(pl.program_id(0) == 1)
-    def _():
-        send[...] = total.astype(BF)
-
-
-def sum_a(own, r, *earlier):
-    return pl.pallas_call(
-        sum_a_kernel,
-        grid=(2,),
-        in_specs=[
-            pl.BlockSpec((1, ROWS_A, 128), lambda e: (e, 0, 0)),
-            pl.BlockSpec((4, 1, ROWS_A, 128), lambda e: (0, e, 0, 0)),
-        ]
-        + [LATER] * len(earlier),
-        out_specs=[whole((ROWS_A, 128))] * 2 + [FLAGGED],
-        out_shape=[
-            jax.ShapeDtypeStruct((ROWS_A, 128), F32),
-            jax.ShapeDtypeStruct((ROWS_A, 128), BF),
-            FLAG,
-        ],
-        compiler_params=params(16),
-        cost_estimate=cost(0, 3_500_000),
-        name="sum_z",
-    )(own, r, *earlier)
-
-
-def sum_b_kernel(own, r, keep, send, flag):
-    z, _, _ = place()
-    k = pl.program_id(0)
-    total = own[0] + r[0].astype(F32)
-    send[(z + k) & 3] = total.astype(BF)
-
-    @pl.when(k == 0)
-    def _():
-        keep[...] = total
-        flag[...] = jnp.zeros_like(flag)
-
-
-def sum_b(own, r):
-    return pl.pallas_call(
-        sum_b_kernel,
-        grid=(4,),
-        in_specs=[pl.BlockSpec((1, ROWS_B, 128), lambda k: (k, 0, 0))] * 2,
-        out_specs=[whole((ROWS_B, 128)), whole((4, ROWS_B, 128)), FLAGGED],
-        out_shape=[
-            jax.ShapeDtypeStruct((ROWS_B, 128), F32),
-            jax.ShapeDtypeStruct((4, ROWS_B, 128), BF),
-            FLAG,
-        ],
-        compiler_params=params(16),
-        cost_estimate=cost(0, 4_500_000),
-        name="sum_y",
-    )(own, r)
-
-
-def sum_all_kernel(keep_a, ra, keep_b, rb, earlier, total, send, flag):
-    z, _, _ = place()
-    a = keep_a[...] + ra[...].astype(F32)
-    b = received_sum(rb, keep_b[...], z)
-    total[:ROWS_A, :] = a
-    total[ROWS_A:, :] = b
-    send[:ROWS_A, :] = a.astype(BF)
-    send[ROWS_A:, :] = b.astype(BF)
-    flag[...] = jnp.zeros_like(flag)
-
-
-def sum_all(*parts):
-    rows = ROWS_A + ROWS_B
-    return pl.pallas_call(
-        sum_all_kernel,
-        grid=(1,),
-        in_specs=[whole(part.shape) for part in parts[:-1]] + [LATER],
-        out_specs=[whole((rows, 128)), whole((rows, 128)), FLAGGED],
-        out_shape=[
-            jax.ShapeDtypeStruct((rows, 128), F32),
-            jax.ShapeDtypeStruct((rows, 128), BF),
-            FLAG,
-        ],
-        compiler_params=params(16),
-        cost_estimate=cost(0, 4_000_000),
-        name="sum_shard",
-    )(*parts)
 
 
 def adamw(master, first, second, grad):
@@ -430,13 +329,14 @@
     return (new_master, new_first, new_second)
 
 
-def adam_kernel(s, own, far, master, first, second, earlier, n_master, n_first, n_second, gain, grad):
-    total = own[...] + far[...].astype(F32)
+def adam_kernel(s, own_a, own_b, far, master, first, second, n_master, n_first, n_second, gain, grad):
+    total_a = own_a[...] + far[:ROWS_A, :].astype(F32)
+    total_b = own_b[...] + far[ROWS_A:, :].astype(F32)
     core = s[0]
-    gain[...] = total[2 * ROWS_A : 2 * ROWS_A + 8]
+    gain[...] = total_b[ROWS_A : ROWS_A + 8]
 
     def both(lo, n):
-        return [total[h * ROWS_A + lo : h * ROWS_A + lo + n] for h in range(2)]
+        return [total[lo : lo + n] for total in (total_a, total_b)]
 
     for i in range(3):
         block = jnp.concatenate(both(i * HALF, HALF), axis=0)
@@ -451,21 +351,19 @@
     )
 
 
-def adam_step(s, own, far, master, first, second, earlier):
+def adam_step(s, own_a, own_b, far, master, first, second):
     shape = jax.ShapeDtypeStruct(master.shape, F32)
     spec = pl.BlockSpec(memory_space=pltpu.VMEM)
     return pl.pallas_call(
         adam_kernel,
-        in_specs=[pl.BlockSpec(memory_space=pltpu.SMEM)]
-        + [spec] * 5
-        + [LATER],
+        in_specs=[pl.BlockSpec(memory_space=pltpu.SMEM)] + [spec] * 6,
         out_specs=[spec] * 4,
         out_shape=[shape] * 3 + [jax.ShapeDtypeStruct((8, 128), F32)],
         scratch_shapes=[pltpu.VMEM(master.shape, F32)],
         compiler_params=params(32),
         cost_estimate=cost(0, 9_000_000),
         name="adamw",
-    )(s, own, far, master, first, second, earlier)
+    )(s, own_a, own_b, far, master, first, second)
 
 
 def input_step(grad, pieces, earlier, begun=None):
@@ -560,44 +458,55 @@
     hidden = hidden_in[0]
     turned = weight[0].T
     other = moved(hidden, to_core)
-    cuts = [cut_weight(turned, [(0, 0)])]
-    cuts.append(cut_weight(turned, [(0, 1)], cuts[0]))
-    cuts.append(cut_weight(turned, [(2, 0), (2, 1)], cuts[1]))
-    here, beside, across = (moved(value, to_before_near) for value in cuts)
+    cut_here = cut_weight(turned, [(0, 0)])
+    here = moved(cut_here, to_before_near)
     rope = rope_step(rope_cot[0])
-    grad = latent_step(hidden, turned, latent_cot[0], gain, rope, cuts[2])
+    grad = latent_step(hidden, turned, latent_cot[0], gain, rope, cut_here)
+    cut_1 = cut_weight(turned, [(0, 1), (2, 0)], grad)
+    cut_2 = cut_weight(turned, [(2, 1), (1, 1)], cut_1)
     grad_other = moved(grad, to_core)
     grad_next = moved(grad, to_before)
+    rest_1 = moved(cut_1, to_before_near)
+    rest_2 = moved(cut_2, to_before_near)
     above, below = moved(here, to_z(-1)), moved(here, to_z(1))
-    def both(value, *blocks):
-        return value, moved(value, to_core), blocks
-
-    pieces = (
-        both(here, (0, 0)),
-        both(across, (2, 0), (2, 1)),
-        both(above, (1, 0)),
-        both(below, (3, 0)),
-        both(beside, (0, 1)),
-    )
-    own_a, send_a, own_b, send_b = weight_step(hidden, other, grad, grad_other, pieces[0][1])
+    side = moved(below, to_ylo)
+    pieces = [
+        (value, moved(value, to_core), blocks)
+        for value, blocks in (
+            (here, [(0, 0)]),
+            (above, [(1, 0)]),
+            (below, [(3, 0)]),
+            (rest_1, [(0, 1), (2, 0)]),
+            (side, [(3, 1)]),
+            (rest_2, [(2, 1), (1, 1)]),
+        )
+    ]
+    far_here, far_above, far_below, far_1, far_side, far_2 = (piece[1] for piece in pieces)
+
+    own_a, send_a, own_b, send_b = weight_step(hidden, other, grad, grad_other, cut_2)
+    z = shard >> 2
     along_z = [[4 * z + k for z in range(4)] for k in range(4)]
 
     def exchanged(value):
         return lax.all_to_all(value, "dp", 0, 0, axis_index_groups=along_z, tiled=True)
 
-    rb = moved(send_b, to_ylo)
-    keep_a, send_a, is_a = sum_a(own_a, exchanged(send_a), *(piece[1] for piece in pieces))
-    ra = moved(send_a, to_ylo)
-    keep_b, send_b, is_b = sum_b(own_b, rb)
-    received, is_begun = input_step(grad_next, pieces, [is_a, is_b])
-    total, send, is_summed = sum_all(keep_a, ra, keep_b, exchanged(send_b), is_begun)
+    ra = exchanged(send_a)
+    rb = moved(after(send_b, above, below), to_ylo)
+    rb = after(rb, grad_next, far_here, far_above, far_below)
+    send_b = (own_b + rb.astype(F32)).astype(BF)
+    rz = exchanged(send_b)
+    ra = after(ra, far_1)
+    send_a = received_sum(own_a[1], ra[:, 1], z).astype(BF)
+    ry = moved(send_a, to_ylo)
+    total_a = received_sum(own_a[0], ra[:, 0], z) + ry.astype(F32)
+    keep_b = lax.dynamic_index_in_dim(own_b, z, 0, False)
+    keep_b += lax.dynamic_index_in_dim(rb, z, 0, False).astype(F32)
+    total_b = received_sum(keep_b, after(rz, far_side), z)
+    send = jnp.concatenate([total_a, total_b], axis=0).astype(BF)
     far = moved(send, to_mirror)
-    beside = after(beside, is_begun)
-    above_2, below_2 = moved(beside, to_z(-1)), moved(beside, to_z(1))
-    pieces = both(above_2, (1, 1)), both(below_2, (3, 1))
-    received, is_received = input_step(grad_next, pieces, [is_summed], received)
+    received, _ = input_step(grad_next, pieces, [send])
     next_master, next_first, next_second, gain_rows = adam_step(
-        s, total, far, master_weight[0], first_moment[0], second_moment[0], is_received
+        s, total_a, total_b, far, master_weight[0], first_moment[0], second_moment[0]
     )
     gain_total = lax.dynamic_slice(gain_rows[:4].reshape(LAT), (shard * 32,), (32,))
     next_gain = adamw(gain_master[0], gain_first[0], gain_second[0], gain_total)

time: 148 us -> 134 us (0.905)
  the two profiles are of different devices: /device:TPU:1 before, /device:TPU:0 now
where the time goes in v4:
time: 134 us
  waiting for transfers between devices  45 us (34%)
  Pallas kernels  41.9 us (31%)
  starting transfers between devices  30.5 us (23%)
  local copies, waits for them, and re-layouts  8.31 us (6%)
  other arithmetic  6.69 us (5%)
    ppermute x18, waiting for transfers between devices, moved(): return lax.ppermute(value, ('pipe', 'dp'), pairs)  43.6 us
    ppermute x18, starting transfers between devices, moved(): return lax.ppermute(value, ('pipe', 'dp'), pairs)  22.2 us
    pallas_call x1, Pallas kernels, weight_step(): pl.pallas_call(weight_kernel, in_specs=[ANYWHERE] * 4 + [LATER], out_spec...  11.6 us
    pallas_call x1, Pallas kernels, input_step(): pl.pallas_call(kernel, in_specs=[inside] + [ANYWHERE] * halves + [LATER]...  11.6 us
    pallas_call x1, Pallas kernels, latent_step(): pl.pallas_call(latent_kernel, in_specs=[ANYWHERE, ANYWHERE, inside, insid...  9.2 us
    all_to_all x2, starting transfers between devices, exchanged(): lax.all_to_all(value, 'dp', 0, 0, axis_index_groups=along_z, tiled=True)  8.37 us
    unnamed x48, local copies, waits for them, and re-layouts  8.3 us
    pallas_call x3, Pallas kernels, cut_weight(): pl.pallas_call(kernel, in_specs=[ANYWHERE] + [LATER] * len(earlier), out_...  6.22 us
  transfers between devices with their start and end apart: 20, of which 7 were waited for; matrix products, arithmetic and copies ran while one was open for 5% of the time, Pallas kernels for 29%

profile of v4, /device:TPU:0, one launch (start us, length us, event | category | flops | bytes accessed | tf_op | source)
XLA Modules:
  0.0 133.5 jit_solution(16440084614428566966)
XLA Ops:
  0.6 0.1 collective-permute-start.13
  0.7 1.9 %cut_weight.3.earlier = bf16[1,288,896]{2,1,0:T(8,128)(2,1)} custom-call(bf16[576,7168]{1,0:T(8,128)(2,1)} %bitcast.88), custom_call_target="tpu_custom_call" | custom-call | bytes 1000 | tf_op jit(solution)/shard_map/cut_weight/pallas_call | solution.py:124
  2.6 1.3 collective-permute-start.1
  4.0 0.3 fusion.7
  4.3 0.6 pad_maximum_fusion.1.rope
  4.9 9.2 %latent_grad.1.rest_0_.grad = bf16[592,512]{1,0:T(8,128)(2,1)} custom-call(bf16[512,7168]{1,0:T(8,128)(2,1)} %bitcast.93, bf16[576,7168]{1,0:T(8,128)(2,1)} %bitcast.89, bf16[512,512]{1,0:T(8,128)(2,1)} %bitcast.95, f32[1,512]{1,0:T(1,128)} %gain.1, bf16[64,512]{1,0:T(8,128)(2,1)} %pad_maximum_fusion.1.rope, bf16[1,288,896]{2,1,0:T(8,128)(2,1)} %cut_weight.3.earlier), custom_call_target="tpu_custom_call" | custom-call | bytes 1000 | tf_op jit(solution)/shard_map/latent_grad/pallas_call | solution.py:182
  14.1 0.6 collective-permute-start.14
  14.7 2.2 %cut_weight.4.rest_0_ = bf16[2,288,896]{2,1,0:T(8,128)(2,1)} custom-call(bf16[576,7168]{1,0:T(8,128)(2,1)} %bitcast.90, bf16[592,512]{1,0:T(8,128)(2,1)} %latent_grad.1.rest_0_.grad), custom_call_target="tpu_custom_call" | custom-call | bytes 1000 | tf_op jit(solution)/shard_map/cut_weight/pallas_call | solution.py:124
  16.9 1.3 collective-permute-start.7
  18.2 2.0 %collective-permute-done.1.rest_0_ = bf16[1,288,896]{2,1,0:T(8,128)(2,1)S(1)} collective-permute-done((bf16[1,288,896]{2,1,0:T(8,128)(2,1)}, bf16[1,288,896]{2,1,0:T(8,128)(2,1)S(1)}, u32[]{:S(2)}, u32[]{:S(2)}) %collective-permute-start.1) | collective-permute-done | bytes 516128 | tf_op jit(solution)/shard_map/ppermute | solution.py:43
  20.2 1.9 %collective-permute-start.5 = (bf16[1,288,896]{2,1,0:T(8,128)(2,1)S(1)}, bf16[1,288,896]{2,1,0:T(8,128)(2,1)}, u32[]{:S(2)}, u32[]{:S(2)}) collective-permute-start(bf16[1,288,896]{2,1,0:T(8,128)(2,1)S(1)} %collective-permute-done.1.rest_0_), channel_id=1, source_target_pairs={{0,4},{1,5},{2,6},{3,7},{4,8},{5,9},{6,10},{7,11},{8,12},{9,13},{1... | collective-permute-start | bytes 1548296 | tf_op jit(solution)/shard_map/ppermute | solution.py:43
  22.1 2.1 %collective-permute-start.3 = (bf16[1,288,896]{2,1,0:T(8,128)(2,1)S(1)}, bf16[1,288,896]{2,1,0:T(8,128)(2,1)S(1)}, u32[]{:S(2)}, u32[]{:S(2)}) collective-permute-start(bf16[1,288,896]{2,1,0:T(8,128)(2,1)S(1)} %collective-permute-done.1.rest_0_), channel_id=1, source_target_pairs={{0,12},{1,13},{2,14},{3,15},{4,0},{5,1},{6,2},{7,3},{8,4},{9,5},{1... | collective-permute-start | bytes 1548296 | tf_op jit(solution)/shard_map/ppermute | solution.py:43
  24.3 2.2 %cut_weight.5.earlier = bf16[2,288,896]{2,1,0:T(8,128)(2,1)} custom-call(bf16[576,7168]{1,0:T(8,128)(2,1)} %bitcast.91, bf16[2,288,896]{2,1,0:T(8,128)(2,1)} %cut_weight.4.rest_0_), custom_call_target="tpu_custom_call" | custom-call | bytes 1000 | tf_op jit(solution)/shard_map/cut_weight/pallas_call | solution.py:124
  26.5 0.9 copy-done.19
  27.3 11.6 %weight_grad.1 = (f32[2,1008,128]{2,1,0:T(8,128)}, bf16[4,2,1008,128]{3,2,1,0:T(8,128)(2,1)}, f32[4,1024,128]{2,1,0:T(8,128)}, bf16[4,1024,128]{2,1,0:T(8,128)(2,1)}) custom-call(bf16[512,7168]{1,0:T(8,128)(2,1)} %bitcast.94, bf16[512,7168]{1,0:T(8,128)(2,1)} %collective-permute-done.13.other, bf16[592,512]{1,0:T(8,128)(2,1)} %latent_grad.1.rest_0_.grad, ...), custom_call_target="tpu_custom_call" | custom-call | bytes 1000 | tf_op jit(solution)/shard_map/weight_grad/pallas_call | solution.py:287
  39.0 3.6 %all-to-all-start = ((bf16[4,2,1008,128]{3,2,1,0:T(8,128)(2,1)}), bf16[4,2,1008,128]{3,2,1,0:T(8,128)(2,1)S(1)}, u32[]{:S(2)}, u32[]{:S(2)}) async-start(bf16[4,2,1008,128]{3,2,1,0:T(8,128)(2,1)} %get-tuple-element.17), calls=%async_computation | async-start | bytes 4128768 | tf_op jit(solution)/shard_map/all_to_all | solution.py:491
  42.6 1.3 collective-permute-start
  43.9 0.4 collective-permute-start.16
  44.3 1.6 %collective-permute-done.7.rest_6_ = bf16[2,288,896]{2,1,0:T(8,128)(2,1)} collective-permute-done((bf16[2,288,896]{2,1,0:T(8,128)(2,1)}, bf16[2,288,896]{2,1,0:T(8,128)(2,1)}, u32[]{:S(2)}, u32[]{:S(2)}) %collective-permute-start.7) | collective-permute-done | bytes 1032224 | tf_op jit(solution)/shard_map/ppermute | solution.py:43
  46.0 0.5 collective-permute-start.6
  46.5 16.3 %collective-permute-done.refs_1_.grad = bf16[592,512]{1,0:T(8,128)(2,1)S(1)} collective-permute-done((bf16[592,512]{1,0:T(8,128)(2,1)}, bf16[592,512]{1,0:T(8,128)(2,1)S(1)}, u32[]{:S(2)}, u32[]{:S(2)}) %collective-permute-start) | collective-permute-done | bytes 606240 | tf_op jit(solution)/shard_map/ppermute | solution.py:43
  62.8 1.3 collective-permute-start.11
  64.1 1.4 %collective-permute-start.9 = (bf16[1,288,896]{2,1,0:T(8,128)(2,1)}, bf16[1,288,896]{2,1,0:T(8,128)(2,1)}, u32[]{:S(2)}, u32[]{:S(2)}) collective-permute-start(bf16[1,288,896]{2,1,0:T(8,128)(2,1)} %collective-permute-done.5.refs_2_.rest_4_), channel_id=1, source_target_pairs={{0,2},{1,3},{2,0},{3,1},{4,6},{5,7},{6,4},{7,5},{8,10},{9,11},{10,... | collective-permute-start | bytes 1548296 | tf_op jit(solution)/shard_map/ppermute | solution.py:43
  65.6 17.7 %collective-permute-done.16.refs_0_ = bf16[4,1024,128]{2,1,0:T(8,128)(2,1)S(1)} collective-permute-done((bf16[4,1024,128]{2,1,0:T(8,128)(2,1)}, bf16[4,1024,128]{2,1,0:T(8,128)(2,1)S(1)}, u32[]{:S(2)}, u32[]{:S(2)}) %collective-permute-start.16) | collective-permute-done | bytes 1048608 | tf_op jit(solution)/shard_map/ppermute | solution.py:43
  83.4 0.0 copy-start
  83.4 1.0 copy-done
  84.3 1.2 add_convert_fusion
  85.5 4.8 %all-to-all-start.1 = ((bf16[4,1024,128]{2,1,0:T(8,128)(2,1)}), bf16[4,1024,128]{2,1,0:T(8,128)(2,1)S(1)}, u32[]{:S(2)}, u32[]{:S(2)}) async-start(bf16[4,1024,128]{2,1,0:T(8,128)(2,1)} %add_convert_fusion), calls=%async_computation.1 | async-start | bytes 2097152 | tf_op jit(solution)/shard_map/all_to_all | solution.py:491
  90.3 1.2 copy-done.18
  91.5 0.2 fusion
  91.7 0.4 collective-permute-start.15
  92.1 2.4 %collective-permute-done.9.rest_8_ = bf16[1,288,896]{2,1,0:T(8,128)(2,1)} collective-permute-done((bf16[1,288,896]{2,1,0:T(8,128)(2,1)}, bf16[1,288,896]{2,1,0:T(8,128)(2,1)}, u32[]{:S(2)}, u32[]{:S(2)}) %collective-permute-start.9) | collective-permute-done | bytes 516128 | tf_op jit(solution)/shard_map/ppermute | solution.py:43
  94.5 0.5 collective-permute-start.12
  95.0 3.5 %collective-permute-done.15 = bf16[1008,128]{1,0:T(8,128)(2,1)} collective-permute-done((bf16[1008,128]{1,0:T(8,128)(2,1)S(1)}, bf16[1008,128]{1,0:T(8,128)(2,1)}, u32[]{:S(2)}, u32[]{:S(2)}) %collective-permute-start.15) | collective-permute-done | bytes 258080 | tf_op jit(solution)/shard_map/ppermute | solution.py:43
  98.5 2.2 %fusion.15 = (bf16[1008,128]{1,0:T(8,128)(2,1)S(1)}, f32[1008,128]{1,0:T(8,128)}) fusion(bf16[1008,128]{1,0:T(8,128)(2,1)} %collective-permute-done.15, bf16[4,2,1008,128]{3,2,1,0:T(8,128)(2,1)S(1)} %after.4, pred[]{:T(512)S(6)} %eq.11, pred[]{:T(512)S(6)} %eq.10, pred[]{:T(512)S(6)} %eq.9, pred[]{:T(512)S(6)} %eq.8, f32[2,1008,128]{2,1,0:T(8,128)} %get-tuple-element.16), kind=kLoop, calls=%fused_computation.36 | loop fusion | flops 1935360 | bytes 2580484 | tf_op jit(solution)/shard_map/convert.2
  100.7 1.4 %all-to-all-done.1.refs_0_ = bf16[4,1024,128]{2,1,0:T(8,128)(2,1)S(1)} async-done(((bf16[4,1024,128]{2,1,0:T(8,128)(2,1)}), bf16[4,1024,128]{2,1,0:T(8,128)(2,1)S(1)}, u32[]{:S(2)}, u32[]{:S(2)}) %all-to-all-start.1) | async-done | bytes 1048608 | tf_op jit(solution)/shard_map/all_to_all | solution.py:491
  102.1 1.4 %fusion.17 = (bf16[1024,128]{1,0:T(8,128)(2,1)S(1)}, f32[1024,128]{1,0:T(8,128)S(1)}) fusion(bf16[4,1024,128]{2,1,0:T(8,128)(2,1)S(1)} %after.7, pred[]{:T(512)S(6)} %eq.11, pred[]{:T(512)S(6)} %eq.10, pred[]{:T(512)S(6)} %eq.9, pred[]{:T(512)S(6)} %eq.8, bf16[4,1024,128]{2,1,0:T(8,128)(2,1)} %copy-done, s32[]{:T(128)S(6)} %select_n.129, ...), kind=kLoop, calls=%fused_computation.37 | loop fusion | flops 1966080 | bytes 2621448 | tf_op jit(solution)/shard_map/convert.3
  103.6 9.1 %collective-permute-start.17 = (bf16[2032,128]{1,0:T(8,128)(2,1)S(1)}, bf16[2032,128]{1,0:T(8,128)(2,1)S(1)}, u32[]{:S(2)}, u32[]{:S(2)}) collective-permute-start(bf16[2032,128]{1,0:T(8,128)(2,1)S(1)} %pad_maximum_fusion.rest_12_), channel_id=1, source_target_pairs={{0,112},{1,113},{2,114},{3,115},{4,116},{5,117},{6,118},{7,119},{8... | collective-permute-start | bytes 1560584 | tf_op jit(solution)/shard_map/ppermute | solution.py:43
  112.7 1.0 copy-done.4
  113.7 1.0 copy-done.6
  114.8 1.0 copy-done.8
  115.8 1.0 copy-done.10
  116.9 1.0 copy-done.16
  117.9 11.6 %input_grad.1 = (bf16[512,7168]{1,0:T(8,128)(2,1)}, f32[8,128]{1,0:T(8,128)}) custom-call(bf16[592,512]{1,0:T(8,128)(2,1)S(1)} %copy-done.2, bf16[1,288,896]{2,1,0:T(8,128)(2,1)S(1)} %copy-done.16, bf16[1,288,896]{2,1,0:T(8,128)(2,1)S(1)} %copy-done.6, bf16[1,288,896]{2,1,0:T(8,128)(2,1)S(1)} %copy-done.4, bf16[1,288,896]{2,1,0:T(8,128)(2,1)S(1)} %copy-done.10, ...), custom_call_target="tpu_custom_call" | custom-call | flops 2113929216 | bytes 8000000 | tf_op jit(solution)/shard_map/input_grad/pallas_call | solution.py:408
  129.6 0.0 copy-start.22
  129.6 0.0 copy-start.23
  129.6 3.3 %adamw.1 = (f32[448,576]{1,0:T(8,128)}, f32[448,576]{1,0:T(8,128)}, f32[448,576]{1,0:T(8,128)}, f32[8,128]{1,0:T(8,128)S(1)}) custom-call(s32[1]{0:T(128)} %bitcast.20.s, f32[1008,128]{1,0:T(8,128)S(1)} %copy-done.11, f32[1024,128]{1,0:T(8,128)S(1)} %get-tuple-element.31.own_b, bf16[2032,128]{1,0:T(8,128)(2,1)S(1)} %collective-permute-done.17.far, ...), custom_call_target="tpu_custom_call" | custom-call | bytes 9000000 | tf_op jit(solution)/shard_map/adamw/pallas_call | solution.py:357
  132.9 0.6 fusion.13
  (63 shorter events, 0.2 us)
Async XLA Ops:
  0.6 25.8 %collective-permute-start.13 = (bf16[512,7168]{1,0:T(8,128)(2,1)}, bf16[512,7168]{1,0:T(8,128)(2,1)}, u32[]{:S(2)}, u32[]{:S(2)}) collective-permute-start(bf16[512,7168]{1,0:T(8,128)(2,1)} %bitcast.92), channel_id=1, source_target_pairs={{0,1},{1,0},{2,3},{3,2},{4,5},{5,4},{6,7},{7,6},{8,9},{9,8},{10,11... | collective-permute-start | bytes 22020104 | tf_op jit(solution)/shard_map/ppermute | solution.py:43
  0.7 3.2 %copy-start.20 = (bf16[1,512,64]{1,2,0:T(8,128)(2,1)S(1)}, bf16[1,512,64]{1,2,0:T(8,128)(2,1)}, u32[]{:S(2)}) copy-start(bf16[1,512,64]{1,2,0:T(8,128)(2,1)} %param.15) | copy-start | bytes 196612
  2.6 17.6 %collective-permute-start.1 = (bf16[1,288,896]{2,1,0:T(8,128)(2,1)}, bf16[1,288,896]{2,1,0:T(8,128)(2,1)S(1)}, u32[]{:S(2)}, u32[]{:S(2)}) collective-permute-start(bf16[1,288,896]{2,1,0:T(8,128)(2,1)} %cut_weight.3.earlier), channel_id=1, source_target_pairs={{16,2},{17,3},{18,0},{19,1},{20,6},{21,7},{22,4},{23,5},{24,10},{2... | collective-permute-start | bytes 1548296 | tf_op jit(solution)/shard_map/ppermute | solution.py:43
  14.1 12.3 %collective-permute-start.14 = (bf16[592,512]{1,0:T(8,128)(2,1)}, bf16[592,512]{1,0:T(8,128)(2,1)S(1)}, u32[]{:S(2)}, u32[]{:S(2)}) collective-permute-start(bf16[592,512]{1,0:T(8,128)(2,1)} %latent_grad.1.rest_0_.grad), channel_id=1, source_target_pairs={{0,1},{1,0},{2,3},{3,2},{4,5},{5,4},{6,7},{7,6},{8,9},{9,8},{10,11... | collective-permute-start | bytes 1818632 | tf_op jit(solution)/shard_map/ppermute | solution.py:43
  16.9 29.1 %collective-permute-start.7 = (bf16[2,288,896]{2,1,0:T(8,128)(2,1)}, bf16[2,288,896]{2,1,0:T(8,128)(2,1)}, u32[]{:S(2)}, u32[]{:S(2)}) collective-permute-start(bf16[2,288,896]{2,1,0:T(8,128)(2,1)} %cut_weight.4.rest_0_), channel_id=1, source_target_pairs={{16,2},{17,3},{18,0},{19,1},{20,6},{21,7},{22,4},{23,5},{24,10},{2... | collective-permute-start | bytes 3096584 | tf_op jit(solution)/shard_map/ppermute | solution.py:43
  20.2 24.1 %copy-start.15 = (bf16[1,288,896]{2,1,0:T(8,128)(2,1)}, bf16[1,288,896]{2,1,0:T(8,128)(2,1)S(1)}, u32[]{:S(2)}) copy-start(bf16[1,288,896]{2,1,0:T(8,128)(2,1)S(1)} %collective-permute-done.1.rest_0_) | copy-start | bytes 1548292
  20.2 23.7 %collective-permute-start.5 = (bf16[1,288,896]{2,1,0:T(8,128)(2,1)S(1)}, bf16[1,288,896]{2,1,0:T(8,128)(2,1)}, u32[]{:S(2)}, u32[]{:S(2)}) collective-permute-start(bf16[1,288,896]{2,1,0:T(8,128)(2,1)S(1)} %collective-permute-done.1.rest_0_), channel_id=1, source_target_pairs={{0,4},{1,5},{2,6},{3,7},{4,8},{5,9},{6,10},{7,11},{8,12},{9,13},{1... | collective-permute-start | bytes 1548296 | tf_op jit(solution)/shard_map/ppermute | solution.py:43
  22.1 21.8 %collective-permute-start.3 = (bf16[1,288,896]{2,1,0:T(8,128)(2,1)S(1)}, bf16[1,288,896]{2,1,0:T(8,128)(2,1)S(1)}, u32[]{:S(2)}, u32[]{:S(2)}) collective-permute-start(bf16[1,288,896]{2,1,0:T(8,128)(2,1)S(1)} %collective-permute-done.1.rest_0_), channel_id=1, source_target_pairs={{0,12},{1,13},{2,14},{3,15},{4,0},{5,1},{6,2},{7,3},{8,4},{9,5},{1... | collective-permute-start | bytes 1548296 | tf_op jit(solution)/shard_map/ppermute | solution.py:43
  26.4 0.9 copy-start.19
  39.0 46.5 %all-to-all-start = ((bf16[4,2,1008,128]{3,2,1,0:T(8,128)(2,1)}), bf16[4,2,1008,128]{3,2,1,0:T(8,128)(2,1)S(1)}, u32[]{:S(2)}, u32[]{:S(2)}) async-start(bf16[4,2,1008,128]{3,2,1,0:T(8,128)(2,1)} %get-tuple-element.17), calls=%async_computation | async-start | bytes 4128768 | tf_op jit(solution)/shard_map/all_to_all | solution.py:491
  42.6 20.2 %collective-permute-start = (bf16[592,512]{1,0:T(8,128)(2,1)}, bf16[592,512]{1,0:T(8,128)(2,1)S(1)}, u32[]{:S(2)}, u32[]{:S(2)}) collective-permute-start(bf16[592,512]{1,0:T(8,128)(2,1)} %latent_grad.1.rest_0_.grad), channel_id=1, source_target_pairs={{16,0},{17,1},{18,2},{19,3},{20,4},{21,5},{22,6},{23,7},{24,8},{25... | collective-permute-start | bytes 1818632 | tf_op jit(solution)/shard_map/ppermute | solution.py:43
  43.9 39.4 %copy-start.3 = (bf16[1,288,896]{2,1,0:T(8,128)(2,1)}, bf16[1,288,896]{2,1,0:T(8,128)(2,1)S(1)}, u32[]{:S(2)}) copy-start(bf16[1,288,896]{2,1,0:T(8,128)(2,1)S(1)} %collective-permute-done.3.refs_1_.rest_2_) | copy-start | bytes 1548292
  43.9 40.4 %copy-start.17 = (f32[4,1024,128]{2,1,0:T(8,128)S(1)}, f32[4,1024,128]{2,1,0:T(8,128)}, u32[]{:S(2)}) copy-start(f32[4,1024,128]{2,1,0:T(8,128)} %get-tuple-element.18) | copy-start | bytes 6291460
  43.9 39.4 %collective-permute-start.16 = (bf16[4,1024,128]{2,1,0:T(8,128)(2,1)}, bf16[4,1024,128]{2,1,0:T(8,128)(2,1)S(1)}, u32[]{:S(2)}, u32[]{:S(2)}) collective-permute-start(bf16[4,1024,128]{2,1,0:T(8,128)(2,1)} %after.5), channel_id=1, source_target_pairs={{0,2},{1,3},{2,0},{3,1},{4,6},{5,7},{6,4},{7,5},{8,10},{9,11},{10,... | collective-permute-start | bytes 3145736 | tf_op jit(solution)/shard_map/ppermute | solution.py:43
  44.3 18.5 %collective-permute-start.2 = (bf16[1,288,896]{2,1,0:T(8,128)(2,1)S(1)}, bf16[1,288,896]{2,1,0:T(8,128)(2,1)S(1)}, u32[]{:S(2)}, u32[]{:S(2)}) collective-permute-start(bf16[1,288,896]{2,1,0:T(8,128)(2,1)S(1)} %collective-permute-done.1.rest_0_), channel_id=1, source_target_pairs={{0,1},{1,0},{2,3},{3,2},{4,5},{5,4},{6,7},{7,6},{8,9},{9,8},{10,11... | collective-permute-start | bytes 1548296 | tf_op jit(solution)/shard_map/ppermute | solution.py:43
  46.0 44.3 %collective-permute-start.8 = (bf16[2,288,896]{2,1,0:T(8,128)(2,1)}, bf16[2,288,896]{2,1,0:T(8,128)(2,1)}, u32[]{:S(2)}, u32[]{:S(2)}) collective-permute-start(bf16[2,288,896]{2,1,0:T(8,128)(2,1)} %collective-permute-done.7.rest_6_), channel_id=1, source_target_pairs={{0,1},{1,0},{2,3},{3,2},{4,5},{5,4},{6,7},{7,6},{8,9},{9,8},{10,11... | collective-permute-start | bytes 3096584 | tf_op jit(solution)/shard_map/ppermute | solution.py:43
  46.0 18.2 %collective-permute-start.6 = (bf16[1,288,896]{2,1,0:T(8,128)(2,1)}, bf16[1,288,896]{2,1,0:T(8,128)(2,1)S(1)}, u32[]{:S(2)}, u32[]{:S(2)}) collective-permute-start(bf16[1,288,896]{2,1,0:T(8,128)(2,1)} %collective-permute-done.5.refs_2_.rest_4_), channel_id=1, source_target_pairs={{0,1},{1,0},{2,3},{3,2},{4,5},{5,4},{6,7},{7,6},{8,9},{9,8},{10,11... | collective-permute-start | bytes 1548296 | tf_op jit(solution)/shard_map/ppermute | solution.py:43
  62.8 20.5 %copy-start.1 = (bf16[592,512]{1,0:T(8,128)(2,1)}, bf16[592,512]{1,0:T(8,128)(2,1)S(1)}, u32[]{:S(2)}) copy-start(bf16[592,512]{1,0:T(8,128)(2,1)S(1)} %collective-permute-done.refs_1_.grad) | copy-start | bytes 1818628
  62.8 2.8 %collective-permute-start.4 = (bf16[1,288,896]{2,1,0:T(8,128)(2,1)S(1)}, bf16[1,288,896]{2,1,0:T(8,128)(2,1)S(1)}, u32[]{:S(2)}, u32[]{:S(2)}) collective-permute-start(bf16[1,288,896]{2,1,0:T(8,128)(2,1)S(1)} %collective-permute-done.3.refs_1_.rest_2_), channel_id=1, source_target_pairs={{0,1},{1,0},{2,3},{3,2},{4,5},{5,4},{6,7},{7,6},{8,9},{9,8},{10,11... | collective-permute-start | bytes 1548296 | tf_op jit(solution)/shard_map/ppermute | solution.py:43
  62.8 20.5 %copy-start.5 = (bf16[1,288,896]{2,1,0:T(8,128)(2,1)}, bf16[1,288,896]{2,1,0:T(8,128)(2,1)S(1)}, u32[]{:S(2)}) copy-start(bf16[1,288,896]{2,1,0:T(8,128)(2,1)S(1)} %collective-permute-done.2.refs_2_.rest_1_) | copy-start | bytes 1548292
  62.8 31.7 %collective-permute-start.11 = (bf16[2,288,896]{2,1,0:T(8,128)(2,1)}, bf16[2,288,896]{2,1,0:T(8,128)(2,1)}, u32[]{:S(2)}, u32[]{:S(2)}) collective-permute-start(bf16[2,288,896]{2,1,0:T(8,128)(2,1)} %cut_weight.5.earlier), channel_id=1, source_target_pairs={{16,2},{17,3},{18,0},{19,1},{20,6},{21,7},{22,4},{23,5},{24,10},{2... | collective-permute-start | bytes 3096584 | tf_op jit(solution)/shard_map/ppermute | solution.py:43
  64.1 19.2 %copy-start.7 = (bf16[1,288,896]{2,1,0:T(8,128)(2,1)}, bf16[1,288,896]{2,1,0:T(8,128)(2,1)S(1)}, u32[]{:S(2)}) copy-start(bf16[1,288,896]{2,1,0:T(8,128)(2,1)S(1)} %collective-permute-done.6.refs_4_.rest_5_) | copy-start | bytes 1548292
  64.1 30.4 %collective-permute-start.9 = (bf16[1,288,896]{2,1,0:T(8,128)(2,1)}, bf16[1,288,896]{2,1,0:T(8,128)(2,1)}, u32[]{:S(2)}, u32[]{:S(2)}) collective-permute-start(bf16[1,288,896]{2,1,0:T(8,128)(2,1)} %collective-permute-done.5.refs_2_.rest_4_), channel_id=1, source_target_pairs={{0,2},{1,3},{2,0},{3,1},{4,6},{5,7},{6,4},{7,5},{8,10},{9,11},{10,... | collective-permute-start | bytes 1548296 | tf_op jit(solution)/shard_map/ppermute | solution.py:43
  65.6 17.8 %copy-start.9 = (bf16[1,288,896]{2,1,0:T(8,128)(2,1)}, bf16[1,288,896]{2,1,0:T(8,128)(2,1)S(1)}, u32[]{:S(2)}) copy-start(bf16[1,288,896]{2,1,0:T(8,128)(2,1)S(1)} %collective-permute-done.4.refs_3_.rest_3_) | copy-start | bytes 1548292
  83.4 1.0 copy-start
  85.5 16.6 %all-to-all-start.1 = ((bf16[4,1024,128]{2,1,0:T(8,128)(2,1)}), bf16[4,1024,128]{2,1,0:T(8,128)(2,1)S(1)}, u32[]{:S(2)}, u32[]{:S(2)}) async-start(bf16[4,1024,128]{2,1,0:T(8,128)(2,1)} %add_convert_fusion), calls=%async_computation.1 | async-start | bytes 2097152 | tf_op jit(solution)/shard_map/all_to_all | solution.py:491
  90.3 1.2 copy-start.18
  91.7 6.8 %collective-permute-start.15 = (bf16[1008,128]{1,0:T(8,128)(2,1)S(1)}, bf16[1008,128]{1,0:T(8,128)(2,1)}, u32[]{:S(2)}, u32[]{:S(2)}) collective-permute-start(bf16[1008,128]{1,0:T(8,128)(2,1)S(1)} %fusion), channel_id=1, source_target_pairs={{0,2},{1,3},{2,0},{3,1},{4,6},{5,7},{6,4},{7,5},{8,10},{9,11},{10,... | collective-permute-start | bytes 774152 | tf_op jit(solution)/shard_map/ppermute | solution.py:43
  94.5 6.2 %collective-permute-start.10 = (bf16[1,288,896]{2,1,0:T(8,128)(2,1)}, bf16[1,288,896]{2,1,0:T(8,128)(2,1)}, u32[]{:S(2)}, u32[]{:S(2)}) collective-permute-start(bf16[1,288,896]{2,1,0:T(8,128)(2,1)} %collective-permute-done.9.rest_8_), channel_id=1, source_target_pairs={{0,1},{1,0},{2,3},{3,2},{4,5},{5,4},{6,7},{7,6},{8,9},{9,8},{10,11... | collective-permute-start | bytes 1548296 | tf_op jit(solution)/shard_map/ppermute | solution.py:43
  94.5 18.2 %collective-permute-start.12 = (bf16[2,288,896]{2,1,0:T(8,128)(2,1)}, bf16[2,288,896]{2,1,0:T(8,128)(2,1)}, u32[]{:S(2)}, u32[]{:S(2)}) collective-permute-start(bf16[2,288,896]{2,1,0:T(8,128)(2,1)} %collective-permute-done.11.rest_10_), channel_id=1, source_target_pairs={{0,1},{1,0},{2,3},{3,2},{4,5},{5,4},{6,7},{7,6},{8,9},{9,8},{10,11... | collective-permute-start | bytes 3096584 | tf_op jit(solution)/shard_map/ppermute | solution.py:43
  102.1 10.6 %copy-start.2 = (bf16[592,512]{1,0:T(8,128)(2,1)S(1)}, bf16[592,512]{1,0:T(8,128)(2,1)}, u32[]{:S(2)}) copy-start(bf16[592,512]{1,0:T(8,128)(2,1)} %copy-done.1) | copy-start | bytes 1818628
  103.6 25.9 %collective-permute-start.17 = (bf16[2032,128]{1,0:T(8,128)(2,1)S(1)}, bf16[2032,128]{1,0:T(8,128)(2,1)S(1)}, u32[]{:S(2)}, u32[]{:S(2)}) collective-permute-start(bf16[2032,128]{1,0:T(8,128)(2,1)S(1)} %pad_maximum_fusion.rest_12_), channel_id=1, source_target_pairs={{0,112},{1,113},{2,114},{3,115},{4,116},{5,117},{6,118},{7,119},{8... | collective-permute-start | bytes 1560584 | tf_op jit(solution)/shard_map/ppermute | solution.py:43
  112.7 1.0 copy-start.4
  113.7 1.0 copy-start.6
  114.8 1.0 copy-start.8
  115.8 1.0 copy-start.10
  116.9 1.0 copy-start.16
  117.9 11.6 %copy-start.11 = (f32[1008,128]{1,0:T(8,128)S(1)}, f32[1008,128]{1,0:T(8,128)}, u32[]{:S(2)}) copy-start(f32[1008,128]{1,0:T(8,128)} %get-tuple-element.29.own_a) | copy-start | bytes 1548292
  117.9 11.6 %copy-start.12 = (f32[1,448,576]{2,1,0:T(8,128)S(1)}, f32[1,448,576]{2,1,0:T(8,128)}, u32[]{:S(2)}) copy-start(f32[1,448,576]{2,1,0:T(8,128)} %param.16) | copy-start | bytes 3096580
  117.9 11.6 %copy-start.13 = (f32[1,448,576]{2,1,0:T(8,128)S(1)}, f32[1,448,576]{2,1,0:T(8,128)}, u32[]{:S(2)}) copy-start(f32[1,448,576]{2,1,0:T(8,128)} %param.17) | copy-start | bytes 3096580
  117.9 11.7 %copy-start.14 = (f32[1,448,576]{2,1,0:T(8,128)S(1)}, f32[1,448,576]{2,1,0:T(8,128)}, u32[]{:S(2)}) copy-start(f32[1,448,576]{2,1,0:T(8,128)} %param.18) | copy-start | bytes 3096580
  129.6 3.3 %copy-start.21 = (f32[1,32]{1,0:T(1,128)S(1)}, f32[1,32]{1,0:T(1,128)}, u32[]{:S(2)}) copy-start(f32[1,32]{1,0:T(1,128)} %param.19) | copy-start | bytes 388
  129.6 3.3 %copy-start.22 = (f32[1,32]{1,0:T(1,128)S(1)}, f32[1,32]{1,0:T(1,128)}, u32[]{:S(2)}) copy-start(f32[1,32]{1,0:T(1,128)} %param.20) | copy-start | bytes 388
  129.6 3.3 %copy-start.23 = (f32[1,32]{1,0:T(1,128)S(1)}, f32[1,32]{1,0:T(1,128)}, u32[]{:S(2)}) copy-start(f32[1,32]{1,0:T(1,128)} %param.21) | copy-start | bytes 388

commit v5 on v4

--- a/solution.py
+++ b/solution.py
@@ -91,7 +91,7 @@
         copy.wait()
 
 
-def after(value, *earlier):
+def after(value, *earlier, mib=1):
     def kernel(*refs):
         pass
 
@@ -101,35 +101,36 @@
         out_specs=ANYWHERE,
         out_shape=jax.ShapeDtypeStruct(value.shape, value.dtype),
         input_output_aliases={0: 0},
-        compiler_params=params(1),
+        compiler_params=params(mib),
         cost_estimate=cost(0, 0),
         name="after",
     )(value, *earlier)
 
 
-def cut_weight(weight, blocks, *earlier):
+def cut_weight(weight, groups):
     def kernel(weight, *rest):
-        out, sems = rest[-2:]
+        outs, sems = rest[:-1], rest[-1]
         z, y, core = place()
         rows = pl.ds(pl.multiple_of(core * HALF, HALF), HALF)
         copies = []
-        for i, (dz, e) in enumerate(blocks):
-            block = 2 * ((z + dz) & 3) + ((1 - y) ^ e)
-            cols = pl.ds(pl.multiple_of(block * BLOCK, BLOCK), BLOCK)
-            copies.append(pltpu.make_async_copy(weight.at[rows, cols], out.at[i], sems.at[i]))
+        for out, group in zip(outs, groups):
+            for i, (dz, e) in enumerate(group):
+                block = 2 * ((z + dz) & 3) + ((1 - y) ^ e)
+                cols = pl.ds(pl.multiple_of(block * BLOCK, BLOCK), BLOCK)
+                sem = sems.at[len(copies)]
+                copies.append(pltpu.make_async_copy(weight.at[rows, cols], out.at[i], sem))
         start_all(copies)
         wait_all(copies)
 
-    count = len(blocks)
     return pl.pallas_call(
         kernel,
-        in_specs=[ANYWHERE] + [LATER] * len(earlier),
-        out_shape=jax.ShapeDtypeStruct((count, HALF, BLOCK), BF),
-        scratch_shapes=[pltpu.SemaphoreType.DMA((count,))],
+        in_specs=[ANYWHERE],
+        out_shape=[jax.ShapeDtypeStruct((len(group), HALF, BLOCK), BF) for group in groups],
+        scratch_shapes=[pltpu.SemaphoreType.DMA((sum(len(group) for group in groups),))],
         compiler_params=params(60),
         cost_estimate=cost(0, 1_000),
         name="cut_weight",
-    )(weight, *earlier)
+    )(weight)
 
 
 PARTS = 7
@@ -199,7 +200,6 @@
     other,
     grad,
     grad_other,
-    earlier,
     own_a,
     send_a,
     own_b,
@@ -235,7 +235,7 @@
         pltpu.make_async_copy(grad_other, turned.at[:, pl.ds(TOK, TOK)], grad_sems.at[1]),
     ]
     start_all(grads)
-    for pair in incoming:
+    for pair in incoming[:2]:
         start_all(pair)
     wait_all(grads)
 
@@ -270,6 +270,8 @@
     outgoing = []
     for i, (k, e) in enumerate(steps):
         wait_all(incoming[i])
+        if i + 2 < len(steps):
+            start_all(incoming[i + 2])
         whole = jnp.dot(turned[:COLS, :], tiles[i], preferred_element_type=F32)
         buffer_a = first_a.at[e] if k == 0 else rest_a.at[2 * (k - 1) + e]
         buffer_b = keep_b.at[k] if e == 0 else give_b.at[k]
@@ -283,10 +285,10 @@
     wait_all(outgoing)
 
 
-def weight_step(hidden, other, grad, grad_other, earlier):
+def weight_step(hidden, other, grad, grad_other):
     return pl.pallas_call(
         weight_kernel,
-        in_specs=[ANYWHERE] * 4 + [LATER],
+        in_specs=[ANYWHERE] * 4,
         out_specs=[ANYWHERE] * 4,
         out_shape=[
             jax.ShapeDtypeStruct((2, ROWS_A, 128), F32),
@@ -309,7 +311,7 @@
         compiler_params=params(60),
         cost_estimate=cost(0, 1_000),
         name="weight_grad",
-    )(hidden, other, grad, grad_other, earlier)
+    )(hidden, other, grad, grad_other)
 
 
 def received_sum(own, parts, z):
@@ -420,7 +422,7 @@
             pltpu.SemaphoreType.DMA((count,)),
         ],
         input_output_aliases={} if begun is None else {len(operands) - 1: 0},
-        compiler_params=params(36),
+        compiler_params=params(60),
         cost_estimate=cost(TOK * WIDTH * COLS, 8_000_000),
         name="input_grad",
     )(*operands)
@@ -458,32 +460,22 @@
     hidden = hidden_in[0]
     turned = weight[0].T
     other = moved(hidden, to_core)
-    cut_here = cut_weight(turned, [(0, 0)])
-    here = moved(cut_here, to_before_near)
+    groups = [[(0, 0)], [(0, 1), (2, 0)], [(2, 1), (1, 1)]]
+    cut_0, cut_1, cut_2 = cut_weight(turned, groups)
+    here = moved(cut_0, to_before_near)
     rope = rope_step(rope_cot[0])
-    grad = latent_step(hidden, turned, latent_cot[0], gain, rope, cut_here)
-    cut_1 = cut_weight(turned, [(0, 1), (2, 0)], grad)
-    cut_2 = cut_weight(turned, [(2, 1), (1, 1)], cut_1)
+    grad = latent_step(hidden, turned, latent_cot[0], gain, rope, cut_0)
+    grad = after(grad, here, mib=62)
     grad_other = moved(grad, to_core)
     grad_next = moved(grad, to_before)
     rest_1 = moved(cut_1, to_before_near)
     rest_2 = moved(cut_2, to_before_near)
     above, below = moved(here, to_z(-1)), moved(here, to_z(1))
-    side = moved(below, to_ylo)
-    pieces = [
-        (value, moved(value, to_core), blocks)
-        for value, blocks in (
-            (here, [(0, 0)]),
-            (above, [(1, 0)]),
-            (below, [(3, 0)]),
-            (rest_1, [(0, 1), (2, 0)]),
-            (side, [(3, 1)]),
-            (rest_2, [(2, 1), (1, 1)]),
-        )
-    ]
-    far_here, far_above, far_below, far_1, far_side, far_2 = (piece[1] for piece in pieces)
-
-    own_a, send_a, own_b, send_b = weight_step(hidden, other, grad, grad_other, cut_2)
+
+    def both(value, *blocks):
+        return value, moved(value, to_core), blocks
+
+    own_a, send_a, own_b, send_b = weight_step(hidden, other, grad, grad_other)
     z = shard >> 2
     along_z = [[4 * z + k for z in range(4)] for k in range(4)]
 
@@ -491,20 +483,24 @@
         return lax.all_to_all(value, "dp", 0, 0, axis_index_groups=along_z, tiled=True)
 
     ra = exchanged(send_a)
-    rb = moved(after(send_b, above, below), to_ylo)
-    rb = after(rb, grad_next, far_here, far_above, far_below)
+    rb = moved(after(send_b, above, below, grad_next, mib=62), to_ylo)
+    pieces = both(here, (0, 0)), both(above, (1, 0)), both(rest_1, (0, 1), (2, 0))
+    received, is_begun = input_step(grad_next, pieces, [])
     send_b = (own_b + rb.astype(F32)).astype(BF)
     rz = exchanged(send_b)
-    ra = after(ra, far_1)
+    ra = after(ra, is_begun)
     send_a = received_sum(own_a[1], ra[:, 1], z).astype(BF)
     ry = moved(send_a, to_ylo)
+    below = after(below, send_b)
+    side = moved(below, to_ylo)
     total_a = received_sum(own_a[0], ra[:, 0], z) + ry.astype(F32)
     keep_b = lax.dynamic_index_in_dim(own_b, z, 0, False)
     keep_b += lax.dynamic_index_in_dim(rb, z, 0, False).astype(F32)
-    total_b = received_sum(keep_b, after(rz, far_side), z)
+    total_b = received_sum(keep_b, after(rz, rest_2), z)
     send = jnp.concatenate([total_a, total_b], axis=0).astype(BF)
     far = moved(send, to_mirror)
-    received, _ = input_step(grad_next, pieces, [send])
+    pieces = both(below, (3, 0)), both(side, (3, 1)), both(rest_2, (2, 1), (1, 1))
+    received, _ = input_step(grad_next, pieces, [send], received)
     next_master, next_first, next_second, gain_rows = adam_step(
         s, total_a, total_b, far, master_weight[0], first_moment[0], second_moment[0]
     )

time: 134 us -> 156 us (1.16)
  the two profiles are of different devices: /device:TPU:0 before, /device:TPU:24 now
where the time goes in v5:
time: 156 us; the launch traced here: 155 us
  waiting for transfers between devices  67 us (43%)
  Pallas kernels  42.5 us (27%)
  starting transfers between devices  28 us (18%)
  other arithmetic  11.2 us (7%)
  local copies, waits for them, and re-layouts  5.6 us (4%)
    ppermute x18, waiting for transfers between devices, moved(): return lax.ppermute(value, ('pipe', 'dp'), pairs)  67 us
    ppermute x18, starting transfers between devices, moved(): return lax.ppermute(value, ('pipe', 'dp'), pairs)  18.2 us
    pallas_call x2, Pallas kernels, input_step(): pl.pallas_call(kernel, in_specs=[inside] + [ANYWHERE] * halves + [LATER]...  15.8 us
    pallas_call x1, Pallas kernels, weight_step(): pl.pallas_call(weight_kernel, in_specs=[ANYWHERE] * 4, out_specs=[ANYWHER...  9.8 us
    all_to_all x2, starting transfers between devices, exchanged(): lax.all_to_all(value, 'dp', 0, 0, axis_index_groups=along_z, tiled=True)  9.77 us
    pallas_call x1, Pallas kernels, latent_step(): pl.pallas_call(latent_kernel, in_specs=[ANYWHERE, ANYWHERE, inside, insid...  9.25 us
    unnamed x40, local copies, waits for them, and re-layouts  5.6 us
    pallas_call x1, Pallas kernels, adam_step(): pl.pallas_call(adam_kernel, in_specs=[pl.BlockSpec(memory_space=pltpu.SME...  4.43 us
  transfers between devices with their start and end apart: 20, of which 5 were waited for; matrix products, arithmetic and copies ran while one was open for 7% of the time, Pallas kernels for 25%

profile of v5, /device:TPU:24, one launch (start us, length us, event | category | flops | bytes accessed | tf_op | source)
XLA Modules:
  0.0 155.3 jit_solution(5226240994980561572)
XLA Ops:
  0.6 0.1 collective-permute-start.3
  0.7 3.2 %cut_weight.1 = (bf16[1,288,896]{2,1,0:T(8,128)(2,1)}, bf16[2,288,896]{2,1,0:T(8,128)(2,1)}, bf16[2,288,896]{2,1,0:T(8,128)(2,1)}) custom-call(bf16[576,7168]{1,0:T(8,128)(2,1)} %bitcast.88), custom_call_target="tpu_custom_call" | custom-call | bytes 1000 | tf_op jit(solution)/shard_map/cut_weight/pallas_call | solution.py:125
  4.0 2.0 %collective-permute-start = (bf16[1,288,896]{2,1,0:T(8,128)(2,1)}, bf16[1,288,896]{2,1,0:T(8,128)(2,1)S(1)}, u32[]{:S(2)}, u32[]{:S(2)}) collective-permute-start(bf16[1,288,896]{2,1,0:T(8,128)(2,1)} %get-tuple-element.21.earlier), channel_id=1, source_target_pairs={{16,2},{17,3},{18,0},{19,1},{20,6},{21,7},{22,4},{23,5},{24,10},{2... | collective-permute-start | bytes 1548296 | tf_op jit(solution)/shard_map/ppermute | solution.py:43
  6.1 0.3 fusion.7
  6.4 0.6 pad_maximum_fusion.1.rope
  7.0 9.3 %latent_grad.1.refs_0_ = bf16[592,512]{1,0:T(8,128)(2,1)} custom-call(bf16[512,7168]{1,0:T(8,128)(2,1)} %bitcast.91, bf16[576,7168]{1,0:T(8,128)(2,1)} %bitcast.89, bf16[512,512]{1,0:T(8,128)(2,1)} %bitcast.94, f32[1,512]{1,0:T(1,128)} %gain.1, bf16[64,512]{1,0:T(8,128)(2,1)} %pad_maximum_fusion.1.rope, bf16[1,288,896]{2,1,0:T(8,128)(2,1)} %get-tuple-element.21.earlier), custom_call_target="tpu_custom_call" | custom-call | bytes 1000 | tf_op jit(solution)/shard_map/latent_grad/pallas_call | solution.py:183
  16.3 6.0 %collective-permute-done.refs_1_.rest_0_ = bf16[1,288,896]{2,1,0:T(8,128)(2,1)S(1)} collective-permute-done((bf16[1,288,896]{2,1,0:T(8,128)(2,1)}, bf16[1,288,896]{2,1,0:T(8,128)(2,1)S(1)}, u32[]{:S(2)}, u32[]{:S(2)}) %collective-permute-start) | collective-permute-done | bytes 516128 | tf_op jit(solution)/shard_map/ppermute | solution.py:43
  22.3 0.8 copy-done.14
  23.1 0.0 collective-permute-start.4
  23.1 1.9 %collective-permute-start.14 = (bf16[2,288,896]{2,1,0:T(8,128)(2,1)}, bf16[2,288,896]{2,1,0:T(8,128)(2,1)}, u32[]{:S(2)}, u32[]{:S(2)}) collective-permute-start(bf16[2,288,896]{2,1,0:T(8,128)(2,1)} %get-tuple-element.27), channel_id=1, source_target_pairs={{16,2},{17,3},{18,0},{19,1},{20,6},{21,7},{22,4},{23,5},{24,10},{2... | collective-permute-start | bytes 3096584 | tf_op jit(solution)/shard_map/ppermute | solution.py:43
  25.0 1.9 %collective-permute-start.1 = (bf16[592,512]{1,0:T(8,128)(2,1)}, bf16[592,512]{1,0:T(8,128)(2,1)S(1)}, u32[]{:S(2)}, u32[]{:S(2)}) collective-permute-start(bf16[592,512]{1,0:T(8,128)(2,1)} %after.5.grad), channel_id=1, source_target_pairs={{16,0},{17,1},{18,2},{19,3},{20,4},{21,5},{22,6},{23,7},{24,8},{25... | collective-permute-start | bytes 1818632 | tf_op jit(solution)/shard_map/ppermute | solution.py:43
  27.0 2.0 %collective-permute-start.2 = (bf16[1,288,896]{2,1,0:T(8,128)(2,1)}, bf16[1,288,896]{2,1,0:T(8,128)(2,1)S(1)}, u32[]{:S(2)}, u32[]{:S(2)}) collective-permute-start(bf16[1,288,896]{2,1,0:T(8,128)(2,1)} %copy-done.14), channel_id=1, source_target_pairs={{0,4},{1,5},{2,6},{3,7},{4,8},{5,9},{6,10},{7,11},{8,12},{9,13},{1... | collective-permute-start | bytes 1548296 | tf_op jit(solution)/shard_map/ppermute | solution.py:43
  28.9 2.2 %collective-permute-start.5 = (bf16[1,288,896]{2,1,0:T(8,128)(2,1)}, bf16[1,288,896]{2,1,0:T(8,128)(2,1)S(1)}, u32[]{:S(2)}, u32[]{:S(2)}) collective-permute-start(bf16[1,288,896]{2,1,0:T(8,128)(2,1)} %copy-done.14), channel_id=1, source_target_pairs={{0,12},{1,13},{2,14},{3,15},{4,0},{5,1},{6,2},{7,3},{8,4},{9,5},{1... | collective-permute-start | bytes 1548296 | tf_op jit(solution)/shard_map/ppermute | solution.py:43
  31.2 0.0 collective-permute-done.3.other
  31.2 9.8 %weight_grad.1 = (f32[2,1008,128]{2,1,0:T(8,128)}, bf16[4,2,1008,128]{3,2,1,0:T(8,128)(2,1)}, f32[4,1024,128]{2,1,0:T(8,128)}, bf16[4,1024,128]{2,1,0:T(8,128)(2,1)}) custom-call(bf16[512,7168]{1,0:T(8,128)(2,1)} %bitcast.92, bf16[512,7168]{1,0:T(8,128)(2,1)} %collective-permute-done.3.other, bf16[592,512]{1,0:T(8,128)(2,1)} %after.5.grad, ...), custom_call_target="tpu_custom_call" | custom-call | bytes 1000 | tf_op jit(solution)/shard_map/weight_grad/pallas_call | solution.py:289
  41.0 4.5 %all-to-all-start = ((bf16[4,2,1008,128]{3,2,1,0:T(8,128)(2,1)}), bf16[4,2,1008,128]{3,2,1,0:T(8,128)(2,1)}, u32[]{:S(2)}, u32[]{:S(2)}) async-start(bf16[4,2,1008,128]{3,2,1,0:T(8,128)(2,1)} %get-tuple-element.26), calls=%async_computation | async-start | bytes 4128768 | tf_op jit(solution)/shard_map/all_to_all | solution.py:483
  45.5 0.0 collective-permute-done.5.refs_1_.rest_2_
  45.5 20.0 %collective-permute-done.1.refs_3_.grad = bf16[592,512]{1,0:T(8,128)(2,1)S(1)} collective-permute-done((bf16[592,512]{1,0:T(8,128)(2,1)}, bf16[592,512]{1,0:T(8,128)(2,1)S(1)}, u32[]{:S(2)}, u32[]{:S(2)}) %collective-permute-start.1) | collective-permute-done | bytes 606240 | tf_op jit(solution)/shard_map/ppermute | solution.py:43
  65.5 0.8 copy-done.9
  66.3 1.2 collective-permute-start.6
  67.6 0.5 collective-permute-start.12
  68.1 0.0 collective-permute-start.13
  68.1 1.9 %collective-permute-start.10 = (bf16[2,288,896]{2,1,0:T(8,128)(2,1)}, bf16[2,288,896]{2,1,0:T(8,128)(2,1)S(1)}, u32[]{:S(2)}, u32[]{:S(2)}) collective-permute-start(bf16[2,288,896]{2,1,0:T(8,128)(2,1)} %get-tuple-element.24), channel_id=1, source_target_pairs={{16,2},{17,3},{18,0},{19,1},{20,6},{21,7},{22,4},{23,5},{24,10},{2... | collective-permute-start | bytes 3096584 | tf_op jit(solution)/shard_map/ppermute | solution.py:43
  70.0 21.2 %collective-permute-done.6 = bf16[4,1024,128]{2,1,0:T(8,128)(2,1)S(1)} collective-permute-done((bf16[4,1024,128]{2,1,0:T(8,128)(2,1)}, bf16[4,1024,128]{2,1,0:T(8,128)(2,1)S(1)}, u32[]{:S(2)}, u32[]{:S(2)}) %collective-permute-start.6) | collective-permute-done | bytes 1048608 | tf_op jit(solution)/shard_map/ppermute | solution.py:43
  91.2 3.2 %add_convert_fusion.refs_1_ = bf16[4,1024,128]{2,1,0:T(8,128)(2,1)} fusion(f32[4,1024,128]{2,1,0:T(8,128)} %get-tuple-element.22, bf16[4,1024,128]{2,1,0:T(8,128)(2,1)S(1)} %collective-permute-done.6), kind=kLoop, calls=%fused_computation | loop fusion | flops 1572864 | bytes 4194304 | tf_op jit(solution)/shard_map/convert_element_type | solution.py:489
  94.5 1.5 collective-permute-start.8
  95.9 5.3 %all-to-all-start.1 = ((bf16[4,1024,128]{2,1,0:T(8,128)(2,1)}), bf16[4,1024,128]{2,1,0:T(8,128)(2,1)S(1)}, u32[]{:S(2)}, u32[]{:S(2)}) async-start(bf16[4,1024,128]{2,1,0:T(8,128)(2,1)} %add_convert_fusion.refs_1_), calls=%async_computation.1 | async-start | bytes 2097152 | tf_op jit(solution)/shard_map/all_to_all | solution.py:483
  101.3 0.8 copy-done.19
  102.1 7.8 %input_grad.2 = (bf16[512,7168]{1,0:T(8,128)(2,1)}, f32[8,128]{1,0:T(8,128)}) custom-call(bf16[592,512]{1,0:T(8,128)(2,1)} %copy-done.9, bf16[1,288,896]{2,1,0:T(8,128)(2,1)} %copy-done.14, bf16[1,288,896]{2,1,0:T(8,128)(2,1)} %copy-done.19, bf16[1,288,896]{2,1,0:T(8,128)(2,1)} %copy-done.13, bf16[1,288,896]{2,1,0:T(8,128)(2,1)} %collective-permute-done.13.rest_3_, ...), custom_call_target="tpu_custom_call" | custom-call | flops 2113929216 | bytes 8000000 | tf_op jit(solution)/shard_map/input_grad/pallas_call | solution.py:410
  109.9 0.7 copy-done.8
  110.6 1.2 copy-done.11
  111.8 1.6 fusion
  113.4 0.7 collective-permute-start.16
  114.1 0.5 collective-permute-start.7
  114.6 0.1 collective-permute-start.9
  114.7 16.4 %collective-permute-done.16 = bf16[1008,128]{1,0:T(8,128)(2,1)S(1)} collective-permute-done((bf16[1008,128]{1,0:T(8,128)(2,1)S(1)}, bf16[1008,128]{1,0:T(8,128)(2,1)S(1)}, u32[]{:S(2)}, u32[]{:S(2)}) %collective-permute-start.16) | collective-permute-done | bytes 258080 | tf_op jit(solution)/shard_map/ppermute | solution.py:43
  131.1 2.6 %fusion.15 = (bf16[1008,128]{1,0:T(8,128)(2,1)S(1)}, f32[1008,128]{1,0:T(8,128)}) fusion(bf16[1008,128]{1,0:T(8,128)(2,1)S(1)} %collective-permute-done.16, bf16[4,2,1008,128]{3,2,1,0:T(8,128)(2,1)} %after.8, pred[]{:T(512)S(6)} %eq.11, pred[]{:T(512)S(6)} %eq.10, pred[]{:T(512)S(6)} %eq.9, pred[]{:T(512)S(6)} %eq.8, f32[2,1008,128]{2,1,0:T(8,128)} %get-tuple-element.25), kind=kLoop, calls=%fused_computation.36 | loop fusion | flops 1935360 | bytes 2580484 | tf_op jit(solution)/shard_map/convert.2
  133.6 1.4 fusion.17
  135.0 0.8 pad_maximum_fusion.rest_6_
  135.9 1.6 %collective-permute-start.17 = (bf16[2032,128]{1,0:T(8,128)(2,1)}, bf16[2032,128]{1,0:T(8,128)(2,1)}, u32[]{:S(2)}, u32[]{:S(2)}) collective-permute-start(bf16[2032,128]{1,0:T(8,128)(2,1)} %pad_maximum_fusion.rest_6_), channel_id=1, source_target_pairs={{0,112},{1,113},{2,114},{3,115},{4,116},{5,117},{6,118},{7,119},{8... | collective-permute-start | bytes 1560584 | tf_op jit(solution)/shard_map/ppermute | solution.py:43
  137.5 0.0 copy-start.5
  137.5 0.0 copy-start.6
  137.5 8.0 %input_grad.3 = (bf16[512,7168]{1,0:T(8,128)(2,1)}, f32[8,128]{1,0:T(8,128)}) custom-call(bf16[592,512]{1,0:T(8,128)(2,1)} %copy-done.9, bf16[1,288,896]{2,1,0:T(8,128)(2,1)} %copy-done.2, bf16[1,288,896]{2,1,0:T(8,128)(2,1)} %collective-permute-done.7.rest_1_, bf16[1,288,896]{2,1,0:T(8,128)(2,1)} %collective-permute-done.8.rest_2_, ...), custom_call_target="tpu_custom_call", output_to_operand_aliasing={{0}: (8, {})} | custom-call | flops 2113929216 | bytes 8000000 | tf_op jit(solution)/shard_map/input_grad/pallas_call | solution.py:410
  145.5 3.4 %collective-permute-done.17.far = bf16[2032,128]{1,0:T(8,128)(2,1)} collective-permute-done((bf16[2032,128]{1,0:T(8,128)(2,1)}, bf16[2032,128]{1,0:T(8,128)(2,1)}, u32[]{:S(2)}, u32[]{:S(2)}) %collective-permute-start.17) | collective-permute-done | bytes 520224 | tf_op jit(solution)/shard_map/ppermute | solution.py:43
  148.9 0.0 copy-start.7
  148.9 1.2 copy-done.7
  150.2 4.4 %adamw.1 = (f32[448,576]{1,0:T(8,128)}, f32[448,576]{1,0:T(8,128)}, f32[448,576]{1,0:T(8,128)}, f32[8,128]{1,0:T(8,128)S(1)}) custom-call(s32[1]{0:T(128)} %bitcast.20.s, f32[1008,128]{1,0:T(8,128)S(1)} %copy-done.4, f32[1024,128]{1,0:T(8,128)S(1)} %get-tuple-element.41.own_b, bf16[2032,128]{1,0:T(8,128)(2,1)} %collective-permute-done.17.far, ...), custom_call_target="tpu_custom_call" | custom-call | bytes 9000000 | tf_op jit(solution)/shard_map/adamw/pallas_call | solution.py:359
  154.7 0.6 fusion.13
  (55 shorter events, 0.1 us)
Async XLA Ops:
  0.6 30.5 %collective-permute-start.3 = (bf16[512,7168]{1,0:T(8,128)(2,1)}, bf16[512,7168]{1,0:T(8,128)(2,1)}, u32[]{:S(2)}, u32[]{:S(2)}) collective-permute-start(bf16[512,7168]{1,0:T(8,128)(2,1)} %bitcast.90), channel_id=1, source_target_pairs={{0,1},{1,0},{2,3},{3,2},{4,5},{5,4},{6,7},{7,6},{8,9},{9,8},{10,11... | collective-permute-start | bytes 22020104 | tf_op jit(solution)/shard_map/ppermute | solution.py:43
  0.7 5.3 %copy-start.15 = (bf16[1,512,64]{1,2,0:T(8,128)(2,1)S(1)}, bf16[1,512,64]{1,2,0:T(8,128)(2,1)}, u32[]{:S(2)}) copy-start(bf16[1,512,64]{1,2,0:T(8,128)(2,1)} %param.15) | copy-start | bytes 196612
  4.0 18.3 %collective-permute-start = (bf16[1,288,896]{2,1,0:T(8,128)(2,1)}, bf16[1,288,896]{2,1,0:T(8,128)(2,1)S(1)}, u32[]{:S(2)}, u32[]{:S(2)}) collective-permute-start(bf16[1,288,896]{2,1,0:T(8,128)(2,1)} %get-tuple-element.21.earlier), channel_id=1, source_target_pairs={{16,2},{17,3},{18,0},{19,1},{20,6},{21,7},{22,4},{23,5},{24,10},{2... | collective-permute-start | bytes 1548296 | tf_op jit(solution)/shard_map/ppermute | solution.py:43
  22.3 0.8 copy-start.14
  23.1 5.8 %collective-permute-start.4 = (bf16[592,512]{1,0:T(8,128)(2,1)}, bf16[592,512]{1,0:T(8,128)(2,1)S(1)}, u32[]{:S(2)}, u32[]{:S(2)}) collective-permute-start(bf16[592,512]{1,0:T(8,128)(2,1)} %after.5.grad), channel_id=1, source_target_pairs={{0,1},{1,0},{2,3},{3,2},{4,5},{5,4},{6,7},{7,6},{8,9},{9,8},{10,11... | collective-permute-start | bytes 1818632 | tf_op jit(solution)/shard_map/ppermute | solution.py:43
  23.1 44.5 %collective-permute-start.14 = (bf16[2,288,896]{2,1,0:T(8,128)(2,1)}, bf16[2,288,896]{2,1,0:T(8,128)(2,1)}, u32[]{:S(2)}, u32[]{:S(2)}) collective-permute-start(bf16[2,288,896]{2,1,0:T(8,128)(2,1)} %get-tuple-element.27), channel_id=1, source_target_pairs={{16,2},{17,3},{18,0},{19,1},{20,6},{21,7},{22,4},{23,5},{24,10},{2... | collective-permute-start | bytes 3096584 | tf_op jit(solution)/shard_map/ppermute | solution.py:43
  25.0 40.5 %collective-permute-start.1 = (bf16[592,512]{1,0:T(8,128)(2,1)}, bf16[592,512]{1,0:T(8,128)(2,1)S(1)}, u32[]{:S(2)}, u32[]{:S(2)}) collective-permute-start(bf16[592,512]{1,0:T(8,128)(2,1)} %after.5.grad), channel_id=1, source_target_pairs={{16,0},{17,1},{18,2},{19,3},{20,4},{21,5},{22,6},{23,7},{24,8},{25... | collective-permute-start | bytes 1818632 | tf_op jit(solution)/shard_map/ppermute | solution.py:43
  27.0 18.5 %collective-permute-start.2 = (bf16[1,288,896]{2,1,0:T(8,128)(2,1)}, bf16[1,288,896]{2,1,0:T(8,128)(2,1)S(1)}, u32[]{:S(2)}, u32[]{:S(2)}) collective-permute-start(bf16[1,288,896]{2,1,0:T(8,128)(2,1)} %copy-done.14), channel_id=1, source_target_pairs={{0,4},{1,5},{2,6},{3,7},{4,8},{5,9},{6,10},{7,11},{8,12},{9,13},{1... | collective-permute-start | bytes 1548296 | tf_op jit(solution)/shard_map/ppermute | solution.py:43
  28.9 2.2 %copy-start.12 = (bf16[592,512]{1,0:T(8,128)(2,1)}, bf16[592,512]{1,0:T(8,128)(2,1)S(1)}, u32[]{:S(2)}) copy-start(bf16[592,512]{1,0:T(8,128)(2,1)S(1)} %collective-permute-done.4.grad_other) | copy-start | bytes 1818628
  28.9 16.5 %collective-permute-start.5 = (bf16[1,288,896]{2,1,0:T(8,128)(2,1)}, bf16[1,288,896]{2,1,0:T(8,128)(2,1)S(1)}, u32[]{:S(2)}, u32[]{:S(2)}) collective-permute-start(bf16[1,288,896]{2,1,0:T(8,128)(2,1)} %copy-done.14), channel_id=1, source_target_pairs={{0,12},{1,13},{2,14},{3,15},{4,0},{5,1},{6,2},{7,3},{8,4},{9,5},{1... | collective-permute-start | bytes 1548296 | tf_op jit(solution)/shard_map/ppermute | solution.py:43
  41.0 55.0 %all-to-all-start = ((bf16[4,2,1008,128]{3,2,1,0:T(8,128)(2,1)}), bf16[4,2,1008,128]{3,2,1,0:T(8,128)(2,1)}, u32[]{:S(2)}, u32[]{:S(2)}) async-start(bf16[4,2,1008,128]{3,2,1,0:T(8,128)(2,1)} %get-tuple-element.26), calls=%async_computation | async-start | bytes 4128768 | tf_op jit(solution)/shard_map/all_to_all | solution.py:483
  45.5 20.1 %copy-start = (bf16[1,288,896]{2,1,0:T(8,128)(2,1)}, bf16[1,288,896]{2,1,0:T(8,128)(2,1)S(1)}, u32[]{:S(2)}) copy-start(bf16[1,288,896]{2,1,0:T(8,128)(2,1)S(1)} %collective-permute-done.2.refs_2_.refs_0_) | copy-start | bytes 1548292
  45.5 20.1 %copy-start.13 = (bf16[1,288,896]{2,1,0:T(8,128)(2,1)}, bf16[1,288,896]{2,1,0:T(8,128)(2,1)S(1)}, u32[]{:S(2)}) copy-start(bf16[1,288,896]{2,1,0:T(8,128)(2,1)S(1)} %collective-permute-done.5.refs_1_.rest_2_) | copy-start | bytes 1548292
  65.5 0.8 copy-start.9
  66.3 24.9 %collective-permute-start.6 = (bf16[4,1024,128]{2,1,0:T(8,128)(2,1)}, bf16[4,1024,128]{2,1,0:T(8,128)(2,1)S(1)}, u32[]{:S(2)}, u32[]{:S(2)}) collective-permute-start(bf16[4,1024,128]{2,1,0:T(8,128)(2,1)} %after.6), channel_id=1, source_target_pairs={{0,2},{1,3},{2,0},{3,1},{4,6},{5,7},{6,4},{7,5},{8,10},{9,11},{10,... | collective-permute-start | bytes 3145736 | tf_op jit(solution)/shard_map/ppermute | solution.py:43
  67.6 33.7 %collective-permute-start.15 = (bf16[2,288,896]{2,1,0:T(8,128)(2,1)}, bf16[2,288,896]{2,1,0:T(8,128)(2,1)}, u32[]{:S(2)}, u32[]{:S(2)}) collective-permute-start(bf16[2,288,896]{2,1,0:T(8,128)(2,1)} %collective-permute-done.14.rest_4_), channel_id=1, source_target_pairs={{0,1},{1,0},{2,3},{3,2},{4,5},{5,4},{6,7},{7,6},{8,9},{9,8},{10,11... | collective-permute-start | bytes 3096584 | tf_op jit(solution)/shard_map/ppermute | solution.py:43
  67.6 33.7 %collective-permute-start.12 = (bf16[1,288,896]{2,1,0:T(8,128)(2,1)}, bf16[1,288,896]{2,1,0:T(8,128)(2,1)S(1)}, u32[]{:S(2)}, u32[]{:S(2)}) collective-permute-start(bf16[1,288,896]{2,1,0:T(8,128)(2,1)} %copy-done.14), channel_id=1, source_target_pairs={{0,1},{1,0},{2,3},{3,2},{4,5},{5,4},{6,7},{7,6},{8,9},{9,8},{10,11... | collective-permute-start | bytes 1548296 | tf_op jit(solution)/shard_map/ppermute | solution.py:43
  68.1 33.2 %collective-permute-start.13 = (bf16[1,288,896]{2,1,0:T(8,128)(2,1)}, bf16[1,288,896]{2,1,0:T(8,128)(2,1)}, u32[]{:S(2)}, u32[]{:S(2)}) collective-permute-start(bf16[1,288,896]{2,1,0:T(8,128)(2,1)} %copy-done.13), channel_id=1, source_target_pairs={{0,1},{1,0},{2,3},{3,2},{4,5},{5,4},{6,7},{7,6},{8,9},{9,8},{10,11... | collective-permute-start | bytes 1548296 | tf_op jit(solution)/shard_map/ppermute | solution.py:43
  68.1 46.0 %collective-permute-start.10 = (bf16[2,288,896]{2,1,0:T(8,128)(2,1)}, bf16[2,288,896]{2,1,0:T(8,128)(2,1)S(1)}, u32[]{:S(2)}, u32[]{:S(2)}) collective-permute-start(bf16[2,288,896]{2,1,0:T(8,128)(2,1)} %get-tuple-element.24), channel_id=1, source_target_pairs={{16,2},{17,3},{18,0},{19,1},{20,6},{21,7},{22,4},{23,5},{24,10},{2... | collective-permute-start | bytes 3096584 | tf_op jit(solution)/shard_map/ppermute | solution.py:43
  91.2 3.2 %copy-start.10 = (bf16[4,1024,128]{2,1,0:T(8,128)(2,1)}, bf16[4,1024,128]{2,1,0:T(8,128)(2,1)S(1)}, u32[]{:S(2)}) copy-start(bf16[4,1024,128]{2,1,0:T(8,128)(2,1)S(1)} %collective-permute-done.6) | copy-start | bytes 3145732
  91.2 3.2 %copy-start.1 = (bf16[1,288,896]{2,1,0:T(8,128)(2,1)S(1)}, bf16[1,288,896]{2,1,0:T(8,128)(2,1)}, u32[]{:S(2)}) copy-start(bf16[1,288,896]{2,1,0:T(8,128)(2,1)} %copy-done) | copy-start | bytes 1548292
  94.5 19.6 %copy-start.2 = (bf16[1,288,896]{2,1,0:T(8,128)(2,1)}, bf16[1,288,896]{2,1,0:T(8,128)(2,1)S(1)}, u32[]{:S(2)}) copy-start(bf16[1,288,896]{2,1,0:T(8,128)(2,1)S(1)} %after.7.rest_0_) | copy-start | bytes 1548292
  94.5 20.1 %collective-permute-start.8 = (bf16[1,288,896]{2,1,0:T(8,128)(2,1)S(1)}, bf16[1,288,896]{2,1,0:T(8,128)(2,1)}, u32[]{:S(2)}, u32[]{:S(2)}) collective-permute-start(bf16[1,288,896]{2,1,0:T(8,128)(2,1)S(1)} %after.7.rest_0_), channel_id=1, source_target_pairs={{0,2},{1,3},{2,0},{3,1},{4,6},{5,7},{6,4},{7,5},{8,10},{9,11},{10,... | collective-permute-start | bytes 1548296 | tf_op jit(solution)/shard_map/ppermute | solution.py:43
  95.9 37.7 %all-to-all-start.1 = ((bf16[4,1024,128]{2,1,0:T(8,128)(2,1)}), bf16[4,1024,128]{2,1,0:T(8,128)(2,1)S(1)}, u32[]{:S(2)}, u32[]{:S(2)}) async-start(bf16[4,1024,128]{2,1,0:T(8,128)(2,1)} %add_convert_fusion.refs_1_), calls=%async_computation.1 | async-start | bytes 2097152 | tf_op jit(solution)/shard_map/all_to_all | solution.py:483
  101.3 0.8 copy-start.19
  109.9 0.7 copy-start.8
  110.6 1.2 copy-start.11
  113.4 17.7 %collective-permute-start.16 = (bf16[1008,128]{1,0:T(8,128)(2,1)S(1)}, bf16[1008,128]{1,0:T(8,128)(2,1)S(1)}, u32[]{:S(2)}, u32[]{:S(2)}) collective-permute-start(bf16[1008,128]{1,0:T(8,128)(2,1)S(1)} %fusion), channel_id=1, source_target_pairs={{0,2},{1,3},{2,0},{3,1},{4,6},{5,7},{6,4},{7,5},{8,10},{9,11},{10,... | collective-permute-start | bytes 774152 | tf_op jit(solution)/shard_map/ppermute | solution.py:43
  114.1 19.5 %copy-start.3 = (bf16[2,288,896]{2,1,0:T(8,128)(2,1)}, bf16[2,288,896]{2,1,0:T(8,128)(2,1)S(1)}, u32[]{:S(2)}) copy-start(bf16[2,288,896]{2,1,0:T(8,128)(2,1)S(1)} %collective-permute-done.10.refs_1_.rest_4_) | copy-start | bytes 3096580
  114.1 23.4 %collective-permute-start.11 = (bf16[2,288,896]{2,1,0:T(8,128)(2,1)S(1)}, bf16[2,288,896]{2,1,0:T(8,128)(2,1)}, u32[]{:S(2)}, u32[]{:S(2)}) collective-permute-start(bf16[2,288,896]{2,1,0:T(8,128)(2,1)S(1)} %collective-permute-done.10.refs_1_.rest_4_), channel_id=1, source_target_pairs={{0,1},{1,0},{2,3},{3,2},{4,5},{5,4},{6,7},{7,6},{8,9},{9,8},{10,11... | collective-permute-start | bytes 3096584 | tf_op jit(solution)/shard_map/ppermute | solution.py:43
  114.1 23.4 %collective-permute-start.7 = (bf16[1,288,896]{2,1,0:T(8,128)(2,1)S(1)}, bf16[1,288,896]{2,1,0:T(8,128)(2,1)}, u32[]{:S(2)}, u32[]{:S(2)}) collective-permute-start(bf16[1,288,896]{2,1,0:T(8,128)(2,1)S(1)} %after.7.rest_0_), channel_id=1, source_target_pairs={{0,1},{1,0},{2,3},{3,2},{4,5},{5,4},{6,7},{7,6},{8,9},{9,8},{10,11... | collective-permute-start | bytes 1548296 | tf_op jit(solution)/shard_map/ppermute | solution.py:43
  114.6 22.9 %collective-permute-start.9 = (bf16[1,288,896]{2,1,0:T(8,128)(2,1)}, bf16[1,288,896]{2,1,0:T(8,128)(2,1)}, u32[]{:S(2)}, u32[]{:S(2)}) collective-permute-start(bf16[1,288,896]{2,1,0:T(8,128)(2,1)} %collective-permute-done.8.rest_2_), channel_id=1, source_target_pairs={{0,1},{1,0},{2,3},{3,2},{4,5},{5,4},{6,7},{7,6},{8,9},{9,8},{10,11... | collective-permute-start | bytes 1548296 | tf_op jit(solution)/shard_map/ppermute | solution.py:43
  135.9 13.1 %collective-permute-start.17 = (bf16[2032,128]{1,0:T(8,128)(2,1)}, bf16[2032,128]{1,0:T(8,128)(2,1)}, u32[]{:S(2)}, u32[]{:S(2)}) collective-permute-start(bf16[2032,128]{1,0:T(8,128)(2,1)} %pad_maximum_fusion.rest_6_), channel_id=1, source_target_pairs={{0,112},{1,113},{2,114},{3,115},{4,116},{5,117},{6,118},{7,119},{8... | collective-permute-start | bytes 1560584 | tf_op jit(solution)/shard_map/ppermute | solution.py:43
  137.5 11.4 %copy-start.4 = (f32[1008,128]{1,0:T(8,128)S(1)}, f32[1008,128]{1,0:T(8,128)}, u32[]{:S(2)}) copy-start(f32[1008,128]{1,0:T(8,128)} %get-tuple-element.39.own_a) | copy-start | bytes 1548292
  137.5 11.4 %copy-start.5 = (f32[1,448,576]{2,1,0:T(8,128)S(1)}, f32[1,448,576]{2,1,0:T(8,128)}, u32[]{:S(2)}) copy-start(f32[1,448,576]{2,1,0:T(8,128)} %param.16) | copy-start | bytes 3096580
  137.5 11.4 %copy-start.6 = (f32[1,448,576]{2,1,0:T(8,128)S(1)}, f32[1,448,576]{2,1,0:T(8,128)}, u32[]{:S(2)}) copy-start(f32[1,448,576]{2,1,0:T(8,128)} %param.17) | copy-start | bytes 3096580
  148.9 1.3 copy-start.7
  150.2 4.4 %copy-start.16 = (f32[1,32]{1,0:T(1,128)S(1)}, f32[1,32]{1,0:T(1,128)}, u32[]{:S(2)}) copy-start(f32[1,32]{1,0:T(1,128)} %param.19) | copy-start | bytes 388
  150.2 4.4 %copy-start.17 = (f32[1,32]{1,0:T(1,128)S(1)}, f32[1,32]{1,0:T(1,128)}, u32[]{:S(2)}) copy-start(f32[1,32]{1,0:T(1,128)} %param.20) | copy-start | bytes 388
  150.2 4.4 %copy-start.18 = (f32[1,32]{1,0:T(1,128)S(1)}, f32[1,32]{1,0:T(1,128)}, u32[]{:S(2)}) copy-start(f32[1,32]{1,0:T(1,128)} %param.21) | copy-start | bytes 388

commit v6 on v5

--- a/solution.py
+++ b/solution.py
@@ -460,17 +460,16 @@
     hidden = hidden_in[0]
     turned = weight[0].T
     other = moved(hidden, to_core)
-    groups = [[(0, 0)], [(0, 1), (2, 0)], [(2, 1), (1, 1)]]
+    groups = [[(0, 0)], [(2, 0), (2, 1)], [(1, 1), (3, 1)]]
     cut_0, cut_1, cut_2 = cut_weight(turned, groups)
     here = moved(cut_0, to_before_near)
     rope = rope_step(rope_cot[0])
     grad = latent_step(hidden, turned, latent_cot[0], gain, rope, cut_0)
-    grad = after(grad, here, mib=62)
     grad_other = moved(grad, to_core)
-    grad_next = moved(grad, to_before)
-    rest_1 = moved(cut_1, to_before_near)
-    rest_2 = moved(cut_2, to_before_near)
+    rest_1 = moved(after(cut_1, here, mib=62), to_before_near)
+    rest_2 = moved(after(cut_2, rest_1, mib=62), to_before_near)
     above, below = moved(here, to_z(-1)), moved(here, to_z(1))
+    beside = moved(here, to_ylo)
 
     def both(value, *blocks):
         return value, moved(value, to_core), blocks
@@ -483,24 +482,28 @@
         return lax.all_to_all(value, "dp", 0, 0, axis_index_groups=along_z, tiled=True)
 
     ra = exchanged(send_a)
-    rb = moved(after(send_b, above, below, grad_next, mib=62), to_ylo)
-    pieces = both(here, (0, 0)), both(above, (1, 0)), both(rest_1, (0, 1), (2, 0))
-    received, is_begun = input_step(grad_next, pieces, [])
+    rb = moved(after(send_b, above, below, beside, rest_1, mib=62), to_ylo)
+    pieces = [
+        both(here, (0, 0)),
+        both(above, (1, 0)),
+        both(below, (3, 0)),
+        both(beside, (0, 1)),
+        both(rest_1, *groups[1]),
+        both(rest_2, *groups[2]),
+    ]
+    rb = after(rb, *(piece[1] for piece in pieces[:4]))
     send_b = (own_b + rb.astype(F32)).astype(BF)
+    grad_next = moved(after(grad, send_b, mib=62), to_before)
     rz = exchanged(send_b)
-    ra = after(ra, is_begun)
     send_a = received_sum(own_a[1], ra[:, 1], z).astype(BF)
     ry = moved(send_a, to_ylo)
-    below = after(below, send_b)
-    side = moved(below, to_ylo)
     total_a = received_sum(own_a[0], ra[:, 0], z) + ry.astype(F32)
     keep_b = lax.dynamic_index_in_dim(own_b, z, 0, False)
     keep_b += lax.dynamic_index_in_dim(rb, z, 0, False).astype(F32)
     total_b = received_sum(keep_b, after(rz, rest_2), z)
     send = jnp.concatenate([total_a, total_b], axis=0).astype(BF)
     far = moved(send, to_mirror)
-    pieces = both(below, (3, 0)), both(side, (3, 1)), both(rest_2, (2, 1), (1, 1))
-    received, _ = input_step(grad_next, pieces, [send], received)
+    received, _ = input_step(grad_next, pieces, [send])
     next_master, next_first, next_second, gain_rows = adam_step(
         s, total_a, total_b, far, master_weight[0], first_moment[0], second_moment[0]
     )

time: 156 us -> 137 us (0.88)
  the two profiles are of different devices: /device:TPU:24 before, /device:TPU:1 now
where the time goes in v6:
time: 137 us; the launch traced here: 136 us
  waiting for transfers between devices  59.9 us (44%)
  Pallas kernels  38.6 us (28%)
  starting transfers between devices  26.4 us (19%)
  other arithmetic  8.43 us (6%)
  local copies, waits for them, and re-layouts  2.1 us (2%)
    ppermute x18, waiting for transfers between devices, moved(): return lax.ppermute(value, ('pipe', 'dp'), pairs)  56.4 us
    ppermute x18, starting transfers between devices, moved(): return lax.ppermute(value, ('pipe', 'dp'), pairs)  16.6 us
    pallas_call x1, Pallas kernels, input_step(): pl.pallas_call(kernel, in_specs=[inside] + [ANYWHERE] * halves + [LATER]...  11.9 us
    all_to_all x2, starting transfers between devices, exchanged(): lax.all_to_all(value, 'dp', 0, 0, axis_index_groups=along_z, tiled=True)  9.8 us
    pallas_call x1, Pallas kernels, weight_step(): pl.pallas_call(weight_kernel, in_specs=[ANYWHERE] * 4, out_specs=[ANYWHER...  9.76 us
    pallas_call x1, Pallas kernels, latent_step(): pl.pallas_call(latent_kernel, in_specs=[ANYWHERE, ANYWHERE, inside, insid...  9.19 us
    pallas_call x1, Pallas kernels, adam_step(): pl.pallas_call(adam_kernel, in_specs=[pl.BlockSpec(memory_space=pltpu.SME...  4.51 us
    another operation x3, other arithmetic  3.48 us
  transfers between devices with their start and end apart: 20, of which 9 were waited for; matrix products, arithmetic and copies ran while one was open for 6% of the time, Pallas kernels for 25%

profile of v6, /device:TPU:1, one launch (start us, length us, event | category | flops | bytes accessed | tf_op | source)
XLA Modules:
  0.0 136.3 jit_solution(10515655684938346279)
XLA Ops:
  0.6 1.5 %collective-permute-start = (bf16[512,7168]{1,0:T(8,128)(2,1)}, bf16[512,7168]{1,0:T(8,128)(2,1)}, u32[]{:S(2)}, u32[]{:S(2)}) collective-permute-start(bf16[512,7168]{1,0:T(8,128)(2,1)} %bitcast.90), channel_id=1, source_target_pairs={{0,1},{1,0},{2,3},{3,2},{4,5},{5,4},{6,7},{7,6},{8,9},{9,8},{10,11... | collective-permute-start | bytes 22020104 | tf_op jit(solution)/shard_map/ppermute | solution.py:43
  2.1 3.2 %cut_weight.1 = (bf16[1,288,896]{2,1,0:T(8,128)(2,1)}, bf16[2,288,896]{2,1,0:T(8,128)(2,1)}, bf16[2,288,896]{2,1,0:T(8,128)(2,1)}) custom-call(bf16[576,7168]{1,0:T(8,128)(2,1)} %bitcast.88), custom_call_target="tpu_custom_call" | custom-call | bytes 1000 | tf_op jit(solution)/shard_map/cut_weight/pallas_call | solution.py:125
  5.4 1.3 collective-permute-start.2
  6.7 0.3 fusion.7
  7.0 0.6 pad_maximum_fusion.1.rope
  7.7 9.2 %latent_grad.1.grad.refs_0_ = bf16[592,512]{1,0:T(8,128)(2,1)} custom-call(bf16[512,7168]{1,0:T(8,128)(2,1)} %bitcast.91, bf16[576,7168]{1,0:T(8,128)(2,1)} %bitcast.89, bf16[512,512]{1,0:T(8,128)(2,1)} %bitcast.93, f32[1,512]{1,0:T(1,128)} %gain.1, bf16[64,512]{1,0:T(8,128)(2,1)} %pad_maximum_fusion.1.rope, bf16[1,288,896]{2,1,0:T(8,128)(2,1)} %get-tuple-element.19.earlier), custom_call_target="tpu_custom_call" | custom-call | bytes 1000 | tf_op jit(solution)/shard_map/latent_grad/pallas_call | solution.py:183
  16.9 0.1 collective-permute-start.1
  17.0 5.3 %collective-permute-done.2.refs_1_.rest_0_ = bf16[1,288,896]{2,1,0:T(8,128)(2,1)S(1)} collective-permute-done((bf16[1,288,896]{2,1,0:T(8,128)(2,1)}, bf16[1,288,896]{2,1,0:T(8,128)(2,1)S(1)}, u32[]{:S(2)}, u32[]{:S(2)}) %collective-permute-start.2) | collective-permute-done | bytes 516128 | tf_op jit(solution)/shard_map/ppermute | solution.py:43
  22.2 0.8 copy-done.6
  23.0 1.3 collective-permute-start.6
  24.3 3.8 %collective-permute-start.3 = (bf16[1,288,896]{2,1,0:T(8,128)(2,1)}, bf16[1,288,896]{2,1,0:T(8,128)(2,1)S(1)}, u32[]{:S(2)}, u32[]{:S(2)}) collective-permute-start(bf16[1,288,896]{2,1,0:T(8,128)(2,1)} %copy-done.6), channel_id=1, source_target_pairs={{0,12},{1,13},{2,14},{3,15},{4,0},{5,1},{6,2},{7,3},{8,4},{9,5},{1... | collective-permute-start | bytes 1548296 | tf_op jit(solution)/shard_map/ppermute | solution.py:43
  28.2 0.0 collective-permute-start.4
  28.2 0.0 collective-permute-done.1.grad_other
  28.2 0.0 collective-permute-start.5
  28.2 0.0 collective-permute-done.other
  28.2 9.8 %weight_grad.1 = (f32[2,1008,128]{2,1,0:T(8,128)}, bf16[4,2,1008,128]{3,2,1,0:T(8,128)(2,1)}, f32[4,1024,128]{2,1,0:T(8,128)}, bf16[4,1024,128]{2,1,0:T(8,128)(2,1)}) custom-call(bf16[512,7168]{1,0:T(8,128)(2,1)} %bitcast.92, bf16[512,7168]{1,0:T(8,128)(2,1)} %collective-permute-done.other, bf16[592,512]{1,0:T(8,128)(2,1)} %latent_grad.1.grad.refs_0_, ...), custom_call_target="tpu_custom_call" | custom-call | bytes 1000 | tf_op jit(solution)/shard_map/weight_grad/pallas_call | solution.py:289
  38.0 4.5 %all-to-all-start = ((bf16[4,2,1008,128]{3,2,1,0:T(8,128)(2,1)}), bf16[4,2,1008,128]{3,2,1,0:T(8,128)(2,1)}, u32[]{:S(2)}, u32[]{:S(2)}) async-start(bf16[4,2,1008,128]{3,2,1,0:T(8,128)(2,1)} %get-tuple-element.25), calls=%async_computation | async-start | bytes 4128768 | tf_op jit(solution)/shard_map/all_to_all | solution.py:482
  42.4 0.0 collective-permute-done.3.refs_1_.rest_2_
  42.5 8.6 %collective-permute-done.6.refs_4_.refs_1_.rest_8_ = bf16[2,288,896]{2,1,0:T(8,128)(2,1)} collective-permute-done((bf16[2,288,896]{2,1,0:T(8,128)(2,1)}, bf16[2,288,896]{2,1,0:T(8,128)(2,1)}, u32[]{:S(2)}, u32[]{:S(2)}) %collective-permute-start.6) | collective-permute-done | bytes 1032224 | tf_op jit(solution)/shard_map/ppermute | solution.py:43
  51.1 0.1 collective-permute-start.7
  51.2 1.5 %collective-permute-start.8 = (bf16[1,288,896]{2,1,0:T(8,128)(2,1)}, bf16[1,288,896]{2,1,0:T(8,128)(2,1)S(1)}, u32[]{:S(2)}, u32[]{:S(2)}) collective-permute-start(bf16[1,288,896]{2,1,0:T(8,128)(2,1)} %copy-done.6), channel_id=1, source_target_pairs={{0,1},{1,0},{2,3},{3,2},{4,5},{5,4},{6,7},{7,6},{8,9},{9,8},{10,11... | collective-permute-start | bytes 1548296 | tf_op jit(solution)/shard_map/ppermute | solution.py:43
  52.7 0.1 collective-permute-start.9
  52.8 0.4 collective-permute-start.10
  53.2 0.1 collective-permute-start.11
  53.3 1.1 collective-permute-done.8.refs_1_.rest_1_
  54.4 1.3 collective-permute-start.14
  55.7 0.3 collective-permute-done.10.refs_3_.rest_5_
  56.0 0.7 collective-permute-done.11.refs_4_.rest_7_
  56.8 18.0 %collective-permute-done.7.refs_0_ = bf16[4,1024,128]{2,1,0:T(8,128)(2,1)S(1)} collective-permute-done((bf16[4,1024,128]{2,1,0:T(8,128)(2,1)}, bf16[4,1024,128]{2,1,0:T(8,128)(2,1)S(1)}, u32[]{:S(2)}, u32[]{:S(2)}) %collective-permute-start.7) | collective-permute-done | bytes 1048608 | tf_op jit(solution)/shard_map/ppermute | solution.py:43
  74.8 1.3 add_convert_fusion.refs_1_
  76.1 5.3 %all-to-all-start.1 = ((bf16[4,1024,128]{2,1,0:T(8,128)(2,1)}), bf16[4,1024,128]{2,1,0:T(8,128)(2,1)S(1)}, u32[]{:S(2)}, u32[]{:S(2)}) async-start(bf16[4,1024,128]{2,1,0:T(8,128)(2,1)} %add_convert_fusion.refs_1_), calls=%async_computation.1 | async-start | bytes 2097152 | tf_op jit(solution)/shard_map/all_to_all | solution.py:482
  81.4 1.6 %fusion = bf16[1008,128]{1,0:T(8,128)(2,1)S(1)} fusion(f32[2,1008,128]{2,1,0:T(8,128)S(1)} %copy-done.10, bf16[4,2,1008,128]{3,2,1,0:T(8,128)(2,1)} %all-to-all-done, pred[]{:T(512)S(6)} %eq.11, pred[]{:T(512)S(6)} %eq.10, pred[]{:T(512)S(6)} %eq.9, pred[]{:T(512)S(6)} %eq.8), kind=kLoop, calls=%fused_computation.4 | loop fusion | flops 1677312 | bytes 1806340 | tf_op jit(solution)/shard_map/convert_element_type | solution.py:498
  83.0 0.4 collective-permute-start.16
  83.4 2.5 %collective-permute-start.13 = (bf16[2,288,896]{2,1,0:T(8,128)(2,1)}, bf16[2,288,896]{2,1,0:T(8,128)(2,1)}, u32[]{:S(2)}, u32[]{:S(2)}) collective-permute-start(bf16[2,288,896]{2,1,0:T(8,128)(2,1)} %collective-permute-done.6.refs_4_.refs_1_.rest_8_), channel_id=1, source_target_pairs={{0,1},{1,0},{2,3},{3,2},{4,5},{5,4},{6,7},{7,6},{8,9},{9,8},{10,11... | collective-permute-start | bytes 3096584 | tf_op jit(solution)/shard_map/ppermute | solution.py:43
  85.9 0.0 collective-permute-start.15
  85.9 1.3 collective-permute-start.12
  87.2 1.4 %collective-permute-done.16 = bf16[1008,128]{1,0:T(8,128)(2,1)S(1)} collective-permute-done((bf16[1008,128]{1,0:T(8,128)(2,1)S(1)}, bf16[1008,128]{1,0:T(8,128)(2,1)S(1)}, u32[]{:S(2)}, u32[]{:S(2)}) %collective-permute-start.16) | collective-permute-done | bytes 258080 | tf_op jit(solution)/shard_map/ppermute | solution.py:43
  88.6 1.8 %fusion.15 = (bf16[1008,128]{1,0:T(8,128)(2,1)S(1)}, f32[1008,128]{1,0:T(8,128)S(1)}) fusion(bf16[1008,128]{1,0:T(8,128)(2,1)S(1)} %collective-permute-done.16, bf16[4,2,1008,128]{3,2,1,0:T(8,128)(2,1)} %all-to-all-done, pred[]{:T(512)S(6)} %eq.11, pred[]{:T(512)S(6)} %eq.10, pred[]{:T(512)S(6)} %eq.9, pred[]{:T(512)S(6)} %eq.8, ...), kind=kLoop, calls=%fused_computation.36 | loop fusion | flops 1935360 | bytes 2580484 | tf_op jit(solution)/shard_map/convert.2
  90.3 3.5 %all-to-all-done.1.refs_0_ = bf16[4,1024,128]{2,1,0:T(8,128)(2,1)S(1)} async-done(((bf16[4,1024,128]{2,1,0:T(8,128)(2,1)}), bf16[4,1024,128]{2,1,0:T(8,128)(2,1)S(1)}, u32[]{:S(2)}, u32[]{:S(2)}) %all-to-all-start.1) | async-done | bytes 1048608 | tf_op jit(solution)/shard_map/all_to_all | solution.py:482
  93.8 1.4 %fusion.17 = (bf16[1024,128]{1,0:T(8,128)(2,1)S(1)}, f32[1024,128]{1,0:T(8,128)S(1)}) fusion(bf16[4,1024,128]{2,1,0:T(8,128)(2,1)S(1)} %after.11, pred[]{:T(512)S(6)} %eq.11, pred[]{:T(512)S(6)} %eq.10, pred[]{:T(512)S(6)} %eq.9, pred[]{:T(512)S(6)} %eq.8, bf16[4,1024,128]{2,1,0:T(8,128)(2,1)} %copy-done, s32[]{:T(128)S(6)} %select_n.129, ...), kind=kLoop, calls=%fused_computation.37 | loop fusion | flops 1966080 | bytes 2621448 | tf_op jit(solution)/shard_map/convert.3
  95.2 0.8 pad_maximum_fusion.rest_12_
  96.0 1.0 collective-permute-start.17
  97.0 21.0 %collective-permute-done.12.grad = bf16[592,512]{1,0:T(8,128)(2,1)} collective-permute-done((bf16[592,512]{1,0:T(8,128)(2,1)}, bf16[592,512]{1,0:T(8,128)(2,1)}, u32[]{:S(2)}, u32[]{:S(2)}) %collective-permute-start.12) | collective-permute-done | bytes 606240 | tf_op jit(solution)/shard_map/ppermute | solution.py:43
  117.9 11.9 %input_grad.1 = (bf16[512,7168]{1,0:T(8,128)(2,1)}, f32[8,128]{1,0:T(8,128)}) custom-call(bf16[592,512]{1,0:T(8,128)(2,1)} %collective-permute-done.12.grad, bf16[1,288,896]{2,1,0:T(8,128)(2,1)} %copy-done.6, bf16[1,288,896]{2,1,0:T(8,128)(2,1)} %copy-done.1, bf16[1,288,896]{2,1,0:T(8,128)(2,1)} %copy-done.7, ...), custom_call_target="tpu_custom_call" | custom-call | flops 2113929216 | bytes 8000000 | tf_op jit(solution)/shard_map/input_grad/pallas_call | solution.py:410
  129.9 0.0 copy-start.4
  129.9 1.2 copy-done.4
  131.1 4.5 %adamw.1 = (f32[448,576]{1,0:T(8,128)}, f32[448,576]{1,0:T(8,128)}, f32[448,576]{1,0:T(8,128)}, f32[8,128]{1,0:T(8,128)S(1)}) custom-call(s32[1]{0:T(128)} %bitcast.20.s, f32[1008,128]{1,0:T(8,128)S(1)} %get-tuple-element.35.own_a, f32[1024,128]{1,0:T(8,128)S(1)} %get-tuple-element.37.own_b, bf16[2032,128]{1,0:T(8,128)(2,1)} %collective-permute-done.17.far, ...), custom_call_target="tpu_custom_call" | custom-call | bytes 9000000 | tf_op jit(solution)/shard_map/adamw/pallas_call | solution.py:359
  135.7 0.6 fusion.13
  (45 shorter events, 0.1 us)
Async XLA Ops:
  0.6 27.5 %collective-permute-start = (bf16[512,7168]{1,0:T(8,128)(2,1)}, bf16[512,7168]{1,0:T(8,128)(2,1)}, u32[]{:S(2)}, u32[]{:S(2)}) collective-permute-start(bf16[512,7168]{1,0:T(8,128)(2,1)} %bitcast.90), channel_id=1, source_target_pairs={{0,1},{1,0},{2,3},{3,2},{4,5},{5,4},{6,7},{7,6},{8,9},{9,8},{10,11... | collective-permute-start | bytes 22020104 | tf_op jit(solution)/shard_map/ppermute | solution.py:43
  2.1 4.5 %copy-start.11 = (bf16[1,512,64]{1,2,0:T(8,128)(2,1)S(1)}, bf16[1,512,64]{1,2,0:T(8,128)(2,1)}, u32[]{:S(2)}) copy-start(bf16[1,512,64]{1,2,0:T(8,128)(2,1)} %param.15) | copy-start | bytes 196612
  5.4 16.9 %collective-permute-start.2 = (bf16[1,288,896]{2,1,0:T(8,128)(2,1)}, bf16[1,288,896]{2,1,0:T(8,128)(2,1)S(1)}, u32[]{:S(2)}, u32[]{:S(2)}) collective-permute-start(bf16[1,288,896]{2,1,0:T(8,128)(2,1)} %get-tuple-element.19.earlier), channel_id=1, source_target_pairs={{16,2},{17,3},{18,0},{19,1},{20,6},{21,7},{22,4},{23,5},{24,10},{2... | collective-permute-start | bytes 1548296 | tf_op jit(solution)/shard_map/ppermute | solution.py:43
  16.9 11.3 %collective-permute-start.1 = (bf16[592,512]{1,0:T(8,128)(2,1)}, bf16[592,512]{1,0:T(8,128)(2,1)}, u32[]{:S(2)}, u32[]{:S(2)}) collective-permute-start(bf16[592,512]{1,0:T(8,128)(2,1)} %latent_grad.1.grad.refs_0_), channel_id=1, source_target_pairs={{0,1},{1,0},{2,3},{3,2},{4,5},{5,4},{6,7},{7,6},{8,9},{9,8},{10,11... | collective-permute-start | bytes 1818632 | tf_op jit(solution)/shard_map/ppermute | solution.py:43
  22.2 0.8 copy-start.6
  23.0 28.1 %collective-permute-start.6 = (bf16[2,288,896]{2,1,0:T(8,128)(2,1)}, bf16[2,288,896]{2,1,0:T(8,128)(2,1)}, u32[]{:S(2)}, u32[]{:S(2)}) collective-permute-start(bf16[2,288,896]{2,1,0:T(8,128)(2,1)} %after.6), channel_id=1, source_target_pairs={{16,2},{17,3},{18,0},{19,1},{20,6},{21,7},{22,4},{23,5},{24,10},{2... | collective-permute-start | bytes 3096584 | tf_op jit(solution)/shard_map/ppermute | solution.py:43
  24.3 18.1 %collective-permute-start.3 = (bf16[1,288,896]{2,1,0:T(8,128)(2,1)}, bf16[1,288,896]{2,1,0:T(8,128)(2,1)S(1)}, u32[]{:S(2)}, u32[]{:S(2)}) collective-permute-start(bf16[1,288,896]{2,1,0:T(8,128)(2,1)} %copy-done.6), channel_id=1, source_target_pairs={{0,12},{1,13},{2,14},{3,15},{4,0},{5,1},{6,2},{7,3},{8,4},{9,5},{1... | collective-permute-start | bytes 1548296 | tf_op jit(solution)/shard_map/ppermute | solution.py:43
  28.2 14.3 %collective-permute-start.4 = (bf16[1,288,896]{2,1,0:T(8,128)(2,1)}, bf16[1,288,896]{2,1,0:T(8,128)(2,1)S(1)}, u32[]{:S(2)}, u32[]{:S(2)}) collective-permute-start(bf16[1,288,896]{2,1,0:T(8,128)(2,1)} %copy-done.6), channel_id=1, source_target_pairs={{0,4},{1,5},{2,6},{3,7},{4,8},{5,9},{6,10},{7,11},{8,12},{9,13},{1... | collective-permute-start | bytes 1548296 | tf_op jit(solution)/shard_map/ppermute | solution.py:43
  28.2 14.3 %collective-permute-start.5 = (bf16[1,288,896]{2,1,0:T(8,128)(2,1)}, bf16[1,288,896]{2,1,0:T(8,128)(2,1)S(1)}, u32[]{:S(2)}, u32[]{:S(2)}) collective-permute-start(bf16[1,288,896]{2,1,0:T(8,128)(2,1)} %copy-done.6), channel_id=1, source_target_pairs={{0,2},{1,3},{2,0},{3,1},{4,6},{5,7},{6,4},{7,5},{8,10},{9,11},{10,... | collective-permute-start | bytes 1548296 | tf_op jit(solution)/shard_map/ppermute | solution.py:43
  38.0 38.1 %all-to-all-start = ((bf16[4,2,1008,128]{3,2,1,0:T(8,128)(2,1)}), bf16[4,2,1008,128]{3,2,1,0:T(8,128)(2,1)}, u32[]{:S(2)}, u32[]{:S(2)}) async-start(bf16[4,2,1008,128]{3,2,1,0:T(8,128)(2,1)} %get-tuple-element.25), calls=%async_computation | async-start | bytes 4128768 | tf_op jit(solution)/shard_map/all_to_all | solution.py:482
  42.4 8.7 %copy-start.7 = (bf16[1,288,896]{2,1,0:T(8,128)(2,1)}, bf16[1,288,896]{2,1,0:T(8,128)(2,1)S(1)}, u32[]{:S(2)}) copy-start(bf16[1,288,896]{2,1,0:T(8,128)(2,1)S(1)} %collective-permute-done.3.refs_1_.rest_2_) | copy-start | bytes 1548292
  42.4 8.7 %copy-start.8 = (bf16[1,288,896]{2,1,0:T(8,128)(2,1)}, bf16[1,288,896]{2,1,0:T(8,128)(2,1)S(1)}, u32[]{:S(2)}) copy-start(bf16[1,288,896]{2,1,0:T(8,128)(2,1)S(1)} %collective-permute-done.4.refs_2_.rest_4_) | copy-start | bytes 1548292
  42.5 8.6 %copy-start.9 = (bf16[1,288,896]{2,1,0:T(8,128)(2,1)}, bf16[1,288,896]{2,1,0:T(8,128)(2,1)S(1)}, u32[]{:S(2)}) copy-start(bf16[1,288,896]{2,1,0:T(8,128)(2,1)S(1)} %collective-permute-done.5.refs_3_.rest_6_) | copy-start | bytes 1548292
  51.1 23.6 %collective-permute-start.7 = (bf16[4,1024,128]{2,1,0:T(8,128)(2,1)}, bf16[4,1024,128]{2,1,0:T(8,128)(2,1)S(1)}, u32[]{:S(2)}, u32[]{:S(2)}) collective-permute-start(bf16[4,1024,128]{2,1,0:T(8,128)(2,1)} %after.7), channel_id=1, source_target_pairs={{0,2},{1,3},{2,0},{3,1},{4,6},{5,7},{6,4},{7,5},{8,10},{9,11},{10,... | collective-permute-start | bytes 3145736 | tf_op jit(solution)/shard_map/ppermute | solution.py:43
  51.2 3.2 %collective-permute-start.8 = (bf16[1,288,896]{2,1,0:T(8,128)(2,1)}, bf16[1,288,896]{2,1,0:T(8,128)(2,1)S(1)}, u32[]{:S(2)}, u32[]{:S(2)}) collective-permute-start(bf16[1,288,896]{2,1,0:T(8,128)(2,1)} %copy-done.6), channel_id=1, source_target_pairs={{0,1},{1,0},{2,3},{3,2},{4,5},{5,4},{6,7},{7,6},{8,9},{9,8},{10,11... | collective-permute-start | bytes 1548296 | tf_op jit(solution)/shard_map/ppermute | solution.py:43
  52.7 3.0 %collective-permute-start.9 = (bf16[1,288,896]{2,1,0:T(8,128)(2,1)}, bf16[1,288,896]{2,1,0:T(8,128)(2,1)}, u32[]{:S(2)}, u32[]{:S(2)}) collective-permute-start(bf16[1,288,896]{2,1,0:T(8,128)(2,1)} %copy-done.7), channel_id=1, source_target_pairs={{0,1},{1,0},{2,3},{3,2},{4,5},{5,4},{6,7},{7,6},{8,9},{9,8},{10,11... | collective-permute-start | bytes 1548296 | tf_op jit(solution)/shard_map/ppermute | solution.py:43
  52.8 3.3 %collective-permute-start.10 = (bf16[1,288,896]{2,1,0:T(8,128)(2,1)}, bf16[1,288,896]{2,1,0:T(8,128)(2,1)}, u32[]{:S(2)}, u32[]{:S(2)}) collective-permute-start(bf16[1,288,896]{2,1,0:T(8,128)(2,1)} %copy-done.8), channel_id=1, source_target_pairs={{0,1},{1,0},{2,3},{3,2},{4,5},{5,4},{6,7},{7,6},{8,9},{9,8},{10,11... | collective-permute-start | bytes 1548296 | tf_op jit(solution)/shard_map/ppermute | solution.py:43
  53.2 3.6 %collective-permute-start.11 = (bf16[1,288,896]{2,1,0:T(8,128)(2,1)}, bf16[1,288,896]{2,1,0:T(8,128)(2,1)}, u32[]{:S(2)}, u32[]{:S(2)}) collective-permute-start(bf16[1,288,896]{2,1,0:T(8,128)(2,1)} %copy-done.9), channel_id=1, source_target_pairs={{0,1},{1,0},{2,3},{3,2},{4,5},{5,4},{6,7},{7,6},{8,9},{9,8},{10,11... | collective-permute-start | bytes 1548296 | tf_op jit(solution)/shard_map/ppermute | solution.py:43
  53.3 21.5 %copy-start.5 = (f32[4,1024,128]{2,1,0:T(8,128)S(1)}, f32[4,1024,128]{2,1,0:T(8,128)}, u32[]{:S(2)}) copy-start(f32[4,1024,128]{2,1,0:T(8,128)} %get-tuple-element.20) | copy-start | bytes 6291460
  54.4 20.3 %copy-start.1 = (bf16[1,288,896]{2,1,0:T(8,128)(2,1)}, bf16[1,288,896]{2,1,0:T(8,128)(2,1)S(1)}, u32[]{:S(2)}) copy-start(bf16[1,288,896]{2,1,0:T(8,128)(2,1)S(1)} %collective-permute-done.8.refs_1_.rest_1_) | copy-start | bytes 1548292
  54.4 31.4 %collective-permute-start.14 = (bf16[2,288,896]{2,1,0:T(8,128)(2,1)}, bf16[2,288,896]{2,1,0:T(8,128)(2,1)}, u32[]{:S(2)}, u32[]{:S(2)}) collective-permute-start(bf16[2,288,896]{2,1,0:T(8,128)(2,1)} %after.10), channel_id=1, source_target_pairs={{16,2},{17,3},{18,0},{19,1},{20,6},{21,7},{22,4},{23,5},{24,10},{2... | collective-permute-start | bytes 3096584 | tf_op jit(solution)/shard_map/ppermute | solution.py:43
  74.8 1.3 copy-start
  76.1 5.4 %copy-start.10 = (f32[2,1008,128]{2,1,0:T(8,128)S(1)}, f32[2,1008,128]{2,1,0:T(8,128)}, u32[]{:S(2)}) copy-start(f32[2,1008,128]{2,1,0:T(8,128)} %get-tuple-element.24) | copy-start | bytes 3096580
  76.1 17.7 %all-to-all-start.1 = ((bf16[4,1024,128]{2,1,0:T(8,128)(2,1)}), bf16[4,1024,128]{2,1,0:T(8,128)(2,1)S(1)}, u32[]{:S(2)}, u32[]{:S(2)}) async-start(bf16[4,1024,128]{2,1,0:T(8,128)(2,1)} %add_convert_fusion.refs_1_), calls=%async_computation.1 | async-start | bytes 2097152 | tf_op jit(solution)/shard_map/all_to_all | solution.py:482
  83.0 5.6 %collective-permute-start.16 = (bf16[1008,128]{1,0:T(8,128)(2,1)S(1)}, bf16[1008,128]{1,0:T(8,128)(2,1)S(1)}, u32[]{:S(2)}, u32[]{:S(2)}) collective-permute-start(bf16[1008,128]{1,0:T(8,128)(2,1)S(1)} %fusion), channel_id=1, source_target_pairs={{0,2},{1,3},{2,0},{3,1},{4,6},{5,7},{6,4},{7,5},{8,10},{9,11},{10,... | collective-permute-start | bytes 774152 | tf_op jit(solution)/shard_map/ppermute | solution.py:43
  83.4 13.6 %collective-permute-start.13 = (bf16[2,288,896]{2,1,0:T(8,128)(2,1)}, bf16[2,288,896]{2,1,0:T(8,128)(2,1)}, u32[]{:S(2)}, u32[]{:S(2)}) collective-permute-start(bf16[2,288,896]{2,1,0:T(8,128)(2,1)} %collective-permute-done.6.refs_4_.refs_1_.rest_8_), channel_id=1, source_target_pairs={{0,1},{1,0},{2,3},{3,2},{4,5},{5,4},{6,7},{7,6},{8,9},{9,8},{10,11... | collective-permute-start | bytes 3096584 | tf_op jit(solution)/shard_map/ppermute | solution.py:43
  85.9 11.1 %collective-permute-start.15 = (bf16[2,288,896]{2,1,0:T(8,128)(2,1)}, bf16[2,288,896]{2,1,0:T(8,128)(2,1)}, u32[]{:S(2)}, u32[]{:S(2)}) collective-permute-start(bf16[2,288,896]{2,1,0:T(8,128)(2,1)} %collective-permute-done.14.refs_1_.rest_10_), channel_id=1, source_target_pairs={{0,1},{1,0},{2,3},{3,2},{4,5},{5,4},{6,7},{7,6},{8,9},{9,8},{10,11... | collective-permute-start | bytes 3096584 | tf_op jit(solution)/shard_map/ppermute | solution.py:43
  85.9 32.1 %collective-permute-start.12 = (bf16[592,512]{1,0:T(8,128)(2,1)}, bf16[592,512]{1,0:T(8,128)(2,1)}, u32[]{:S(2)}, u32[]{:S(2)}) collective-permute-start(bf16[592,512]{1,0:T(8,128)(2,1)} %after.9), channel_id=1, source_target_pairs={{16,0},{17,1},{18,2},{19,3},{20,4},{21,5},{22,6},{23,7},{24,8},{25... | collective-permute-start | bytes 1818632 | tf_op jit(solution)/shard_map/ppermute | solution.py:43
  96.0 33.9 %collective-permute-start.17 = (bf16[2032,128]{1,0:T(8,128)(2,1)}, bf16[2032,128]{1,0:T(8,128)(2,1)}, u32[]{:S(2)}, u32[]{:S(2)}) collective-permute-start(bf16[2032,128]{1,0:T(8,128)(2,1)} %pad_maximum_fusion.rest_12_), channel_id=1, source_target_pairs={{0,112},{1,113},{2,114},{3,115},{4,116},{5,117},{6,118},{7,119},{8... | collective-permute-start | bytes 1560584 | tf_op jit(solution)/shard_map/ppermute | solution.py:43
  97.0 32.9 %copy-start.2 = (f32[1,448,576]{2,1,0:T(8,128)S(1)}, f32[1,448,576]{2,1,0:T(8,128)}, u32[]{:S(2)}) copy-start(f32[1,448,576]{2,1,0:T(8,128)} %param.16) | copy-start | bytes 3096580
  97.0 32.9 %copy-start.3 = (f32[1,448,576]{2,1,0:T(8,128)S(1)}, f32[1,448,576]{2,1,0:T(8,128)}, u32[]{:S(2)}) copy-start(f32[1,448,576]{2,1,0:T(8,128)} %param.17) | copy-start | bytes 3096580
  129.9 1.3 copy-start.4
  131.1 4.5 %copy-start.12 = (f32[1,32]{1,0:T(1,128)S(1)}, f32[1,32]{1,0:T(1,128)}, u32[]{:S(2)}) copy-start(f32[1,32]{1,0:T(1,128)} %param.19) | copy-start | bytes 388
  131.1 4.5 %copy-start.13 = (f32[1,32]{1,0:T(1,128)S(1)}, f32[1,32]{1,0:T(1,128)}, u32[]{:S(2)}) copy-start(f32[1,32]{1,0:T(1,128)} %param.20) | copy-start | bytes 388
  131.1 4.5 %copy-start.14 = (f32[1,32]{1,0:T(1,128)S(1)}, f32[1,32]{1,0:T(1,128)}, u32[]{:S(2)}) copy-start(f32[1,32]{1,0:T(1,128)} %param.21) | copy-start | bytes 388

commit v7 on v5

--- a/solution.py
+++ b/solution.py
@@ -331,11 +331,24 @@
     return (new_master, new_first, new_second)
 
 
-def adam_kernel(s, own_a, own_b, far, master, first, second, n_master, n_first, n_second, gain, grad):
-    total_a = own_a[...] + far[:ROWS_A, :].astype(F32)
-    total_b = own_b[...] + far[ROWS_A:, :].astype(F32)
-    core = s[0]
+def adam_kernel(own_a, own_b, far, *rest):
+    state, outs, gain_out = rest[:3], rest[3:6], rest[6]
+    sum_a, sum_b, sum_far, held, new, grad, gain, sems, out_sems, gain_sem = rest[7:]
+    sums = [
+        pltpu.make_async_copy(source, target, sems.at[i])
+        for i, (source, target) in enumerate(((own_a, sum_a), (own_b, sum_b), (far, sum_far)))
+    ]
+    loads = [
+        pltpu.make_async_copy(ref, held.at[i], sems.at[3 + i]) for i, ref in enumerate(state)
+    ]
+    start_all(sums + loads)
+    wait_all(sums)
+    total_a = sum_a[...] + sum_far[:ROWS_A, :].astype(F32)
+    total_b = sum_b[...] + sum_far[ROWS_A:, :].astype(F32)
+    _, _, core = place()
     gain[...] = total_b[ROWS_A : ROWS_A + 8]
+    gain_copy = pltpu.make_async_copy(gain, gain_out, gain_sem)
+    gain_copy.start()
 
     def both(lo, n):
         return [total[lo : lo + n] for total in (total_a, total_b)]
@@ -348,24 +361,45 @@
         edge += [part, pltpu.roll(part, 64, 1)]
     block = jnp.concatenate(edge, axis=0)
     grad[pl.ds(pl.multiple_of(384 * (1 - core), 64), 64), :] = block.T[:64]
-    n_master[...], n_first[...], n_second[...] = adamw(
-        master[...], first[...], second[...], grad[...]
-    )
-
-
-def adam_step(s, own_a, own_b, far, master, first, second):
+    wait_all(loads)
+    rows, stores = held.shape[1] // 4, []
+    for n in range(4):
+        at = slice(n * rows, n * rows + rows)
+        values = adamw(held[0, at], held[1, at], held[2, at], grad[at])
+        for i, value in enumerate(values):
+            new[i, at] = value
+            part = pl.ds(n * rows, rows)
+            stores.append(
+                pltpu.make_async_copy(new.at[i, part], outs[i].at[part], out_sems.at[n, i])
+            )
+            stores[-1].start()
+    wait_all(stores)
+    gain_copy.wait()
+
+
+def adam_step(own_a, own_b, far, master, first, second):
     shape = jax.ShapeDtypeStruct(master.shape, F32)
-    spec = pl.BlockSpec(memory_space=pltpu.VMEM)
     return pl.pallas_call(
         adam_kernel,
-        in_specs=[pl.BlockSpec(memory_space=pltpu.SMEM)] + [spec] * 6,
-        out_specs=[spec] * 4,
+        in_specs=[LATER] * 6,
+        out_specs=[LATER] * 4,
         out_shape=[shape] * 3 + [jax.ShapeDtypeStruct((8, 128), F32)],
-        scratch_shapes=[pltpu.VMEM(master.shape, F32)],
-        compiler_params=params(32),
+        scratch_shapes=[
+            pltpu.VMEM(own_a.shape, F32),
+            pltpu.VMEM(own_b.shape, F32),
+            pltpu.VMEM(far.shape, BF),
+            pltpu.VMEM((3, *master.shape), F32),
+            pltpu.VMEM((3, *master.shape), F32),
+            pltpu.VMEM(master.shape, F32),
+            pltpu.VMEM((8, 128), F32),
+            pltpu.SemaphoreType.DMA((6,)),
+            pltpu.SemaphoreType.DMA((4, 3)),
+            pltpu.SemaphoreType.DMA,
+        ],
+        compiler_params=params(60),
         cost_estimate=cost(0, 9_000_000),
         name="adamw",
-    )(s, own_a, own_b, far, master, first, second)
+    )(own_a, own_b, far, master, first, second)
 
 
 def input_step(grad, pieces, earlier, begun=None):
@@ -456,21 +490,15 @@
     gain_second,
 ):
     shard = lax.axis_index("dp")
-    s = (shard & 1).astype(jnp.int32)[None]
     hidden = hidden_in[0]
     turned = weight[0].T
     other = moved(hidden, to_core)
-    groups = [[(0, 0)], [(0, 1), (2, 0)], [(2, 1), (1, 1)]]
-    cut_0, cut_1, cut_2 = cut_weight(turned, groups)
-    here = moved(cut_0, to_before_near)
+    groups = [[(0, 0), (0, 1)], [(2, 0), (2, 1)]]
+    cut_1, cut_2 = cut_weight(turned, groups)
+    rest_1 = moved(cut_1, to_before_near)
     rope = rope_step(rope_cot[0])
-    grad = latent_step(hidden, turned, latent_cot[0], gain, rope, cut_0)
-    grad = after(grad, here, mib=62)
+    grad = latent_step(hidden, turned, latent_cot[0], gain, rope, cut_1)
     grad_other = moved(grad, to_core)
-    grad_next = moved(grad, to_before)
-    rest_1 = moved(cut_1, to_before_near)
-    rest_2 = moved(cut_2, to_before_near)
-    above, below = moved(here, to_z(-1)), moved(here, to_z(1))
 
     def both(value, *blocks):
         return value, moved(value, to_core), blocks
@@ -483,26 +511,30 @@
         return lax.all_to_all(value, "dp", 0, 0, axis_index_groups=along_z, tiled=True)
 
     ra = exchanged(send_a)
-    rb = moved(after(send_b, above, below, grad_next, mib=62), to_ylo)
-    pieces = both(here, (0, 0)), both(above, (1, 0)), both(rest_1, (0, 1), (2, 0))
-    received, is_begun = input_step(grad_next, pieces, [])
+    rb = moved(after(send_b, rest_1, mib=62), to_ylo)
+    rest_2 = moved(after(cut_2, own_a, mib=62), to_before_near)
+    piece_2 = both(rest_2, *groups[1])
     send_b = (own_b + rb.astype(F32)).astype(BF)
+    grad_next = moved(after(grad, send_b, mib=62), to_before)
     rz = exchanged(send_b)
-    ra = after(ra, is_begun)
     send_a = received_sum(own_a[1], ra[:, 1], z).astype(BF)
-    ry = moved(send_a, to_ylo)
-    below = after(below, send_b)
-    side = moved(below, to_ylo)
+    ry = after(moved(send_a, to_ylo), grad_next, piece_2[1])
     total_a = received_sum(own_a[0], ra[:, 0], z) + ry.astype(F32)
     keep_b = lax.dynamic_index_in_dim(own_b, z, 0, False)
     keep_b += lax.dynamic_index_in_dim(rb, z, 0, False).astype(F32)
-    total_b = received_sum(keep_b, after(rz, rest_2), z)
+    total_b = received_sum(keep_b, rz, z)
     send = jnp.concatenate([total_a, total_b], axis=0).astype(BF)
     far = moved(send, to_mirror)
-    pieces = both(below, (3, 0)), both(side, (3, 1)), both(rest_2, (2, 1), (1, 1))
-    received, _ = input_step(grad_next, pieces, [send], received)
+    here = after(rest_1, send_a, mib=62)
+    above, below = moved(here, to_z(-1)), moved(here, to_z(1))
+    pieces = [both(here, *groups[0]), piece_2]
+    received, is_begun = input_step(grad_next, pieces, [send])
+    above = after(above, is_begun, far, mib=62)
+    below = after(below, is_begun, far, mib=62)
+    pieces = [both(above, (1, 0), (1, 1)), both(below, (3, 0), (3, 1))]
+    received, _ = input_step(grad_next, pieces, [], received)
     next_master, next_first, next_second, gain_rows = adam_step(
-        s, total_a, total_b, far, master_weight[0], first_moment[0], second_moment[0]
+        total_a, total_b, far, master_weight[0], first_moment[0], second_moment[0]
     )
     gain_total = lax.dynamic_slice(gain_rows[:4].reshape(LAT), (shard * 32,), (32,))
     next_gain = adamw(gain_master[0], gain_first[0], gain_second[0], gain_total)

time: 156 us -> 134 us (0.86)
  the two profiles are of different devices: /device:TPU:24 before, /device:TPU:1 now
where the time goes in v7:
time: 134 us; the launch traced here: 132 us
  Pallas kernels  42.1 us (31%)
  waiting for transfers between devices  39.7 us (30%)
  starting transfers between devices  32 us (24%)
  other arithmetic  12.5 us (9%)
  local copies, waits for them, and re-layouts  4.62 us (3%)
    ppermute x14, waiting for transfers between devices, moved(): return lax.ppermute(value, ('pipe', 'dp'), pairs)  39.7 us
    ppermute x14, starting transfers between devices, moved(): return lax.ppermute(value, ('pipe', 'dp'), pairs)  22.2 us
    pallas_call x2, Pallas kernels, input_step(): pl.pallas_call(kernel, in_specs=[inside] + [ANYWHERE] * halves + [LATER]...  15.7 us
    all_to_all x2, starting transfers between devices, exchanged(): lax.all_to_all(value, 'dp', 0, 0, axis_index_groups=along_z, tiled=True)  9.82 us
    pallas_call x1, Pallas kernels, weight_step(): pl.pallas_call(weight_kernel, in_specs=[ANYWHERE] * 4, out_specs=[ANYWHER...  9.75 us
    pallas_call x1, Pallas kernels, latent_step(): pl.pallas_call(latent_kernel, in_specs=[ANYWHERE, ANYWHERE, inside, insid...  9.19 us
    another operation x3, other arithmetic  5.68 us
    pallas_call x1, Pallas kernels, adam_step(): pl.pallas_call(adam_kernel, in_specs=[LATER] * 6, out_specs=[LATER] * 4,...  4.64 us
  transfers between devices with their start and end apart: 16, of which 5 were waited for; matrix products, arithmetic and copies ran while one was open for 10% of the time, Pallas kernels for 26%

profile of v7, /device:TPU:1, one launch (start us, length us, event | category | flops | bytes accessed | tf_op | source)
XLA Modules:
  0.0 132.0 jit_solution(1936014158421424017)
XLA Ops:
  0.6 1.5 %collective-permute-start = (bf16[512,7168]{1,0:T(8,128)(2,1)}, bf16[512,7168]{1,0:T(8,128)(2,1)}, u32[]{:S(2)}, u32[]{:S(2)}) collective-permute-start(bf16[512,7168]{1,0:T(8,128)(2,1)} %bitcast.86), channel_id=1, source_target_pairs={{0,1},{1,0},{2,3},{3,2},{4,5},{5,4},{6,7},{7,6},{8,9},{9,8},{10,11... | collective-permute-start | bytes 22020104 | tf_op jit(solution)/shard_map/ppermute | solution.py:43
  2.1 2.9 %cut_weight.1 = (bf16[2,288,896]{2,1,0:T(8,128)(2,1)}, bf16[2,288,896]{2,1,0:T(8,128)(2,1)}) custom-call(bf16[576,7168]{1,0:T(8,128)(2,1)} %bitcast.84), custom_call_target="tpu_custom_call" | custom-call | bytes 1000 | tf_op jit(solution)/shard_map/cut_weight/pallas_call | solution.py:125
  5.0 1.3 collective-permute-start.2
  6.4 0.3 fusion.7
  6.7 0.6 pad_maximum_fusion.1.rope
  7.3 9.2 %latent_grad.1.grad.refs_0_ = bf16[592,512]{1,0:T(8,128)(2,1)} custom-call(bf16[512,7168]{1,0:T(8,128)(2,1)} %bitcast.87, bf16[576,7168]{1,0:T(8,128)(2,1)} %bitcast.85, bf16[512,512]{1,0:T(8,128)(2,1)} %bitcast.93, f32[1,512]{1,0:T(1,128)} %gain.1, bf16[64,512]{1,0:T(8,128)(2,1)} %pad_maximum_fusion.1.rope, bf16[2,288,896]{2,1,0:T(8,128)(2,1)} %get-tuple-element.20.earlier), custom_call_target="tpu_custom_call" | custom-call | bytes 1000 | tf_op jit(solution)/shard_map/latent_grad/pallas_call | solution.py:183
  16.5 0.1 collective-permute-start.1
  16.6 2.2 %collective-permute-done.1.grad_other = bf16[592,512]{1,0:T(8,128)(2,1)S(1)} collective-permute-done((bf16[592,512]{1,0:T(8,128)(2,1)}, bf16[592,512]{1,0:T(8,128)(2,1)S(1)}, u32[]{:S(2)}, u32[]{:S(2)}) %collective-permute-start.1) | collective-permute-done | bytes 606240 | tf_op jit(solution)/shard_map/ppermute | solution.py:43
  18.9 0.0 collective-permute-done.other
  18.9 0.8 copy-done.9
  19.7 9.7 %weight_grad.1 = (f32[2,1008,128]{2,1,0:T(8,128)}, bf16[4,2,1008,128]{3,2,1,0:T(8,128)(2,1)}, f32[4,1024,128]{2,1,0:T(8,128)}, bf16[4,1024,128]{2,1,0:T(8,128)(2,1)}) custom-call(bf16[512,7168]{1,0:T(8,128)(2,1)} %bitcast.88, bf16[512,7168]{1,0:T(8,128)(2,1)} %collective-permute-done.other, bf16[592,512]{1,0:T(8,128)(2,1)} %latent_grad.1.grad.refs_0_, ...), custom_call_target="tpu_custom_call" | custom-call | bytes 1000 | tf_op jit(solution)/shard_map/weight_grad/pallas_call | solution.py:289
  29.4 5.1 %all-to-all-start = ((bf16[4,2,1008,128]{3,2,1,0:T(8,128)(2,1)}), bf16[4,2,1008,128]{3,2,1,0:T(8,128)(2,1)}, u32[]{:S(2)}, u32[]{:S(2)}) async-start(bf16[4,2,1008,128]{3,2,1,0:T(8,128)(2,1)} %get-tuple-element.24), calls=%async_computation | async-start | bytes 4128768 | tf_op jit(solution)/shard_map/all_to_all | solution.py:511
  34.6 0.0 collective-permute-done.2.refs_1_.refs_0_
  34.6 1.0 copy-done.4
  35.5 1.3 collective-permute-start.3
  36.8 1.3 collective-permute-start.7
  38.1 22.0 %collective-permute-done.3 = bf16[4,1024,128]{2,1,0:T(8,128)(2,1)S(1)} collective-permute-done((bf16[4,1024,128]{2,1,0:T(8,128)(2,1)}, bf16[4,1024,128]{2,1,0:T(8,128)(2,1)S(1)}, u32[]{:S(2)}, u32[]{:S(2)}) %collective-permute-start.3) | collective-permute-done | bytes 1048608 | tf_op jit(solution)/shard_map/ppermute | solution.py:43
  60.1 3.1 %add_convert_fusion.refs_1_ = bf16[4,1024,128]{2,1,0:T(8,128)(2,1)} fusion(f32[4,1024,128]{2,1,0:T(8,128)} %get-tuple-element.21, bf16[4,1024,128]{2,1,0:T(8,128)(2,1)S(1)} %collective-permute-done.3), kind=kLoop, calls=%fused_computation | loop fusion | flops 1572864 | bytes 4194304 | tf_op jit(solution)/shard_map/convert_element_type | solution.py:517
  63.3 0.0 all-to-all-done
  63.3 4.7 %all-to-all-start.1 = ((bf16[4,1024,128]{2,1,0:T(8,128)(2,1)}), bf16[4,1024,128]{2,1,0:T(8,128)(2,1)}, u32[]{:S(2)}, u32[]{:S(2)}) async-start(bf16[4,1024,128]{2,1,0:T(8,128)(2,1)} %add_convert_fusion.refs_1_), calls=%async_computation.1 | async-start | bytes 2097152 | tf_op jit(solution)/shard_map/all_to_all | solution.py:511
  68.0 0.0 collective-permute-done.7.rest_2_
  68.0 1.2 collective-permute-start.8
  69.2 1.3 collective-permute-start.4
  70.5 2.4 %fusion.1.refs_1_ = bf16[1008,128]{1,0:T(8,128)(2,1)} fusion(f32[2,1008,128]{2,1,0:T(8,128)} %get-tuple-element.23.refs_1_, bf16[4,2,1008,128]{3,2,1,0:T(8,128)(2,1)} %all-to-all-done, pred[]{:T(512)S(6)} %eq.11, pred[]{:T(512)S(6)} %eq.10, pred[]{:T(512)S(6)} %eq.9, pred[]{:T(512)S(6)} %eq.8), kind=kLoop, calls=%fused_computation.9 | loop fusion | flops 1677312 | bytes 1806340 | tf_op jit(solution)/shard_map/convert_element_type | solution.py:520
  72.8 1.3 collective-permute-start.9
  74.2 3.0 %collective-permute-start.5 = (bf16[2,288,896]{2,1,0:T(8,128)(2,1)}, bf16[2,288,896]{2,1,0:T(8,128)(2,1)S(1)}, u32[]{:S(2)}, u32[]{:S(2)}) collective-permute-start(bf16[2,288,896]{2,1,0:T(8,128)(2,1)} %after.9.rest_0_), channel_id=1, source_target_pairs={{0,12},{1,13},{2,14},{3,15},{4,0},{5,1},{6,2},{7,3},{8,4},{9,5},{1... | collective-permute-start | bytes 3096584 | tf_op jit(solution)/shard_map/ppermute | solution.py:43
  77.1 0.6 collective-permute-start.6
  77.7 11.3 %collective-permute-done.4.refs_1_.grad = bf16[592,512]{1,0:T(8,128)(2,1)S(1)} collective-permute-done((bf16[592,512]{1,0:T(8,128)(2,1)}, bf16[592,512]{1,0:T(8,128)(2,1)S(1)}, u32[]{:S(2)}, u32[]{:S(2)}) %collective-permute-start.4) | collective-permute-done | bytes 606240 | tf_op jit(solution)/shard_map/ppermute | solution.py:43
  89.0 1.8 %collective-permute-start.12 = (bf16[2,288,896]{2,1,0:T(8,128)(2,1)}, bf16[2,288,896]{2,1,0:T(8,128)(2,1)}, u32[]{:S(2)}, u32[]{:S(2)}) collective-permute-start(bf16[2,288,896]{2,1,0:T(8,128)(2,1)} %after.9.rest_0_), channel_id=1, source_target_pairs={{0,4},{1,5},{2,6},{3,7},{4,8},{5,9},{6,10},{7,11},{8,12},{9,13},{1... | collective-permute-start | bytes 3096584 | tf_op jit(solution)/shard_map/ppermute | solution.py:43
  90.8 0.0 all-to-all-done.1
  90.8 2.6 %fusion.17 = (bf16[1024,128]{1,0:T(8,128)(2,1)S(1)}, f32[1024,128]{1,0:T(8,128)}) fusion(bf16[4,1024,128]{2,1,0:T(8,128)(2,1)} %all-to-all-done.1, pred[]{:T(512)S(6)} %eq.11, pred[]{:T(512)S(6)} %eq.10, pred[]{:T(512)S(6)} %eq.9, pred[]{:T(512)S(6)} %eq.8, bf16[4,1024,128]{2,1,0:T(8,128)(2,1)} %copy-done.6, s32[]{:T(128)S(6)} %select_n.129, ...), kind=kLoop, calls=%fused_computation.37 | loop fusion | flops 1966080 | bytes 2621448 | tf_op jit(solution)/shard_map/convert.3
  93.4 0.5 collective-permute-done.9.refs_0_
  93.9 0.0 collective-permute-done.8.refs_2_.rest_3_
  93.9 2.8 %fusion.15 = (bf16[1008,128]{1,0:T(8,128)(2,1)S(1)}, f32[1008,128]{1,0:T(8,128)}) fusion(bf16[1008,128]{1,0:T(8,128)(2,1)S(1)} %after.11, bf16[4,2,1008,128]{3,2,1,0:T(8,128)(2,1)} %all-to-all-done, pred[]{:T(512)S(6)} %eq.11, pred[]{:T(512)S(6)} %eq.10, pred[]{:T(512)S(6)} %eq.9, pred[]{:T(512)S(6)} %eq.8, f32[2,1008,128]{2,1,0:T(8,128)S(1)} %copy-done.5), kind=kLoop, calls=%fused_computation.36 | loop fusion | flops 1935360 | bytes 2580484 | tf_op jit(solution)/shard_map/convert.2
  96.7 0.0 copy-start.10
  96.7 6.3 %collective-permute-start.10 = (bf16[2032,128]{1,0:T(8,128)(2,1)S(1)}, bf16[2032,128]{1,0:T(8,128)(2,1)S(1)}, u32[]{:S(2)}, u32[]{:S(2)}) collective-permute-start(bf16[2032,128]{1,0:T(8,128)(2,1)S(1)} %pad_maximum_fusion.rest_4_), channel_id=1, source_target_pairs={{0,112},{1,113},{2,114},{3,115},{4,116},{5,117},{6,118},{7,119},{8... | collective-permute-start | bytes 1560584 | tf_op jit(solution)/shard_map/ppermute | solution.py:43
  103.0 7.8 %input_grad.2 = (bf16[512,7168]{1,0:T(8,128)(2,1)}, f32[8,128]{1,0:T(8,128)}) custom-call(bf16[592,512]{1,0:T(8,128)(2,1)} %copy-done, bf16[2,288,896]{2,1,0:T(8,128)(2,1)} %after.9.rest_0_, bf16[2,288,896]{2,1,0:T(8,128)(2,1)} %collective-permute-done.6.rest_1_, bf16[2,288,896]{2,1,0:T(8,128)(2,1)} %collective-permute-done.7.rest_2_, ...), custom_call_target="tpu_custom_call" | custom-call | flops 2113929216 | bytes 8000000 | tf_op jit(solution)/shard_map/input_grad/pallas_call | solution.py:444
  110.9 3.7 %collective-permute-done.10.refs_2_.far = bf16[2032,128]{1,0:T(8,128)(2,1)S(1)} collective-permute-done((bf16[2032,128]{1,0:T(8,128)(2,1)S(1)}, bf16[2032,128]{1,0:T(8,128)(2,1)S(1)}, u32[]{:S(2)}, u32[]{:S(2)}) %collective-permute-start.10) | collective-permute-done | bytes 520224 | tf_op jit(solution)/shard_map/ppermute | solution.py:43
  114.6 0.8 copy-done.2
  115.3 1.3 collective-permute-start.11
  116.6 0.0 collective-permute-done.12.refs_0_
  116.6 0.1 collective-permute-start.13
  116.7 4.6 %adamw.1 = (f32[448,576]{1,0:T(8,128)}, f32[448,576]{1,0:T(8,128)}, f32[448,576]{1,0:T(8,128)}, f32[8,128]{1,0:T(8,128)}) custom-call(f32[1008,128]{1,0:T(8,128)} %get-tuple-element.37.own_a, f32[1024,128]{1,0:T(8,128)} %get-tuple-element.39.own_b, bf16[2032,128]{1,0:T(8,128)(2,1)} %copy-done.2, f32[448,576]{1,0:T(8,128)} %bitcast.90, f32[448,576]{1,0:T(8,128)} %bitcast.91, ...), custom_call_target="tpu_custom_call" | custom-call | bytes 9000000 | tf_op jit(solution)/shard_map/adamw/pallas_call | solution.py:382
  121.3 0.7 slice_bitcast_fusion
  122.0 0.6 fusion.13
  122.7 1.0 copy-done.7
  123.6 0.4 copy-done.8
  124.0 7.8 %input_grad.3 = (bf16[512,7168]{1,0:T(8,128)(2,1)}, f32[8,128]{1,0:T(8,128)}) custom-call(bf16[592,512]{1,0:T(8,128)(2,1)} %copy-done, bf16[2,288,896]{2,1,0:T(8,128)(2,1)} %after.12.rest_0_, bf16[2,288,896]{2,1,0:T(8,128)(2,1)} %copy-done.7, bf16[2,288,896]{2,1,0:T(8,128)(2,1)} %after.13.rest_2_, ...), custom_call_target="tpu_custom_call", output_to_operand_aliasing={{0}: (5, {})} | custom-call | flops 2113929216 | bytes 8000000 | tf_op jit(solution)/shard_map/input_grad/pallas_call | solution.py:444
  (39 shorter events, 0.1 us)
Async XLA Ops:
  0.6 18.2 %collective-permute-start = (bf16[512,7168]{1,0:T(8,128)(2,1)}, bf16[512,7168]{1,0:T(8,128)(2,1)}, u32[]{:S(2)}, u32[]{:S(2)}) collective-permute-start(bf16[512,7168]{1,0:T(8,128)(2,1)} %bitcast.86), channel_id=1, source_target_pairs={{0,1},{1,0},{2,3},{3,2},{4,5},{5,4},{6,7},{7,6},{8,9},{9,8},{10,11... | collective-permute-start | bytes 22020104 | tf_op jit(solution)/shard_map/ppermute | solution.py:43
  2.1 4.2 %copy-start.11 = (bf16[1,512,64]{1,2,0:T(8,128)(2,1)S(1)}, bf16[1,512,64]{1,2,0:T(8,128)(2,1)}, u32[]{:S(2)}) copy-start(bf16[1,512,64]{1,2,0:T(8,128)(2,1)} %param.15) | copy-start | bytes 196612
  5.0 29.5 %collective-permute-start.2 = (bf16[2,288,896]{2,1,0:T(8,128)(2,1)}, bf16[2,288,896]{2,1,0:T(8,128)(2,1)S(1)}, u32[]{:S(2)}, u32[]{:S(2)}) collective-permute-start(bf16[2,288,896]{2,1,0:T(8,128)(2,1)} %get-tuple-element.20.earlier), channel_id=1, source_target_pairs={{16,2},{17,3},{18,0},{19,1},{20,6},{21,7},{22,4},{23,5},{24,10},{2... | collective-permute-start | bytes 3096584 | tf_op jit(solution)/shard_map/ppermute | solution.py:43
  16.5 2.3 %collective-permute-start.1 = (bf16[592,512]{1,0:T(8,128)(2,1)}, bf16[592,512]{1,0:T(8,128)(2,1)S(1)}, u32[]{:S(2)}, u32[]{:S(2)}) collective-permute-start(bf16[592,512]{1,0:T(8,128)(2,1)} %latent_grad.1.grad.refs_0_), channel_id=1, source_target_pairs={{0,1},{1,0},{2,3},{3,2},{4,5},{5,4},{6,7},{7,6},{8,9},{9,8},{10,11... | collective-permute-start | bytes 1818632 | tf_op jit(solution)/shard_map/ppermute | solution.py:43
  18.8 0.8 copy-start.9
  29.4 33.8 %all-to-all-start = ((bf16[4,2,1008,128]{3,2,1,0:T(8,128)(2,1)}), bf16[4,2,1008,128]{3,2,1,0:T(8,128)(2,1)}, u32[]{:S(2)}, u32[]{:S(2)}) async-start(bf16[4,2,1008,128]{3,2,1,0:T(8,128)(2,1)} %get-tuple-element.24), calls=%async_computation | async-start | bytes 4128768 | tf_op jit(solution)/shard_map/all_to_all | solution.py:511
  34.6 1.0 copy-start.4
  35.5 24.6 %collective-permute-start.3 = (bf16[4,1024,128]{2,1,0:T(8,128)(2,1)}, bf16[4,1024,128]{2,1,0:T(8,128)(2,1)S(1)}, u32[]{:S(2)}, u32[]{:S(2)}) collective-permute-start(bf16[4,1024,128]{2,1,0:T(8,128)(2,1)} %after.7), channel_id=1, source_target_pairs={{0,2},{1,3},{2,0},{3,1},{4,6},{5,7},{6,4},{7,5},{8,10},{9,11},{10,... | collective-permute-start | bytes 3145736 | tf_op jit(solution)/shard_map/ppermute | solution.py:43
  36.8 31.2 %collective-permute-start.7 = (bf16[2,288,896]{2,1,0:T(8,128)(2,1)}, bf16[2,288,896]{2,1,0:T(8,128)(2,1)}, u32[]{:S(2)}, u32[]{:S(2)}) collective-permute-start(bf16[2,288,896]{2,1,0:T(8,128)(2,1)} %after.10), channel_id=1, source_target_pairs={{16,2},{17,3},{18,0},{19,1},{20,6},{21,7},{22,4},{23,5},{24,10},{2... | collective-permute-start | bytes 3096584 | tf_op jit(solution)/shard_map/ppermute | solution.py:43
  60.1 3.1 %copy-start.6 = (bf16[4,1024,128]{2,1,0:T(8,128)(2,1)}, bf16[4,1024,128]{2,1,0:T(8,128)(2,1)S(1)}, u32[]{:S(2)}) copy-start(bf16[4,1024,128]{2,1,0:T(8,128)(2,1)S(1)} %collective-permute-done.3) | copy-start | bytes 3145732
  63.3 27.5 %all-to-all-start.1 = ((bf16[4,1024,128]{2,1,0:T(8,128)(2,1)}), bf16[4,1024,128]{2,1,0:T(8,128)(2,1)}, u32[]{:S(2)}, u32[]{:S(2)}) async-start(bf16[4,1024,128]{2,1,0:T(8,128)(2,1)} %add_convert_fusion.refs_1_), calls=%async_computation.1 | async-start | bytes 2097152 | tf_op jit(solution)/shard_map/all_to_all | solution.py:511
  68.0 25.9 %collective-permute-start.8 = (bf16[2,288,896]{2,1,0:T(8,128)(2,1)}, bf16[2,288,896]{2,1,0:T(8,128)(2,1)S(1)}, u32[]{:S(2)}, u32[]{:S(2)}) collective-permute-start(bf16[2,288,896]{2,1,0:T(8,128)(2,1)} %collective-permute-done.7.rest_2_), channel_id=1, source_target_pairs={{0,1},{1,0},{2,3},{3,2},{4,5},{5,4},{6,7},{7,6},{8,9},{9,8},{10,11... | collective-permute-start | bytes 3096584 | tf_op jit(solution)/shard_map/ppermute | solution.py:43
  69.2 19.8 %collective-permute-start.4 = (bf16[592,512]{1,0:T(8,128)(2,1)}, bf16[592,512]{1,0:T(8,128)(2,1)S(1)}, u32[]{:S(2)}, u32[]{:S(2)}) collective-permute-start(bf16[592,512]{1,0:T(8,128)(2,1)} %after.8), channel_id=1, source_target_pairs={{16,0},{17,1},{18,2},{19,3},{20,4},{21,5},{22,6},{23,7},{24,8},{25... | collective-permute-start | bytes 1818632 | tf_op jit(solution)/shard_map/ppermute | solution.py:43
  72.8 21.0 %collective-permute-start.9 = (bf16[1008,128]{1,0:T(8,128)(2,1)}, bf16[1008,128]{1,0:T(8,128)(2,1)S(1)}, u32[]{:S(2)}, u32[]{:S(2)}) collective-permute-start(bf16[1008,128]{1,0:T(8,128)(2,1)} %fusion.1.refs_1_), channel_id=1, source_target_pairs={{0,2},{1,3},{2,0},{3,1},{4,6},{5,7},{6,4},{7,5},{8,10},{9,11},{10,... | collective-permute-start | bytes 774152 | tf_op jit(solution)/shard_map/ppermute | solution.py:43
  74.2 36.7 %collective-permute-start.5 = (bf16[2,288,896]{2,1,0:T(8,128)(2,1)}, bf16[2,288,896]{2,1,0:T(8,128)(2,1)S(1)}, u32[]{:S(2)}, u32[]{:S(2)}) collective-permute-start(bf16[2,288,896]{2,1,0:T(8,128)(2,1)} %after.9.rest_0_), channel_id=1, source_target_pairs={{0,12},{1,13},{2,14},{3,15},{4,0},{5,1},{6,2},{7,3},{8,4},{9,5},{1... | collective-permute-start | bytes 3096584 | tf_op jit(solution)/shard_map/ppermute | solution.py:43
  77.1 25.9 %collective-permute-start.6 = (bf16[2,288,896]{2,1,0:T(8,128)(2,1)}, bf16[2,288,896]{2,1,0:T(8,128)(2,1)}, u32[]{:S(2)}, u32[]{:S(2)}) collective-permute-start(bf16[2,288,896]{2,1,0:T(8,128)(2,1)} %after.9.rest_0_), channel_id=1, source_target_pairs={{0,1},{1,0},{2,3},{3,2},{4,5},{5,4},{6,7},{7,6},{8,9},{9,8},{10,11... | collective-permute-start | bytes 3096584 | tf_op jit(solution)/shard_map/ppermute | solution.py:43
  89.0 4.9 %copy-start = (bf16[592,512]{1,0:T(8,128)(2,1)}, bf16[592,512]{1,0:T(8,128)(2,1)S(1)}, u32[]{:S(2)}) copy-start(bf16[592,512]{1,0:T(8,128)(2,1)S(1)} %collective-permute-done.4.refs_1_.grad) | copy-start | bytes 1818628
  89.0 27.6 %collective-permute-start.12 = (bf16[2,288,896]{2,1,0:T(8,128)(2,1)}, bf16[2,288,896]{2,1,0:T(8,128)(2,1)}, u32[]{:S(2)}, u32[]{:S(2)}) collective-permute-start(bf16[2,288,896]{2,1,0:T(8,128)(2,1)} %after.9.rest_0_), channel_id=1, source_target_pairs={{0,4},{1,5},{2,6},{3,7},{4,8},{5,9},{6,10},{7,11},{8,12},{9,13},{1... | collective-permute-start | bytes 3096584 | tf_op jit(solution)/shard_map/ppermute | solution.py:43
  90.8 3.1 %copy-start.5 = (f32[2,1008,128]{2,1,0:T(8,128)S(1)}, f32[2,1008,128]{2,1,0:T(8,128)}, u32[]{:S(2)}) copy-start(f32[2,1008,128]{2,1,0:T(8,128)} %get-tuple-element.23.refs_1_) | copy-start | bytes 3096580
  93.9 2.8 %copy-start.1 = (bf16[2,288,896]{2,1,0:T(8,128)(2,1)}, bf16[2,288,896]{2,1,0:T(8,128)(2,1)S(1)}, u32[]{:S(2)}) copy-start(bf16[2,288,896]{2,1,0:T(8,128)(2,1)S(1)} %collective-permute-done.8.refs_2_.rest_3_) | copy-start | bytes 3096580
  96.7 6.3 %copy-start.10 = (bf16[2032,128]{1,0:T(8,128)(2,1)}, bf16[2032,128]{1,0:T(8,128)(2,1)S(1)}, u32[]{:S(2)}) copy-start(bf16[2032,128]{1,0:T(8,128)(2,1)S(1)} %pad_maximum_fusion.rest_4_) | copy-start | bytes 1560580
  96.7 17.9 %collective-permute-start.10 = (bf16[2032,128]{1,0:T(8,128)(2,1)S(1)}, bf16[2032,128]{1,0:T(8,128)(2,1)S(1)}, u32[]{:S(2)}, u32[]{:S(2)}) collective-permute-start(bf16[2032,128]{1,0:T(8,128)(2,1)S(1)} %pad_maximum_fusion.rest_4_), channel_id=1, source_target_pairs={{0,112},{1,113},{2,114},{3,115},{4,116},{5,117},{6,118},{7,119},{8... | collective-permute-start | bytes 1560584 | tf_op jit(solution)/shard_map/ppermute | solution.py:43
  110.9 3.7 %copy-start.3 = (bf16[2,288,896]{2,1,0:T(8,128)(2,1)}, bf16[2,288,896]{2,1,0:T(8,128)(2,1)S(1)}, u32[]{:S(2)}) copy-start(bf16[2,288,896]{2,1,0:T(8,128)(2,1)S(1)} %collective-permute-done.5.refs_0_) | copy-start | bytes 3096580
  114.6 0.8 copy-start.2
  115.3 7.3 %collective-permute-start.11 = (bf16[2,288,896]{2,1,0:T(8,128)(2,1)}, bf16[2,288,896]{2,1,0:T(8,128)(2,1)S(1)}, u32[]{:S(2)}, u32[]{:S(2)}) collective-permute-start(bf16[2,288,896]{2,1,0:T(8,128)(2,1)} %after.12.rest_0_), channel_id=1, source_target_pairs={{0,1},{1,0},{2,3},{3,2},{4,5},{5,4},{6,7},{7,6},{8,9},{9,8},{10,11... | collective-permute-start | bytes 3096584 | tf_op jit(solution)/shard_map/ppermute | solution.py:43
  116.6 6.0 %collective-permute-start.13 = (bf16[2,288,896]{2,1,0:T(8,128)(2,1)}, bf16[2,288,896]{2,1,0:T(8,128)(2,1)S(1)}, u32[]{:S(2)}, u32[]{:S(2)}) collective-permute-start(bf16[2,288,896]{2,1,0:T(8,128)(2,1)} %after.13.rest_2_), channel_id=1, source_target_pairs={{0,1},{1,0},{2,3},{3,2},{4,5},{5,4},{6,7},{7,6},{8,9},{9,8},{10,11... | collective-permute-start | bytes 3096584 | tf_op jit(solution)/shard_map/ppermute | solution.py:43
  116.7 5.3 %copy-start.12 = (f32[1,32]{1,0:T(1,128)S(1)}, f32[1,32]{1,0:T(1,128)}, u32[]{:S(2)}) copy-start(f32[1,32]{1,0:T(1,128)} %param.19) | copy-start | bytes 388
  116.7 5.3 %copy-start.13 = (f32[1,32]{1,0:T(1,128)S(1)}, f32[1,32]{1,0:T(1,128)}, u32[]{:S(2)}) copy-start(f32[1,32]{1,0:T(1,128)} %param.20) | copy-start | bytes 388
  116.7 5.3 %copy-start.14 = (f32[1,32]{1,0:T(1,128)S(1)}, f32[1,32]{1,0:T(1,128)}, u32[]{:S(2)}) copy-start(f32[1,32]{1,0:T(1,128)} %param.21) | copy-start | bytes 388
  122.7 1.0 copy-start.7
  122.7 1.3 %copy-start.8 = (bf16[2,288,896]{2,1,0:T(8,128)(2,1)}, bf16[2,288,896]{2,1,0:T(8,128)(2,1)S(1)}, u32[]{:S(2)}) copy-start(bf16[2,288,896]{2,1,0:T(8,128)(2,1)S(1)} %collective-permute-done.13.rest_3_) | copy-start | bytes 3096580

commit v8 on v7

--- a/solution.py
+++ b/solution.py
@@ -515,10 +515,11 @@
     rest_2 = moved(after(cut_2, own_a, mib=62), to_before_near)
     piece_2 = both(rest_2, *groups[1])
     send_b = (own_b + rb.astype(F32)).astype(BF)
-    grad_next = moved(after(grad, send_b, mib=62), to_before)
+    grad_next = moved(after(grad, rb, mib=1), to_before)
     rz = exchanged(send_b)
+    ra = after(ra, grad_next)
     send_a = received_sum(own_a[1], ra[:, 1], z).astype(BF)
-    ry = after(moved(send_a, to_ylo), grad_next, piece_2[1])
+    ry = moved(send_a, to_ylo)
     total_a = received_sum(own_a[0], ra[:, 0], z) + ry.astype(F32)
     keep_b = lax.dynamic_index_in_dim(own_b, z, 0, False)
     keep_b += lax.dynamic_index_in_dim(rb, z, 0, False).astype(F32)

time: 134 us -> 132 us (0.985)
  other arithmetic: 12.5 us -> 9.23 us
  waiting for transfers between devices: 39.7 us -> 42 us
  starting transfers between devices: 32 us -> 30.1 us
    ppermute x14, waiting for transfers between devices: 39.7 us -> 42 us  [moved(): return lax.ppermute(value, ('pipe', 'dp'), pairs)]
    ppermute x14, starting transfers between devices: 22.2 us -> 20.2 us  [moved(): return lax.ppermute(value, ('pipe', 'dp'), pairs)]
    convert_element_type x1, other arithmetic: 3.14 us -> 1.23 us  [on_device(): send_b = (own_b + rb.astype(F32)).astype(BF)]
    unnamed x30 -> x32, local copies, waits for them, and re-layouts: 3.95 us -> 4.59 us
  transfers between devices with their start and end apart: 16 -> 16, of which waited for: 5 -> 6; matrix products, arithmetic and copies ran while one was open for 10% -> 8% of each run, Pallas kernels for 26% -> 26%
where the time goes in v8:
time: 132 us; the launch traced here: 130 us
  Pallas kernels  42.1 us (32%)
  waiting for transfers between devices  42 us (32%)
  starting transfers between devices  30.1 us (23%)
  other arithmetic  9.23 us (7%)
  local copies, waits for them, and re-layouts  5.28 us (4%)
    ppermute x14, waiting for transfers between devices, moved(): return lax.ppermute(value, ('pipe', 'dp'), pairs)  42 us
    ppermute x14, starting transfers between devices, moved(): return lax.ppermute(value, ('pipe', 'dp'), pairs)  20.2 us
    pallas_call x2, Pallas kernels, input_step(): pl.pallas_call(kernel, in_specs=[inside] + [ANYWHERE] * halves + [LATER]...  15.7 us
    all_to_all x2, starting transfers between devices, exchanged(): lax.all_to_all(value, 'dp', 0, 0, axis_index_groups=along_z, tiled=True)  9.85 us
    pallas_call x1, Pallas kernels, weight_step(): pl.pallas_call(weight_kernel, in_specs=[ANYWHERE] * 4, out_specs=[ANYWHER...  9.75 us
    pallas_call x1, Pallas kernels, latent_step(): pl.pallas_call(latent_kernel, in_specs=[ANYWHERE, ANYWHERE, inside, insid...  9.19 us
    another operation x3, other arithmetic  5.14 us
    pallas_call x1, Pallas kernels, adam_step(): pl.pallas_call(adam_kernel, in_specs=[LATER] * 6, out_specs=[LATER] * 4,...  4.64 us
  transfers between devices with their start and end apart: 16, of which 6 were waited for; matrix products, arithmetic and copies ran while one was open for 8% of the time, Pallas kernels for 26%

profile of v8, /device:TPU:1, one launch (start us, length us, event | category | flops | bytes accessed | tf_op | source)
XLA Modules:
  0.0 129.6 jit_solution(11300477986579670545)
XLA Ops:
  0.6 1.5 %collective-permute-start = (bf16[512,7168]{1,0:T(8,128)(2,1)}, bf16[512,7168]{1,0:T(8,128)(2,1)}, u32[]{:S(2)}, u32[]{:S(2)}) collective-permute-start(bf16[512,7168]{1,0:T(8,128)(2,1)} %bitcast.86), channel_id=1, source_target_pairs={{0,1},{1,0},{2,3},{3,2},{4,5},{5,4},{6,7},{7,6},{8,9},{9,8},{10,11... | collective-permute-start | bytes 22020104 | tf_op jit(solution)/shard_map/ppermute | solution.py:43
  2.1 2.9 %cut_weight.1 = (bf16[2,288,896]{2,1,0:T(8,128)(2,1)}, bf16[2,288,896]{2,1,0:T(8,128)(2,1)}) custom-call(bf16[576,7168]{1,0:T(8,128)(2,1)} %bitcast.84), custom_call_target="tpu_custom_call" | custom-call | bytes 1000 | tf_op jit(solution)/shard_map/cut_weight/pallas_call | solution.py:125
  5.0 1.3 collective-permute-start.2
  6.4 0.3 fusion.7
  6.7 0.6 pad_maximum_fusion.1.rope
  7.3 9.2 %latent_grad.1.grad.refs_0_ = bf16[592,512]{1,0:T(8,128)(2,1)} custom-call(bf16[512,7168]{1,0:T(8,128)(2,1)} %bitcast.87, bf16[576,7168]{1,0:T(8,128)(2,1)} %bitcast.85, bf16[512,512]{1,0:T(8,128)(2,1)} %bitcast.93, f32[1,512]{1,0:T(1,128)} %gain.1, bf16[64,512]{1,0:T(8,128)(2,1)} %pad_maximum_fusion.1.rope, bf16[2,288,896]{2,1,0:T(8,128)(2,1)} %get-tuple-element.20.earlier), custom_call_target="tpu_custom_call" | custom-call | bytes 1000 | tf_op jit(solution)/shard_map/latent_grad/pallas_call | solution.py:183
  16.5 0.1 collective-permute-start.1
  16.6 2.2 %collective-permute-done.1.grad_other = bf16[592,512]{1,0:T(8,128)(2,1)S(1)} collective-permute-done((bf16[592,512]{1,0:T(8,128)(2,1)}, bf16[592,512]{1,0:T(8,128)(2,1)S(1)}, u32[]{:S(2)}, u32[]{:S(2)}) %collective-permute-start.1) | collective-permute-done | bytes 606240 | tf_op jit(solution)/shard_map/ppermute | solution.py:43
  18.9 0.8 copy-done.10
  19.7 9.7 %weight_grad.1 = (f32[2,1008,128]{2,1,0:T(8,128)}, bf16[4,2,1008,128]{3,2,1,0:T(8,128)(2,1)}, f32[4,1024,128]{2,1,0:T(8,128)}, bf16[4,1024,128]{2,1,0:T(8,128)(2,1)}) custom-call(bf16[512,7168]{1,0:T(8,128)(2,1)} %bitcast.88, bf16[512,7168]{1,0:T(8,128)(2,1)} %collective-permute-done.other, bf16[592,512]{1,0:T(8,128)(2,1)} %latent_grad.1.grad.refs_0_, ...), custom_call_target="tpu_custom_call" | custom-call | bytes 1000 | tf_op jit(solution)/shard_map/weight_grad/pallas_call | solution.py:289
  29.4 5.1 %all-to-all-start = ((bf16[4,2,1008,128]{3,2,1,0:T(8,128)(2,1)}), bf16[4,2,1008,128]{3,2,1,0:T(8,128)(2,1)}, u32[]{:S(2)}, u32[]{:S(2)}) async-start(bf16[4,2,1008,128]{3,2,1,0:T(8,128)(2,1)} %get-tuple-element.23), calls=%async_computation | async-start | bytes 4128768 | tf_op jit(solution)/shard_map/all_to_all | solution.py:511
  34.5 1.0 copy-done.3
  35.5 1.3 %collective-permute-start.3 = (bf16[4,1024,128]{2,1,0:T(8,128)(2,1)}, bf16[4,1024,128]{2,1,0:T(8,128)(2,1)S(1)}, u32[]{:S(2)}, u32[]{:S(2)}) collective-permute-start(bf16[4,1024,128]{2,1,0:T(8,128)(2,1)} %after.7), channel_id=1, source_target_pairs={{0,2},{1,3},{2,0},{3,1},{4,6},{5,7},{6,4},{7,5},{8,10},{9,11},{10,... | collective-permute-start | bytes 3145736 | tf_op jit(solution)/shard_map/ppermute | solution.py:43
  36.8 1.4 %collective-permute-start.7 = (bf16[2,288,896]{2,1,0:T(8,128)(2,1)}, bf16[2,288,896]{2,1,0:T(8,128)(2,1)}, u32[]{:S(2)}, u32[]{:S(2)}) collective-permute-start(bf16[2,288,896]{2,1,0:T(8,128)(2,1)} %after.11), channel_id=1, source_target_pairs={{16,2},{17,3},{18,0},{19,1},{20,6},{21,7},{22,4},{23,5},{24,10},{2... | collective-permute-start | bytes 3096584 | tf_op jit(solution)/shard_map/ppermute | solution.py:43
  38.2 21.9 %collective-permute-done.3.refs_1_ = bf16[4,1024,128]{2,1,0:T(8,128)(2,1)S(1)} collective-permute-done((bf16[4,1024,128]{2,1,0:T(8,128)(2,1)}, bf16[4,1024,128]{2,1,0:T(8,128)(2,1)S(1)}, u32[]{:S(2)}, u32[]{:S(2)}) %collective-permute-start.3) | collective-permute-done | bytes 1048608 | tf_op jit(solution)/shard_map/ppermute | solution.py:43
  60.1 1.3 collective-permute-start.4
  61.4 1.2 add_convert_fusion
  62.7 0.0 all-to-all-done.refs_0_
  62.7 4.7 %all-to-all-start.1 = ((bf16[4,1024,128]{2,1,0:T(8,128)(2,1)}), bf16[4,1024,128]{2,1,0:T(8,128)(2,1)}, u32[]{:S(2)}, u32[]{:S(2)}) async-start(bf16[4,1024,128]{2,1,0:T(8,128)(2,1)} %add_convert_fusion), calls=%async_computation.1 | async-start | bytes 2097152 | tf_op jit(solution)/shard_map/all_to_all | solution.py:511
  67.4 10.7 %collective-permute-done.4.refs_1_.grad = bf16[592,512]{1,0:T(8,128)(2,1)S(1)} collective-permute-done((bf16[592,512]{1,0:T(8,128)(2,1)S(1)}, bf16[592,512]{1,0:T(8,128)(2,1)S(1)}, u32[]{:S(2)}, u32[]{:S(2)}) %collective-permute-start.4) | collective-permute-done | bytes 606240 | tf_op jit(solution)/shard_map/ppermute | solution.py:43
  78.2 0.9 copy-done.1
  79.0 1.6 %fusion.1.refs_1_ = bf16[1008,128]{1,0:T(8,128)(2,1)S(1)} fusion(f32[2,1008,128]{2,1,0:T(8,128)S(1)} %copy-done.4, bf16[4,2,1008,128]{3,2,1,0:T(8,128)(2,1)} %after.9, pred[]{:T(512)S(6)} %eq.11, pred[]{:T(512)S(6)} %eq.10, pred[]{:T(512)S(6)} %eq.9, pred[]{:T(512)S(6)} %eq.8), kind=kLoop, calls=%fused_computation.9 | loop fusion | flops 1677312 | bytes 1806340 | tf_op jit(solution)/shard_map/convert_element_type | solution.py:521
  80.6 0.9 collective-permute-start.9
  81.5 2.3 %collective-permute-start.8 = (bf16[2,288,896]{2,1,0:T(8,128)(2,1)}, bf16[2,288,896]{2,1,0:T(8,128)(2,1)}, u32[]{:S(2)}, u32[]{:S(2)}) collective-permute-start(bf16[2,288,896]{2,1,0:T(8,128)(2,1)} %collective-permute-done.7.rest_2_), channel_id=1, source_target_pairs={{0,1},{1,0},{2,3},{3,2},{4,5},{5,4},{6,7},{7,6},{8,9},{9,8},{10,11... | collective-permute-start | bytes 3096584 | tf_op jit(solution)/shard_map/ppermute | solution.py:43
  83.7 3.5 %collective-permute-start.5 = (bf16[2,288,896]{2,1,0:T(8,128)(2,1)}, bf16[2,288,896]{2,1,0:T(8,128)(2,1)}, u32[]{:S(2)}, u32[]{:S(2)}) collective-permute-start(bf16[2,288,896]{2,1,0:T(8,128)(2,1)} %after.10.rest_0_), channel_id=1, source_target_pairs={{0,12},{1,13},{2,14},{3,15},{4,0},{5,1},{6,2},{7,3},{8,4},{9,5},{1... | collective-permute-start | bytes 3096584 | tf_op jit(solution)/shard_map/ppermute | solution.py:43
  87.2 0.4 collective-permute-start.6
  87.6 0.0 collective-permute-start.12
  87.6 0.0 all-to-all-done.1
  87.6 2.4 %fusion.17 = (bf16[1024,128]{1,0:T(8,128)(2,1)S(1)}, f32[1024,128]{1,0:T(8,128)}) fusion(bf16[4,1024,128]{2,1,0:T(8,128)(2,1)} %all-to-all-done.1, pred[]{:T(512)S(6)} %eq.11, pred[]{:T(512)S(6)} %eq.10, pred[]{:T(512)S(6)} %eq.9, pred[]{:T(512)S(6)} %eq.8, bf16[4,1024,128]{2,1,0:T(8,128)(2,1)S(1)} %collective-permute-done.3.refs_1_, s32[]{:T(128)S(6)} %select_n.129, ...), kind=kLoop, calls=%fused_computation.37 | loop fusion | flops 1966080 | bytes 2621448 | tf_op jit(solution)/shard_map/convert.3
  90.0 0.0 collective-permute-done.9
  90.0 2.4 %fusion.15 = (bf16[1008,128]{1,0:T(8,128)(2,1)S(1)}, f32[1008,128]{1,0:T(8,128)}) fusion(bf16[1008,128]{1,0:T(8,128)(2,1)S(1)} %collective-permute-done.9, bf16[4,2,1008,128]{3,2,1,0:T(8,128)(2,1)} %after.9, pred[]{:T(512)S(6)} %eq.11, pred[]{:T(512)S(6)} %eq.10, pred[]{:T(512)S(6)} %eq.9, pred[]{:T(512)S(6)} %eq.8, f32[2,1008,128]{2,1,0:T(8,128)S(1)} %copy-done.5), kind=kLoop, calls=%fused_computation.36 | loop fusion | flops 1935360 | bytes 2580484 | tf_op jit(solution)/shard_map/convert.2
  92.5 0.0 copy-start.11
  92.5 4.4 %collective-permute-start.10 = (bf16[2032,128]{1,0:T(8,128)(2,1)S(1)}, bf16[2032,128]{1,0:T(8,128)(2,1)S(1)}, u32[]{:S(2)}, u32[]{:S(2)}) collective-permute-start(bf16[2032,128]{1,0:T(8,128)(2,1)S(1)} %pad_maximum_fusion.rest_4_), channel_id=1, source_target_pairs={{0,112},{1,113},{2,114},{3,115},{4,116},{5,117},{6,118},{7,119},{8... | collective-permute-start | bytes 1560584 | tf_op jit(solution)/shard_map/ppermute | solution.py:43
  96.9 0.0 collective-permute-done.8.rest_3_
  96.9 0.0 collective-permute-done.6.rest_1_
  96.9 7.8 %input_grad.2 = (bf16[512,7168]{1,0:T(8,128)(2,1)}, f32[8,128]{1,0:T(8,128)}) custom-call(bf16[592,512]{1,0:T(8,128)(2,1)} %copy-done.1, bf16[2,288,896]{2,1,0:T(8,128)(2,1)} %after.10.rest_0_, bf16[2,288,896]{2,1,0:T(8,128)(2,1)} %collective-permute-done.6.rest_1_, bf16[2,288,896]{2,1,0:T(8,128)(2,1)} %collective-permute-done.7.rest_2_, ...), custom_call_target="tpu_custom_call" | custom-call | flops 2113929216 | bytes 8000000 | tf_op jit(solution)/shard_map/input_grad/pallas_call | solution.py:444
  104.7 4.7 %collective-permute-done.10.refs_2_.far = bf16[2032,128]{1,0:T(8,128)(2,1)S(1)} collective-permute-done((bf16[2032,128]{1,0:T(8,128)(2,1)S(1)}, bf16[2032,128]{1,0:T(8,128)(2,1)S(1)}, u32[]{:S(2)}, u32[]{:S(2)}) %collective-permute-start.10) | collective-permute-done | bytes 520224 | tf_op jit(solution)/shard_map/ppermute | solution.py:43
  109.4 0.2 collective-permute-done.5.refs_0_
  109.7 0.5 copy-done.2
  110.2 1.0 collective-permute-start.11
  111.2 2.1 %collective-permute-done.12.refs_0_ = bf16[2,288,896]{2,1,0:T(8,128)(2,1)} collective-permute-done((bf16[2,288,896]{2,1,0:T(8,128)(2,1)}, bf16[2,288,896]{2,1,0:T(8,128)(2,1)}, u32[]{:S(2)}, u32[]{:S(2)}) %collective-permute-start.12) | collective-permute-done | bytes 1032224 | tf_op jit(solution)/shard_map/ppermute | solution.py:43
  113.4 1.0 collective-permute-start.13
  114.3 4.6 %adamw.1 = (f32[448,576]{1,0:T(8,128)}, f32[448,576]{1,0:T(8,128)}, f32[448,576]{1,0:T(8,128)}, f32[8,128]{1,0:T(8,128)}) custom-call(f32[1008,128]{1,0:T(8,128)} %get-tuple-element.37.own_a, f32[1024,128]{1,0:T(8,128)} %get-tuple-element.39.own_b, bf16[2032,128]{1,0:T(8,128)(2,1)} %copy-done.2, f32[448,576]{1,0:T(8,128)} %bitcast.90, f32[448,576]{1,0:T(8,128)} %bitcast.91, ...), custom_call_target="tpu_custom_call" | custom-call | bytes 9000000 | tf_op jit(solution)/shard_map/adamw/pallas_call | solution.py:382
  119.0 0.7 slice_bitcast_fusion
  119.7 0.6 fusion.13
  120.3 1.0 copy-done.7
  121.3 0.4 copy-done.8
  121.6 7.8 %input_grad.3 = (bf16[512,7168]{1,0:T(8,128)(2,1)}, f32[8,128]{1,0:T(8,128)}) custom-call(bf16[592,512]{1,0:T(8,128)(2,1)} %copy-done.1, bf16[2,288,896]{2,1,0:T(8,128)(2,1)} %after.12.rest_0_, bf16[2,288,896]{2,1,0:T(8,128)(2,1)} %copy-done.7, bf16[2,288,896]{2,1,0:T(8,128)(2,1)} %after.13.rest_2_, ...), custom_call_target="tpu_custom_call", output_to_operand_aliasing={{0}: (5, {})} | custom-call | flops 2113929216 | bytes 8000000 | tf_op jit(solution)/shard_map/input_grad/pallas_call | solution.py:444
  (41 shorter events, 0.1 us)
Async XLA Ops:
  0.6 18.2 %collective-permute-start = (bf16[512,7168]{1,0:T(8,128)(2,1)}, bf16[512,7168]{1,0:T(8,128)(2,1)}, u32[]{:S(2)}, u32[]{:S(2)}) collective-permute-start(bf16[512,7168]{1,0:T(8,128)(2,1)} %bitcast.86), channel_id=1, source_target_pairs={{0,1},{1,0},{2,3},{3,2},{4,5},{5,4},{6,7},{7,6},{8,9},{9,8},{10,11... | collective-permute-start | bytes 22020104 | tf_op jit(solution)/shard_map/ppermute | solution.py:43
  2.1 4.2 %copy-start.12 = (bf16[1,512,64]{1,2,0:T(8,128)(2,1)S(1)}, bf16[1,512,64]{1,2,0:T(8,128)(2,1)}, u32[]{:S(2)}) copy-start(bf16[1,512,64]{1,2,0:T(8,128)(2,1)} %param.15) | copy-start | bytes 196612
  5.0 29.5 %collective-permute-start.2 = (bf16[2,288,896]{2,1,0:T(8,128)(2,1)}, bf16[2,288,896]{2,1,0:T(8,128)(2,1)S(1)}, u32[]{:S(2)}, u32[]{:S(2)}) collective-permute-start(bf16[2,288,896]{2,1,0:T(8,128)(2,1)} %get-tuple-element.20.earlier), channel_id=1, source_target_pairs={{16,2},{17,3},{18,0},{19,1},{20,6},{21,7},{22,4},{23,5},{24,10},{2... | collective-permute-start | bytes 3096584 | tf_op jit(solution)/shard_map/ppermute | solution.py:43
  16.5 2.3 %collective-permute-start.1 = (bf16[592,512]{1,0:T(8,128)(2,1)}, bf16[592,512]{1,0:T(8,128)(2,1)S(1)}, u32[]{:S(2)}, u32[]{:S(2)}) collective-permute-start(bf16[592,512]{1,0:T(8,128)(2,1)} %latent_grad.1.grad.refs_0_), channel_id=1, source_target_pairs={{0,1},{1,0},{2,3},{3,2},{4,5},{5,4},{6,7},{7,6},{8,9},{9,8},{10,11... | collective-permute-start | bytes 1818632 | tf_op jit(solution)/shard_map/ppermute | solution.py:43
  18.8 0.8 copy-start.10
  29.4 33.2 %all-to-all-start = ((bf16[4,2,1008,128]{3,2,1,0:T(8,128)(2,1)}), bf16[4,2,1008,128]{3,2,1,0:T(8,128)(2,1)}, u32[]{:S(2)}, u32[]{:S(2)}) async-start(bf16[4,2,1008,128]{3,2,1,0:T(8,128)(2,1)} %get-tuple-element.23), calls=%async_computation | async-start | bytes 4128768 | tf_op jit(solution)/shard_map/all_to_all | solution.py:511
  34.5 1.0 copy-start.3
  35.5 24.6 %copy-start = (bf16[592,512]{1,0:T(8,128)(2,1)S(1)}, bf16[592,512]{1,0:T(8,128)(2,1)}, u32[]{:S(2)}) copy-start(bf16[592,512]{1,0:T(8,128)(2,1)} %latent_grad.1.grad.refs_0_) | copy-start | bytes 1818628
  35.5 24.6 %collective-permute-start.3 = (bf16[4,1024,128]{2,1,0:T(8,128)(2,1)}, bf16[4,1024,128]{2,1,0:T(8,128)(2,1)S(1)}, u32[]{:S(2)}, u32[]{:S(2)}) collective-permute-start(bf16[4,1024,128]{2,1,0:T(8,128)(2,1)} %after.7), channel_id=1, source_target_pairs={{0,2},{1,3},{2,0},{3,1},{4,6},{5,7},{6,4},{7,5},{8,10},{9,11},{10,... | collective-permute-start | bytes 3145736 | tf_op jit(solution)/shard_map/ppermute | solution.py:43
  36.8 24.6 %copy-start.6 = (f32[4,1024,128]{2,1,0:T(8,128)S(1)}, f32[4,1024,128]{2,1,0:T(8,128)}, u32[]{:S(2)}) copy-start(f32[4,1024,128]{2,1,0:T(8,128)} %get-tuple-element.25) | copy-start | bytes 6291460
  36.8 44.6 %collective-permute-start.7 = (bf16[2,288,896]{2,1,0:T(8,128)(2,1)}, bf16[2,288,896]{2,1,0:T(8,128)(2,1)}, u32[]{:S(2)}, u32[]{:S(2)}) collective-permute-start(bf16[2,288,896]{2,1,0:T(8,128)(2,1)} %after.11), channel_id=1, source_target_pairs={{16,2},{17,3},{18,0},{19,1},{20,6},{21,7},{22,4},{23,5},{24,10},{2... | collective-permute-start | bytes 3096584 | tf_op jit(solution)/shard_map/ppermute | solution.py:43
  60.1 18.0 %collective-permute-start.4 = (bf16[592,512]{1,0:T(8,128)(2,1)S(1)}, bf16[592,512]{1,0:T(8,128)(2,1)S(1)}, u32[]{:S(2)}, u32[]{:S(2)}) collective-permute-start(bf16[592,512]{1,0:T(8,128)(2,1)S(1)} %after.8), channel_id=1, source_target_pairs={{16,0},{17,1},{18,2},{19,3},{20,4},{21,5},{22,6},{23,7},{24,8},{25... | collective-permute-start | bytes 1818632 | tf_op jit(solution)/shard_map/ppermute | solution.py:43
  62.7 24.9 %all-to-all-start.1 = ((bf16[4,1024,128]{2,1,0:T(8,128)(2,1)}), bf16[4,1024,128]{2,1,0:T(8,128)(2,1)}, u32[]{:S(2)}, u32[]{:S(2)}) async-start(bf16[4,1024,128]{2,1,0:T(8,128)(2,1)} %add_convert_fusion), calls=%async_computation.1 | async-start | bytes 2097152 | tf_op jit(solution)/shard_map/all_to_all | solution.py:511
  67.4 11.6 %copy-start.4 = (f32[2,1008,128]{2,1,0:T(8,128)S(1)}, f32[2,1008,128]{2,1,0:T(8,128)}, u32[]{:S(2)}) copy-start(f32[2,1008,128]{2,1,0:T(8,128)} %get-tuple-element.22.refs_1_) | copy-start | bytes 3096580
  78.2 0.9 copy-start.1
  80.6 3.1 %copy-start.9 = (bf16[1008,128]{1,0:T(8,128)(2,1)}, bf16[1008,128]{1,0:T(8,128)(2,1)S(1)}, u32[]{:S(2)}) copy-start(bf16[1008,128]{1,0:T(8,128)(2,1)S(1)} %fusion.1.refs_1_) | copy-start | bytes 774148
  80.6 9.4 %collective-permute-start.9 = (bf16[1008,128]{1,0:T(8,128)(2,1)S(1)}, bf16[1008,128]{1,0:T(8,128)(2,1)S(1)}, u32[]{:S(2)}, u32[]{:S(2)}) collective-permute-start(bf16[1008,128]{1,0:T(8,128)(2,1)S(1)} %fusion.1.refs_1_), channel_id=1, source_target_pairs={{0,2},{1,3},{2,0},{3,1},{4,6},{5,7},{6,4},{7,5},{8,10},{9,11},{10,... | collective-permute-start | bytes 774152 | tf_op jit(solution)/shard_map/ppermute | solution.py:43
  81.5 15.4 %collective-permute-start.8 = (bf16[2,288,896]{2,1,0:T(8,128)(2,1)}, bf16[2,288,896]{2,1,0:T(8,128)(2,1)}, u32[]{:S(2)}, u32[]{:S(2)}) collective-permute-start(bf16[2,288,896]{2,1,0:T(8,128)(2,1)} %collective-permute-done.7.rest_2_), channel_id=1, source_target_pairs={{0,1},{1,0},{2,3},{3,2},{4,5},{5,4},{6,7},{7,6},{8,9},{9,8},{10,11... | collective-permute-start | bytes 3096584 | tf_op jit(solution)/shard_map/ppermute | solution.py:43
  83.7 6.3 %copy-start.5 = (f32[2,1008,128]{2,1,0:T(8,128)S(1)}, f32[2,1008,128]{2,1,0:T(8,128)}, u32[]{:S(2)}) copy-start(f32[2,1008,128]{2,1,0:T(8,128)} %get-tuple-element.22.refs_1_) | copy-start | bytes 3096580
  83.7 25.9 %collective-permute-start.5 = (bf16[2,288,896]{2,1,0:T(8,128)(2,1)}, bf16[2,288,896]{2,1,0:T(8,128)(2,1)}, u32[]{:S(2)}, u32[]{:S(2)}) collective-permute-start(bf16[2,288,896]{2,1,0:T(8,128)(2,1)} %after.10.rest_0_), channel_id=1, source_target_pairs={{0,12},{1,13},{2,14},{3,15},{4,0},{5,1},{6,2},{7,3},{8,4},{9,5},{1... | collective-permute-start | bytes 3096584 | tf_op jit(solution)/shard_map/ppermute | solution.py:43
  87.2 9.7 %collective-permute-start.6 = (bf16[2,288,896]{2,1,0:T(8,128)(2,1)}, bf16[2,288,896]{2,1,0:T(8,128)(2,1)}, u32[]{:S(2)}, u32[]{:S(2)}) collective-permute-start(bf16[2,288,896]{2,1,0:T(8,128)(2,1)} %after.10.rest_0_), channel_id=1, source_target_pairs={{0,1},{1,0},{2,3},{3,2},{4,5},{5,4},{6,7},{7,6},{8,9},{9,8},{10,11... | collective-permute-start | bytes 3096584 | tf_op jit(solution)/shard_map/ppermute | solution.py:43
  87.6 25.8 %collective-permute-start.12 = (bf16[2,288,896]{2,1,0:T(8,128)(2,1)}, bf16[2,288,896]{2,1,0:T(8,128)(2,1)}, u32[]{:S(2)}, u32[]{:S(2)}) collective-permute-start(bf16[2,288,896]{2,1,0:T(8,128)(2,1)} %after.10.rest_0_), channel_id=1, source_target_pairs={{0,4},{1,5},{2,6},{3,7},{4,8},{5,9},{6,10},{7,11},{8,12},{9,13},{1... | collective-permute-start | bytes 3096584 | tf_op jit(solution)/shard_map/ppermute | solution.py:43
  92.5 4.4 %copy-start.11 = (bf16[2032,128]{1,0:T(8,128)(2,1)}, bf16[2032,128]{1,0:T(8,128)(2,1)S(1)}, u32[]{:S(2)}) copy-start(bf16[2032,128]{1,0:T(8,128)(2,1)S(1)} %pad_maximum_fusion.rest_4_) | copy-start | bytes 1560580
  92.5 17.0 %collective-permute-start.10 = (bf16[2032,128]{1,0:T(8,128)(2,1)S(1)}, bf16[2032,128]{1,0:T(8,128)(2,1)S(1)}, u32[]{:S(2)}, u32[]{:S(2)}) collective-permute-start(bf16[2032,128]{1,0:T(8,128)(2,1)S(1)} %pad_maximum_fusion.rest_4_), channel_id=1, source_target_pairs={{0,112},{1,113},{2,114},{3,115},{4,116},{5,117},{6,118},{7,119},{8... | collective-permute-start | bytes 1560584 | tf_op jit(solution)/shard_map/ppermute | solution.py:43
  109.4 0.8 copy-start.2
  110.2 10.1 %collective-permute-start.11 = (bf16[2,288,896]{2,1,0:T(8,128)(2,1)}, bf16[2,288,896]{2,1,0:T(8,128)(2,1)S(1)}, u32[]{:S(2)}, u32[]{:S(2)}) collective-permute-start(bf16[2,288,896]{2,1,0:T(8,128)(2,1)} %after.12.rest_0_), channel_id=1, source_target_pairs={{0,1},{1,0},{2,3},{3,2},{4,5},{5,4},{6,7},{7,6},{8,9},{9,8},{10,11... | collective-permute-start | bytes 3096584 | tf_op jit(solution)/shard_map/ppermute | solution.py:43
  113.4 6.9 %collective-permute-start.13 = (bf16[2,288,896]{2,1,0:T(8,128)(2,1)}, bf16[2,288,896]{2,1,0:T(8,128)(2,1)S(1)}, u32[]{:S(2)}, u32[]{:S(2)}) collective-permute-start(bf16[2,288,896]{2,1,0:T(8,128)(2,1)} %after.13.rest_2_), channel_id=1, source_target_pairs={{0,1},{1,0},{2,3},{3,2},{4,5},{5,4},{6,7},{7,6},{8,9},{9,8},{10,11... | collective-permute-start | bytes 3096584 | tf_op jit(solution)/shard_map/ppermute | solution.py:43
  114.3 5.3 %copy-start.13 = (f32[1,32]{1,0:T(1,128)S(1)}, f32[1,32]{1,0:T(1,128)}, u32[]{:S(2)}) copy-start(f32[1,32]{1,0:T(1,128)} %param.19) | copy-start | bytes 388
  114.3 5.3 %copy-start.14 = (f32[1,32]{1,0:T(1,128)S(1)}, f32[1,32]{1,0:T(1,128)}, u32[]{:S(2)}) copy-start(f32[1,32]{1,0:T(1,128)} %param.20) | copy-start | bytes 388
  114.3 5.3 %copy-start.15 = (f32[1,32]{1,0:T(1,128)S(1)}, f32[1,32]{1,0:T(1,128)}, u32[]{:S(2)}) copy-start(f32[1,32]{1,0:T(1,128)} %param.21) | copy-start | bytes 388
  120.3 1.0 copy-start.7
  120.3 1.3 %copy-start.8 = (bf16[2,288,896]{2,1,0:T(8,128)(2,1)}, bf16[2,288,896]{2,1,0:T(8,128)(2,1)S(1)}, u32[]{:S(2)}) copy-start(bf16[2,288,896]{2,1,0:T(8,128)(2,1)S(1)} %collective-permute-done.13.rest_3_) | copy-start | bytes 3096580

commit v9 on v8

--- a/solution.py
+++ b/solution.py
@@ -493,12 +493,14 @@
     hidden = hidden_in[0]
     turned = weight[0].T
     other = moved(hidden, to_core)
-    groups = [[(0, 0), (0, 1)], [(2, 0), (2, 1)]]
-    cut_1, cut_2 = cut_weight(turned, groups)
+    groups = [[(0, 0)], [(0, 1), (2, 0), (2, 1)], [(1, 1), (3, 1)]]
+    cut_1, cut_2, cut_3 = cut_weight(turned, groups)
     rest_1 = moved(cut_1, to_before_near)
     rope = rope_step(rope_cot[0])
     grad = latent_step(hidden, turned, latent_cot[0], gain, rope, cut_1)
+    grad = after(grad, rest_1, mib=62)
     grad_other = moved(grad, to_core)
+    grad_next = moved(grad, to_before)
 
     def both(value, *blocks):
         return value, moved(value, to_core), blocks
@@ -511,28 +513,29 @@
         return lax.all_to_all(value, "dp", 0, 0, axis_index_groups=along_z, tiled=True)
 
     ra = exchanged(send_a)
-    rb = moved(after(send_b, rest_1, mib=62), to_ylo)
-    rest_2 = moved(after(cut_2, own_a, mib=62), to_before_near)
-    piece_2 = both(rest_2, *groups[1])
+    rb = moved(after(send_b, grad_next, mib=62), to_ylo)
+    rest_2 = moved(after(cut_2, grad_next, mib=62), to_before_near)
     send_b = (own_b + rb.astype(F32)).astype(BF)
-    grad_next = moved(after(grad, rb, mib=1), to_before)
     rz = exchanged(send_b)
-    ra = after(ra, grad_next)
     send_a = received_sum(own_a[1], ra[:, 1], z).astype(BF)
     ry = moved(send_a, to_ylo)
+    rest_2 = after(rest_2, send_a, mib=62)
+    piece_2 = both(rest_2, *groups[1])
+    rest_3 = moved(after(cut_3, rest_2, mib=62), to_before_near)
     total_a = received_sum(own_a[0], ra[:, 0], z) + ry.astype(F32)
     keep_b = lax.dynamic_index_in_dim(own_b, z, 0, False)
     keep_b += lax.dynamic_index_in_dim(rb, z, 0, False).astype(F32)
     total_b = received_sum(keep_b, rz, z)
     send = jnp.concatenate([total_a, total_b], axis=0).astype(BF)
     far = moved(send, to_mirror)
-    here = after(rest_1, send_a, mib=62)
+    here = after(rest_1, total_a, mib=62)
     above, below = moved(here, to_z(-1)), moved(here, to_z(1))
     pieces = [both(here, *groups[0]), piece_2]
     received, is_begun = input_step(grad_next, pieces, [send])
     above = after(above, is_begun, far, mib=62)
     below = after(below, is_begun, far, mib=62)
-    pieces = [both(above, (1, 0), (1, 1)), both(below, (3, 0), (3, 1))]
+    rest_3 = after(rest_3, is_begun, mib=62)
+    pieces = [both(above, (1, 0)), both(below, (3, 0)), both(rest_3, *groups[2])]
     received, _ = input_step(grad_next, pieces, [], received)
     next_master, next_first, next_second, gain_rows = adam_step(
         total_a, total_b, far, master_weight[0], first_moment[0], second_moment[0]

time: 132 us -> 153 us (1.16); the launches traced: 130 us -> 152 us
  waiting for transfers between devices: 42 us -> 63.1 us
  starting transfers between devices: 30.1 us -> 26.8 us
  other arithmetic: 9.23 us -> 11.8 us
  local copies, waits for them, and re-layouts: 5.28 us -> 6.98 us
    all_to_all x2, waiting for transfers between devices: 0.01 us -> 21.6 us  [exchanged(): lax.all_to_all(value, 'dp', 0, 0, axis_index_groups=along_z, tiled=True)]
    ppermute x14 -> x16, starting transfers between devices: 20.2 us -> 16.6 us  [moved(): return lax.ppermute(value, ('pipe', 'dp'), pairs)]
    convert_element_type x1, other arithmetic: 1.23 us -> 3.03 us  [on_device(): send_b = (own_b + rb.astype(F32)).astype(BF)]
    unnamed x32 -> x30, local copies, waits for them, and re-layouts: 4.59 us -> 6.3 us
    ppermute x14 -> x16, waiting for transfers between devices: 42 us -> 41.5 us  [moved(): return lax.ppermute(value, ('pipe', 'dp'), pairs)]
  transfers between devices with their start and end apart: 16 -> 18, of which waited for: 6 -> 8; matrix products, arithmetic and copies ran while one was open for 8% -> 8% of each run, Pallas kernels for 26% -> 23%
where the time goes in v9:
time: 153 us; the launch traced here: 152 us
  waiting for transfers between devices  63.1 us (41%)
  Pallas kernels  42.8 us (28%)
  starting transfers between devices  26.8 us (18%)
  other arithmetic  11.8 us (8%)
  local copies, waits for them, and re-layouts  6.98 us (5%)
    ppermute x16, waiting for transfers between devices, moved(): return lax.ppermute(value, ('pipe', 'dp'), pairs)  41.5 us
    all_to_all x2, waiting for transfers between devices, exchanged(): lax.all_to_all(value, 'dp', 0, 0, axis_index_groups=along_z, tiled=True)  21.6 us
    ppermute x16, starting transfers between devices, moved(): return lax.ppermute(value, ('pipe', 'dp'), pairs)  16.6 us
    pallas_call x2, Pallas kernels, input_step(): pl.pallas_call(kernel, in_specs=[inside] + [ANYWHERE] * halves + [LATER]...  15.7 us
    all_to_all x2, starting transfers between devices, exchanged(): lax.all_to_all(value, 'dp', 0, 0, axis_index_groups=along_z, tiled=True)  10.2 us
    pallas_call x1, Pallas kernels, weight_step(): pl.pallas_call(weight_kernel, in_specs=[ANYWHERE] * 4, out_specs=[ANYWHER...  9.76 us
    pallas_call x1, Pallas kernels, latent_step(): pl.pallas_call(latent_kernel, in_specs=[ANYWHERE, ANYWHERE, inside, insid...  9.2 us
    unnamed x30, local copies, waits for them, and re-layouts  6.3 us
  transfers between devices with their start and end apart: 18, of which 8 were waited for; matrix products, arithmetic and copies ran while one was open for 8% of the time, Pallas kernels for 23%

profile of v9, /device:TPU:1, one launch (start us, length us, event | category | flops | bytes accessed | tf_op | source)
XLA Modules:
  0.0 152.5 jit_solution(17909206100230311260)
XLA Ops:
  0.6 1.5 collective-permute-start.2
  2.1 3.5 %cut_weight.1 = (bf16[1,288,896]{2,1,0:T(8,128)(2,1)}, bf16[3,288,896]{2,1,0:T(8,128)(2,1)}, bf16[2,288,896]{2,1,0:T(8,128)(2,1)}) custom-call(bf16[576,7168]{1,0:T(8,128)(2,1)} %bitcast.84), custom_call_target="tpu_custom_call" | custom-call | bytes 1000 | tf_op jit(solution)/shard_map/cut_weight/pallas_call | solution.py:125
  5.7 1.3 collective-permute-start
  7.0 0.3 fusion.7
  7.4 0.6 pad_maximum_fusion.1.rope
  8.0 9.2 %latent_grad.1.refs_0_ = bf16[592,512]{1,0:T(8,128)(2,1)} custom-call(bf16[512,7168]{1,0:T(8,128)(2,1)} %bitcast.87, bf16[576,7168]{1,0:T(8,128)(2,1)} %bitcast.85, bf16[512,512]{1,0:T(8,128)(2,1)} %bitcast.93, f32[1,512]{1,0:T(1,128)} %gain.1, bf16[64,512]{1,0:T(8,128)(2,1)} %pad_maximum_fusion.1.rope, bf16[1,288,896]{2,1,0:T(8,128)(2,1)} %get-tuple-element.21.earlier), custom_call_target="tpu_custom_call" | custom-call | bytes 1000 | tf_op jit(solution)/shard_map/latent_grad/pallas_call | solution.py:183
  17.2 5.4 %collective-permute-done.refs_1_.refs_0_ = bf16[1,288,896]{2,1,0:T(8,128)(2,1)S(1)} collective-permute-done((bf16[1,288,896]{2,1,0:T(8,128)(2,1)}, bf16[1,288,896]{2,1,0:T(8,128)(2,1)S(1)}, u32[]{:S(2)}, u32[]{:S(2)}) %collective-permute-start) | collective-permute-done | bytes 516128 | tf_op jit(solution)/shard_map/ppermute | solution.py:43
  22.6 0.8 copy-done.4
  23.4 0.7 collective-permute-start.3
  24.2 1.3 collective-permute-start.1
  25.4 0.6 collective-permute-done.3.grad_other
  26.0 0.8 copy-done.6
  26.9 9.8 %weight_grad.1 = (f32[2,1008,128]{2,1,0:T(8,128)}, bf16[4,2,1008,128]{3,2,1,0:T(8,128)(2,1)}, f32[4,1024,128]{2,1,0:T(8,128)}, bf16[4,1024,128]{2,1,0:T(8,128)(2,1)}) custom-call(bf16[512,7168]{1,0:T(8,128)(2,1)} %bitcast.88, bf16[512,7168]{1,0:T(8,128)(2,1)} %collective-permute-done.2.other, bf16[592,512]{1,0:T(8,128)(2,1)} %after.9.grad, ...), custom_call_target="tpu_custom_call" | custom-call | bytes 1000 | tf_op jit(solution)/shard_map/weight_grad/pallas_call | solution.py:289
  36.6 5.0 %all-to-all-start = ((bf16[4,2,1008,128]{3,2,1,0:T(8,128)(2,1)}), bf16[4,2,1008,128]{3,2,1,0:T(8,128)(2,1)}, u32[]{:S(2)}, u32[]{:S(2)}) async-start(bf16[4,2,1008,128]{3,2,1,0:T(8,128)(2,1)} %get-tuple-element.23), calls=%async_computation | async-start | bytes 4128768 | tf_op jit(solution)/shard_map/all_to_all | solution.py:513
  41.6 1.4 collective-permute-done.1.refs_1_.grad
  43.1 0.8 copy-done.1
  43.9 1.3 collective-permute-start.7
  45.2 1.5 collective-permute-start.9
  46.7 20.5 %all-to-all-done = bf16[4,2,1008,128]{3,2,1,0:T(8,128)(2,1)} async-done(((bf16[4,2,1008,128]{3,2,1,0:T(8,128)(2,1)}), bf16[4,2,1008,128]{3,2,1,0:T(8,128)(2,1)}, u32[]{:S(2)}, u32[]{:S(2)}) %all-to-all-start) | async-done | bytes 2064416 | tf_op jit(solution)/shard_map/all_to_all | solution.py:513
  67.2 2.4 %fusion.refs_1_ = bf16[1008,128]{1,0:T(8,128)(2,1)} fusion(f32[2,1008,128]{2,1,0:T(8,128)} %get-tuple-element.22, bf16[4,2,1008,128]{3,2,1,0:T(8,128)(2,1)} %all-to-all-done, pred[]{:T(512)S(6)} %eq.11, pred[]{:T(512)S(6)} %eq.10, pred[]{:T(512)S(6)} %eq.9, pred[]{:T(512)S(6)} %eq.8), kind=kLoop, calls=%fused_computation.4 | loop fusion | flops 1677312 | bytes 1806340 | tf_op jit(solution)/shard_map/convert_element_type | solution.py:520
  69.6 14.3 %collective-permute-done.7.refs_0_ = bf16[3,288,896]{2,1,0:T(8,128)(2,1)S(1)} collective-permute-done((bf16[3,288,896]{2,1,0:T(8,128)(2,1)}, bf16[3,288,896]{2,1,0:T(8,128)(2,1)S(1)}, u32[]{:S(2)}, u32[]{:S(2)}) %collective-permute-start.7) | collective-permute-done | bytes 1548320 | tf_op jit(solution)/shard_map/ppermute | solution.py:43
  83.9 1.2 copy-done
  85.1 1.4 collective-permute-start.8
  86.5 3.0 %add_convert_fusion = bf16[4,1024,128]{2,1,0:T(8,128)(2,1)} fusion(f32[4,1024,128]{2,1,0:T(8,128)} %get-tuple-element.25, bf16[4,1024,128]{2,1,0:T(8,128)(2,1)} %collective-permute-done.9), kind=kLoop, calls=%fused_computation | loop fusion | flops 1572864 | bytes 4194304 | tf_op jit(solution)/shard_map/convert_element_type | solution.py:518
  89.5 5.2 %all-to-all-start.1 = ((bf16[4,1024,128]{2,1,0:T(8,128)(2,1)}), bf16[4,1024,128]{2,1,0:T(8,128)(2,1)S(1)}, u32[]{:S(2)}, u32[]{:S(2)}) async-start(bf16[4,1024,128]{2,1,0:T(8,128)(2,1)} %add_convert_fusion), calls=%async_computation.1 | async-start | bytes 2097152 | tf_op jit(solution)/shard_map/all_to_all | solution.py:513
  94.7 1.3 collective-permute-start.14
  96.0 6.3 %collective-permute-done.4 = bf16[1008,128]{1,0:T(8,128)(2,1)S(1)} collective-permute-done((bf16[1008,128]{1,0:T(8,128)(2,1)S(1)}, bf16[1008,128]{1,0:T(8,128)(2,1)S(1)}, u32[]{:S(2)}, u32[]{:S(2)}) %collective-permute-start.4) | collective-permute-done | bytes 258080 | tf_op jit(solution)/shard_map/ppermute | solution.py:43
  102.3 2.6 %fusion.15 = (bf16[1008,128]{1,0:T(8,128)(2,1)S(1)}, f32[1008,128]{1,0:T(8,128)}) fusion(bf16[1008,128]{1,0:T(8,128)(2,1)S(1)} %collective-permute-done.4, bf16[4,2,1008,128]{3,2,1,0:T(8,128)(2,1)} %all-to-all-done, pred[]{:T(512)S(6)} %eq.11, pred[]{:T(512)S(6)} %eq.10, pred[]{:T(512)S(6)} %eq.9, pred[]{:T(512)S(6)} %eq.8, f32[2,1008,128]{2,1,0:T(8,128)} %get-tuple-element.22), kind=kLoop, calls=%fused_computation.36 | loop fusion | flops 1935360 | bytes 2580484 | tf_op jit(solution)/shard_map/convert.2
  104.9 1.0 collective-permute-start.6
  105.9 2.7 %collective-permute-start.5 = (bf16[1,288,896]{2,1,0:T(8,128)(2,1)}, bf16[1,288,896]{2,1,0:T(8,128)(2,1)}, u32[]{:S(2)}, u32[]{:S(2)}) collective-permute-start(bf16[1,288,896]{2,1,0:T(8,128)(2,1)} %after.10.rest_0_), channel_id=1, source_target_pairs={{0,12},{1,13},{2,14},{3,15},{4,0},{5,1},{6,2},{7,3},{8,4},{9,5},{1... | collective-permute-start | bytes 1548296 | tf_op jit(solution)/shard_map/ppermute | solution.py:43
  108.5 1.1 all-to-all-done.1
  109.6 2.2 %fusion.17 = (bf16[1024,128]{1,0:T(8,128)(2,1)S(1)}, f32[1024,128]{1,0:T(8,128)}) fusion(bf16[4,1024,128]{2,1,0:T(8,128)(2,1)S(1)} %all-to-all-done.1, pred[]{:T(512)S(6)} %eq.11, pred[]{:T(512)S(6)} %eq.10, pred[]{:T(512)S(6)} %eq.9, pred[]{:T(512)S(6)} %eq.8, bf16[4,1024,128]{2,1,0:T(8,128)(2,1)} %collective-permute-done.9, s32[]{:T(128)S(6)} %select_n.129, ...), kind=kLoop, calls=%fused_computation.37 | loop fusion | flops 1966080 | bytes 2621448 | tf_op jit(solution)/shard_map/convert.3
  111.8 0.0 copy-start.7
  111.8 0.0 copy-start.14
  111.9 1.4 collective-permute-start.10
  113.3 7.8 %input_grad.2 = (bf16[512,7168]{1,0:T(8,128)(2,1)}, f32[8,128]{1,0:T(8,128)}) custom-call(bf16[592,512]{1,0:T(8,128)(2,1)} %copy-done.1, bf16[1,288,896]{2,1,0:T(8,128)(2,1)} %after.10.rest_0_, bf16[1,288,896]{2,1,0:T(8,128)(2,1)} %copy-done.14, bf16[3,288,896]{2,1,0:T(8,128)(2,1)} %after.12.rest_2_.refs_1_, ...), custom_call_target="tpu_custom_call" | custom-call | flops 2113929216 | bytes 8000000 | tf_op jit(solution)/shard_map/input_grad/pallas_call | solution.py:444
  121.1 13.4 %collective-permute-done.14.refs_0_ = bf16[2,288,896]{2,1,0:T(8,128)(2,1)} collective-permute-done((bf16[2,288,896]{2,1,0:T(8,128)(2,1)}, bf16[2,288,896]{2,1,0:T(8,128)(2,1)}, u32[]{:S(2)}, u32[]{:S(2)}) %collective-permute-start.14) | collective-permute-done | bytes 1032224 | tf_op jit(solution)/shard_map/ppermute | solution.py:43
  134.6 0.8 collective-permute-start.15
  135.4 0.8 copy-done.2
  136.2 0.0 collective-permute-start.11
  136.2 0.8 copy-done.3
  137.0 0.5 collective-permute-start.13
  137.5 4.6 %adamw.1 = (f32[448,576]{1,0:T(8,128)}, f32[448,576]{1,0:T(8,128)}, f32[448,576]{1,0:T(8,128)}, f32[8,128]{1,0:T(8,128)}) custom-call(f32[1008,128]{1,0:T(8,128)} %get-tuple-element.39.refs_1_.own_a, f32[1024,128]{1,0:T(8,128)} %get-tuple-element.41.own_b, bf16[2032,128]{1,0:T(8,128)(2,1)} %copy-done.2, f32[448,576]{1,0:T(8,128)} %bitcast.90, ...), custom_call_target="tpu_custom_call" | custom-call | bytes 9000000 | tf_op jit(solution)/shard_map/adamw/pallas_call | solution.py:382
  142.2 0.7 slice_bitcast_fusion
  142.8 0.6 fusion.13
  143.5 0.8 copy-done.8
  144.3 0.2 copy-done.9
  144.5 7.8 %input_grad.3 = (bf16[512,7168]{1,0:T(8,128)(2,1)}, f32[8,128]{1,0:T(8,128)}) custom-call(bf16[592,512]{1,0:T(8,128)(2,1)} %copy-done.1, bf16[1,288,896]{2,1,0:T(8,128)(2,1)} %after.14.rest_0_, bf16[1,288,896]{2,1,0:T(8,128)(2,1)} %copy-done.8, bf16[1,288,896]{2,1,0:T(8,128)(2,1)} %after.15.rest_2_, ...), custom_call_target="tpu_custom_call", output_to_operand_aliasing={{0}: (7, {})} | custom-call | flops 2113929216 | bytes 8000000 | tf_op jit(solution)/shard_map/input_grad/pallas_call | solution.py:444
  (45 shorter events, 0.1 us)
Async XLA Ops:
  0.6 25.4 %collective-permute-start.2 = (bf16[512,7168]{1,0:T(8,128)(2,1)}, bf16[512,7168]{1,0:T(8,128)(2,1)}, u32[]{:S(2)}, u32[]{:S(2)}) collective-permute-start(bf16[512,7168]{1,0:T(8,128)(2,1)} %bitcast.86), channel_id=1, source_target_pairs={{0,1},{1,0},{2,3},{3,2},{4,5},{5,4},{6,7},{7,6},{8,9},{9,8},{10,11... | collective-permute-start | bytes 22020104 | tf_op jit(solution)/shard_map/ppermute | solution.py:43
  2.1 4.9 %copy-start.10 = (bf16[1,512,64]{1,2,0:T(8,128)(2,1)S(1)}, bf16[1,512,64]{1,2,0:T(8,128)(2,1)}, u32[]{:S(2)}) copy-start(bf16[1,512,64]{1,2,0:T(8,128)(2,1)} %param.15) | copy-start | bytes 196612
  5.7 16.9 %collective-permute-start = (bf16[1,288,896]{2,1,0:T(8,128)(2,1)}, bf16[1,288,896]{2,1,0:T(8,128)(2,1)S(1)}, u32[]{:S(2)}, u32[]{:S(2)}) collective-permute-start(bf16[1,288,896]{2,1,0:T(8,128)(2,1)} %get-tuple-element.21.earlier), channel_id=1, source_target_pairs={{16,2},{17,3},{18,0},{19,1},{20,6},{21,7},{22,4},{23,5},{24,10},{2... | collective-permute-start | bytes 1548296 | tf_op jit(solution)/shard_map/ppermute | solution.py:43
  22.6 0.8 copy-start.4
  23.4 2.6 %collective-permute-start.3 = (bf16[592,512]{1,0:T(8,128)(2,1)}, bf16[592,512]{1,0:T(8,128)(2,1)S(1)}, u32[]{:S(2)}, u32[]{:S(2)}) collective-permute-start(bf16[592,512]{1,0:T(8,128)(2,1)} %after.9.grad), channel_id=1, source_target_pairs={{0,1},{1,0},{2,3},{3,2},{4,5},{5,4},{6,7},{7,6},{8,9},{9,8},{10,11... | collective-permute-start | bytes 1818632 | tf_op jit(solution)/shard_map/ppermute | solution.py:43
  24.2 18.9 %collective-permute-start.1 = (bf16[592,512]{1,0:T(8,128)(2,1)}, bf16[592,512]{1,0:T(8,128)(2,1)S(1)}, u32[]{:S(2)}, u32[]{:S(2)}) collective-permute-start(bf16[592,512]{1,0:T(8,128)(2,1)} %after.9.grad), channel_id=1, source_target_pairs={{16,0},{17,1},{18,2},{19,3},{20,4},{21,5},{22,6},{23,7},{24,8},{25... | collective-permute-start | bytes 1818632 | tf_op jit(solution)/shard_map/ppermute | solution.py:43
  26.0 0.8 copy-start.6
  36.6 30.6 %all-to-all-start = ((bf16[4,2,1008,128]{3,2,1,0:T(8,128)(2,1)}), bf16[4,2,1008,128]{3,2,1,0:T(8,128)(2,1)}, u32[]{:S(2)}, u32[]{:S(2)}) async-start(bf16[4,2,1008,128]{3,2,1,0:T(8,128)(2,1)} %get-tuple-element.23), calls=%async_computation | async-start | bytes 4128768 | tf_op jit(solution)/shard_map/all_to_all | solution.py:513
  43.1 0.8 copy-start.1
  43.9 40.0 %collective-permute-start.7 = (bf16[3,288,896]{2,1,0:T(8,128)(2,1)}, bf16[3,288,896]{2,1,0:T(8,128)(2,1)S(1)}, u32[]{:S(2)}, u32[]{:S(2)}) collective-permute-start(bf16[3,288,896]{2,1,0:T(8,128)(2,1)} %after.11), channel_id=1, source_target_pairs={{16,2},{17,3},{18,0},{19,1},{20,6},{21,7},{22,4},{23,5},{24,10},{2... | collective-permute-start | bytes 4644872 | tf_op jit(solution)/shard_map/ppermute | solution.py:43
  45.2 41.3 %collective-permute-start.9 = (bf16[4,1024,128]{2,1,0:T(8,128)(2,1)}, bf16[4,1024,128]{2,1,0:T(8,128)(2,1)}, u32[]{:S(2)}, u32[]{:S(2)}) collective-permute-start(bf16[4,1024,128]{2,1,0:T(8,128)(2,1)} %after.13), channel_id=1, source_target_pairs={{0,2},{1,3},{2,0},{3,1},{4,6},{5,7},{6,4},{7,5},{8,10},{9,11},{10,... | collective-permute-start | bytes 3145736 | tf_op jit(solution)/shard_map/ppermute | solution.py:43
  83.9 1.2 copy-start
  85.1 28.2 %collective-permute-start.8 = (bf16[3,288,896]{2,1,0:T(8,128)(2,1)}, bf16[3,288,896]{2,1,0:T(8,128)(2,1)}, u32[]{:S(2)}, u32[]{:S(2)}) collective-permute-start(bf16[3,288,896]{2,1,0:T(8,128)(2,1)} %after.12.rest_2_.refs_1_), channel_id=1, source_target_pairs={{0,1},{1,0},{2,3},{3,2},{4,5},{5,4},{6,7},{7,6},{8,9},{9,8},{10,11... | collective-permute-start | bytes 4644872 | tf_op jit(solution)/shard_map/ppermute | solution.py:43
  89.5 5.2 %copy-start.5 = (bf16[1008,128]{1,0:T(8,128)(2,1)S(1)}, bf16[1008,128]{1,0:T(8,128)(2,1)}, u32[]{:S(2)}) copy-start(bf16[1008,128]{1,0:T(8,128)(2,1)} %fusion.refs_1_) | copy-start | bytes 774148
  89.5 20.1 %all-to-all-start.1 = ((bf16[4,1024,128]{2,1,0:T(8,128)(2,1)}), bf16[4,1024,128]{2,1,0:T(8,128)(2,1)S(1)}, u32[]{:S(2)}, u32[]{:S(2)}) async-start(bf16[4,1024,128]{2,1,0:T(8,128)(2,1)} %add_convert_fusion), calls=%async_computation.1 | async-start | bytes 2097152 | tf_op jit(solution)/shard_map/all_to_all | solution.py:513
  94.7 7.6 %collective-permute-start.4 = (bf16[1008,128]{1,0:T(8,128)(2,1)S(1)}, bf16[1008,128]{1,0:T(8,128)(2,1)S(1)}, u32[]{:S(2)}, u32[]{:S(2)}) collective-permute-start(bf16[1008,128]{1,0:T(8,128)(2,1)S(1)} %copy-done.5), channel_id=1, source_target_pairs={{0,2},{1,3},{2,0},{3,1},{4,6},{5,7},{6,4},{7,5},{8,10},{9,11},{10,... | collective-permute-start | bytes 774152 | tf_op jit(solution)/shard_map/ppermute | solution.py:43
  94.7 39.9 %collective-permute-start.14 = (bf16[2,288,896]{2,1,0:T(8,128)(2,1)}, bf16[2,288,896]{2,1,0:T(8,128)(2,1)}, u32[]{:S(2)}, u32[]{:S(2)}) collective-permute-start(bf16[2,288,896]{2,1,0:T(8,128)(2,1)} %after.16), channel_id=1, source_target_pairs={{16,2},{17,3},{18,0},{19,1},{20,6},{21,7},{22,4},{23,5},{24,10},{2... | collective-permute-start | bytes 3096584 | tf_op jit(solution)/shard_map/ppermute | solution.py:43
  104.9 7.0 %collective-permute-start.6 = (bf16[1,288,896]{2,1,0:T(8,128)(2,1)}, bf16[1,288,896]{2,1,0:T(8,128)(2,1)S(1)}, u32[]{:S(2)}, u32[]{:S(2)}) collective-permute-start(bf16[1,288,896]{2,1,0:T(8,128)(2,1)} %after.10.rest_0_), channel_id=1, source_target_pairs={{0,1},{1,0},{2,3},{3,2},{4,5},{5,4},{6,7},{7,6},{8,9},{9,8},{10,11... | collective-permute-start | bytes 1548296 | tf_op jit(solution)/shard_map/ppermute | solution.py:43
  105.9 29.5 %collective-permute-start.5 = (bf16[1,288,896]{2,1,0:T(8,128)(2,1)}, bf16[1,288,896]{2,1,0:T(8,128)(2,1)}, u32[]{:S(2)}, u32[]{:S(2)}) collective-permute-start(bf16[1,288,896]{2,1,0:T(8,128)(2,1)} %after.10.rest_0_), channel_id=1, source_target_pairs={{0,12},{1,13},{2,14},{3,15},{4,0},{5,1},{6,2},{7,3},{8,4},{9,5},{1... | collective-permute-start | bytes 1548296 | tf_op jit(solution)/shard_map/ppermute | solution.py:43
  108.5 27.7 %collective-permute-start.12 = (bf16[1,288,896]{2,1,0:T(8,128)(2,1)}, bf16[1,288,896]{2,1,0:T(8,128)(2,1)S(1)}, u32[]{:S(2)}, u32[]{:S(2)}) collective-permute-start(bf16[1,288,896]{2,1,0:T(8,128)(2,1)} %after.10.rest_0_), channel_id=1, source_target_pairs={{0,4},{1,5},{2,6},{3,7},{4,8},{5,9},{6,10},{7,11},{8,12},{9,13},{1... | collective-permute-start | bytes 1548296 | tf_op jit(solution)/shard_map/ppermute | solution.py:43
  111.8 1.5 copy-start.7
  111.8 1.4 copy-start.14
  111.9 23.5 %collective-permute-start.10 = (bf16[2032,128]{1,0:T(8,128)(2,1)S(1)}, bf16[2032,128]{1,0:T(8,128)(2,1)S(1)}, u32[]{:S(2)}, u32[]{:S(2)}) collective-permute-start(bf16[2032,128]{1,0:T(8,128)(2,1)S(1)} %pad_maximum_fusion.rest_4_), channel_id=1, source_target_pairs={{0,112},{1,113},{2,114},{3,115},{4,116},{5,117},{6,118},{7,119},{8... | collective-permute-start | bytes 1560584 | tf_op jit(solution)/shard_map/ppermute | solution.py:43
  134.6 8.9 %collective-permute-start.15 = (bf16[2,288,896]{2,1,0:T(8,128)(2,1)}, bf16[2,288,896]{2,1,0:T(8,128)(2,1)}, u32[]{:S(2)}, u32[]{:S(2)}) collective-permute-start(bf16[2,288,896]{2,1,0:T(8,128)(2,1)} %after.17.rest_4_), channel_id=1, source_target_pairs={{0,1},{1,0},{2,3},{3,2},{4,5},{5,4},{6,7},{7,6},{8,9},{9,8},{10,11... | collective-permute-start | bytes 3096584 | tf_op jit(solution)/shard_map/ppermute | solution.py:43
  135.4 0.8 copy-start.2
  136.2 7.2 %collective-permute-start.11 = (bf16[1,288,896]{2,1,0:T(8,128)(2,1)}, bf16[1,288,896]{2,1,0:T(8,128)(2,1)S(1)}, u32[]{:S(2)}, u32[]{:S(2)}) collective-permute-start(bf16[1,288,896]{2,1,0:T(8,128)(2,1)} %after.14.rest_0_), channel_id=1, source_target_pairs={{0,1},{1,0},{2,3},{3,2},{4,5},{5,4},{6,7},{7,6},{8,9},{9,8},{10,11... | collective-permute-start | bytes 1548296 | tf_op jit(solution)/shard_map/ppermute | solution.py:43
  136.2 0.8 copy-start.3
  137.0 6.5 %collective-permute-start.13 = (bf16[1,288,896]{2,1,0:T(8,128)(2,1)}, bf16[1,288,896]{2,1,0:T(8,128)(2,1)S(1)}, u32[]{:S(2)}, u32[]{:S(2)}) collective-permute-start(bf16[1,288,896]{2,1,0:T(8,128)(2,1)} %after.15.rest_2_), channel_id=1, source_target_pairs={{0,1},{1,0},{2,3},{3,2},{4,5},{5,4},{6,7},{7,6},{8,9},{9,8},{10,11... | collective-permute-start | bytes 1548296 | tf_op jit(solution)/shard_map/ppermute | solution.py:43
  137.5 5.3 %copy-start.11 = (f32[1,32]{1,0:T(1,128)S(1)}, f32[1,32]{1,0:T(1,128)}, u32[]{:S(2)}) copy-start(f32[1,32]{1,0:T(1,128)} %param.19) | copy-start | bytes 388
  137.5 5.3 %copy-start.12 = (f32[1,32]{1,0:T(1,128)S(1)}, f32[1,32]{1,0:T(1,128)}, u32[]{:S(2)}) copy-start(f32[1,32]{1,0:T(1,128)} %param.20) | copy-start | bytes 388
  137.5 5.3 %copy-start.13 = (f32[1,32]{1,0:T(1,128)S(1)}, f32[1,32]{1,0:T(1,128)}, u32[]{:S(2)}) copy-start(f32[1,32]{1,0:T(1,128)} %param.21) | copy-start | bytes 388
  143.5 0.8 copy-start.8
  143.5 1.0 copy-start.9

commit v10 on v8

--- a/solution.py
+++ b/solution.py
@@ -332,8 +332,8 @@
 
 
 def adam_kernel(own_a, own_b, far, *rest):
-    state, outs, gain_out = rest[:3], rest[3:6], rest[6]
-    sum_a, sum_b, sum_far, held, new, grad, gain, sems, out_sems, gain_sem = rest[7:]
+    state, outs, gain_out = rest[:3], rest[4:7], rest[7]
+    sum_a, sum_b, sum_far, held, new, grad, gain, sems, out_sems, gain_sem = rest[8:]
     sums = [
         pltpu.make_async_copy(source, target, sems.at[i])
         for i, (source, target) in enumerate(((own_a, sum_a), (own_b, sum_b), (far, sum_far)))
@@ -377,11 +377,11 @@
     gain_copy.wait()
 
 
-def adam_step(own_a, own_b, far, master, first, second):
+def adam_step(own_a, own_b, far, master, first, second, earlier):
     shape = jax.ShapeDtypeStruct(master.shape, F32)
     return pl.pallas_call(
         adam_kernel,
-        in_specs=[LATER] * 6,
+        in_specs=[LATER] * 7,
         out_specs=[LATER] * 4,
         out_shape=[shape] * 3 + [jax.ShapeDtypeStruct((8, 128), F32)],
         scratch_shapes=[
@@ -399,7 +399,7 @@
         compiler_params=params(60),
         cost_estimate=cost(0, 9_000_000),
         name="adamw",
-    )(own_a, own_b, far, master, first, second)
+    )(own_a, own_b, far, master, first, second, earlier)
 
 
 def input_step(grad, pieces, earlier, begun=None):
@@ -517,26 +517,25 @@
     send_b = (own_b + rb.astype(F32)).astype(BF)
     grad_next = moved(after(grad, rb, mib=1), to_before)
     rz = exchanged(send_b)
-    ra = after(ra, grad_next)
     send_a = received_sum(own_a[1], ra[:, 1], z).astype(BF)
-    ry = moved(send_a, to_ylo)
+    ry = after(moved(send_a, to_ylo), grad_next)
     total_a = received_sum(own_a[0], ra[:, 0], z) + ry.astype(F32)
     keep_b = lax.dynamic_index_in_dim(own_b, z, 0, False)
     keep_b += lax.dynamic_index_in_dim(rb, z, 0, False).astype(F32)
     total_b = received_sum(keep_b, rz, z)
     send = jnp.concatenate([total_a, total_b], axis=0).astype(BF)
     far = moved(send, to_mirror)
-    here = after(rest_1, send_a, mib=62)
+    here = after(rest_1, grad_next, mib=62)
     above, below = moved(here, to_z(-1)), moved(here, to_z(1))
     pieces = [both(here, *groups[0]), piece_2]
     received, is_begun = input_step(grad_next, pieces, [send])
-    above = after(above, is_begun, far, mib=62)
-    below = after(below, is_begun, far, mib=62)
+    next_master, next_first, next_second, gain_rows = adam_step(
+        total_a, total_b, far, master_weight[0], first_moment[0], second_moment[0], is_begun
+    )
+    above = after(above, is_begun, gain_rows, mib=62)
+    below = after(below, is_begun, gain_rows, mib=62)
     pieces = [both(above, (1, 0), (1, 1)), both(below, (3, 0), (3, 1))]
     received, _ = input_step(grad_next, pieces, [], received)
-    next_master, next_first, next_second, gain_rows = adam_step(
-        total_a, total_b, far, master_weight[0], first_moment[0], second_moment[0]
-    )
     gain_total = lax.dynamic_slice(gain_rows[:4].reshape(LAT), (shard * 32,), (32,))
     next_gain = adamw(gain_master[0], gain_first[0], gain_second[0], gain_total)
     return (

time: 132 us -> 132 us (level)
  waiting for transfers between devices: 42 us -> 35.6 us
  starting transfers between devices: 30.1 us -> 33.1 us
  other arithmetic: 9.23 us -> 10.7 us
    ppermute x14, waiting for transfers between devices: 42 us -> 35.6 us  [moved(): return lax.ppermute(value, ('pipe', 'dp'), pairs)]
    ppermute x14, starting transfers between devices: 20.2 us -> 23.1 us  [moved(): return lax.ppermute(value, ('pipe', 'dp'), pairs)]
    unnamed x32, local copies, waits for them, and re-layouts: 4.59 us -> 6.47 us
  transfers between devices with their start and end apart: 16 -> 16, of which waited for: 6 -> 7; matrix products, arithmetic and copies ran while one was open for 8% -> 8% of each run, Pallas kernels for 26% -> 27%
where the time goes in v10:
time: 132 us; the launch traced here: 129 us
  Pallas kernels  42.1 us (32%)
  waiting for transfers between devices  35.6 us (27%)
  starting transfers between devices  33.1 us (25%)
  other arithmetic  10.7 us (8%)
  local copies, waits for them, and re-layouts  6.47 us (5%)
    ppermute x14, waiting for transfers between devices, moved(): return lax.ppermute(value, ('pipe', 'dp'), pairs)  35.6 us
    ppermute x14, starting transfers between devices, moved(): return lax.ppermute(value, ('pipe', 'dp'), pairs)  23.1 us
    pallas_call x2, Pallas kernels, input_step(): pl.pallas_call(kernel, in_specs=[inside] + [ANYWHERE] * halves + [LATER]...  15.7 us
    all_to_all x2, starting transfers between devices, exchanged(): lax.all_to_all(value, 'dp', 0, 0, axis_index_groups=along_z, tiled=True)  9.98 us
    pallas_call x1, Pallas kernels, weight_step(): pl.pallas_call(weight_kernel, in_specs=[ANYWHERE] * 4, out_specs=[ANYWHER...  9.75 us
    pallas_call x1, Pallas kernels, latent_step(): pl.pallas_call(latent_kernel, in_specs=[ANYWHERE, ANYWHERE, inside, insid...  9.2 us
    unnamed x32, local copies, waits for them, and re-layouts  6.47 us
    another operation x3, other arithmetic  5.38 us
  transfers between devices with their start and end apart: 16, of which 7 were waited for; matrix products, arithmetic and copies ran while one was open for 8% of the time, Pallas kernels for 27%

profile of v10, /device:TPU:1, one launch (start us, length us, event | category | flops | bytes accessed | tf_op | source)
XLA Modules:
  0.0 129.0 jit_solution(870484094546500509)
XLA Ops:
  0.6 1.5 %collective-permute-start = (bf16[512,7168]{1,0:T(8,128)(2,1)}, bf16[512,7168]{1,0:T(8,128)(2,1)}, u32[]{:S(2)}, u32[]{:S(2)}) collective-permute-start(bf16[512,7168]{1,0:T(8,128)(2,1)} %bitcast.86), channel_id=1, source_target_pairs={{0,1},{1,0},{2,3},{3,2},{4,5},{5,4},{6,7},{7,6},{8,9},{9,8},{10,11... | collective-permute-start | bytes 22020104 | tf_op jit(solution)/shard_map/ppermute | solution.py:43
  2.1 2.9 %cut_weight.1 = (bf16[2,288,896]{2,1,0:T(8,128)(2,1)}, bf16[2,288,896]{2,1,0:T(8,128)(2,1)}) custom-call(bf16[576,7168]{1,0:T(8,128)(2,1)} %bitcast.84), custom_call_target="tpu_custom_call" | custom-call | bytes 1000 | tf_op jit(solution)/shard_map/cut_weight/pallas_call | solution.py:125
  5.0 1.3 %collective-permute-start.2 = (bf16[2,288,896]{2,1,0:T(8,128)(2,1)}, bf16[2,288,896]{2,1,0:T(8,128)(2,1)S(1)}, u32[]{:S(2)}, u32[]{:S(2)}) collective-permute-start(bf16[2,288,896]{2,1,0:T(8,128)(2,1)} %get-tuple-element.20.earlier), channel_id=1, source_target_pairs={{16,2},{17,3},{18,0},{19,1},{20,6},{21,7},{22,4},{23,5},{24,10},{2... | collective-permute-start | bytes 3096584 | tf_op jit(solution)/shard_map/ppermute | solution.py:43
  6.4 0.3 fusion.7
  6.7 0.6 pad_maximum_fusion.1.rope
  7.3 9.2 %latent_grad.1.grad.refs_0_ = bf16[592,512]{1,0:T(8,128)(2,1)} custom-call(bf16[512,7168]{1,0:T(8,128)(2,1)} %bitcast.87, bf16[576,7168]{1,0:T(8,128)(2,1)} %bitcast.85, bf16[512,512]{1,0:T(8,128)(2,1)} %bitcast.93, f32[1,512]{1,0:T(1,128)} %gain.1, bf16[64,512]{1,0:T(8,128)(2,1)} %pad_maximum_fusion.1.rope, bf16[2,288,896]{2,1,0:T(8,128)(2,1)} %get-tuple-element.20.earlier), custom_call_target="tpu_custom_call" | custom-call | bytes 1000 | tf_op jit(solution)/shard_map/latent_grad/pallas_call | solution.py:183
  16.5 0.1 collective-permute-start.1
  16.6 2.2 %collective-permute-done.1.grad_other = bf16[592,512]{1,0:T(8,128)(2,1)S(1)} collective-permute-done((bf16[592,512]{1,0:T(8,128)(2,1)}, bf16[592,512]{1,0:T(8,128)(2,1)S(1)}, u32[]{:S(2)}, u32[]{:S(2)}) %collective-permute-start.1) | collective-permute-done | bytes 606240 | tf_op jit(solution)/shard_map/ppermute | solution.py:43
  18.9 0.0 collective-permute-done.other
  18.9 0.8 copy-done.8
  19.7 9.7 %weight_grad.1 = (f32[2,1008,128]{2,1,0:T(8,128)}, bf16[4,2,1008,128]{3,2,1,0:T(8,128)(2,1)}, f32[4,1024,128]{2,1,0:T(8,128)}, bf16[4,1024,128]{2,1,0:T(8,128)(2,1)}) custom-call(bf16[512,7168]{1,0:T(8,128)(2,1)} %bitcast.88, bf16[512,7168]{1,0:T(8,128)(2,1)} %collective-permute-done.other, bf16[592,512]{1,0:T(8,128)(2,1)} %latent_grad.1.grad.refs_0_, ...), custom_call_target="tpu_custom_call" | custom-call | bytes 1000 | tf_op jit(solution)/shard_map/weight_grad/pallas_call | solution.py:289
  29.4 5.1 %all-to-all-start = ((bf16[4,2,1008,128]{3,2,1,0:T(8,128)(2,1)}), bf16[4,2,1008,128]{3,2,1,0:T(8,128)(2,1)}, u32[]{:S(2)}, u32[]{:S(2)}) async-start(bf16[4,2,1008,128]{3,2,1,0:T(8,128)(2,1)} %get-tuple-element.24), calls=%async_computation | async-start | bytes 4128768 | tf_op jit(solution)/shard_map/all_to_all | solution.py:511
  34.5 0.9 copy-done.3
  35.5 1.3 %collective-permute-start.3 = (bf16[4,1024,128]{2,1,0:T(8,128)(2,1)}, bf16[4,1024,128]{2,1,0:T(8,128)(2,1)}, u32[]{:S(2)}, u32[]{:S(2)}) collective-permute-start(bf16[4,1024,128]{2,1,0:T(8,128)(2,1)} %after.7), channel_id=1, source_target_pairs={{0,2},{1,3},{2,0},{3,1},{4,6},{5,7},{6,4},{7,5},{8,10},{9,11},{10,... | collective-permute-start | bytes 3145736 | tf_op jit(solution)/shard_map/ppermute | solution.py:43
  36.8 1.4 %collective-permute-start.7 = (bf16[2,288,896]{2,1,0:T(8,128)(2,1)}, bf16[2,288,896]{2,1,0:T(8,128)(2,1)}, u32[]{:S(2)}, u32[]{:S(2)}) collective-permute-start(bf16[2,288,896]{2,1,0:T(8,128)(2,1)} %after.10), channel_id=1, source_target_pairs={{16,2},{17,3},{18,0},{19,1},{20,6},{21,7},{22,4},{23,5},{24,10},{2... | collective-permute-start | bytes 3096584 | tf_op jit(solution)/shard_map/ppermute | solution.py:43
  38.2 21.9 %collective-permute-done.3.refs_1_ = bf16[4,1024,128]{2,1,0:T(8,128)(2,1)} collective-permute-done((bf16[4,1024,128]{2,1,0:T(8,128)(2,1)}, bf16[4,1024,128]{2,1,0:T(8,128)(2,1)}, u32[]{:S(2)}, u32[]{:S(2)}) %collective-permute-start.3) | collective-permute-done | bytes 1048608 | tf_op jit(solution)/shard_map/ppermute | solution.py:43
  60.1 1.3 collective-permute-start.4
  61.4 2.4 %add_convert_fusion = bf16[4,1024,128]{2,1,0:T(8,128)(2,1)} fusion(f32[4,1024,128]{2,1,0:T(8,128)S(1)} %copy-done.6, bf16[4,1024,128]{2,1,0:T(8,128)(2,1)} %collective-permute-done.3.refs_1_), kind=kLoop, calls=%fused_computation | loop fusion | flops 1572864 | bytes 4194304 | tf_op jit(solution)/shard_map/convert_element_type | solution.py:517
  63.9 4.9 %all-to-all-start.1 = ((bf16[4,1024,128]{2,1,0:T(8,128)(2,1)}), bf16[4,1024,128]{2,1,0:T(8,128)(2,1)}, u32[]{:S(2)}, u32[]{:S(2)}) async-start(bf16[4,1024,128]{2,1,0:T(8,128)(2,1)} %add_convert_fusion), calls=%async_computation.1 | async-start | bytes 2097152 | tf_op jit(solution)/shard_map/all_to_all | solution.py:511
  68.7 1.6 %fusion = bf16[1008,128]{1,0:T(8,128)(2,1)S(1)} fusion(f32[2,1008,128]{2,1,0:T(8,128)S(1)} %copy-done.5, bf16[4,2,1008,128]{3,2,1,0:T(8,128)(2,1)} %all-to-all-done, pred[]{:T(512)S(6)} %eq.11, pred[]{:T(512)S(6)} %eq.10, pred[]{:T(512)S(6)} %eq.9, pred[]{:T(512)S(6)} %eq.8), kind=kLoop, calls=%fused_computation.4 | loop fusion | flops 1677312 | bytes 1806340 | tf_op jit(solution)/shard_map/convert_element_type | solution.py:520
  70.3 1.4 %collective-permute-start.9 = (bf16[1008,128]{1,0:T(8,128)(2,1)S(1)}, bf16[1008,128]{1,0:T(8,128)(2,1)S(1)}, u32[]{:S(2)}, u32[]{:S(2)}) collective-permute-start(bf16[1008,128]{1,0:T(8,128)(2,1)S(1)} %fusion), channel_id=1, source_target_pairs={{0,2},{1,3},{2,0},{3,1},{4,6},{5,7},{6,4},{7,5},{8,10},{9,11},{10,... | collective-permute-start | bytes 774152 | tf_op jit(solution)/shard_map/ppermute | solution.py:43
  71.7 1.6 %collective-permute-start.8 = (bf16[2,288,896]{2,1,0:T(8,128)(2,1)}, bf16[2,288,896]{2,1,0:T(8,128)(2,1)}, u32[]{:S(2)}, u32[]{:S(2)}) collective-permute-start(bf16[2,288,896]{2,1,0:T(8,128)(2,1)} %collective-permute-done.7.rest_2_), channel_id=1, source_target_pairs={{0,1},{1,0},{2,3},{3,2},{4,5},{5,4},{6,7},{7,6},{8,9},{9,8},{10,11... | collective-permute-start | bytes 3096584 | tf_op jit(solution)/shard_map/ppermute | solution.py:43
  73.2 4.8 %collective-permute-done.4.refs_1_.grad = bf16[592,512]{1,0:T(8,128)(2,1)S(1)} collective-permute-done((bf16[592,512]{1,0:T(8,128)(2,1)S(1)}, bf16[592,512]{1,0:T(8,128)(2,1)S(1)}, u32[]{:S(2)}, u32[]{:S(2)}) %collective-permute-start.4) | collective-permute-done | bytes 606240 | tf_op jit(solution)/shard_map/ppermute | solution.py:43
  78.0 0.9 copy-done
  78.9 0.8 collective-permute-start.12
  79.7 4.7 %collective-permute-start.6 = (bf16[2,288,896]{2,1,0:T(8,128)(2,1)}, bf16[2,288,896]{2,1,0:T(8,128)(2,1)}, u32[]{:S(2)}, u32[]{:S(2)}) collective-permute-start(bf16[2,288,896]{2,1,0:T(8,128)(2,1)} %after.9.rest_0_), channel_id=1, source_target_pairs={{0,1},{1,0},{2,3},{3,2},{4,5},{5,4},{6,7},{7,6},{8,9},{9,8},{10,11... | collective-permute-start | bytes 3096584 | tf_op jit(solution)/shard_map/ppermute | solution.py:43
  84.5 1.4 %collective-permute-start.5 = (bf16[2,288,896]{2,1,0:T(8,128)(2,1)}, bf16[2,288,896]{2,1,0:T(8,128)(2,1)}, u32[]{:S(2)}, u32[]{:S(2)}) collective-permute-start(bf16[2,288,896]{2,1,0:T(8,128)(2,1)} %after.9.rest_0_), channel_id=1, source_target_pairs={{0,12},{1,13},{2,14},{3,15},{4,0},{5,1},{6,2},{7,3},{8,4},{9,5},{1... | collective-permute-start | bytes 3096584 | tf_op jit(solution)/shard_map/ppermute | solution.py:43
  85.9 0.5 collective-permute-done.9.refs_0_
  86.4 1.1 copy-done.1
  87.5 2.6 %fusion.15 = (bf16[1008,128]{1,0:T(8,128)(2,1)S(1)}, f32[1008,128]{1,0:T(8,128)}) fusion(bf16[1008,128]{1,0:T(8,128)(2,1)S(1)} %after.11, bf16[4,2,1008,128]{3,2,1,0:T(8,128)(2,1)} %all-to-all-done, pred[]{:T(512)S(6)} %eq.11, pred[]{:T(512)S(6)} %eq.10, pred[]{:T(512)S(6)} %eq.9, pred[]{:T(512)S(6)} %eq.8, f32[2,1008,128]{2,1,0:T(8,128)} %get-tuple-element.23.refs_1_), kind=kLoop, calls=%fused_computation.36 | loop fusion | flops 1935360 | bytes 2580484 | tf_op jit(solution)/shard_map/convert.2
  90.0 2.5 %fusion.17 = (bf16[1024,128]{1,0:T(8,128)(2,1)S(1)}, f32[1024,128]{1,0:T(8,128)}) fusion(bf16[4,1024,128]{2,1,0:T(8,128)(2,1)} %all-to-all-done.1, pred[]{:T(512)S(6)} %eq.11, pred[]{:T(512)S(6)} %eq.10, pred[]{:T(512)S(6)} %eq.9, pred[]{:T(512)S(6)} %eq.8, bf16[4,1024,128]{2,1,0:T(8,128)(2,1)} %collective-permute-done.3.refs_1_, s32[]{:T(128)S(6)} %select_n.129, ...), kind=kLoop, calls=%fused_computation.37 | loop fusion | flops 1966080 | bytes 2621448 | tf_op jit(solution)/shard_map/convert.3
  92.6 0.0 copy-start.10
  92.6 4.2 %collective-permute-start.10 = (bf16[2032,128]{1,0:T(8,128)(2,1)S(1)}, bf16[2032,128]{1,0:T(8,128)(2,1)S(1)}, u32[]{:S(2)}, u32[]{:S(2)}) collective-permute-start(bf16[2032,128]{1,0:T(8,128)(2,1)S(1)} %pad_maximum_fusion.rest_4_), channel_id=1, source_target_pairs={{0,112},{1,113},{2,114},{3,115},{4,116},{5,117},{6,118},{7,119},{8... | collective-permute-start | bytes 1560584 | tf_op jit(solution)/shard_map/ppermute | solution.py:43
  96.8 7.8 %input_grad.2 = (bf16[512,7168]{1,0:T(8,128)(2,1)}, f32[8,128]{1,0:T(8,128)}) custom-call(bf16[592,512]{1,0:T(8,128)(2,1)} %copy-done, bf16[2,288,896]{2,1,0:T(8,128)(2,1)} %after.9.rest_0_, bf16[2,288,896]{2,1,0:T(8,128)(2,1)} %collective-permute-done.6.rest_1_, bf16[2,288,896]{2,1,0:T(8,128)(2,1)} %collective-permute-done.7.rest_2_, ...), custom_call_target="tpu_custom_call" | custom-call | flops 2113929216 | bytes 8000000 | tf_op jit(solution)/shard_map/input_grad/pallas_call | solution.py:444
  104.7 3.9 %collective-permute-done.10.far = bf16[2032,128]{1,0:T(8,128)(2,1)S(1)} collective-permute-done((bf16[2032,128]{1,0:T(8,128)(2,1)S(1)}, bf16[2032,128]{1,0:T(8,128)(2,1)S(1)}, u32[]{:S(2)}, u32[]{:S(2)}) %collective-permute-start.10) | collective-permute-done | bytes 520224 | tf_op jit(solution)/shard_map/ppermute | solution.py:43
  108.6 0.8 copy-done.9
  109.3 4.6 %adamw.1 = (f32[448,576]{1,0:T(8,128)}, f32[448,576]{1,0:T(8,128)}, f32[448,576]{1,0:T(8,128)}, f32[8,128]{1,0:T(8,128)}) custom-call(f32[1008,128]{1,0:T(8,128)} %get-tuple-element.37.own_a, f32[1024,128]{1,0:T(8,128)} %get-tuple-element.39.own_b, bf16[2032,128]{1,0:T(8,128)(2,1)} %copy-done.9, f32[448,576]{1,0:T(8,128)} %bitcast.90, f32[448,576]{1,0:T(8,128)} %bitcast.91, ...), custom_call_target="tpu_custom_call" | custom-call | bytes 9000000 | tf_op jit(solution)/shard_map/adamw/pallas_call | solution.py:382
  114.0 0.0 copy-start.13
  114.0 0.0 copy-start.14
  114.0 0.0 copy-start.15
  114.0 2.1 %collective-permute-start.11 = (bf16[2,288,896]{2,1,0:T(8,128)(2,1)}, bf16[2,288,896]{2,1,0:T(8,128)(2,1)}, u32[]{:S(2)}, u32[]{:S(2)}) collective-permute-start(bf16[2,288,896]{2,1,0:T(8,128)(2,1)} %after.12.rest_0_), channel_id=1, source_target_pairs={{0,1},{1,0},{2,3},{3,2},{4,5},{5,4},{6,7},{7,6},{8,9},{9,8},{10,11... | collective-permute-start | bytes 3096584 | tf_op jit(solution)/shard_map/ppermute | solution.py:43
  116.1 1.0 copy-done.4
  117.1 0.0 collective-permute-start.13
  117.1 0.6 fusion.13
  117.7 1.0 collective-permute-done.11.rest_1_
  118.7 1.3 %collective-permute-done.13.rest_3_ = bf16[2,288,896]{2,1,0:T(8,128)(2,1)S(1)} collective-permute-done((bf16[2,288,896]{2,1,0:T(8,128)(2,1)}, bf16[2,288,896]{2,1,0:T(8,128)(2,1)S(1)}, u32[]{:S(2)}, u32[]{:S(2)}) %collective-permute-start.13) | collective-permute-done | bytes 1032224 | tf_op jit(solution)/shard_map/ppermute | solution.py:43
  120.0 1.0 copy-done.7
  121.0 7.8 %input_grad.3 = (bf16[512,7168]{1,0:T(8,128)(2,1)}, f32[8,128]{1,0:T(8,128)}) custom-call(bf16[592,512]{1,0:T(8,128)(2,1)} %copy-done, bf16[2,288,896]{2,1,0:T(8,128)(2,1)} %after.12.rest_0_, bf16[2,288,896]{2,1,0:T(8,128)(2,1)} %collective-permute-done.11.rest_1_, bf16[2,288,896]{2,1,0:T(8,128)(2,1)} %after.13.rest_2_, ...), custom_call_target="tpu_custom_call", output_to_operand_aliasing={{0}: (5, {})} | custom-call | flops 2113929216 | bytes 8000000 | tf_op jit(solution)/shard_map/input_grad/pallas_call | solution.py:444
  (41 shorter events, 0.1 us)
Async XLA Ops:
  0.6 18.2 %collective-permute-start = (bf16[512,7168]{1,0:T(8,128)(2,1)}, bf16[512,7168]{1,0:T(8,128)(2,1)}, u32[]{:S(2)}, u32[]{:S(2)}) collective-permute-start(bf16[512,7168]{1,0:T(8,128)(2,1)} %bitcast.86), channel_id=1, source_target_pairs={{0,1},{1,0},{2,3},{3,2},{4,5},{5,4},{6,7},{7,6},{8,9},{9,8},{10,11... | collective-permute-start | bytes 22020104 | tf_op jit(solution)/shard_map/ppermute | solution.py:43
  2.1 4.2 %copy-start.11 = (bf16[1,512,64]{1,2,0:T(8,128)(2,1)S(1)}, bf16[1,512,64]{1,2,0:T(8,128)(2,1)}, u32[]{:S(2)}) copy-start(bf16[1,512,64]{1,2,0:T(8,128)(2,1)} %param.15) | copy-start | bytes 196612
  5.0 29.5 %collective-permute-start.2 = (bf16[2,288,896]{2,1,0:T(8,128)(2,1)}, bf16[2,288,896]{2,1,0:T(8,128)(2,1)S(1)}, u32[]{:S(2)}, u32[]{:S(2)}) collective-permute-start(bf16[2,288,896]{2,1,0:T(8,128)(2,1)} %get-tuple-element.20.earlier), channel_id=1, source_target_pairs={{16,2},{17,3},{18,0},{19,1},{20,6},{21,7},{22,4},{23,5},{24,10},{2... | collective-permute-start | bytes 3096584 | tf_op jit(solution)/shard_map/ppermute | solution.py:43
  16.5 2.3 %collective-permute-start.1 = (bf16[592,512]{1,0:T(8,128)(2,1)}, bf16[592,512]{1,0:T(8,128)(2,1)S(1)}, u32[]{:S(2)}, u32[]{:S(2)}) collective-permute-start(bf16[592,512]{1,0:T(8,128)(2,1)} %latent_grad.1.grad.refs_0_), channel_id=1, source_target_pairs={{0,1},{1,0},{2,3},{3,2},{4,5},{5,4},{6,7},{7,6},{8,9},{9,8},{10,11... | collective-permute-start | bytes 1818632 | tf_op jit(solution)/shard_map/ppermute | solution.py:43
  18.9 0.8 copy-start.8
  29.4 34.4 %all-to-all-start = ((bf16[4,2,1008,128]{3,2,1,0:T(8,128)(2,1)}), bf16[4,2,1008,128]{3,2,1,0:T(8,128)(2,1)}, u32[]{:S(2)}, u32[]{:S(2)}) async-start(bf16[4,2,1008,128]{3,2,1,0:T(8,128)(2,1)} %get-tuple-element.24), calls=%async_computation | async-start | bytes 4128768 | tf_op jit(solution)/shard_map/all_to_all | solution.py:511
  34.5 0.9 copy-start.3
  35.5 24.6 %copy-start.2 = (bf16[592,512]{1,0:T(8,128)(2,1)S(1)}, bf16[592,512]{1,0:T(8,128)(2,1)}, u32[]{:S(2)}) copy-start(bf16[592,512]{1,0:T(8,128)(2,1)} %latent_grad.1.grad.refs_0_) | copy-start | bytes 1818628
  35.5 24.6 %collective-permute-start.3 = (bf16[4,1024,128]{2,1,0:T(8,128)(2,1)}, bf16[4,1024,128]{2,1,0:T(8,128)(2,1)}, u32[]{:S(2)}, u32[]{:S(2)}) collective-permute-start(bf16[4,1024,128]{2,1,0:T(8,128)(2,1)} %after.7), channel_id=1, source_target_pairs={{0,2},{1,3},{2,0},{3,1},{4,6},{5,7},{6,4},{7,5},{8,10},{9,11},{10,... | collective-permute-start | bytes 3145736 | tf_op jit(solution)/shard_map/ppermute | solution.py:43
  36.8 24.6 %copy-start.6 = (f32[4,1024,128]{2,1,0:T(8,128)S(1)}, f32[4,1024,128]{2,1,0:T(8,128)}, u32[]{:S(2)}) copy-start(f32[4,1024,128]{2,1,0:T(8,128)} %get-tuple-element.25) | copy-start | bytes 6291460
  36.8 34.9 %collective-permute-start.7 = (bf16[2,288,896]{2,1,0:T(8,128)(2,1)}, bf16[2,288,896]{2,1,0:T(8,128)(2,1)}, u32[]{:S(2)}, u32[]{:S(2)}) collective-permute-start(bf16[2,288,896]{2,1,0:T(8,128)(2,1)} %after.10), channel_id=1, source_target_pairs={{16,2},{17,3},{18,0},{19,1},{20,6},{21,7},{22,4},{23,5},{24,10},{2... | collective-permute-start | bytes 3096584 | tf_op jit(solution)/shard_map/ppermute | solution.py:43
  60.1 17.9 %collective-permute-start.4 = (bf16[592,512]{1,0:T(8,128)(2,1)S(1)}, bf16[592,512]{1,0:T(8,128)(2,1)S(1)}, u32[]{:S(2)}, u32[]{:S(2)}) collective-permute-start(bf16[592,512]{1,0:T(8,128)(2,1)S(1)} %after.8), channel_id=1, source_target_pairs={{16,0},{17,1},{18,2},{19,3},{20,4},{21,5},{22,6},{23,7},{24,8},{25... | collective-permute-start | bytes 1818632 | tf_op jit(solution)/shard_map/ppermute | solution.py:43
  63.9 4.9 %copy-start.5 = (f32[2,1008,128]{2,1,0:T(8,128)S(1)}, f32[2,1008,128]{2,1,0:T(8,128)}, u32[]{:S(2)}) copy-start(f32[2,1008,128]{2,1,0:T(8,128)} %get-tuple-element.23.refs_1_) | copy-start | bytes 3096580
  63.9 26.2 %all-to-all-start.1 = ((bf16[4,1024,128]{2,1,0:T(8,128)(2,1)}), bf16[4,1024,128]{2,1,0:T(8,128)(2,1)}, u32[]{:S(2)}, u32[]{:S(2)}) async-start(bf16[4,1024,128]{2,1,0:T(8,128)(2,1)} %add_convert_fusion), calls=%async_computation.1 | async-start | bytes 2097152 | tf_op jit(solution)/shard_map/all_to_all | solution.py:511
  70.3 16.1 %collective-permute-start.9 = (bf16[1008,128]{1,0:T(8,128)(2,1)S(1)}, bf16[1008,128]{1,0:T(8,128)(2,1)S(1)}, u32[]{:S(2)}, u32[]{:S(2)}) collective-permute-start(bf16[1008,128]{1,0:T(8,128)(2,1)S(1)} %fusion), channel_id=1, source_target_pairs={{0,2},{1,3},{2,0},{3,1},{4,6},{5,7},{6,4},{7,5},{8,10},{9,11},{10,... | collective-permute-start | bytes 774152 | tf_op jit(solution)/shard_map/ppermute | solution.py:43
  71.7 25.1 %collective-permute-start.8 = (bf16[2,288,896]{2,1,0:T(8,128)(2,1)}, bf16[2,288,896]{2,1,0:T(8,128)(2,1)}, u32[]{:S(2)}, u32[]{:S(2)}) collective-permute-start(bf16[2,288,896]{2,1,0:T(8,128)(2,1)} %collective-permute-done.7.rest_2_), channel_id=1, source_target_pairs={{0,1},{1,0},{2,3},{3,2},{4,5},{5,4},{6,7},{7,6},{8,9},{9,8},{10,11... | collective-permute-start | bytes 3096584 | tf_op jit(solution)/shard_map/ppermute | solution.py:43
  78.0 0.9 copy-start
  78.9 37.2 %collective-permute-start.12 = (bf16[2,288,896]{2,1,0:T(8,128)(2,1)}, bf16[2,288,896]{2,1,0:T(8,128)(2,1)S(1)}, u32[]{:S(2)}, u32[]{:S(2)}) collective-permute-start(bf16[2,288,896]{2,1,0:T(8,128)(2,1)} %after.9.rest_0_), channel_id=1, source_target_pairs={{0,4},{1,5},{2,6},{3,7},{4,8},{5,9},{6,10},{7,11},{8,12},{9,13},{1... | collective-permute-start | bytes 3096584 | tf_op jit(solution)/shard_map/ppermute | solution.py:43
  79.7 17.1 %collective-permute-start.6 = (bf16[2,288,896]{2,1,0:T(8,128)(2,1)}, bf16[2,288,896]{2,1,0:T(8,128)(2,1)}, u32[]{:S(2)}, u32[]{:S(2)}) collective-permute-start(bf16[2,288,896]{2,1,0:T(8,128)(2,1)} %after.9.rest_0_), channel_id=1, source_target_pairs={{0,1},{1,0},{2,3},{3,2},{4,5},{5,4},{6,7},{7,6},{8,9},{9,8},{10,11... | collective-permute-start | bytes 3096584 | tf_op jit(solution)/shard_map/ppermute | solution.py:43
  84.5 29.5 %collective-permute-start.5 = (bf16[2,288,896]{2,1,0:T(8,128)(2,1)}, bf16[2,288,896]{2,1,0:T(8,128)(2,1)}, u32[]{:S(2)}, u32[]{:S(2)}) collective-permute-start(bf16[2,288,896]{2,1,0:T(8,128)(2,1)} %after.9.rest_0_), channel_id=1, source_target_pairs={{0,12},{1,13},{2,14},{3,15},{4,0},{5,1},{6,2},{7,3},{8,4},{9,5},{1... | collective-permute-start | bytes 3096584 | tf_op jit(solution)/shard_map/ppermute | solution.py:43
  86.4 1.1 copy-start.1
  92.6 4.2 %copy-start.10 = (bf16[2032,128]{1,0:T(8,128)(2,1)}, bf16[2032,128]{1,0:T(8,128)(2,1)S(1)}, u32[]{:S(2)}) copy-start(bf16[2032,128]{1,0:T(8,128)(2,1)S(1)} %pad_maximum_fusion.rest_4_) | copy-start | bytes 1560580
  92.6 16.0 %collective-permute-start.10 = (bf16[2032,128]{1,0:T(8,128)(2,1)S(1)}, bf16[2032,128]{1,0:T(8,128)(2,1)S(1)}, u32[]{:S(2)}, u32[]{:S(2)}) collective-permute-start(bf16[2032,128]{1,0:T(8,128)(2,1)S(1)} %pad_maximum_fusion.rest_4_), channel_id=1, source_target_pairs={{0,112},{1,113},{2,114},{3,115},{4,116},{5,117},{6,118},{7,119},{8... | collective-permute-start | bytes 1560584 | tf_op jit(solution)/shard_map/ppermute | solution.py:43
  108.6 0.8 copy-start.9
  114.0 3.1 %copy-start.12 = (f32[8,128]{1,0:T(8,128)S(1)}, f32[8,128]{1,0:T(8,128)}, u32[]{:S(2)}) copy-start(f32[8,128]{1,0:T(8,128)} %get-tuple-element.27.refs_2_) | copy-start | bytes 12292
  114.0 3.1 %copy-start.13 = (f32[1,32]{1,0:T(1,128)S(1)}, f32[1,32]{1,0:T(1,128)}, u32[]{:S(2)}) copy-start(f32[1,32]{1,0:T(1,128)} %param.19) | copy-start | bytes 388
  114.0 3.1 %copy-start.14 = (f32[1,32]{1,0:T(1,128)S(1)}, f32[1,32]{1,0:T(1,128)}, u32[]{:S(2)}) copy-start(f32[1,32]{1,0:T(1,128)} %param.20) | copy-start | bytes 388
  114.0 3.1 %copy-start.15 = (f32[1,32]{1,0:T(1,128)S(1)}, f32[1,32]{1,0:T(1,128)}, u32[]{:S(2)}) copy-start(f32[1,32]{1,0:T(1,128)} %param.21) | copy-start | bytes 388
  114.0 4.7 %collective-permute-start.11 = (bf16[2,288,896]{2,1,0:T(8,128)(2,1)}, bf16[2,288,896]{2,1,0:T(8,128)(2,1)}, u32[]{:S(2)}, u32[]{:S(2)}) collective-permute-start(bf16[2,288,896]{2,1,0:T(8,128)(2,1)} %after.12.rest_0_), channel_id=1, source_target_pairs={{0,1},{1,0},{2,3},{3,2},{4,5},{5,4},{6,7},{7,6},{8,9},{9,8},{10,11... | collective-permute-start | bytes 3096584 | tf_op jit(solution)/shard_map/ppermute | solution.py:43
  116.1 1.0 copy-start.4
  117.1 3.0 %collective-permute-start.13 = (bf16[2,288,896]{2,1,0:T(8,128)(2,1)}, bf16[2,288,896]{2,1,0:T(8,128)(2,1)S(1)}, u32[]{:S(2)}, u32[]{:S(2)}) collective-permute-start(bf16[2,288,896]{2,1,0:T(8,128)(2,1)} %after.13.rest_2_), channel_id=1, source_target_pairs={{0,1},{1,0},{2,3},{3,2},{4,5},{5,4},{6,7},{7,6},{8,9},{9,8},{10,11... | collective-permute-start | bytes 3096584 | tf_op jit(solution)/shard_map/ppermute | solution.py:43
  120.0 1.0 copy-start.7

commit v11 on v10

--- a/solution.py
+++ b/solution.py
@@ -456,7 +456,7 @@
             pltpu.SemaphoreType.DMA((count,)),
         ],
         input_output_aliases={} if begun is None else {len(operands) - 1: 0},
-        compiler_params=params(60),
+        compiler_params=params(60 if begun is None else 36),
         cost_estimate=cost(TOK * WIDTH * COLS, 8_000_000),
         name="input_grad",
     )(*operands)

time: 132 us -> 131 us (level)
    unnamed x32 -> x34, local copies, waits for them, and re-layouts: 6.47 us -> 6.76 us
where the time goes in v11:
time: 131 us; the launch traced here: 129 us
  Pallas kernels  41.4 us (32%)
  waiting for transfers between devices  35.7 us (27%)
  starting transfers between devices  33.1 us (25%)
  other arithmetic  10.7 us (8%)
  local copies, waits for them, and re-layouts  6.76 us (5%)
    ppermute x14, waiting for transfers between devices, moved(): return lax.ppermute(value, ('pipe', 'dp'), pairs)  35.6 us
    ppermute x14, starting transfers between devices, moved(): return lax.ppermute(value, ('pipe', 'dp'), pairs)  23.1 us
    pallas_call x2, Pallas kernels, input_step(): pl.pallas_call(kernel, in_specs=[inside] + [ANYWHERE] * halves + [LATER]...  15 us
    all_to_all x2, starting transfers between devices, exchanged(): lax.all_to_all(value, 'dp', 0, 0, axis_index_groups=along_z, tiled=True)  9.97 us
    pallas_call x1, Pallas kernels, weight_step(): pl.pallas_call(weight_kernel, in_specs=[ANYWHERE] * 4, out_specs=[ANYWHER...  9.74 us
    pallas_call x1, Pallas kernels, latent_step(): pl.pallas_call(latent_kernel, in_specs=[ANYWHERE, ANYWHERE, inside, insid...  9.19 us
    unnamed x34, local copies, waits for them, and re-layouts  6.76 us
    another operation x3, other arithmetic  5.38 us
  transfers between devices with their start and end apart: 16, of which 7 were waited for; matrix products, arithmetic and copies ran while one was open for 8% of the time, Pallas kernels for 27%

profile of v11, /device:TPU:1, one launch (start us, length us, event | category | flops | bytes accessed | tf_op | source)
XLA Modules:
  0.0 128.6 jit_solution(16740507249658781)
XLA Ops:
  0.6 1.5 %collective-permute-start = (bf16[512,7168]{1,0:T(8,128)(2,1)}, bf16[512,7168]{1,0:T(8,128)(2,1)}, u32[]{:S(2)}, u32[]{:S(2)}) collective-permute-start(bf16[512,7168]{1,0:T(8,128)(2,1)} %bitcast.86), channel_id=1, source_target_pairs={{0,1},{1,0},{2,3},{3,2},{4,5},{5,4},{6,7},{7,6},{8,9},{9,8},{10,11... | collective-permute-start | bytes 22020104 | tf_op jit(solution)/shard_map/ppermute | solution.py:43
  2.1 2.9 %cut_weight.1 = (bf16[2,288,896]{2,1,0:T(8,128)(2,1)}, bf16[2,288,896]{2,1,0:T(8,128)(2,1)}) custom-call(bf16[576,7168]{1,0:T(8,128)(2,1)} %bitcast.84), custom_call_target="tpu_custom_call" | custom-call | bytes 1000 | tf_op jit(solution)/shard_map/cut_weight/pallas_call | solution.py:125
  5.0 1.3 %collective-permute-start.2 = (bf16[2,288,896]{2,1,0:T(8,128)(2,1)}, bf16[2,288,896]{2,1,0:T(8,128)(2,1)S(1)}, u32[]{:S(2)}, u32[]{:S(2)}) collective-permute-start(bf16[2,288,896]{2,1,0:T(8,128)(2,1)} %get-tuple-element.20.earlier), channel_id=1, source_target_pairs={{16,2},{17,3},{18,0},{19,1},{20,6},{21,7},{22,4},{23,5},{24,10},{2... | collective-permute-start | bytes 3096584 | tf_op jit(solution)/shard_map/ppermute | solution.py:43
  6.4 0.3 fusion.7
  6.7 0.6 pad_maximum_fusion.1.rope
  7.3 9.2 %latent_grad.1.grad.refs_0_ = bf16[592,512]{1,0:T(8,128)(2,1)} custom-call(bf16[512,7168]{1,0:T(8,128)(2,1)} %bitcast.87, bf16[576,7168]{1,0:T(8,128)(2,1)} %bitcast.85, bf16[512,512]{1,0:T(8,128)(2,1)} %bitcast.93, f32[1,512]{1,0:T(1,128)} %gain.1, bf16[64,512]{1,0:T(8,128)(2,1)} %pad_maximum_fusion.1.rope, bf16[2,288,896]{2,1,0:T(8,128)(2,1)} %get-tuple-element.20.earlier), custom_call_target="tpu_custom_call" | custom-call | bytes 1000 | tf_op jit(solution)/shard_map/latent_grad/pallas_call | solution.py:183
  16.5 0.1 collective-permute-start.1
  16.6 2.2 %collective-permute-done.1.grad_other = bf16[592,512]{1,0:T(8,128)(2,1)S(1)} collective-permute-done((bf16[592,512]{1,0:T(8,128)(2,1)}, bf16[592,512]{1,0:T(8,128)(2,1)S(1)}, u32[]{:S(2)}, u32[]{:S(2)}) %collective-permute-start.1) | collective-permute-done | bytes 606240 | tf_op jit(solution)/shard_map/ppermute | solution.py:43
  18.9 0.0 collective-permute-done.other
  18.9 0.8 copy-done.9
  19.7 9.7 %weight_grad.1 = (f32[2,1008,128]{2,1,0:T(8,128)}, bf16[4,2,1008,128]{3,2,1,0:T(8,128)(2,1)}, f32[4,1024,128]{2,1,0:T(8,128)}, bf16[4,1024,128]{2,1,0:T(8,128)(2,1)}) custom-call(bf16[512,7168]{1,0:T(8,128)(2,1)} %bitcast.88, bf16[512,7168]{1,0:T(8,128)(2,1)} %collective-permute-done.other, bf16[592,512]{1,0:T(8,128)(2,1)} %latent_grad.1.grad.refs_0_, ...), custom_call_target="tpu_custom_call" | custom-call | bytes 1000 | tf_op jit(solution)/shard_map/weight_grad/pallas_call | solution.py:289
  29.4 5.1 %all-to-all-start = ((bf16[4,2,1008,128]{3,2,1,0:T(8,128)(2,1)}), bf16[4,2,1008,128]{3,2,1,0:T(8,128)(2,1)}, u32[]{:S(2)}, u32[]{:S(2)}) async-start(bf16[4,2,1008,128]{3,2,1,0:T(8,128)(2,1)} %get-tuple-element.24), calls=%async_computation | async-start | bytes 4128768 | tf_op jit(solution)/shard_map/all_to_all | solution.py:511
  34.6 1.0 copy-done.6
  35.5 1.3 %collective-permute-start.3 = (bf16[4,1024,128]{2,1,0:T(8,128)(2,1)}, bf16[4,1024,128]{2,1,0:T(8,128)(2,1)}, u32[]{:S(2)}, u32[]{:S(2)}) collective-permute-start(bf16[4,1024,128]{2,1,0:T(8,128)(2,1)} %after.7), channel_id=1, source_target_pairs={{0,2},{1,3},{2,0},{3,1},{4,6},{5,7},{6,4},{7,5},{8,10},{9,11},{10,... | collective-permute-start | bytes 3145736 | tf_op jit(solution)/shard_map/ppermute | solution.py:43
  36.8 1.4 %collective-permute-start.7 = (bf16[2,288,896]{2,1,0:T(8,128)(2,1)}, bf16[2,288,896]{2,1,0:T(8,128)(2,1)}, u32[]{:S(2)}, u32[]{:S(2)}) collective-permute-start(bf16[2,288,896]{2,1,0:T(8,128)(2,1)} %after.10), channel_id=1, source_target_pairs={{16,2},{17,3},{18,0},{19,1},{20,6},{21,7},{22,4},{23,5},{24,10},{2... | collective-permute-start | bytes 3096584 | tf_op jit(solution)/shard_map/ppermute | solution.py:43
  38.2 21.9 %collective-permute-done.3.refs_1_ = bf16[4,1024,128]{2,1,0:T(8,128)(2,1)} collective-permute-done((bf16[4,1024,128]{2,1,0:T(8,128)(2,1)}, bf16[4,1024,128]{2,1,0:T(8,128)(2,1)}, u32[]{:S(2)}, u32[]{:S(2)}) %collective-permute-start.3) | collective-permute-done | bytes 1048608 | tf_op jit(solution)/shard_map/ppermute | solution.py:43
  60.1 1.3 collective-permute-start.4
  61.4 2.4 %add_convert_fusion = bf16[4,1024,128]{2,1,0:T(8,128)(2,1)} fusion(f32[4,1024,128]{2,1,0:T(8,128)S(1)} %copy-done.8, bf16[4,1024,128]{2,1,0:T(8,128)(2,1)} %collective-permute-done.3.refs_1_), kind=kLoop, calls=%fused_computation | loop fusion | flops 1572864 | bytes 4194304 | tf_op jit(solution)/shard_map/convert_element_type | solution.py:517
  63.9 4.9 %all-to-all-start.1 = ((bf16[4,1024,128]{2,1,0:T(8,128)(2,1)}), bf16[4,1024,128]{2,1,0:T(8,128)(2,1)}, u32[]{:S(2)}, u32[]{:S(2)}) async-start(bf16[4,1024,128]{2,1,0:T(8,128)(2,1)} %add_convert_fusion), calls=%async_computation.1 | async-start | bytes 2097152 | tf_op jit(solution)/shard_map/all_to_all | solution.py:511
  68.8 1.6 %fusion = bf16[1008,128]{1,0:T(8,128)(2,1)S(1)} fusion(f32[2,1008,128]{2,1,0:T(8,128)S(1)} %copy-done.7, bf16[4,2,1008,128]{3,2,1,0:T(8,128)(2,1)} %all-to-all-done, pred[]{:T(512)S(6)} %eq.11, pred[]{:T(512)S(6)} %eq.10, pred[]{:T(512)S(6)} %eq.9, pred[]{:T(512)S(6)} %eq.8), kind=kLoop, calls=%fused_computation.4 | loop fusion | flops 1677312 | bytes 1806340 | tf_op jit(solution)/shard_map/convert_element_type | solution.py:520
  70.3 1.4 %collective-permute-start.9 = (bf16[1008,128]{1,0:T(8,128)(2,1)S(1)}, bf16[1008,128]{1,0:T(8,128)(2,1)S(1)}, u32[]{:S(2)}, u32[]{:S(2)}) collective-permute-start(bf16[1008,128]{1,0:T(8,128)(2,1)S(1)} %fusion), channel_id=1, source_target_pairs={{0,2},{1,3},{2,0},{3,1},{4,6},{5,7},{6,4},{7,5},{8,10},{9,11},{10,... | collective-permute-start | bytes 774152 | tf_op jit(solution)/shard_map/ppermute | solution.py:43
  71.7 1.6 %collective-permute-start.8 = (bf16[2,288,896]{2,1,0:T(8,128)(2,1)}, bf16[2,288,896]{2,1,0:T(8,128)(2,1)}, u32[]{:S(2)}, u32[]{:S(2)}) collective-permute-start(bf16[2,288,896]{2,1,0:T(8,128)(2,1)} %collective-permute-done.7.rest_2_), channel_id=1, source_target_pairs={{0,1},{1,0},{2,3},{3,2},{4,5},{5,4},{6,7},{7,6},{8,9},{9,8},{10,11... | collective-permute-start | bytes 3096584 | tf_op jit(solution)/shard_map/ppermute | solution.py:43
  73.3 4.8 %collective-permute-done.4.refs_1_.grad = bf16[592,512]{1,0:T(8,128)(2,1)S(1)} collective-permute-done((bf16[592,512]{1,0:T(8,128)(2,1)S(1)}, bf16[592,512]{1,0:T(8,128)(2,1)S(1)}, u32[]{:S(2)}, u32[]{:S(2)}) %collective-permute-start.4) | collective-permute-done | bytes 606240 | tf_op jit(solution)/shard_map/ppermute | solution.py:43
  78.1 0.9 copy-done
  78.9 0.8 collective-permute-start.12
  79.8 4.7 %collective-permute-start.6 = (bf16[2,288,896]{2,1,0:T(8,128)(2,1)}, bf16[2,288,896]{2,1,0:T(8,128)(2,1)}, u32[]{:S(2)}, u32[]{:S(2)}) collective-permute-start(bf16[2,288,896]{2,1,0:T(8,128)(2,1)} %after.9.rest_0_), channel_id=1, source_target_pairs={{0,1},{1,0},{2,3},{3,2},{4,5},{5,4},{6,7},{7,6},{8,9},{9,8},{10,11... | collective-permute-start | bytes 3096584 | tf_op jit(solution)/shard_map/ppermute | solution.py:43
  84.5 1.4 %collective-permute-start.5 = (bf16[2,288,896]{2,1,0:T(8,128)(2,1)}, bf16[2,288,896]{2,1,0:T(8,128)(2,1)}, u32[]{:S(2)}, u32[]{:S(2)}) collective-permute-start(bf16[2,288,896]{2,1,0:T(8,128)(2,1)} %after.9.rest_0_), channel_id=1, source_target_pairs={{0,12},{1,13},{2,14},{3,15},{4,0},{5,1},{6,2},{7,3},{8,4},{9,5},{1... | collective-permute-start | bytes 3096584 | tf_op jit(solution)/shard_map/ppermute | solution.py:43
  85.9 0.5 collective-permute-done.9.refs_0_
  86.4 1.1 copy-done.1
  87.5 2.6 %fusion.15 = (bf16[1008,128]{1,0:T(8,128)(2,1)S(1)}, f32[1008,128]{1,0:T(8,128)}) fusion(bf16[1008,128]{1,0:T(8,128)(2,1)S(1)} %after.11, bf16[4,2,1008,128]{3,2,1,0:T(8,128)(2,1)} %all-to-all-done, pred[]{:T(512)S(6)} %eq.11, pred[]{:T(512)S(6)} %eq.10, pred[]{:T(512)S(6)} %eq.9, pred[]{:T(512)S(6)} %eq.8, f32[2,1008,128]{2,1,0:T(8,128)} %get-tuple-element.23.refs_1_), kind=kLoop, calls=%fused_computation.36 | loop fusion | flops 1935360 | bytes 2580484 | tf_op jit(solution)/shard_map/convert.2
  90.1 2.5 %fusion.17 = (bf16[1024,128]{1,0:T(8,128)(2,1)S(1)}, f32[1024,128]{1,0:T(8,128)}) fusion(bf16[4,1024,128]{2,1,0:T(8,128)(2,1)} %all-to-all-done.1, pred[]{:T(512)S(6)} %eq.11, pred[]{:T(512)S(6)} %eq.10, pred[]{:T(512)S(6)} %eq.9, pred[]{:T(512)S(6)} %eq.8, bf16[4,1024,128]{2,1,0:T(8,128)(2,1)} %collective-permute-done.3.refs_1_, s32[]{:T(128)S(6)} %select_n.129, ...), kind=kLoop, calls=%fused_computation.37 | loop fusion | flops 1966080 | bytes 2621448 | tf_op jit(solution)/shard_map/convert.3
  92.6 0.0 copy-start.11
  92.6 4.2 %collective-permute-start.10 = (bf16[2032,128]{1,0:T(8,128)(2,1)S(1)}, bf16[2032,128]{1,0:T(8,128)(2,1)S(1)}, u32[]{:S(2)}, u32[]{:S(2)}) collective-permute-start(bf16[2032,128]{1,0:T(8,128)(2,1)S(1)} %pad_maximum_fusion.rest_4_), channel_id=1, source_target_pairs={{0,112},{1,113},{2,114},{3,115},{4,116},{5,117},{6,118},{7,119},{8... | collective-permute-start | bytes 1560584 | tf_op jit(solution)/shard_map/ppermute | solution.py:43
  96.9 7.8 %input_grad.2 = (bf16[512,7168]{1,0:T(8,128)(2,1)}, f32[8,128]{1,0:T(8,128)}) custom-call(bf16[592,512]{1,0:T(8,128)(2,1)} %copy-done, bf16[2,288,896]{2,1,0:T(8,128)(2,1)} %after.9.rest_0_, bf16[2,288,896]{2,1,0:T(8,128)(2,1)} %collective-permute-done.6.rest_1_, bf16[2,288,896]{2,1,0:T(8,128)(2,1)} %collective-permute-done.7.rest_2_, ...), custom_call_target="tpu_custom_call" | custom-call | flops 2113929216 | bytes 8000000 | tf_op jit(solution)/shard_map/input_grad/pallas_call | solution.py:444
  104.7 3.9 %collective-permute-done.10.far = bf16[2032,128]{1,0:T(8,128)(2,1)S(1)} collective-permute-done((bf16[2032,128]{1,0:T(8,128)(2,1)S(1)}, bf16[2032,128]{1,0:T(8,128)(2,1)S(1)}, u32[]{:S(2)}, u32[]{:S(2)}) %collective-permute-start.10) | collective-permute-done | bytes 520224 | tf_op jit(solution)/shard_map/ppermute | solution.py:43
  108.6 0.8 copy-done.10
  109.4 4.6 %adamw.1 = (f32[448,576]{1,0:T(8,128)}, f32[448,576]{1,0:T(8,128)}, f32[448,576]{1,0:T(8,128)}, f32[8,128]{1,0:T(8,128)}) custom-call(f32[1008,128]{1,0:T(8,128)} %get-tuple-element.37.own_a, f32[1024,128]{1,0:T(8,128)} %get-tuple-element.39.own_b, bf16[2032,128]{1,0:T(8,128)(2,1)} %copy-done.10, f32[448,576]{1,0:T(8,128)} %bitcast.90, f32[448,576]{1,0:T(8,128)} %bitcast.91, ...), custom_call_target="tpu_custom_call" | custom-call | bytes 9000000 | tf_op jit(solution)/shard_map/adamw/pallas_call | solution.py:382
  114.0 0.0 copy-start.14
  114.0 0.0 copy-start.15
  114.0 0.0 copy-start.16
  114.1 2.0 %collective-permute-start.11 = (bf16[2,288,896]{2,1,0:T(8,128)(2,1)}, bf16[2,288,896]{2,1,0:T(8,128)(2,1)}, u32[]{:S(2)}, u32[]{:S(2)}) collective-permute-start(bf16[2,288,896]{2,1,0:T(8,128)(2,1)} %after.12.rest_0_), channel_id=1, source_target_pairs={{0,1},{1,0},{2,3},{3,2},{4,5},{5,4},{6,7},{7,6},{8,9},{9,8},{10,11... | collective-permute-start | bytes 3096584 | tf_op jit(solution)/shard_map/ppermute | solution.py:43
  116.1 1.0 copy-done.4
  117.1 0.0 collective-permute-start.13
  117.1 0.6 fusion.13
  117.7 1.0 collective-permute-done.11.rest_1_
  118.7 1.3 %collective-permute-done.13.rest_3_ = bf16[2,288,896]{2,1,0:T(8,128)(2,1)S(1)} collective-permute-done((bf16[2,288,896]{2,1,0:T(8,128)(2,1)}, bf16[2,288,896]{2,1,0:T(8,128)(2,1)S(1)}, u32[]{:S(2)}, u32[]{:S(2)}) %collective-permute-start.13) | collective-permute-done | bytes 1032224 | tf_op jit(solution)/shard_map/ppermute | solution.py:43
  120.1 1.2 copy-done.5
  121.3 7.2 %input_grad.3 = (bf16[512,7168]{1,0:T(8,128)(2,1)}, f32[8,128]{1,0:T(8,128)}) custom-call(bf16[592,512]{1,0:T(8,128)(2,1)S(1)} %copy-done.2, bf16[2,288,896]{2,1,0:T(8,128)(2,1)} %after.12.rest_0_, bf16[2,288,896]{2,1,0:T(8,128)(2,1)} %collective-permute-done.11.rest_1_, bf16[2,288,896]{2,1,0:T(8,128)(2,1)S(1)} %copy-done.5, ...), custom_call_target="tpu_custom_call", output_to_operand_aliasing={{0}: (5, {})} | custom-call | flops 2113929216 | bytes 8000000 | tf_op jit(solution)/shard_map/input_grad/pallas_call | solution.py:444
  (43 shorter events, 0.1 us)
Async XLA Ops:
  0.6 18.2 %collective-permute-start = (bf16[512,7168]{1,0:T(8,128)(2,1)}, bf16[512,7168]{1,0:T(8,128)(2,1)}, u32[]{:S(2)}, u32[]{:S(2)}) collective-permute-start(bf16[512,7168]{1,0:T(8,128)(2,1)} %bitcast.86), channel_id=1, source_target_pairs={{0,1},{1,0},{2,3},{3,2},{4,5},{5,4},{6,7},{7,6},{8,9},{9,8},{10,11... | collective-permute-start | bytes 22020104 | tf_op jit(solution)/shard_map/ppermute | solution.py:43
  2.1 4.2 %copy-start.12 = (bf16[1,512,64]{1,2,0:T(8,128)(2,1)S(1)}, bf16[1,512,64]{1,2,0:T(8,128)(2,1)}, u32[]{:S(2)}) copy-start(bf16[1,512,64]{1,2,0:T(8,128)(2,1)} %param.15) | copy-start | bytes 196612
  5.0 29.5 %collective-permute-start.2 = (bf16[2,288,896]{2,1,0:T(8,128)(2,1)}, bf16[2,288,896]{2,1,0:T(8,128)(2,1)S(1)}, u32[]{:S(2)}, u32[]{:S(2)}) collective-permute-start(bf16[2,288,896]{2,1,0:T(8,128)(2,1)} %get-tuple-element.20.earlier), channel_id=1, source_target_pairs={{16,2},{17,3},{18,0},{19,1},{20,6},{21,7},{22,4},{23,5},{24,10},{2... | collective-permute-start | bytes 3096584 | tf_op jit(solution)/shard_map/ppermute | solution.py:43
  16.5 2.3 %collective-permute-start.1 = (bf16[592,512]{1,0:T(8,128)(2,1)}, bf16[592,512]{1,0:T(8,128)(2,1)S(1)}, u32[]{:S(2)}, u32[]{:S(2)}) collective-permute-start(bf16[592,512]{1,0:T(8,128)(2,1)} %latent_grad.1.grad.refs_0_), channel_id=1, source_target_pairs={{0,1},{1,0},{2,3},{3,2},{4,5},{5,4},{6,7},{7,6},{8,9},{9,8},{10,11... | collective-permute-start | bytes 1818632 | tf_op jit(solution)/shard_map/ppermute | solution.py:43
  18.9 0.8 copy-start.9
  29.4 34.5 %all-to-all-start = ((bf16[4,2,1008,128]{3,2,1,0:T(8,128)(2,1)}), bf16[4,2,1008,128]{3,2,1,0:T(8,128)(2,1)}, u32[]{:S(2)}, u32[]{:S(2)}) async-start(bf16[4,2,1008,128]{3,2,1,0:T(8,128)(2,1)} %get-tuple-element.24), calls=%async_computation | async-start | bytes 4128768 | tf_op jit(solution)/shard_map/all_to_all | solution.py:511
  34.6 1.0 copy-start.6
  35.5 24.6 %copy-start.3 = (bf16[592,512]{1,0:T(8,128)(2,1)S(1)}, bf16[592,512]{1,0:T(8,128)(2,1)}, u32[]{:S(2)}) copy-start(bf16[592,512]{1,0:T(8,128)(2,1)} %latent_grad.1.grad.refs_0_) | copy-start | bytes 1818628
  35.5 24.6 %collective-permute-start.3 = (bf16[4,1024,128]{2,1,0:T(8,128)(2,1)}, bf16[4,1024,128]{2,1,0:T(8,128)(2,1)}, u32[]{:S(2)}, u32[]{:S(2)}) collective-permute-start(bf16[4,1024,128]{2,1,0:T(8,128)(2,1)} %after.7), channel_id=1, source_target_pairs={{0,2},{1,3},{2,0},{3,1},{4,6},{5,7},{6,4},{7,5},{8,10},{9,11},{10,... | collective-permute-start | bytes 3145736 | tf_op jit(solution)/shard_map/ppermute | solution.py:43
  36.8 24.6 %copy-start.8 = (f32[4,1024,128]{2,1,0:T(8,128)S(1)}, f32[4,1024,128]{2,1,0:T(8,128)}, u32[]{:S(2)}) copy-start(f32[4,1024,128]{2,1,0:T(8,128)} %get-tuple-element.25) | copy-start | bytes 6291460
  36.8 34.9 %collective-permute-start.7 = (bf16[2,288,896]{2,1,0:T(8,128)(2,1)}, bf16[2,288,896]{2,1,0:T(8,128)(2,1)}, u32[]{:S(2)}, u32[]{:S(2)}) collective-permute-start(bf16[2,288,896]{2,1,0:T(8,128)(2,1)} %after.10), channel_id=1, source_target_pairs={{16,2},{17,3},{18,0},{19,1},{20,6},{21,7},{22,4},{23,5},{24,10},{2... | collective-permute-start | bytes 3096584 | tf_op jit(solution)/shard_map/ppermute | solution.py:43
  60.1 17.9 %collective-permute-start.4 = (bf16[592,512]{1,0:T(8,128)(2,1)S(1)}, bf16[592,512]{1,0:T(8,128)(2,1)S(1)}, u32[]{:S(2)}, u32[]{:S(2)}) collective-permute-start(bf16[592,512]{1,0:T(8,128)(2,1)S(1)} %after.8), channel_id=1, source_target_pairs={{16,0},{17,1},{18,2},{19,3},{20,4},{21,5},{22,6},{23,7},{24,8},{25... | collective-permute-start | bytes 1818632 | tf_op jit(solution)/shard_map/ppermute | solution.py:43
  63.9 4.9 %copy-start.7 = (f32[2,1008,128]{2,1,0:T(8,128)S(1)}, f32[2,1008,128]{2,1,0:T(8,128)}, u32[]{:S(2)}) copy-start(f32[2,1008,128]{2,1,0:T(8,128)} %get-tuple-element.23.refs_1_) | copy-start | bytes 3096580
  63.9 26.2 %all-to-all-start.1 = ((bf16[4,1024,128]{2,1,0:T(8,128)(2,1)}), bf16[4,1024,128]{2,1,0:T(8,128)(2,1)}, u32[]{:S(2)}, u32[]{:S(2)}) async-start(bf16[4,1024,128]{2,1,0:T(8,128)(2,1)} %add_convert_fusion), calls=%async_computation.1 | async-start | bytes 2097152 | tf_op jit(solution)/shard_map/all_to_all | solution.py:511
  70.3 16.1 %collective-permute-start.9 = (bf16[1008,128]{1,0:T(8,128)(2,1)S(1)}, bf16[1008,128]{1,0:T(8,128)(2,1)S(1)}, u32[]{:S(2)}, u32[]{:S(2)}) collective-permute-start(bf16[1008,128]{1,0:T(8,128)(2,1)S(1)} %fusion), channel_id=1, source_target_pairs={{0,2},{1,3},{2,0},{3,1},{4,6},{5,7},{6,4},{7,5},{8,10},{9,11},{10,... | collective-permute-start | bytes 774152 | tf_op jit(solution)/shard_map/ppermute | solution.py:43
  71.7 25.2 %collective-permute-start.8 = (bf16[2,288,896]{2,1,0:T(8,128)(2,1)}, bf16[2,288,896]{2,1,0:T(8,128)(2,1)}, u32[]{:S(2)}, u32[]{:S(2)}) collective-permute-start(bf16[2,288,896]{2,1,0:T(8,128)(2,1)} %collective-permute-done.7.rest_2_), channel_id=1, source_target_pairs={{0,1},{1,0},{2,3},{3,2},{4,5},{5,4},{6,7},{7,6},{8,9},{9,8},{10,11... | collective-permute-start | bytes 3096584 | tf_op jit(solution)/shard_map/ppermute | solution.py:43
  78.1 0.9 copy-start
  78.9 37.2 %collective-permute-start.12 = (bf16[2,288,896]{2,1,0:T(8,128)(2,1)}, bf16[2,288,896]{2,1,0:T(8,128)(2,1)S(1)}, u32[]{:S(2)}, u32[]{:S(2)}) collective-permute-start(bf16[2,288,896]{2,1,0:T(8,128)(2,1)} %after.9.rest_0_), channel_id=1, source_target_pairs={{0,4},{1,5},{2,6},{3,7},{4,8},{5,9},{6,10},{7,11},{8,12},{9,13},{1... | collective-permute-start | bytes 3096584 | tf_op jit(solution)/shard_map/ppermute | solution.py:43
  79.8 17.1 %collective-permute-start.6 = (bf16[2,288,896]{2,1,0:T(8,128)(2,1)}, bf16[2,288,896]{2,1,0:T(8,128)(2,1)}, u32[]{:S(2)}, u32[]{:S(2)}) collective-permute-start(bf16[2,288,896]{2,1,0:T(8,128)(2,1)} %after.9.rest_0_), channel_id=1, source_target_pairs={{0,1},{1,0},{2,3},{3,2},{4,5},{5,4},{6,7},{7,6},{8,9},{9,8},{10,11... | collective-permute-start | bytes 3096584 | tf_op jit(solution)/shard_map/ppermute | solution.py:43
  84.5 29.5 %collective-permute-start.5 = (bf16[2,288,896]{2,1,0:T(8,128)(2,1)}, bf16[2,288,896]{2,1,0:T(8,128)(2,1)}, u32[]{:S(2)}, u32[]{:S(2)}) collective-permute-start(bf16[2,288,896]{2,1,0:T(8,128)(2,1)} %after.9.rest_0_), channel_id=1, source_target_pairs={{0,12},{1,13},{2,14},{3,15},{4,0},{5,1},{6,2},{7,3},{8,4},{9,5},{1... | collective-permute-start | bytes 3096584 | tf_op jit(solution)/shard_map/ppermute | solution.py:43
  86.4 1.1 copy-start.1
  92.6 4.2 %copy-start.11 = (bf16[2032,128]{1,0:T(8,128)(2,1)}, bf16[2032,128]{1,0:T(8,128)(2,1)S(1)}, u32[]{:S(2)}) copy-start(bf16[2032,128]{1,0:T(8,128)(2,1)S(1)} %pad_maximum_fusion.rest_4_) | copy-start | bytes 1560580
  92.6 16.0 %collective-permute-start.10 = (bf16[2032,128]{1,0:T(8,128)(2,1)S(1)}, bf16[2032,128]{1,0:T(8,128)(2,1)S(1)}, u32[]{:S(2)}, u32[]{:S(2)}) collective-permute-start(bf16[2032,128]{1,0:T(8,128)(2,1)S(1)} %pad_maximum_fusion.rest_4_), channel_id=1, source_target_pairs={{0,112},{1,113},{2,114},{3,115},{4,116},{5,117},{6,118},{7,119},{8... | collective-permute-start | bytes 1560584 | tf_op jit(solution)/shard_map/ppermute | solution.py:43
  108.6 0.8 copy-start.10
  114.0 3.1 %copy-start.13 = (f32[8,128]{1,0:T(8,128)S(1)}, f32[8,128]{1,0:T(8,128)}, u32[]{:S(2)}) copy-start(f32[8,128]{1,0:T(8,128)} %get-tuple-element.27.refs_2_) | copy-start | bytes 12292
  114.0 3.1 %copy-start.14 = (f32[1,32]{1,0:T(1,128)S(1)}, f32[1,32]{1,0:T(1,128)}, u32[]{:S(2)}) copy-start(f32[1,32]{1,0:T(1,128)} %param.19) | copy-start | bytes 388
  114.0 3.1 %copy-start.15 = (f32[1,32]{1,0:T(1,128)S(1)}, f32[1,32]{1,0:T(1,128)}, u32[]{:S(2)}) copy-start(f32[1,32]{1,0:T(1,128)} %param.20) | copy-start | bytes 388
  114.0 3.1 %copy-start.16 = (f32[1,32]{1,0:T(1,128)S(1)}, f32[1,32]{1,0:T(1,128)}, u32[]{:S(2)}) copy-start(f32[1,32]{1,0:T(1,128)} %param.21) | copy-start | bytes 388
  114.0 6.0 %copy-start.2 = (bf16[592,512]{1,0:T(8,128)(2,1)S(1)}, bf16[592,512]{1,0:T(8,128)(2,1)}, u32[]{:S(2)}) copy-start(bf16[592,512]{1,0:T(8,128)(2,1)} %copy-done) | copy-start | bytes 1818628
  114.1 4.6 %collective-permute-start.11 = (bf16[2,288,896]{2,1,0:T(8,128)(2,1)}, bf16[2,288,896]{2,1,0:T(8,128)(2,1)}, u32[]{:S(2)}, u32[]{:S(2)}) collective-permute-start(bf16[2,288,896]{2,1,0:T(8,128)(2,1)} %after.12.rest_0_), channel_id=1, source_target_pairs={{0,1},{1,0},{2,3},{3,2},{4,5},{5,4},{6,7},{7,6},{8,9},{9,8},{10,11... | collective-permute-start | bytes 3096584 | tf_op jit(solution)/shard_map/ppermute | solution.py:43
  116.1 1.0 copy-start.4
  117.1 3.0 %collective-permute-start.13 = (bf16[2,288,896]{2,1,0:T(8,128)(2,1)}, bf16[2,288,896]{2,1,0:T(8,128)(2,1)S(1)}, u32[]{:S(2)}, u32[]{:S(2)}) collective-permute-start(bf16[2,288,896]{2,1,0:T(8,128)(2,1)} %after.13.rest_2_), channel_id=1, source_target_pairs={{0,1},{1,0},{2,3},{3,2},{4,5},{5,4},{6,7},{7,6},{8,9},{9,8},{10,11... | collective-permute-start | bytes 3096584 | tf_op jit(solution)/shard_map/ppermute | solution.py:43
  120.1 1.2 copy-start.5
